TPU v7x, 32 devices: a whole 2x2x4 slice. The times are simulated.
32 devices in a mesh: groups: 2 (over y), tm: 4 (over z), space: 4 (over x, core).
Axes of the slice: x: 2, y: 2, z: 4, core: 2. Of those that a mesh axis runs over, the one named last changes fastest.
Arguments:
- forcing: bfloat16 [128, 512, 128], P('tm', ('groups', 'space')), parts along dimension 1, may hold values from -6 to 6
- initial_state: float32 [512, 128], P(('groups', 'space')), parts along dimension 0, may hold values from -6 to 6
- connectivity: int32 [256, 6], P('space'), may hold values from -16 to 271, as said below
- pattern: int32 [256, 6], P('space'), may hold values 0 or 1
- diag_block: float32 [128, 128], replicated, may hold values from -0.3125 to 0.3125
- face_blocks: float32 [6, 128, 128], replicated, may hold values from -0.15625 to 0.15625
- coarse_block: float32 [128, 128], replicated, may hold values from -1 to 1
Outputs:
- solution: float32 [128, 512, 128], P('tm', ('groups', 'space')), parts along dimension 1
There are 2 independent parts, one for each index of `groups`. A program takes and returns all parts, laid end to end along the dimension named above; an argument that names none is the same for every part. Nothing has to cross between parts.
Inputs may be any that keep to these rules, and one draw needn't show every extreme that they name: `connectivity`: faces 0 and 3 of element e connect to e - 1 and e + 1, faces 2 and 5 to e - 16 and e + 16, face 1 to an element 2 to 15 below e and face 4 to one 2 to 15 above e; values outside 0 to 255 stand for no element.
All inputs are finite; a program needn't handle non-finite values. No bound on the sum of `pattern` on one device may be relied on, other than what follows from the above.
Results may differ from a plain program's by a relative error of at most 0.0003.
Values may be sent and summed in bfloat16 or wider, within the bound.
No kernel may reach another device: no remote copies, remote signals or barrier semaphores. Data moves between devices by JAX's collectives and lax.ppermute only.
A program may use at most 64 MiB of HBM per device.

v0:
```python
import functools

import jax
import jax.numpy as jnp
from jax import lax
from jax.experimental import pallas as pl
from jax.experimental.pallas import tpu as pltpu
from jax.sharding import PartitionSpec as P

COARSEN = 4
REACH = 16
F32 = jnp.float32
BF16 = jnp.bfloat16
CHUNK = 32
SCAN = 64


def shifted(value, steps):
    count = lax.axis_size("space")
    pairs = [(i, i + steps) for i in range(count) if 0 <= i + steps < count]
    return lax.ppermute(value, "space", pairs)


def split(u):
    lead = u.astype(BF16).astype(F32)
    return jnp.concatenate([u, u - lead], axis=1).astype(BF16)


def product(x, weights):
    m = x.shape[0] // 16
    r = jnp.dot(x, weights, preferred_element_type=F32).reshape(m, 16, 256)
    return r[:, :8, :128] + (r[:, 8:, :128] + r[:, :8, 128:])


def product_rows(u, weights):
    return product(split(u).reshape(-1, 128), weights)


def put_halves(ref, w):
    lead = w.astype(BF16)
    ref[:, 0:128] = lead
    ref[:, 128:256] = (w - lead.astype(F32)).astype(BF16)


def scan_tiles(y, pw):
    row = lax.broadcasted_iota(jnp.int32, y.shape, 1)
    for level in range(3):
        d = 1 << level
        z = product_rows(y, pw[pl.ds(level * 128, 128), :])
        y = y + jnp.where(row >= d, pltpu.roll(z, d, axis=1), 0.0)
    return y


def apply_phi(src, idx, w, low, high, emit):
    def body(c, carry):
        base = low + c * CHUNK
        cols = [src[pl.ds(base, CHUNK)].reshape(CHUNK * 16, 128)]
        for f in range(6):
            cols.append(jnp.concatenate([src[idx[f, base + e]] for e in range(CHUNK)], axis=0))
        emit(base, product(jnp.concatenate(cols, axis=1), w[...]))
        return carry

    lax.fori_loop(0, (high - low) // CHUNK, body, 0)


def entering(ag, we, out, n):
    t, x, count = lax.axis_index("tm"), lax.axis_index("space"), lax.axis_size("space")
    left_on = (x > 0).astype(F32)
    right_on = (x < count - 1).astype(F32)
    at = [jnp.maximum(x - 1, 0) * n, x * n, jnp.minimum(x + 1, count - 1) * n]
    out[...] = jnp.zeros_like(out)

    def body(s, carry):
        parts = [ag[s, pl.ds(pl.multiple_of(a, n), n), :] for a in at]
        value = jnp.concatenate([parts[0] * left_on, parts[1], parts[2] * right_on], axis=0)
        m = value.shape[0]
        lead = value.astype(BF16)
        rest = (value - lead.astype(F32)).astype(BF16)
        r = jnp.dot(jnp.concatenate([lead, rest], axis=0), we[s], preferred_element_type=F32)
        out[...] += r[:m, :128] + (r[m:, :128] + r[:m, 128:])
        return carry

    lax.fori_loop(0, t, body, 0)


def pack_kernel(forcing, init, conn, pattern, fe, tab, pay_left, pay_right, rows, square):
    n = init.shape[0]
    stride = COARSEN * n
    step = 256
    for at in range(0, rows.shape[0], step):
        rows[pl.ds(at, step), :] = forcing[pl.ds(at, step), :].astype(F32)

    def body(pair, carry):
        e = pair * 2
        for k in range(COARSEN):
            two = [rows[pl.ds(k * n + e + j, 8, stride=stride), :] for j in range(2)]
            fe[k, pl.ds(pl.multiple_of(e * 8, 16), 16), :] = jnp.concatenate(two, axis=0).astype(BF16)
        return carry

    lax.fori_loop(0, n // 2, body, 0, unroll=4)
    place = lax.broadcasted_iota(jnp.int32, (n, 6), 0) + lax.axis_index("space") * n
    offs = ((conn[...] - place) * pattern[...]).astype(F32)
    square[...] = jnp.zeros_like(square)
    square[0:n, 0:6] = offs
    square[n : 2 * n, 0:6] = offs
    tab[...] = square[...].T[0:16, :].astype(BF16)
    lead = init[...].astype(BF16)
    rest = (init[...] - lead.astype(F32)).astype(BF16)
    at = 0
    for k in range(COARSEN - 1):
        width = (COARSEN - 1 - k) * REACH * 8
        pay_left[pl.ds(at, width), :] = fe[k, pl.ds(0, width), :]
        pay_right[pl.ds(at, width), :] = fe[k, pl.ds(n * 8 - width, width), :]
        at += width
    for pay in (pay_left, pay_right):
        pay[pl.ds(at, n), :] = lead
        pay[pl.ds(at + n, n), :] = rest
        pay[pl.ds(at + 2 * n, 16), :] = tab[...]


def weight_kernel(diag, faces, coarse, w, pw, we):
    put_halves(w.at[pl.ds(0, 128)], diag[...].T)
    for f in range(6):
        put_halves(w.at[pl.ds(128 * (f + 1), 128)], faces[f].T)

    def thirds(a):
        one = a.astype(BF16)
        rest = a - one.astype(F32)
        two = rest.astype(BF16)
        return one, two, (rest - two.astype(F32)).astype(BF16)

    def mul(a, b):
        (a1, a2, a3), (b1, b2, b3) = thirds(a), thirds(b)
        total = jnp.zeros((128, 128), F32)
        for x, y in ((a3, b1), (a1, b3), (a2, b2), (a2, b1), (a1, b2), (a1, b1)):
            total += jnp.dot(x, y, preferred_element_type=F32)
        return total

    power = coarse[...].T
    for level in range(3):
        put_halves(pw.at[pl.ds(128 * level, 128)], power)
        power = mul(power, power)
    t = lax.axis_index("tm")
    we[...] = jnp.zeros_like(we)
    one = (lax.broadcasted_iota(jnp.int32, (128, 128), 0) == lax.broadcasted_iota(jnp.int32, (128, 128), 1)).astype(F32)

    def body(k, current):
        put_halves(we.at[t - 1 - k], current)
        return mul(current, power)

    lax.fori_loop(0, t, body, one)


def window(dst, left, own, right, k, low, n):
    at = sum((COARSEN - 1 - j) * REACH * 8 for j in range(k))
    have = (COARSEN - 1 - k) * REACH * 8
    side = (n - low) * 8
    if side:
        dst[pl.ds(0, side), :] = left[pl.ds(at + have - side, side), :]
        dst[pl.ds(side + n * 8, side), :] = right[pl.ds(at, side), :]
    dst[pl.ds(side, n * 8), :] = own[k]


def first_kernel(fe, tab, init, left, right, w, pw, w1, end, idx_out, iw, s0, s1, fx, y, idx_v, idx, sem):
    n = init.shape[0]
    full = 3 * n
    tail = left.shape[0] - 16
    lane = lax.broadcasted_iota(jnp.int32, (8, 128), 1)

    def table(ref, at):
        return ref[pl.ds(at, 16), :].astype(F32)[0:8]

    low = jnp.where(lane < n, table(left, tail), table(tab, 0))
    high = jnp.where(lane < n, table(right, tail), 0.0)
    for at, offs in ((0, low), (128, high)):
        value = jnp.where(offs != 0.0, lane + at + offs.astype(jnp.int32), full)
        idx_v[:, pl.ds(at, 128)] = value
        idx_out[:, pl.ds(at, 128)] = value
    copy = pltpu.make_async_copy(idx_v, idx, sem)
    copy.start()

    first = (lax.axis_index("tm") == 0).astype(F32)

    def joined(ref):
        return ref[pl.ds(tail - 2 * n, n), :].astype(F32) + ref[pl.ds(tail - n, n), :].astype(F32)

    iw[pl.ds(0, n), :] = joined(left) * first
    iw[pl.ds(n, n), :] = init[...] * first
    iw[pl.ds(2 * n, n), :] = joined(right) * first
    y[...] = jnp.zeros_like(y)
    y[pl.ds(0, full, stride=8), :] = iw[...]

    def fill(c, carry):
        at = c * CHUNK
        s0[pl.ds(at, CHUNK)] = split(y[pl.ds(pl.multiple_of(at * 8, CHUNK * 8), CHUNK * 8), :].reshape(CHUNK, 8, 128))
        return carry

    lax.fori_loop(0, full // CHUNK, fill, 0)
    s0[full] = jnp.zeros((16, 128), BF16)
    s1[full] = jnp.zeros((16, 128), BF16)
    copy.wait()
    bufs = [s0, s1]
    for k in range(COARSEN):
        lo = (k + 1) * REACH
        window(fx, left, fe, right, k, lo, n)
        src, dst = bufs[k % 2], bufs[(k + 1) % 2]

        def emit(base, value, lo=lo, dst=dst, last=k == COARSEN - 1):
            at = pl.multiple_of((base - lo) * 8, CHUNK * 8)
            value = value + fx[pl.ds(at, CHUNK * 8), :].astype(F32).reshape(CHUNK, 8, 128)
            if last:
                w1[pl.ds(base - lo, CHUNK)] = value
            else:
                dst[pl.ds(base, CHUNK)] = split(value)

        apply_phi(src, idx, w, lo, full - lo, emit)
    y[pl.ds(0, n * 8), :] = scan_tiles(w1[...], pw).reshape(n * 8, 128)
    end[...] = y[pl.ds(7, n, stride=8), :]


def second_kernel(idx, own, left, right, ag, w, pw, we, res, res_left, res_right, end, total, start, s0, s1, y, ent):
    n = own.shape[0]
    full = 3 * n
    entering(ag, we, ent, n)
    for j, ref in enumerate((left, own, right)):
        y[pl.ds(j * n * 8, n * 8), :] = pltpu.roll(ref[...], 1, axis=1).reshape(n * 8, 128)
    y[pl.ds(0, full, stride=8), :] = ent[...]

    def scan(c, carry):
        rows = pl.ds(pl.multiple_of(c * SCAN * 8, SCAN * 8), SCAN * 8)
        value = scan_tiles(y[rows, :].reshape(SCAN, 8, 128), pw)
        y[rows, :] = value.reshape(SCAN * 8, 128)
        s0[pl.ds(c * SCAN, SCAN)] = split(value)
        return carry

    lax.fori_loop(0, full // SCAN, scan, 0)
    start[...] = y[pl.ds(REACH * 8, (full - 2 * REACH) * 8), :]
    s0[full] = jnp.zeros((16, 128), BF16)
    s1[full] = jnp.zeros((16, 128), BF16)
    bufs = [s0, s1]
    for k in range(COARSEN):
        lo = (k + 1) * REACH
        src, dst = bufs[k % 2], bufs[(k + 1) % 2]

        def emit(base, value, lo=lo, dst=dst, last=k == COARSEN - 1):
            if last:
                at = base - lo
                total[pl.ds(at, CHUNK)] = value + own[pl.ds(at, CHUNK)]
                before = y[pl.ds(pl.multiple_of(base * 8, CHUNK * 8), CHUNK * 8), :].reshape(CHUNK, 8, 128)
                res[pl.ds(at, CHUNK)] = value - product_rows(before, pw[pl.ds(0, 128), :])
            else:
                dst[pl.ds(base, CHUNK)] = split(value)

        apply_phi(src, idx, w, lo, full - lo, emit)
    side = (COARSEN - 1) * REACH
    res_left[...] = res[pl.ds(0, side)]
    res_right[...] = res[pl.ds(n - side, side)]
    y[pl.ds(0, n * 8), :] = scan_tiles(res[...], pw).reshape(n * 8, 128)
    end[...] = y[pl.ds(7, n, stride=8), :]


def third_kernel(
    idx, own, left, right, ag, total, start, iw, fe, pay_left, pay_right, w, pw, we, out, s0, s1, fx, y, u, ent
):
    n = own.shape[0]
    full = 3 * n
    side = (COARSEN - 1) * REACH
    entering(ag, we, ent, n)
    y[pl.ds((n - side) * 8, side * 8), :] = pltpu.roll(left[...], 1, axis=1).reshape(side * 8, 128)
    y[pl.ds(n * 8, n * 8), :] = pltpu.roll(own[...], 1, axis=1).reshape(n * 8, 128)
    y[pl.ds(2 * n * 8, side * 8), :] = pltpu.roll(right[...], 1, axis=1).reshape(side * 8, 128)
    count = full - 2 * REACH
    y[pl.ds(REACH * 8, count, stride=8), :] = ent[pl.ds(REACH, count), :]
    stride = COARSEN * n

    def scan(c, carry):
        rows = pl.ds(pl.multiple_of((REACH + c * CHUNK) * 8, REACH * 8), CHUNK * 8)
        y[rows, :] = scan_tiles(y[rows, :].reshape(CHUNK, 8, 128), pw).reshape(CHUNK * 8, 128)
        return carry

    lax.fori_loop(0, count // CHUNK, scan, 0)
    corr = y[pl.ds(n * 8, n * 8), :].reshape(n, 8, 128)
    u[...] = product_rows(corr, pw[pl.ds(0, 128), :]) + total[...]

    def put(k):
        def body(e, carry):
            out[pl.ds(k * n + e, 8, stride=stride), :] = u[e]
            return carry

        lax.fori_loop(0, n, body, 0, unroll=8)

    put(COARSEN - 1)
    y[pl.ds(REACH * 8, count * 8), :] = y[pl.ds(REACH * 8, count * 8), :] + start[...]
    y[pl.ds(REACH * 8, count, stride=8), :] = y[pl.ds(REACH * 8, count, stride=8), :] + iw[pl.ds(REACH, count), :]

    def fill(c, carry):
        at = REACH + c * CHUNK
        rows = pl.ds(pl.multiple_of(at * 8, REACH * 8), CHUNK * 8)
        s0[pl.ds(at, CHUNK)] = split(y[rows, :].reshape(CHUNK, 8, 128))
        return carry

    lax.fori_loop(0, count // CHUNK, fill, 0)
    s0[full] = jnp.zeros((16, 128), BF16)
    s1[full] = jnp.zeros((16, 128), BF16)
    bufs = [s0, s1]
    for k in range(COARSEN - 1):
        lo = (k + 2) * REACH
        window(fx, pay_left, fe, pay_right, k, lo, n)
        src, dst = bufs[k % 2], bufs[(k + 1) % 2]

        def emit(base, value, lo=lo, dst=dst, last=k == COARSEN - 2):
            at = pl.multiple_of((base - lo) * 8, CHUNK * 8)
            value = value + fx[pl.ds(at, CHUNK * 8), :].astype(F32).reshape(CHUNK, 8, 128)
            y[pl.ds(pl.multiple_of(base * 8, REACH * 8), CHUNK * 8), :] = value.reshape(CHUNK * 8, 128)
            if not last:
                dst[pl.ds(base, CHUNK)] = split(value)

        apply_phi(src, idx, w, lo, full - lo, emit)
        u[...] = y[pl.ds(n * 8, n * 8), :].reshape(n, 8, 128)
        put(k)


def call(kernel, inputs, outs, scratch, smem=0, flops=0):
    specs = [pl.BlockSpec(memory_space=pltpu.SMEM)] * smem
    specs += [pl.BlockSpec(memory_space=pltpu.VMEM)] * (len(inputs) - smem)
    moved = sum(a.size * a.dtype.itemsize for a in list(inputs) + list(outs))
    return pl.pallas_call(
        kernel,
        out_shape=outs,
        name=kernel.__name__,
        in_specs=specs,
        out_specs=[pl.BlockSpec(memory_space=pltpu.VMEM)] * len(outs),
        scratch_shapes=scratch,
        compiler_params=pltpu.CompilerParams(vmem_limit_bytes=40 * 1024 * 1024),
        cost_estimate=pl.CostEstimate(flops=flops, bytes_accessed=moved, transcendentals=0),
    )(*inputs)


def local(forcing, initial_state, connectivity, pattern, diag_block, face_blocks, coarse_block):
    n, width = initial_state.shape
    steps = forcing.shape[0]
    full = 3 * n
    tm = lax.axis_size("tm")
    space = lax.axis_size("space")
    shape = jax.ShapeDtypeStruct
    tile = shape((n, 8, width), F32)
    ends = shape((n, width), F32)
    step_flops = 2 * 16 * 7 * width * 2 * width
    pay_rows = sum((COARSEN - 1 - k) * REACH * 8 for k in range(COARSEN)) + 2 * n + 16
    pay = shape((pay_rows, width), BF16)
    fe, tab, pay_left, pay_right = call(
        pack_kernel,
        (forcing.reshape(steps * n, width), initial_state, connectivity, pattern),
        (shape((COARSEN, n * 8, width), BF16), shape((16, 128), BF16), pay, pay),
        [pltpu.VMEM((steps * n, width), F32), pltpu.VMEM((128, 128), F32)],
        flops=10**6,
    )
    from_left, from_right = shifted(pay_right, 1), shifted(pay_left, -1)
    w, pw, we = call(
        weight_kernel,
        (diag_block, face_blocks, coarse_block),
        (shape((7 * width, 2 * width), BF16), shape((3 * width, 2 * width), BF16), shape((tm, width, 2 * width), BF16)),
        [],
        flops=10**9,
    )
    state = pltpu.VMEM((full + 1, 16, width), BF16)
    rows = pltpu.VMEM((full * 8, width), F32)
    force = pltpu.VMEM(((full - 2 * REACH) * 8, width), BF16)
    w1, end, idx, iw = call(
        first_kernel,
        (fe, tab, initial_state, from_left, from_right, w, pw),
        (tile, ends, shape((8, 256), jnp.int32), shape((full, width), F32)),
        [state, state, force, rows, pltpu.VMEM((8, 256), jnp.int32), pltpu.SMEM((8, 256), jnp.int32), pltpu.SemaphoreType.DMA],
        flops=step_flops * 7 * n,
    )

    def gathered(value):
        return lax.all_gather(value, ("tm", "space"), axis=0, tiled=True).reshape(tm, space * n, width)

    ag = gathered(end)
    left, right = shifted(w1, 1), shifted(w1, -1)
    side = shape(((COARSEN - 1) * REACH, 8, width), F32)
    entry = pltpu.VMEM((full, width), F32)
    res, res_left, res_right, end, total, start = call(
        second_kernel,
        (idx, w1, left, right, ag, w, pw, we),
        (tile, side, side, ends, tile, shape(((full - 2 * REACH) * 8, width), F32)),
        [state, state, rows, entry],
        smem=1,
        flops=step_flops * 7 * n,
    )
    ag = gathered(end)
    left, right = shifted(res_right, 1), shifted(res_left, -1)
    (out,) = call(
        third_kernel,
        (idx, res, left, right, ag, total, start, iw, fe, from_left, from_right, w, pw, we),
        (shape((steps * n, width), F32),),
        [state, state, force, rows, pltpu.VMEM((n, 8, width), F32), entry],
        smem=1,
        flops=step_flops * 5 * n,
    )
    return out.reshape(steps, n, width)


def solution(mesh):
    return jax.shard_map(
        local,
        mesh=mesh,
        in_specs=(
            P("tm", ("groups", "space"), None),
            P(("groups", "space"), None),
            P("space", None),
            P("space", None),
            P(),
            P(),
            P(),
        ),
        out_specs=P("tm", ("groups", "space"), None),
        check_vma=False,
    )
```

profile of v0, /device:TPU:1, one launch (start us, length us, event | category | flops | bytes accessed | tf_op | source)
XLA Modules:
  0.0 95.5 jit_solution(10927663036088345843)
XLA Ops:
  0.0 0.8 copy.8.conn
  0.8 0.0 copy-done.5
  0.8 0.1 copy.9.pattern
  0.9 0.0 copy-done.1
  0.9 1.0 %copy-done = bf16[32,64,128]{2,1,0:T(8,128)(2,1)S(1)} copy-done((bf16[32,64,128]{2,1,0:T(8,128)(2,1)S(1)}, bf16[32,64,128]{2,1,0:T(8,128)(2,1)}, u32[]{:S(2)}) %copy-start) | copy-done | bytes 524312
  1.9 0.8 pack_kernel.1
  2.7 4.5 %collective-permute-start = (bf16[912,128]{1,0:T(8,128)(2,1)S(1)}, bf16[912,128]{1,0:T(8,128)(2,1)S(1)}, u32[]{:S(2)}, u32[]{:S(2)}) collective-permute-start(bf16[912,128]{1,0:T(8,128)(2,1)S(1)} %get-tuple-element.24), channel_id=1, source_target_pairs={{0,1},{1,2},{2,3},{4,5},{5,6},{6,7},{8,9},{9,10},{10,11},{12,13},{... | collective-permute-start | bytes 700424 | tf_op jit(solution)/shard_map/ppermute | solution.py:21
  7.2 1.9 %collective-permute-start.1 = (bf16[912,128]{1,0:T(8,128)(2,1)S(1)}, bf16[912,128]{1,0:T(8,128)(2,1)S(1)}, u32[]{:S(2)}, u32[]{:S(2)}) collective-permute-start(bf16[912,128]{1,0:T(8,128)(2,1)S(1)} %get-tuple-element.25), channel_id=1, source_target_pairs={{1,0},{2,1},{3,2},{5,4},{6,5},{7,6},{9,8},{10,9},{11,10},{13,12},{... | collective-permute-start | bytes 700424 | tf_op jit(solution)/shard_map/ppermute | solution.py:21
  9.2 0.7 weight_kernel.1
  9.9 0.3 collective-permute-done.left.pay_left
  10.2 4.4 %collective-permute-done.1.right.pay_right = bf16[912,128]{1,0:T(8,128)(2,1)S(1)} collective-permute-done((bf16[912,128]{1,0:T(8,128)(2,1)S(1)}, bf16[912,128]{1,0:T(8,128)(2,1)S(1)}, u32[]{:S(2)}, u32[]{:S(2)}) %collective-permute-start.1) | collective-permute-done | bytes 233504 | tf_op jit(solution)/shard_map/ppermute | solution.py:21
  14.6 8.2 %first_kernel.1 = (f32[64,8,128]{2,1,0:T(8,128)S(1)}, f32[64,128]{1,0:T(8,128)S(1)}, s32[8,256]{1,0:T(8,128)S(1)}, f32[192,128]{1,0:T(8,128)S(1)}) custom-call(bf16[4,512,128]{2,1,0:T(8,128)(2,1)S(1)} %get-tuple-element.22.fe, bf16[16,128]{1,0:T(8,128)(2,1)S(1)} %get-tuple-element.23.tab, f32[64,128]{1,0:T(8,128)S(1)} %copy-done.1, ...), custom_call_target="tpu_custom_call" | custom-call | flops 3288334336 | bytes 2084864 | tf_op jit(solution)/shard_map/first_kernel/pallas_call | solution.py:327
  22.8 1.9 %collective-permute-start.3 = (f32[64,8,128]{2,1,0:T(8,128)S(1)}, f32[64,8,128]{2,1,0:T(8,128)S(1)}, u32[]{:S(2)}, u32[]{:S(2)}) collective-permute-start(f32[64,8,128]{2,1,0:T(8,128)S(1)} %get-tuple-element.29.own), channel_id=1, source_target_pairs={{1,0},{2,1},{3,2},{5,4},{6,5},{7,6},{9,8},{10,9},{11,10},{13,12},{... | collective-permute-start | bytes 786440 | tf_op jit(solution)/shard_map/ppermute | solution.py:21
  24.8 3.6 %collective-permute-start.2 = (f32[64,8,128]{2,1,0:T(8,128)S(1)}, f32[64,8,128]{2,1,0:T(8,128)S(1)}, u32[]{:S(2)}, u32[]{:S(2)}) collective-permute-start(f32[64,8,128]{2,1,0:T(8,128)S(1)} %get-tuple-element.29.own), channel_id=1, source_target_pairs={{0,1},{1,2},{2,3},{4,5},{5,6},{6,7},{8,9},{9,10},{10,11},{12,13},{... | collective-permute-start | bytes 786440 | tf_op jit(solution)/shard_map/ppermute | solution.py:21
  28.4 22.0 %all_gather.6 = f32[1024,128]{1,0:T(8,128)S(1)} all-gather(f32[64,128]{1,0:T(8,128)S(1)} %get-tuple-element.30), channel_id=1, replica_groups=mesh['groups'=2,'tm'=4,'space'=4] {'tm','space'}, dimensions={0}, use_global_device_ids=true | all-gather | bytes 557056 | tf_op jit(solution)/shard_map/all_gather | solution.py:378
  50.4 0.0 collective-permute-done.3.right
  50.4 0.0 collective-permute-done.2.left
  50.4 10.5 %second_kernel.1 = (f32[64,8,128]{2,1,0:T(8,128)S(1)}, f32[48,8,128]{2,1,0:T(8,128)S(1)}, f32[48,8,128]{2,1,0:T(8,128)S(1)}, f32[64,128]{1,0:T(8,128)S(1)}, f32[...) custom-call(s32[8,256]{1,0:T(8,128)S(1)} %get-tuple-element.28.idx, f32[64,8,128]{2,1,0:T(8,128)S(1)} %get-tuple-element.29.own, ...), custom_call_target="tpu_custom_call" | custom-call | flops 3288334336 | bytes 3842048 | tf_op jit(solution)/shard_map/second_kernel/pallas_call | solution.py:327
  61.0 1.9 %collective-permute-start.4 = (f32[48,8,128]{2,1,0:T(8,128)S(1)}, f32[48,8,128]{2,1,0:T(8,128)S(1)}, u32[]{:S(2)}, u32[]{:S(2)}) collective-permute-start(f32[48,8,128]{2,1,0:T(8,128)S(1)} %get-tuple-element.33), channel_id=1, source_target_pairs={{0,1},{1,2},{2,3},{4,5},{5,6},{6,7},{8,9},{9,10},{10,11},{12,13},{... | collective-permute-start | bytes 589832 | tf_op jit(solution)/shard_map/ppermute | solution.py:21
  62.9 2.4 %collective-permute-start.5 = (f32[48,8,128]{2,1,0:T(8,128)S(1)}, f32[48,8,128]{2,1,0:T(8,128)S(1)}, u32[]{:S(2)}, u32[]{:S(2)}) collective-permute-start(f32[48,8,128]{2,1,0:T(8,128)S(1)} %get-tuple-element.34), channel_id=1, source_target_pairs={{1,0},{2,1},{3,2},{5,4},{6,5},{7,6},{9,8},{10,9},{11,10},{13,12},{... | collective-permute-start | bytes 589832 | tf_op jit(solution)/shard_map/ppermute | solution.py:21
  65.3 20.1 %all_gather.7 = f32[1024,128]{1,0:T(8,128)S(1)} all-gather(f32[64,128]{1,0:T(8,128)S(1)} %get-tuple-element.35), channel_id=1, replica_groups=mesh['groups'=2,'tm'=4,'space'=4] {'tm','space'}, dimensions={0}, use_global_device_ids=true | all-gather | bytes 557056 | tf_op jit(solution)/shard_map/all_gather | solution.py:378
  85.4 0.0 collective-permute-done.4.left
  85.4 0.0 collective-permute-done.5.right
  85.4 10.1 %third_kernel.1 = f32[2048,128]{1,0:T(8,128)} custom-call(s32[8,256]{1,0:T(8,128)S(1)} %get-tuple-element.28.idx, f32[64,8,128]{2,1,0:T(8,128)S(1)} %get-tuple-element.32.own, f32[48,8,128]{2,1,0:T(8,128)S(1)} %collective-permute-done.4.left, f32[48,8,128]{2,1,0:T(8,128)S(1)} %collective-permute-done.5.right, f32[4,256,128]{2,1,0:T(8,128)S(1)} %bitcast.5, ...), custom_call_target="tpu_custom_call" | custom-call | flops 2348810240 | bytes 5160960 | tf_op jit(solution)/shard_map/third_kernel/pallas_call | solution.py:327
  (9 shorter events, 0.0 us)
Async XLA Ops:
  0.0 0.8 copy-start.5
  0.0 0.9 copy-start.1
  0.9 1.0 %copy-start = (bf16[32,64,128]{2,1,0:T(8,128)(2,1)S(1)}, bf16[32,64,128]{2,1,0:T(8,128)(2,1)}, u32[]{:S(2)}) copy-start(bf16[32,64,128]{2,1,0:T(8,128)(2,1)} %param.7) | copy-start | bytes 1572868
  1.9 7.2 %copy-start.2 = (f32[6,128,128]{2,1,0:T(8,128)S(1)}, f32[6,128,128]{2,1,0:T(8,128)}, u32[]{:S(2)}) copy-start(f32[6,128,128]{2,1,0:T(8,128)} %faces.1) | copy-start | bytes 1179652
  1.9 7.2 %copy-start.3 = (f32[128,128]{1,0:T(8,128)S(1)}, f32[128,128]{1,0:T(8,128)}, u32[]{:S(2)}) copy-start(f32[128,128]{1,0:T(8,128)} %diag.1) | copy-start | bytes 196612
  1.9 7.2 %copy-start.4 = (f32[128,128]{1,0:T(8,128)S(1)}, f32[128,128]{1,0:T(8,128)}, u32[]{:S(2)}) copy-start(f32[128,128]{1,0:T(8,128)} %coarse.1) | copy-start | bytes 196612
  2.7 7.5 %collective-permute-start = (bf16[912,128]{1,0:T(8,128)(2,1)S(1)}, bf16[912,128]{1,0:T(8,128)(2,1)S(1)}, u32[]{:S(2)}, u32[]{:S(2)}) collective-permute-start(bf16[912,128]{1,0:T(8,128)(2,1)S(1)} %get-tuple-element.24), channel_id=1, source_target_pairs={{0,1},{1,2},{2,3},{4,5},{5,6},{6,7},{8,9},{9,10},{10,11},{12,13},{... | collective-permute-start | bytes 700424 | tf_op jit(solution)/shard_map/ppermute | solution.py:21
  7.2 7.4 %collective-permute-start.1 = (bf16[912,128]{1,0:T(8,128)(2,1)S(1)}, bf16[912,128]{1,0:T(8,128)(2,1)S(1)}, u32[]{:S(2)}, u32[]{:S(2)}) collective-permute-start(bf16[912,128]{1,0:T(8,128)(2,1)S(1)} %get-tuple-element.25), channel_id=1, source_target_pairs={{1,0},{2,1},{3,2},{5,4},{6,5},{7,6},{9,8},{10,9},{11,10},{13,12},{... | collective-permute-start | bytes 700424 | tf_op jit(solution)/shard_map/ppermute | solution.py:21
  22.8 27.6 %collective-permute-start.3 = (f32[64,8,128]{2,1,0:T(8,128)S(1)}, f32[64,8,128]{2,1,0:T(8,128)S(1)}, u32[]{:S(2)}, u32[]{:S(2)}) collective-permute-start(f32[64,8,128]{2,1,0:T(8,128)S(1)} %get-tuple-element.29.own), channel_id=1, source_target_pairs={{1,0},{2,1},{3,2},{5,4},{6,5},{7,6},{9,8},{10,9},{11,10},{13,12},{... | collective-permute-start | bytes 786440 | tf_op jit(solution)/shard_map/ppermute | solution.py:21
  24.8 25.7 %collective-permute-start.2 = (f32[64,8,128]{2,1,0:T(8,128)S(1)}, f32[64,8,128]{2,1,0:T(8,128)S(1)}, u32[]{:S(2)}, u32[]{:S(2)}) collective-permute-start(f32[64,8,128]{2,1,0:T(8,128)S(1)} %get-tuple-element.29.own), channel_id=1, source_target_pairs={{0,1},{1,2},{2,3},{4,5},{5,6},{6,7},{8,9},{9,10},{10,11},{12,13},{... | collective-permute-start | bytes 786440 | tf_op jit(solution)/shard_map/ppermute | solution.py:21
  61.0 24.5 %collective-permute-start.4 = (f32[48,8,128]{2,1,0:T(8,128)S(1)}, f32[48,8,128]{2,1,0:T(8,128)S(1)}, u32[]{:S(2)}, u32[]{:S(2)}) collective-permute-start(f32[48,8,128]{2,1,0:T(8,128)S(1)} %get-tuple-element.33), channel_id=1, source_target_pairs={{0,1},{1,2},{2,3},{4,5},{5,6},{6,7},{8,9},{9,10},{10,11},{12,13},{... | collective-permute-start | bytes 589832 | tf_op jit(solution)/shard_map/ppermute | solution.py:21
  62.9 22.5 %collective-permute-start.5 = (f32[48,8,128]{2,1,0:T(8,128)S(1)}, f32[48,8,128]{2,1,0:T(8,128)S(1)}, u32[]{:S(2)}, u32[]{:S(2)}) collective-permute-start(f32[48,8,128]{2,1,0:T(8,128)S(1)} %get-tuple-element.34), channel_id=1, source_target_pairs={{1,0},{2,1},{3,2},{5,4},{6,5},{7,6},{9,8},{10,9},{11,10},{13,12},{... | collective-permute-start | bytes 589832 | tf_op jit(solution)/shard_map/ppermute | solution.py:21
where the time goes:
time: 96 us; the launch traced here: 95.5 us
  blocking collectives  42.1 us (44%)
  Pallas kernels  30.4 us (32%)
  starting transfers between devices  16.3 us (17%)
  waiting for transfers between devices  4.69 us (5%)
  local copies, waits for them, and re-layouts  1.94 us (2%)
    all_gather x2, blocking collectives, gathered(): lax.all_gather(value, ('tm', 'space'), axis=0, tiled=True)  42.1 us
    pallas_call x5, Pallas kernels, call(): pl.pallas_call(kernel, out_shape=outs, name=kernel.__name__, in_specs=spe...  30.4 us
    ppermute x6, starting transfers between devices, shifted(): return lax.ppermute(value, 'space', pairs)  16.3 us
    ppermute x6, waiting for transfers between devices, shifted(): return lax.ppermute(value, 'space', pairs)  4.69 us
    unnamed x14, local copies, waits for them, and re-layouts  1.94 us
  transfers between devices with their start and end apart: 6, of which 2 were waited for; matrix products, arithmetic and copies ran while one was open for 0% of the time, Pallas kernels for 1%

commit v1 on v0

v1 whole, which is shorter than its diff:
```python
import functools

import jax
import jax.numpy as jnp
from jax import lax
from jax.experimental import pallas as pl
from jax.experimental.pallas import tpu as pltpu
from jax.sharding import PartitionSpec as P

COARSEN = 4
REACH = 16
F32 = jnp.float32
BF16 = jnp.bfloat16
CHUNK = 32


def swapped(value, first):
    count = lax.axis_size("space")
    pairs = []
    for i in range(first, count - 1, 2):
        pairs += [(i, i + 1), (i + 1, i)]
    return lax.ppermute(value, "space", pairs)


def earlier(value):
    count = lax.axis_size("tm")
    if count <= 8:
        return [lax.ppermute(value, "tm", [(i, i + s) for i in range(count - s)]) for s in range(1, count)]
    every = lax.all_gather(value, "tm")
    at = lax.axis_index("tm") - jnp.arange(1, count)
    picked = jnp.where((at >= 0)[:, None, None], jnp.take(every, jnp.maximum(at, 0), axis=0), 0.0)
    return [picked[s] for s in range(count - 1)]


def split(u):
    lead = u.astype(BF16).astype(F32)
    return jnp.concatenate([u, u - lead], axis=1).astype(BF16)


def split_rows(u):
    lead = u.astype(BF16)
    return jnp.concatenate([lead, (u - lead.astype(F32)).astype(BF16)], axis=0)


def product(x, weights):
    m = x.shape[0] // 16
    r = jnp.dot(x, weights, preferred_element_type=F32).reshape(m, 16, 256)
    return r[:, :8, :128] + (r[:, 8:, :128] + r[:, :8, 128:])


def product_rows(x, weights):
    m = x.shape[0] // 2
    r = jnp.dot(x, weights, preferred_element_type=F32)
    return r[:m, :128] + (r[m:, :128] + r[:m, 128:])


def put_halves(ref, w):
    lead = w.astype(BF16)
    ref[:, 0:128] = lead
    ref[:, 128:256] = (w - lead.astype(F32)).astype(BF16)


def power(pk, k):
    return pk[pl.ds(128 * (7 - k), 128), :]


def scan_starts(values, pk):
    y = values
    row = lax.broadcasted_iota(jnp.int32, y.shape, 1)
    for d in (1, 2, 4):
        z = product(split(y).reshape(-1, 128), power(pk, d))
        y = y + jnp.where(row >= d, pltpu.roll(z, d, axis=1), 0.0)
    return jnp.where(row >= 1, pltpu.roll(y, 1, axis=1), 0.0)


def block_end(y, pk, n):
    parts = [y[pl.ds(i, n, stride=8), :] for i in range(8)]
    return product_rows(split_rows(jnp.concatenate(parts, axis=1)), pk[...])


def enter(arrivals, we, pk, y, n):
    value = jnp.concatenate([a[...] for a in arrivals], axis=1)
    entry = product_rows(split_rows(value), we[...])
    y[pl.ds(0, n, stride=8), :] = entry
    rows = split_rows(entry)
    for i in range(1, 8):
        y[pl.ds(i, n, stride=8), :] = product_rows(rows, power(pk, i))
    return y[...].reshape(n, 8, 128)


def apply_phi(src, idx, w, low, high, emit):
    size = (high - low) // 2 if high - low > 64 else high - low

    def body(c, carry):
        base = low + c * size
        cols = [src[pl.ds(base, size)].reshape(size * 16, 128)]
        for f in range(6):
            cols.append(jnp.concatenate([src[idx[f, base + e]] for e in range(size)], axis=0))
        emit(base, size, product(jnp.concatenate(cols, axis=1), w[...]))
        return carry

    lax.fori_loop(0, (high - low) // size, body, 0)


def even_place():
    return lax.rem(lax.axis_index("space"), 2) == 0


def pack_kernel(forcing, init, conn, pattern, fe, tab, pay_even, pay_odd, rows, offs):
    n = init.shape[0]
    stride = COARSEN * n
    step = 256
    for at in range(0, rows.shape[0], step):
        rows[pl.ds(at, step), :] = forcing[pl.ds(at, step), :].astype(F32)

    def body(pair, carry):
        e = pair * 2
        for k in range(COARSEN):
            two = [rows[pl.ds(k * n + e + j, 8, stride=stride), :] for j in range(2)]
            fe[k, pl.ds(pl.multiple_of(e * 8, 16), 16), :] = jnp.concatenate(two, axis=0).astype(BF16)
        return carry

    lax.fori_loop(0, n // 2, body, 0, unroll=4)
    place = lax.broadcasted_iota(jnp.int32, (6, n), 1) + lax.axis_index("space") * n
    value = ((conn[...] - place) * pattern[...]).astype(F32)
    offs[...] = jnp.zeros_like(offs)
    offs[0:6, 0:n] = value
    offs[0:6, n : 2 * n] = value
    tab[...] = offs[...].astype(BF16)
    lead = init[...].astype(BF16)
    rest = (init[...] - lead.astype(F32)).astype(BF16)
    even = even_place()
    at = 0
    for k in range(COARSEN - 1):
        width = (COARSEN - 1 - k) * REACH * 8
        for pay, right in ((pay_even, even), (pay_odd, jnp.logical_not(even))):
            begin = pl.multiple_of(jnp.where(right, n * 8 - width, 0), 128)
            pay[pl.ds(at, width), :] = fe[k, pl.ds(begin, width), :]
        at += width
    for pay in (pay_even, pay_odd):
        pay[pl.ds(at, n), :] = lead
        pay[pl.ds(at + n, n), :] = rest
        pay[pl.ds(at + 2 * n, 16), :] = tab[...]


def weight_kernel(diag, faces, coarse, w, pk, we):
    put_halves(w.at[pl.ds(0, 128)], diag[...].T)
    for f in range(6):
        put_halves(w.at[pl.ds(128 * (f + 1), 128)], faces[f].T)

    def thirds(a):
        one = a.astype(BF16)
        rest = a - one.astype(F32)
        two = rest.astype(BF16)
        return one, two, (rest - two.astype(F32)).astype(BF16)

    def mul(a, b):
        (a1, a2, a3), (b1, b2, b3) = thirds(a), thirds(b)
        total = jnp.zeros((128, 128), F32)
        for x, y in ((a3, b1), (a1, b3), (a2, b2), (a2, b1), (a1, b2), (a1, b1)):
            total += jnp.dot(x, y, preferred_element_type=F32)
        return total

    rows = lax.broadcasted_iota(jnp.int32, (128, 128), 0)
    one = (rows == lax.broadcasted_iota(jnp.int32, (128, 128), 1)).astype(F32)
    powers = [one, coarse[...].T]
    for k in range(2, 9):
        powers.append(mul(powers[k // 2], powers[k - k // 2]))
    for k in range(8):
        put_halves(pk.at[pl.ds(128 * (7 - k), 128)], powers[k])

    def body(k, current):
        put_halves(we.at[pl.ds(pl.multiple_of(k * 128, 128), 128)], current)
        return mul(current, powers[8])

    lax.fori_loop(0, we.shape[0] // 128, body, one)


def window(dst, even_ref, odd_ref, own, k, low, n):
    at = sum((COARSEN - 1 - j) * REACH * 8 for j in range(k))
    have = (COARSEN - 1 - k) * REACH * 8
    side = (n - low) * 8
    even = even_place()
    if side:
        for ref, right in ((even_ref, even), (odd_ref, jnp.logical_not(even))):
            begin = pl.multiple_of(jnp.where(right, at, at + have - side), 128)
            to = pl.multiple_of(jnp.where(right, side + n * 8, 0), 128)
            dst[pl.ds(to, side), :] = ref[pl.ds(begin, side), :]
    dst[pl.ds(side, n * 8), :] = own[k]


def first_kernel(
    fe, tab, init, got_even, got_odd, w, pk, w1, end, idx_out, s0, s1, fx, y, i16, square, idx_v, idx, sem
):
    n = init.shape[0]
    full = 3 * n
    tail = got_even.shape[0] - 16
    even = even_place()
    lane = lax.broadcasted_iota(jnp.int32, (8, 128), 1)

    def table(ref, at):
        return ref[pl.ds(at, 16), :].astype(F32)[0:8]

    from_even, from_odd = table(got_even, tail), table(got_odd, tail)
    low = jnp.where(lane < n, jnp.where(even, from_odd, from_even), table(tab, 0))
    high = jnp.where(lane < n, jnp.where(even, from_even, from_odd), 0.0)
    columns = []
    for at, offs in ((0, low), (128, high)):
        value = jnp.where(offs != 0.0, lane + at + offs.astype(jnp.int32), full)
        idx_v[:, pl.ds(at, 128)] = value
        idx_out[:, pl.ds(at, 128)] = value
        square[...] = jnp.zeros_like(square)
        square[0:8, :] = value.astype(F32)
        columns.append(square[...].T)
    copy = pltpu.make_async_copy(idx_v, idx, sem)
    copy.start()

    i16[pl.ds(full, i16.shape[0] - full), :] = jnp.zeros((i16.shape[0] - full, 256), BF16)
    lead = init[...].astype(BF16)
    i16[pl.ds(n, n), 0:128] = lead
    i16[pl.ds(n, n), 128:256] = (init[...] - lead.astype(F32)).astype(BF16)
    for ref, right in ((got_even, even), (got_odd, jnp.logical_not(even))):
        to = pl.multiple_of(jnp.where(right, 2 * n, 0), n)
        i16[pl.ds(to, n), 0:128] = ref[pl.ds(tail - 2 * n, n), :]
        i16[pl.ds(to, n), 128:256] = ref[pl.ds(tail - n, n), :]
    count = full - 2 * REACH
    place = jnp.concatenate([columns[0][REACH:128], columns[1][0 : full - REACH - 128]], axis=0)
    spot = lax.broadcasted_iota(jnp.int32, (count, 256), 1).astype(F32)
    cols = [i16[pl.ds(REACH, count), :]]
    for f in range(6):
        hot = (spot == place[:, f : f + 1]).astype(F32).astype(BF16)
        cols.append(jnp.dot(hot, i16[...], preferred_element_type=F32).astype(BF16))
    leads = jnp.concatenate([c[:, 0:128] for c in cols], axis=1)
    rests = jnp.concatenate([c[:, 128:256] for c in cols], axis=1)
    pushed = product_rows(jnp.concatenate([leads, rests], axis=0), w[...])
    window(fx, got_even, got_odd, fe, 0, REACH, n)
    y[pl.ds(0, count * 8), :] = fx[pl.ds(0, count * 8), :].astype(F32)
    first = (lax.axis_index("tm") == 0).astype(F32)
    y[pl.ds(0, count, stride=8), :] = y[pl.ds(0, count, stride=8), :] + pushed * first

    def fill(c, carry):
        rows = pl.ds(pl.multiple_of(c * CHUNK * 8, CHUNK * 8), CHUNK * 8)
        s1[pl.ds(REACH + c * CHUNK, CHUNK)] = split(y[rows, :].reshape(CHUNK, 8, 128))
        return carry

    lax.fori_loop(0, count // CHUNK, fill, 0)
    s0[full] = jnp.zeros((16, 128), BF16)
    s1[full] = jnp.zeros((16, 128), BF16)
    copy.wait()
    bufs = [s0, s1]
    for k in range(1, COARSEN):
        lo = (k + 1) * REACH
        window(fx, got_even, got_odd, fe, k, lo, n)
        src, dst = bufs[k % 2], bufs[(k + 1) % 2]

        def emit(base, size, value, lo=lo, dst=dst, last=k == COARSEN - 1):
            at = pl.multiple_of((base - lo) * 8, 128)
            value = value + fx[pl.ds(at, size * 8), :].astype(F32).reshape(size, 8, 128)
            if last:
                w1[pl.ds(base - lo, size)] = value
                y[pl.ds(at, size * 8), :] = value.reshape(size * 8, 128)
            else:
                dst[pl.ds(base, size)] = split(value)

        apply_phi(src, idx, w, lo, full - lo, emit)
    end[...] = block_end(y, pk, n)


def scan_kernel(values, pk, starts):
    starts[...] = scan_starts(values[...], pk)


def enter_first_kernel(*refs):
    *arrivals, starts, we, pk, state, y = refs
    n = starts.shape[0]
    state[...] = split(enter(arrivals, we, pk, y, n) + starts[...])


def enter_second_kernel(*refs):
    *arrivals, starts, before, init, we, pk, state, pay_even, pay_odd, corr, y = refs
    n = starts.shape[0]
    value = enter(arrivals, we, pk, y, n) + starts[...]
    corr[...] = value
    old = before[...].astype(F32)
    y[...] = (value + (old[:, 0:8] + old[:, 8:16])).reshape(n * 8, 128)
    first = (lax.axis_index("tm") == 0).astype(F32)
    y[pl.ds(0, n, stride=8), :] = y[pl.ds(0, n, stride=8), :] + init[...] * first
    state[...] = split(y[...].reshape(n, 8, 128))
    side = (COARSEN - 1) * REACH
    even = even_place()
    pay_even[...] = state[pl.ds(jnp.where(even, n - side, 0), side)]
    pay_odd[...] = state[pl.ds(jnp.where(even, 0, n - side), side)]


def point_kernel(corr, total, pk, points):
    points[...] = product(split(corr[...]).reshape(-1, 128), power(pk, 1)) + total[...]


def gather_blocks(dst, own, got_even, got_odd, n):
    side = got_even.shape[0]
    even = even_place()
    dst[pl.ds(n, n)] = own[...]
    for ref, right in ((got_even, even), (got_odd, jnp.logical_not(even))):
        dst[pl.ds(jnp.where(right, 2 * n, n - side), side)] = ref[...]
    dst[3 * n] = jnp.zeros((16, 128), BF16)


def second_kernel(idx, own, got_even, got_odd, w1, w, pk, res, end, total, s0, s1, y):
    n = own.shape[0]
    full = 3 * n
    gather_blocks(s0, own, got_even, got_odd, n)
    s1[full] = jnp.zeros((16, 128), BF16)
    bufs = [s0, s1]
    for k in range(COARSEN):
        lo = (k + 1) * REACH
        src, dst = bufs[k % 2], bufs[(k + 1) % 2]

        def emit(base, size, value, lo=lo, dst=dst, last=k == COARSEN - 1):
            if last:
                at = base - lo
                total[pl.ds(at, size)] = value + w1[pl.ds(at, size)]
                value = value - product(own[pl.ds(at, size)].reshape(size * 16, 128), power(pk, 1))
                res[pl.ds(at, size)] = value
                y[pl.ds(pl.multiple_of(at * 8, 128), size * 8), :] = value.reshape(size * 8, 128)
            else:
                dst[pl.ds(base, size)] = split(value)

        apply_phi(src, idx, w, lo, full - lo, emit)
    end[...] = block_end(y, pk, n)


def third_kernel(idx, own, got_even, got_odd, points, fe, pay_even, pay_odd, w, out, s0, s1, fx, u):
    n = own.shape[0]
    full = 3 * n
    stride = COARSEN * n
    gather_blocks(s0, own, got_even, got_odd, n)
    s1[full] = jnp.zeros((16, 128), BF16)

    def put(k, ref, at):
        def body(e, carry):
            out[pl.ds(k * n + e, 8, stride=stride), :] = ref[at + e]
            return carry

        lax.fori_loop(0, n, body, 0, unroll=8)

    put(COARSEN - 1, points, 0)
    bufs = [s0, s1]
    for k in range(COARSEN - 1):
        lo = (k + 2) * REACH
        window(fx, pay_even, pay_odd, fe, k, lo, n)
        src, dst = bufs[k % 2], bufs[(k + 1) % 2]

        def emit(base, size, value, lo=lo, dst=dst, last=k == COARSEN - 2):
            at = pl.multiple_of((base - lo) * 8, 128)
            value = value + fx[pl.ds(at, size * 8), :].astype(F32).reshape(size, 8, 128)
            u[pl.ds(base, size)] = value
            if not last:
                dst[pl.ds(base, size)] = split(value)

        apply_phi(src, idx, w, lo, full - lo, emit)
        put(k, u, n)


def call(kernel, inputs, outs, scratch, smem=0, flops=10**7):
    specs = [pl.BlockSpec(memory_space=pltpu.SMEM)] * smem
    specs += [pl.BlockSpec(memory_space=pltpu.VMEM)] * (len(inputs) - smem)
    moved = sum(a.size * a.dtype.itemsize for a in list(inputs) + list(outs))
    return pl.pallas_call(
        kernel,
        out_shape=outs,
        name=kernel.__name__,
        in_specs=specs,
        out_specs=[pl.BlockSpec(memory_space=pltpu.VMEM)] * len(outs),
        scratch_shapes=scratch,
        compiler_params=pltpu.CompilerParams(vmem_limit_bytes=32 * 1024 * 1024),
        cost_estimate=pl.CostEstimate(flops=flops, bytes_accessed=moved, transcendentals=0),
    )(*inputs)


def local(forcing, initial_state, connectivity, pattern, diag_block, face_blocks, coarse_block):
    n, width = initial_state.shape
    steps = forcing.shape[0]
    full = 3 * n
    tm = lax.axis_size("tm")
    shape = jax.ShapeDtypeStruct
    tiles = shape((n, 8, width), F32)
    state = shape((n, 16, width), BF16)
    ends = shape((n, width), F32)
    step_flops = 2 * 16 * 7 * width * 2 * width
    pay_rows = sum((COARSEN - 1 - k) * REACH * 8 for k in range(COARSEN)) + 2 * n + 16
    pay = shape((pay_rows, width), BF16)
    fe, tab, pay_even, pay_odd = call(
        pack_kernel,
        (forcing.reshape(steps * n, width), initial_state, connectivity.T, pattern.T),
        (shape((COARSEN, n * 8, width), BF16), shape((16, 128), BF16), pay, pay),
        [pltpu.VMEM((steps * n, width), F32), pltpu.VMEM((16, 128), F32)],
    )
    pay_odd, pay_even = swapped(pay_odd, 1), swapped(pay_even, 0)
    w, pk, we = call(
        weight_kernel,
        (diag_block, face_blocks, coarse_block),
        (
            shape((7 * width, 2 * width), BF16),
            shape((8 * width, 2 * width), BF16),
            shape(((tm - 1) * width, 2 * width), BF16),
        ),
        [],
        flops=10**9,
    )
    spaces = pltpu.VMEM((full + 1, 16, width), BF16)
    force = pltpu.VMEM(((full - 2 * REACH) * 8, width), BF16)
    rows = pltpu.VMEM((n * 8, width), F32)
    w1, end, idx = call(
        first_kernel,
        (fe, tab, initial_state, pay_even, pay_odd, w, pk),
        (tiles, ends, shape((8, 256), jnp.int32)),
        [
            spaces,
            spaces,
            force,
            pltpu.VMEM(((full - 2 * REACH) * 8, width), F32),
            pltpu.VMEM((256, 256), BF16),
            pltpu.VMEM((128, 128), F32),
            pltpu.VMEM((8, 256), jnp.int32),
            pltpu.SMEM((8, 256), jnp.int32),
            pltpu.SemaphoreType.DMA,
        ],
        flops=step_flops * 5 * n,
    )
    arrivals = earlier(end)
    (starts,) = call(scan_kernel, (w1, pk), (tiles,), [])
    (coarse,) = call(enter_first_kernel, (*arrivals, starts, we, pk), (state,), [rows])
    got_odd, got_even = swapped(coarse, 1), swapped(coarse, 0)
    res, end, total = call(
        second_kernel,
        (idx, coarse, got_even, got_odd, w1, w, pk),
        (tiles, ends, tiles),
        [spaces, spaces, rows],
        smem=1,
        flops=step_flops * 7 * n,
    )
    arrivals = earlier(end)
    (starts,) = call(scan_kernel, (res, pk), (tiles,), [])
    side = shape(((COARSEN - 1) * REACH, 16, width), BF16)
    coarse, end_even, end_odd, corr = call(
        enter_second_kernel,
        (*arrivals, starts, coarse, initial_state, we, pk),
        (state, side, side, tiles),
        [rows],
    )
    got_odd, got_even = swapped(end_odd, 1), swapped(end_even, 0)
    (points,) = call(point_kernel, (corr, total, pk), (tiles,), [])
    (out,) = call(
        third_kernel,
        (idx, coarse, got_even, got_odd, points, fe, pay_even, pay_odd, w),
        (shape((steps * n, width), F32),),
        [spaces, spaces, force, pltpu.VMEM((full, 8, width), F32)],
        smem=1,
        flops=step_flops * 5 * n,
    )
    return out.reshape(steps, n, width)


def solution(mesh):
    return jax.shard_map(
        local,
        mesh=mesh,
        in_specs=(
            P("tm", ("groups", "space"), None),
            P(("groups", "space"), None),
            P("space", None),
            P("space", None),
            P(),
            P(),
            P(),
        ),
        out_specs=P("tm", ("groups", "space"), None),
        check_vma=False,
    )
```

time: 96 us -> 67.7 us (0.71)
  blocking collectives: 42.1 us -> 0 us
  starting transfers between devices: 16.3 us -> 29.4 us
  Pallas kernels: 30.4 us -> 24.9 us
  waiting for transfers between devices: 4.69 us -> 9.54 us
  local copies, waits for them, and re-layouts: 1.94 us -> 3.19 us
    all_gather x2 -> x0, blocking collectives: 42.1 us -> none  [gathered(): lax.all_gather(value, ('tm', 'space'), axis=0, tiled=True)]
    ppermute x6 -> x12, starting transfers between devices: 16.3 us -> 29.4 us  [the longest x6 15.7 us: earlier(): lax.ppermute(value, 'tm', [(i, i + s) for i in range(count - s)])]
    pallas_call x5 -> x10, Pallas kernels: 30.4 us -> 24.9 us  [call(): pl.pallas_call(kernel, out_shape=outs, name=kernel.__name__, in_specs=spe...]
    ppermute x6 -> x12, waiting for transfers between devices: 4.69 us -> 9.54 us  [the longest x6 8.96 us: swapped(): return lax.ppermute(value, 'space', pairs)]
    unnamed x14 -> x16, local copies, waits for them, and re-layouts: 1.94 us -> 3.19 us
  transfers between devices with their start and end apart: 6 -> 12, of which waited for: 2 -> 5; matrix products, arithmetic and copies ran while one was open for 0% -> 0% of each run, Pallas kernels for 1% -> 5%
where the time goes in v1:
time: 67.7 us; the launch traced here: 67.2 us
  starting transfers between devices  29.4 us (43%)
  Pallas kernels  24.9 us (37%)
  waiting for transfers between devices  9.54 us (14%)
  local copies, waits for them, and re-layouts  3.19 us (5%)
    pallas_call x10, Pallas kernels, call(): pl.pallas_call(kernel, out_shape=outs, name=kernel.__name__, in_specs=spe...  24.9 us
    ppermute x6, starting transfers between devices, earlier(): lax.ppermute(value, 'tm', [(i, i + s) for i in range(count - s)])  15.7 us
    ppermute x6, starting transfers between devices, swapped(): return lax.ppermute(value, 'space', pairs)  13.7 us
    ppermute x6, waiting for transfers between devices, swapped(): return lax.ppermute(value, 'space', pairs)  8.96 us
    unnamed x16, local copies, waits for them, and re-layouts  3.19 us
  transfers between devices with their start and end apart: 12, of which 5 were waited for; matrix products, arithmetic and copies ran while one was open for 0% of the time, Pallas kernels for 5%

profile of v1, /device:TPU:1, one launch (start us, length us, event | category | flops | bytes accessed | tf_op | source)
XLA Modules:
  0.0 67.2 jit_solution(17073699476228762963)
XLA Ops:
  0.0 0.7 %copy-done.3 = s32[64,6]{0,1:T(8,128)S(1)} copy-done((s32[64,6]{0,1:T(8,128)S(1)}, s32[64,6]{0,1:T(8,128)}, u32[]{:S(2)}) %copy-start.3) | copy-done | bytes 1560
  0.7 1.0 %copy-done = bf16[32,64,128]{2,1,0:T(8,128)(2,1)S(1)} copy-done((bf16[32,64,128]{2,1,0:T(8,128)(2,1)S(1)}, bf16[32,64,128]{2,1,0:T(8,128)(2,1)}, u32[]{:S(2)}) %copy-start) | copy-done | bytes 524312
  1.7 0.8 %copy-done.1 = f32[64,128]{1,0:T(8,128)S(1)} copy-done((f32[64,128]{1,0:T(8,128)S(1)}, f32[64,128]{1,0:T(8,128)}, u32[]{:S(2)}) %copy-start.1) | copy-done | bytes 32792
  2.5 0.7 %copy-done.4 = s32[64,6]{0,1:T(8,128)S(1)} copy-done((s32[64,6]{0,1:T(8,128)S(1)}, s32[64,6]{0,1:T(8,128)}, u32[]{:S(2)}) %copy-start.4) | copy-done | bytes 1560
  3.2 0.8 %pack_kernel.1 = (bf16[4,512,128]{2,1,0:T(8,128)(2,1)S(1)}, bf16[16,128]{1,0:T(8,128)(2,1)S(1)}, bf16[912,128]{1,0:T(8,128)(2,1)S(1)}, bf16[912,128]{1,0:T(8,128)(2,1)S(1)}) custom-call(bf16[2048,128]{1,0:T(8,128)(2,1)S(1)} %bitcast.4, f32[64,128]{1,0:T(8,128)S(1)} %copy-done.1, s32[6,64]{1,0:T(8,128)S(1)} %bitcast.5, s32[6,64]{1,0:T(8,128)S(1)} %bitcast.6), custom_call_target="tpu_custom_call" | custom-call | flops 10000000 | bytes 1555456 | tf_op jit(solution)/shard_map/pack_kernel/pallas_call | solution.py:368
  4.0 4.5 %collective-permute-start.1 = (bf16[912,128]{1,0:T(8,128)(2,1)S(1)}, bf16[912,128]{1,0:T(8,128)(2,1)S(1)}, u32[]{:S(2)}, u32[]{:S(2)}) collective-permute-start(bf16[912,128]{1,0:T(8,128)(2,1)S(1)} %get-tuple-element.25), channel_id=1, source_target_pairs={{1,2},{2,1},{5,6},{6,5},{9,10},{10,9},{13,14},{14,13},{17,18},{18,... | collective-permute-start | bytes 700424 | tf_op jit(solution)/shard_map/ppermute | solution.py:22
  8.6 1.5 %weight_kernel.1 = (bf16[896,256]{1,0:T(8,128)(2,1)S(1)}, bf16[1024,256]{1,0:T(8,128)(2,1)S(1)}, bf16[384,256]{1,0:T(8,128)(2,1)S(1)}) custom-call(f32[128,128]{1,0:T(8,128)S(1)} %copy-done.6, f32[6,128,128]{2,1,0:T(8,128)S(1)} %copy-done.5, f32[128,128]{1,0:T(8,128)S(1)} %copy-done.7), custom_call_target="tpu_custom_call" | custom-call | flops 1000000000 | bytes 1703936 | tf_op jit(solution)/shard_map/weight_kernel/pallas_call | solution.py:368
  10.1 2.1 %collective-permute-done.1.got_odd.pay_odd = bf16[912,128]{1,0:T(8,128)(2,1)S(1)} collective-permute-done((bf16[912,128]{1,0:T(8,128)(2,1)S(1)}, bf16[912,128]{1,0:T(8,128)(2,1)S(1)}, u32[]{:S(2)}, u32[]{:S(2)}) %collective-permute-start.1) | collective-permute-done | bytes 233504 | tf_op jit(solution)/shard_map/ppermute | solution.py:22
  12.3 5.4 %first_kernel.1 = (f32[64,8,128]{2,1,0:T(8,128)S(1)}, f32[64,128]{1,0:T(8,128)S(1)}, s32[8,256]{1,0:T(8,128)S(1)}) custom-call(bf16[4,512,128]{2,1,0:T(8,128)(2,1)S(1)} %get-tuple-element.22.fe, bf16[16,128]{1,0:T(8,128)(2,1)S(1)} %get-tuple-element.23.tab, f32[64,128]{1,0:T(8,128)S(1)} %copy-done.2, ...), custom_call_target="tpu_custom_call" | custom-call | flops 2348810240 | bytes 2314240 | tf_op jit(solution)/shard_map/first_kernel/pallas_call | solution.py:368
  17.7 6.0 %collective-permute-start.4 = (f32[64,128]{1,0:T(8,128)S(1)}, f32[64,128]{1,0:T(8,128)S(1)}, u32[]{:S(2)}, u32[]{:S(2)}) collective-permute-start(f32[64,128]{1,0:T(8,128)S(1)} %get-tuple-element.29), channel_id=1, source_target_pairs={{0,12},{1,13},{2,14},{3,15},{16,28},{17,29},{18,30},{19,31}} | collective-permute-start | bytes 98312 | tf_op jit(solution)/shard_map/ppermute | solution.py:28
  23.6 1.3 %collective-permute-start.3 = (f32[64,128]{1,0:T(8,128)S(1)}, f32[64,128]{1,0:T(8,128)S(1)}, u32[]{:S(2)}, u32[]{:S(2)}) collective-permute-start(f32[64,128]{1,0:T(8,128)S(1)} %get-tuple-element.29), channel_id=1, source_target_pairs={{0,8},{4,12},{1,9},{5,13},{2,10},{6,14},{3,11},{7,15},{16,24},{20,... | collective-permute-start | bytes 98312 | tf_op jit(solution)/shard_map/ppermute | solution.py:28
  24.9 2.2 %collective-permute-start.2 = (f32[64,128]{1,0:T(8,128)S(1)}, f32[64,128]{1,0:T(8,128)S(1)}, u32[]{:S(2)}, u32[]{:S(2)}) collective-permute-start(f32[64,128]{1,0:T(8,128)S(1)} %get-tuple-element.29), channel_id=1, source_target_pairs={{0,4},{4,8},{8,12},{1,5},{5,9},{9,13},{2,6},{6,10},{10,14},{3,7},{... | collective-permute-start | bytes 98312 | tf_op jit(solution)/shard_map/ppermute | solution.py:28
  27.1 0.7 %scan_kernel.2.refs_3_ = f32[64,8,128]{2,1,0:T(8,128)S(1)} custom-call(f32[64,8,128]{2,1,0:T(8,128)S(1)} %get-tuple-element.30.values.w1, bf16[1024,256]{1,0:T(8,128)(2,1)S(1)} %get-tuple-element.27.pk.refs_5_.refs_7_), custom_call_target="tpu_custom_call" | custom-call | flops 10000000 | bytes 1048576 | tf_op jit(solution)/shard_map/scan_kernel/pallas_call | solution.py:368
  28.7 4.1 %collective-permute-start.6 = (bf16[64,16,128]{2,1,0:T(8,128)(2,1)S(1)}, bf16[64,16,128]{2,1,0:T(8,128)(2,1)S(1)}, u32[]{:S(2)}, u32[]{:S(2)}) collective-permute-start(bf16[64,16,128]{2,1,0:T(8,128)(2,1)S(1)} %enter_first_kernel.1.own.refs_4_), channel_id=1, source_target_pairs={{1,2},{2,1},{5,6},{6,5},{9,10},{10,9},{13,14},{14,13},{17,18},{18,... | collective-permute-start | bytes 786440 | tf_op jit(solution)/shard_map/ppermute | solution.py:22
  32.8 4.0 %collective-permute-done.6.got_odd = bf16[64,16,128]{2,1,0:T(8,128)(2,1)S(1)} collective-permute-done((bf16[64,16,128]{2,1,0:T(8,128)(2,1)S(1)}, bf16[64,16,128]{2,1,0:T(8,128)(2,1)S(1)}, u32[]{:S(2)}, u32[]{:S(2)}) %collective-permute-start.6) | collective-permute-done | bytes 262176 | tf_op jit(solution)/shard_map/ppermute | solution.py:22
  36.8 7.7 %second_kernel.1 = (f32[64,8,128]{2,1,0:T(8,128)S(1)}, f32[64,128]{1,0:T(8,128)S(1)}, f32[64,8,128]{2,1,0:T(8,128)S(1)}) custom-call(s32[8,256]{1,0:T(8,128)S(1)} %get-tuple-element.28.idx, bf16[64,16,128]{2,1,0:T(8,128)(2,1)S(1)} %enter_first_kernel.1.own.refs_4_, bf16[64,16,128]{2,1,0:T(8,128)(2,1)S(1)} %collective-permute-done.5.got_even, ...), custom_call_target="tpu_custom_call" | custom-call | flops 3288334336 | bytes 2596864 | tf_op jit(solution)/shard_map/second_kernel/pallas_call | solution.py:368
  44.5 2.7 %collective-permute-start.9 = (f32[64,128]{1,0:T(8,128)S(1)}, f32[64,128]{1,0:T(8,128)S(1)}, u32[]{:S(2)}, u32[]{:S(2)}) collective-permute-start(f32[64,128]{1,0:T(8,128)S(1)} %get-tuple-element.32), channel_id=1, source_target_pairs={{0,12},{1,13},{2,14},{3,15},{16,28},{17,29},{18,30},{19,31}} | collective-permute-start | bytes 98312 | tf_op jit(solution)/shard_map/ppermute | solution.py:28
  47.3 1.3 %collective-permute-start.8 = (f32[64,128]{1,0:T(8,128)S(1)}, f32[64,128]{1,0:T(8,128)S(1)}, u32[]{:S(2)}, u32[]{:S(2)}) collective-permute-start(f32[64,128]{1,0:T(8,128)S(1)} %get-tuple-element.32), channel_id=1, source_target_pairs={{0,8},{4,12},{1,9},{5,13},{2,10},{6,14},{3,11},{7,15},{16,24},{20,... | collective-permute-start | bytes 98312 | tf_op jit(solution)/shard_map/ppermute | solution.py:28
  48.6 2.2 %collective-permute-start.7 = (f32[64,128]{1,0:T(8,128)S(1)}, f32[64,128]{1,0:T(8,128)S(1)}, u32[]{:S(2)}, u32[]{:S(2)}) collective-permute-start(f32[64,128]{1,0:T(8,128)S(1)} %get-tuple-element.32), channel_id=1, source_target_pairs={{0,4},{4,8},{8,12},{1,5},{5,9},{9,13},{2,6},{6,10},{10,14},{3,7},{... | collective-permute-start | bytes 98312 | tf_op jit(solution)/shard_map/ppermute | solution.py:28
  50.8 0.7 %scan_kernel.3.refs_3_ = f32[64,8,128]{2,1,0:T(8,128)S(1)} custom-call(f32[64,8,128]{2,1,0:T(8,128)S(1)} %get-tuple-element.33.values, bf16[1024,256]{1,0:T(8,128)(2,1)S(1)} %get-tuple-element.27.pk.refs_5_.refs_7_), custom_call_target="tpu_custom_call" | custom-call | flops 10000000 | bytes 1048576 | tf_op jit(solution)/shard_map/scan_kernel/pallas_call | solution.py:368
  51.8 0.6 enter_second_kernel.1
  52.5 5.0 %collective-permute-start.11 = (bf16[48,16,128]{2,1,0:T(8,128)(2,1)S(1)}, bf16[48,16,128]{2,1,0:T(8,128)(2,1)S(1)}, u32[]{:S(2)}, u32[]{:S(2)}) collective-permute-start(bf16[48,16,128]{2,1,0:T(8,128)(2,1)S(1)} %get-tuple-element.36), channel_id=1, source_target_pairs={{1,2},{2,1},{5,6},{6,5},{9,10},{10,9},{13,14},{14,13},{17,18},{18,... | collective-permute-start | bytes 589832 | tf_op jit(solution)/shard_map/ppermute | solution.py:22
  57.7 2.8 %collective-permute-done.11.got_odd = bf16[48,16,128]{2,1,0:T(8,128)(2,1)S(1)} collective-permute-done((bf16[48,16,128]{2,1,0:T(8,128)(2,1)S(1)}, bf16[48,16,128]{2,1,0:T(8,128)(2,1)S(1)}, u32[]{:S(2)}, u32[]{:S(2)}) %collective-permute-start.11) | collective-permute-done | bytes 196640 | tf_op jit(solution)/shard_map/ppermute | solution.py:22
  60.6 6.6 %third_kernel.1 = f32[2048,128]{1,0:T(8,128)} custom-call(s32[8,256]{1,0:T(8,128)S(1)} %get-tuple-element.28.idx, bf16[64,16,128]{2,1,0:T(8,128)(2,1)S(1)} %get-tuple-element.34.own, bf16[48,16,128]{2,1,0:T(8,128)(2,1)S(1)} %collective-permute-done.10.got_even, bf16[48,16,128]{2,1,0:T(8,128)(2,1)S(1)} %collective-permute-done.11.got_odd, ...), custom_call_target="tpu_custom_call" | custom-call | flops 2348810240 | bytes 3424256 | tf_op jit(solution)/shard_map/third_kernel/pallas_call | solution.py:368
  (26 shorter events, 1.7 us)
Async XLA Ops:
  0.0 0.7 %copy-start.3 = (s32[64,6]{0,1:T(8,128)S(1)}, s32[64,6]{0,1:T(8,128)}, u32[]{:S(2)}) copy-start(s32[64,6]{0,1:T(8,128)} %param.9) | copy-start | bytes 4612
  0.7 1.0 %copy-start = (bf16[32,64,128]{2,1,0:T(8,128)(2,1)S(1)}, bf16[32,64,128]{2,1,0:T(8,128)(2,1)}, u32[]{:S(2)}) copy-start(bf16[32,64,128]{2,1,0:T(8,128)(2,1)} %param.7) | copy-start | bytes 1572868
  1.7 0.8 %copy-start.1 = (f32[64,128]{1,0:T(8,128)S(1)}, f32[64,128]{1,0:T(8,128)}, u32[]{:S(2)}) copy-start(f32[64,128]{1,0:T(8,128)} %refs_5_.1) | copy-start | bytes 98308
  2.5 0.7 %copy-start.4 = (s32[64,6]{0,1:T(8,128)S(1)}, s32[64,6]{0,1:T(8,128)}, u32[]{:S(2)}) copy-start(s32[64,6]{0,1:T(8,128)} %param.10) | copy-start | bytes 4612
  3.2 5.4 %copy-start.5 = (f32[6,128,128]{2,1,0:T(8,128)S(1)}, f32[6,128,128]{2,1,0:T(8,128)}, u32[]{:S(2)}) copy-start(f32[6,128,128]{2,1,0:T(8,128)} %faces.1) | copy-start | bytes 1179652
  3.2 5.4 %copy-start.6 = (f32[128,128]{1,0:T(8,128)S(1)}, f32[128,128]{1,0:T(8,128)}, u32[]{:S(2)}) copy-start(f32[128,128]{1,0:T(8,128)} %diag.1) | copy-start | bytes 196612
  3.2 5.4 %copy-start.7 = (f32[128,128]{1,0:T(8,128)S(1)}, f32[128,128]{1,0:T(8,128)}, u32[]{:S(2)}) copy-start(f32[128,128]{1,0:T(8,128)} %coarse.1) | copy-start | bytes 196612
  4.0 6.2 %collective-permute-start = (bf16[912,128]{1,0:T(8,128)(2,1)S(1)}, bf16[912,128]{1,0:T(8,128)(2,1)S(1)}, u32[]{:S(2)}, u32[]{:S(2)}) collective-permute-start(bf16[912,128]{1,0:T(8,128)(2,1)S(1)} %get-tuple-element.24), channel_id=1, source_target_pairs={{0,1},{1,0},{2,3},{3,2},{4,5},{5,4},{6,7},{7,6},{8,9},{9,8},{10,11... | collective-permute-start | bytes 700424 | tf_op jit(solution)/shard_map/ppermute | solution.py:22
  4.0 8.2 %copy-start.2 = (f32[64,128]{1,0:T(8,128)S(1)}, f32[64,128]{1,0:T(8,128)}, u32[]{:S(2)}) copy-start(f32[64,128]{1,0:T(8,128)} %refs_5_.1) | copy-start | bytes 98308
  4.0 8.2 %collective-permute-start.1 = (bf16[912,128]{1,0:T(8,128)(2,1)S(1)}, bf16[912,128]{1,0:T(8,128)(2,1)S(1)}, u32[]{:S(2)}, u32[]{:S(2)}) collective-permute-start(bf16[912,128]{1,0:T(8,128)(2,1)S(1)} %get-tuple-element.25), channel_id=1, source_target_pairs={{1,2},{2,1},{5,6},{6,5},{9,10},{10,9},{13,14},{14,13},{17,18},{18,... | collective-permute-start | bytes 700424 | tf_op jit(solution)/shard_map/ppermute | solution.py:22
  17.7 10.2 %collective-permute-start.4 = (f32[64,128]{1,0:T(8,128)S(1)}, f32[64,128]{1,0:T(8,128)S(1)}, u32[]{:S(2)}, u32[]{:S(2)}) collective-permute-start(f32[64,128]{1,0:T(8,128)S(1)} %get-tuple-element.29), channel_id=1, source_target_pairs={{0,12},{1,13},{2,14},{3,15},{16,28},{17,29},{18,30},{19,31}} | collective-permute-start | bytes 98312 | tf_op jit(solution)/shard_map/ppermute | solution.py:28
  23.6 4.2 %collective-permute-start.3 = (f32[64,128]{1,0:T(8,128)S(1)}, f32[64,128]{1,0:T(8,128)S(1)}, u32[]{:S(2)}, u32[]{:S(2)}) collective-permute-start(f32[64,128]{1,0:T(8,128)S(1)} %get-tuple-element.29), channel_id=1, source_target_pairs={{0,8},{4,12},{1,9},{5,13},{2,10},{6,14},{3,11},{7,15},{16,24},{20,... | collective-permute-start | bytes 98312 | tf_op jit(solution)/shard_map/ppermute | solution.py:28
  24.9 3.2 %collective-permute-start.2 = (f32[64,128]{1,0:T(8,128)S(1)}, f32[64,128]{1,0:T(8,128)S(1)}, u32[]{:S(2)}, u32[]{:S(2)}) collective-permute-start(f32[64,128]{1,0:T(8,128)S(1)} %get-tuple-element.29), channel_id=1, source_target_pairs={{0,4},{4,8},{8,12},{1,5},{5,9},{9,13},{2,6},{6,10},{10,14},{3,7},{... | collective-permute-start | bytes 98312 | tf_op jit(solution)/shard_map/ppermute | solution.py:28
  28.7 8.1 %collective-permute-start.6 = (bf16[64,16,128]{2,1,0:T(8,128)(2,1)S(1)}, bf16[64,16,128]{2,1,0:T(8,128)(2,1)S(1)}, u32[]{:S(2)}, u32[]{:S(2)}) collective-permute-start(bf16[64,16,128]{2,1,0:T(8,128)(2,1)S(1)} %enter_first_kernel.1.own.refs_4_), channel_id=1, source_target_pairs={{1,2},{2,1},{5,6},{6,5},{9,10},{10,9},{13,14},{14,13},{17,18},{18,... | collective-permute-start | bytes 786440 | tf_op jit(solution)/shard_map/ppermute | solution.py:22
  32.7 4.0 %collective-permute-start.5 = (bf16[64,16,128]{2,1,0:T(8,128)(2,1)S(1)}, bf16[64,16,128]{2,1,0:T(8,128)(2,1)S(1)}, u32[]{:S(2)}, u32[]{:S(2)}) collective-permute-start(bf16[64,16,128]{2,1,0:T(8,128)(2,1)S(1)} %enter_first_kernel.1.own.refs_4_), channel_id=1, source_target_pairs={{0,1},{1,0},{2,3},{3,2},{4,5},{5,4},{6,7},{7,6},{8,9},{9,8},{10,11... | collective-permute-start | bytes 786440 | tf_op jit(solution)/shard_map/ppermute | solution.py:22
  44.5 7.0 %collective-permute-start.9 = (f32[64,128]{1,0:T(8,128)S(1)}, f32[64,128]{1,0:T(8,128)S(1)}, u32[]{:S(2)}, u32[]{:S(2)}) collective-permute-start(f32[64,128]{1,0:T(8,128)S(1)} %get-tuple-element.32), channel_id=1, source_target_pairs={{0,12},{1,13},{2,14},{3,15},{16,28},{17,29},{18,30},{19,31}} | collective-permute-start | bytes 98312 | tf_op jit(solution)/shard_map/ppermute | solution.py:28
  47.3 4.2 %collective-permute-start.8 = (f32[64,128]{1,0:T(8,128)S(1)}, f32[64,128]{1,0:T(8,128)S(1)}, u32[]{:S(2)}, u32[]{:S(2)}) collective-permute-start(f32[64,128]{1,0:T(8,128)S(1)} %get-tuple-element.32), channel_id=1, source_target_pairs={{0,8},{4,12},{1,9},{5,13},{2,10},{6,14},{3,11},{7,15},{16,24},{20,... | collective-permute-start | bytes 98312 | tf_op jit(solution)/shard_map/ppermute | solution.py:28
  48.6 3.2 %collective-permute-start.7 = (f32[64,128]{1,0:T(8,128)S(1)}, f32[64,128]{1,0:T(8,128)S(1)}, u32[]{:S(2)}, u32[]{:S(2)}) collective-permute-start(f32[64,128]{1,0:T(8,128)S(1)} %get-tuple-element.32), channel_id=1, source_target_pairs={{0,4},{4,8},{8,12},{1,5},{5,9},{9,13},{2,6},{6,10},{10,14},{3,7},{... | collective-permute-start | bytes 98312 | tf_op jit(solution)/shard_map/ppermute | solution.py:28
  52.4 5.3 %collective-permute-start.10 = (bf16[48,16,128]{2,1,0:T(8,128)(2,1)S(1)}, bf16[48,16,128]{2,1,0:T(8,128)(2,1)S(1)}, u32[]{:S(2)}, u32[]{:S(2)}) collective-permute-start(bf16[48,16,128]{2,1,0:T(8,128)(2,1)S(1)} %get-tuple-element.35), channel_id=1, source_target_pairs={{0,1},{1,0},{2,3},{3,2},{4,5},{5,4},{6,7},{7,6},{8,9},{9,8},{10,11... | collective-permute-start | bytes 589832 | tf_op jit(solution)/shard_map/ppermute | solution.py:22
  52.5 8.1 %collective-permute-start.11 = (bf16[48,16,128]{2,1,0:T(8,128)(2,1)S(1)}, bf16[48,16,128]{2,1,0:T(8,128)(2,1)S(1)}, u32[]{:S(2)}, u32[]{:S(2)}) collective-permute-start(bf16[48,16,128]{2,1,0:T(8,128)(2,1)S(1)} %get-tuple-element.36), channel_id=1, source_target_pairs={{1,2},{2,1},{5,6},{6,5},{9,10},{10,9},{13,14},{14,13},{17,18},{18,... | collective-permute-start | bytes 589832 | tf_op jit(solution)/shard_map/ppermute | solution.py:22

commit v2 on v1

v2 whole, which is shorter than its diff:
```python
import functools

import jax
import jax.numpy as jnp
from jax import lax
from jax.experimental import pallas as pl
from jax.experimental.pallas import tpu as pltpu
from jax.sharding import PartitionSpec as P

COARSEN = 4
REACH = 16
F32 = jnp.float32
BF16 = jnp.bfloat16
CHUNK = 32


def swapped(value, first):
    count = lax.axis_size("space")
    pairs = []
    for i in range(first, count - 1, 2):
        pairs += [(i, i + 1), (i + 1, i)]
    return lax.ppermute(value, "space", pairs)


def earlier(value):
    count = lax.axis_size("tm")
    if count <= 8:
        return [lax.ppermute(value, "tm", [(i, i + s) for i in range(count - s)]) for s in range(1, count)]
    every = lax.all_gather(value, "tm")
    at = lax.axis_index("tm") - jnp.arange(1, count)
    picked = jnp.where((at >= 0)[:, None, None], jnp.take(every, jnp.maximum(at, 0), axis=0), 0.0)
    return [picked[s] for s in range(count - 1)]


def split(u):
    lead = u.astype(BF16).astype(F32)
    return jnp.concatenate([u, u - lead], axis=1).astype(BF16)


def split_rows(u):
    lead = u.astype(BF16)
    return jnp.concatenate([lead, (u - lead.astype(F32)).astype(BF16)], axis=0)


def product(x, weights):
    m = x.shape[0] // 16
    r = jnp.dot(x, weights, preferred_element_type=F32).reshape(m, 16, 256)
    return r[:, :8, :128] + (r[:, 8:, :128] + r[:, :8, 128:])


def product_rows(x, weights):
    m = x.shape[0] // 2
    r = jnp.dot(x, weights, preferred_element_type=F32)
    return r[:m, :128] + (r[m:, :128] + r[:m, 128:])


def put_halves(ref, w):
    lead = w.astype(BF16)
    ref[:, 0:128] = lead
    ref[:, 128:256] = (w - lead.astype(F32)).astype(BF16)


def power(pk, k):
    return pk[pl.ds(128 * (7 - k), 128), :]


def scan_starts(values, pk):
    y = values
    row = lax.broadcasted_iota(jnp.int32, y.shape, 1)
    for d in (1, 2, 4):
        z = product(split(y).reshape(-1, 128), power(pk, d))
        y = y + jnp.where(row >= d, pltpu.roll(z, d, axis=1), 0.0)
    return jnp.where(row >= 1, pltpu.roll(y, 1, axis=1), 0.0)


def block_end(y, pk, n):
    parts = [y[pl.ds(i, n, stride=8), :] for i in range(8)]
    return product_rows(split_rows(jnp.concatenate(parts, axis=1)), pk[...])


def enter(arrivals, we, pk, y, n):
    value = jnp.concatenate([a[...] for a in arrivals], axis=1)
    entry = product_rows(split_rows(value), we[...])
    y[pl.ds(0, n, stride=8), :] = entry
    rows = split_rows(entry)
    for i in range(1, 8):
        y[pl.ds(i, n, stride=8), :] = product_rows(rows, power(pk, i))
    return y[...].reshape(n, 8, 128)


def apply_phi(src, idx, w, base, size):
    cols = [src[pl.ds(base, size)].reshape(size * 16, 128)]
    for f in range(6):
        cols.append(jnp.concatenate([src[idx[f, base + e]] for e in range(size)], axis=0))
    return product(jnp.concatenate(cols, axis=1), w[...])


def even_place():
    return lax.rem(lax.axis_index("space"), 2) == 0


def mirrored(low, size, full):
    return jnp.where(even_place(), full - low - size, low)


def pack_kernel(
    forcing, init, conn, pattern, fe, tab, pay_even, pay_odd, landed, rows, init_v, conn_v, pattern_v, offs, sems
):
    n = init_v.shape[0]
    copies = [pltpu.make_async_copy(forcing.at[:, k], landed.at[k], sems.at[k]) for k in range(COARSEN)]
    small = ((conn, conn_v), (pattern, pattern_v), (init, init_v))
    copies += [pltpu.make_async_copy(src, dst, sems.at[COARSEN + i]) for i, (src, dst) in enumerate(small)]
    for copy in copies:
        copy.start()
    for copy in copies[COARSEN:]:
        copy.wait()
    place = lax.broadcasted_iota(jnp.int32, (6, n), 1) + lax.axis_index("space") * n
    value = ((conn_v[...] - place) * pattern_v[...]).astype(F32)
    offs[...] = jnp.zeros_like(offs)
    offs[0:6, 0:n] = value
    offs[0:6, n : 2 * n] = value
    tab[...] = offs[...].astype(BF16)
    lead = init_v[...].astype(BF16)
    rest = (init_v[...] - lead.astype(F32)).astype(BF16)
    even = even_place()
    at = sum((COARSEN - 1 - k) * REACH * 8 for k in range(COARSEN))
    for pay in (pay_even, pay_odd):
        pay[pl.ds(at, n), :] = lead
        pay[pl.ds(at + n, n), :] = rest
        pay[pl.ds(at + 2 * n, 16), :] = tab[...]
    at = 0
    for k in range(COARSEN):
        copies[k].wait()
        for i in range(8):
            rows[pl.ds(i * n, n), :] = landed[k, i].astype(F32)

        def body(pair, carry, k=k):
            e = pair * 2
            two = [rows[pl.ds(e + j, 8, stride=n), :] for j in range(2)]
            fe[k, pl.ds(pl.multiple_of(e * 8, 16), 16), :] = jnp.concatenate(two, axis=0).astype(BF16)
            return carry

        lax.fori_loop(0, n // 2, body, 0, unroll=8)
        width = (COARSEN - 1 - k) * REACH * 8
        if width:
            for pay, right in ((pay_even, even), (pay_odd, jnp.logical_not(even))):
                begin = pl.multiple_of(jnp.where(right, n * 8 - width, 0), 128)
                pay[pl.ds(at, width), :] = fe[k, pl.ds(begin, width), :]
        at += width


def weight_kernel(diag, faces, coarse, w, pk, we):
    put_halves(w.at[pl.ds(0, 128)], diag[...].T)
    for f in range(6):
        put_halves(w.at[pl.ds(128 * (f + 1), 128)], faces[f].T)

    def thirds(a):
        one = a.astype(BF16)
        rest = a - one.astype(F32)
        two = rest.astype(BF16)
        return one, two, (rest - two.astype(F32)).astype(BF16)

    def mul(a, b):
        (a1, a2, a3), (b1, b2, b3) = thirds(a), thirds(b)
        total = jnp.zeros((128, 128), F32)
        for x, y in ((a3, b1), (a1, b3), (a2, b2), (a2, b1), (a1, b2), (a1, b1)):
            total += jnp.dot(x, y, preferred_element_type=F32)
        return total

    rows = lax.broadcasted_iota(jnp.int32, (128, 128), 0)
    one = (rows == lax.broadcasted_iota(jnp.int32, (128, 128), 1)).astype(F32)
    powers = [one, coarse[...].T]
    for k in range(2, 9):
        powers.append(mul(powers[k // 2], powers[k - k // 2]))
    for k in range(8):
        put_halves(pk.at[pl.ds(128 * (7 - k), 128)], powers[k])

    def body(k, current):
        put_halves(we.at[pl.ds(pl.multiple_of(k * 128, 128), 128)], current)
        return mul(current, powers[8])

    lax.fori_loop(0, we.shape[0] // 128, body, one)


def put_force(dst, own, got, right, k, n):
    at = sum((COARSEN - 1 - j) * REACH * 8 for j in range(k))
    width = (COARSEN - 1 - k) * REACH * 8
    dst[pl.ds(n * 8, n * 8), :] = own[k]
    if width:
        to = pl.multiple_of(jnp.where(right, 2 * n * 8, n * 8 - width), 128)
        dst[pl.ds(to, width), :] = got[pl.ds(at, width), :]


def force_at(src, base, size):
    at = pl.multiple_of(base * 8, 128)
    return src[pl.ds(at, size * 8), :].astype(F32).reshape(size, 8, 128)


def put_tables(tab, got_even, got_odd, idx_v, columns, square, full, n):
    even = even_place()
    lane = lax.broadcasted_iota(jnp.int32, (8, 128), 1)

    def table(ref):
        return 0.0 if ref is None else ref[pl.ds(ref.shape[0] - 16, 16), :].astype(F32)[0:8]

    from_even, from_odd = table(got_even), table(got_odd)
    low = jnp.where(lane < n, jnp.where(even, from_odd, from_even), table(tab))
    high = jnp.where(lane < n, jnp.where(even, from_even, from_odd), 0.0)
    for at, offs in ((0, low), (128, high)):
        value = jnp.where(offs != 0.0, lane + at + offs.astype(jnp.int32), full)
        idx_v[:, pl.ds(at, 128)] = value
        square[...] = jnp.zeros_like(square)
        square[0:8, :] = value.astype(F32)
        columns[pl.ds(at, 128), :] = square[...].T


def push_init(init, got_even, got_odd, w, columns, i16, base, count, n):
    even = even_place()
    i16[...] = jnp.zeros_like(i16)
    lead = init[...].astype(BF16)
    i16[pl.ds(n, n), 0:128] = lead
    i16[pl.ds(n, n), 128:256] = (init[...] - lead.astype(F32)).astype(BF16)
    for ref, right in ((got_even, even), (got_odd, jnp.logical_not(even))):
        if ref is not None:
            at = ref.shape[0] - 16
            to = pl.multiple_of(jnp.where(right, 2 * n, 0), n)
            i16[pl.ds(to, n), 0:128] = ref[pl.ds(at - 2 * n, n), :]
            i16[pl.ds(to, n), 128:256] = ref[pl.ds(at - n, n), :]
    rows = pl.ds(pl.multiple_of(base, REACH), count)
    place = columns[rows, :]
    spot = lax.broadcasted_iota(jnp.int32, (count, 256), 1).astype(F32)
    cols = [i16[rows, :]]
    for f in range(6):
        hot = (spot == place[:, f : f + 1]).astype(F32).astype(BF16)
        cols.append(jnp.dot(hot, i16[...], preferred_element_type=F32).astype(BF16))
    leads = jnp.concatenate([c[:, 0:128] for c in cols], axis=1)
    rests = jnp.concatenate([c[:, 128:256] for c in cols], axis=1)
    pushed = product_rows(jnp.concatenate([leads, rests], axis=0), w[...])
    return pushed * (lax.axis_index("tm") == 0).astype(F32)


STRIPS = (5 * REACH, 4 * REACH, 3 * REACH)
STRIP = 2 * REACH


def put_strips(strips, states, full):
    for strip, state, low in zip(strips, states, STRIPS):
        strip[...] = state[pl.ds(mirrored(low, STRIP, full), STRIP)]


def get_strips(strips, states, full):
    for strip, state, low in zip(strips, states, STRIPS):
        state[pl.ds(mirrored(low, STRIP, full), STRIP)] = strip[...]
        state[full] = jnp.zeros((16, 128), BF16)


def first_early_kernel(
    fe, tab, init, got, w, strip1, strip2, strip3, s1, s2, s3, force, y, i16, columns, square, idx_v, idx, sem
):
    n = init.shape[0]
    full = 3 * n
    even = even_place()
    put_tables(tab, got, None, idx_v, columns, square, full, n)
    copy = pltpu.make_async_copy(idx_v, idx, sem)
    copy.start()
    count = 6 * REACH
    base = mirrored(REACH, count, full)
    pushed = push_init(init, got, None, w, columns, i16, base, count, n)
    put_force(force, fe, got, even, 0, n)
    y[pl.ds(0, count * 8), :] = force[pl.ds(pl.multiple_of(base * 8, 128), count * 8), :].astype(F32)
    y[pl.ds(0, count, stride=8), :] = y[pl.ds(0, count, stride=8), :] + pushed
    s1[pl.ds(base, count)] = split(y[pl.ds(0, count * 8), :].reshape(count, 8, 128))
    for state in (s1, s2, s3):
        state[full] = jnp.zeros((16, 128), BF16)
    copy.wait()
    for k, src, dst in ((1, s1, s2), (2, s2, s3)):
        put_force(force, fe, got, even, k, n)
        size = (6 - 2 * k) * REACH
        base = mirrored((k + 1) * REACH, size, full)
        dst[pl.ds(base, size)] = split(apply_phi(src, idx, w, base, size) + force_at(force, base, size))
    put_strips((strip1, strip2, strip3), (s1, s2, s3), full)


def first_late_kernel(
    fe, tab, init, got_even, got_odd, strip1, strip2, strip3, w, pk, w1, end, idx_out,
    s1, s2, s3, force, y, i16, columns, square, idx, sem
):
    n = init.shape[0]
    full = 3 * n
    odd = jnp.logical_not(even_place())
    put_tables(tab, got_even, got_odd, idx_out, columns, square, full, n)
    copy = pltpu.make_async_copy(idx_out, idx, sem)
    copy.start()
    count = 4 * REACH
    base = mirrored(7 * REACH, count, full)
    pushed = push_init(init, got_even, got_odd, w, columns, i16, base, count, n)
    put_force(force, fe, got_odd, odd, 0, n)
    y[...] = force[pl.ds(pl.multiple_of(base * 8, 128), count * 8), :].astype(F32)
    y[pl.ds(0, count, stride=8), :] = y[pl.ds(0, count, stride=8), :] + pushed
    s1[pl.ds(base, count)] = split(y[...].reshape(count, 8, 128))
    get_strips((strip1, strip2, strip3), (s1, s2, s3), full)
    copy.wait()
    for k, src, dst in ((1, s1, s2), (2, s2, s3), (3, s3, None)):
        put_force(force, fe, got_odd, odd, k, n)
        base = mirrored((7 - k) * REACH, count, full)
        value = apply_phi(src, idx, w, base, count) + force_at(force, base, count)
        if dst is None:
            w1[...] = value
            y[...] = value.reshape(n * 8, 128)
        else:
            dst[pl.ds(base, count)] = split(value)
    end[...] = block_end(y, pk, n)


def scan_kernel(values, pk, starts):
    starts[...] = scan_starts(values[...], pk)


def enter_first_kernel(*refs):
    *arrivals, starts, we, pk, state, y = refs
    n = starts.shape[0]
    state[...] = split(enter(arrivals, we, pk, y, n) + starts[...])


def enter_second_kernel(*refs):
    *arrivals, starts, before, init, we, pk, state, pay_even, pay_odd, corr, y = refs
    n = starts.shape[0]
    value = enter(arrivals, we, pk, y, n) + starts[...]
    corr[...] = value
    old = before[...].astype(F32)
    y[...] = (value + (old[:, 0:8] + old[:, 8:16])).reshape(n * 8, 128)
    first = (lax.axis_index("tm") == 0).astype(F32)
    y[pl.ds(0, n, stride=8), :] = y[pl.ds(0, n, stride=8), :] + init[...] * first
    state[...] = split(y[...].reshape(n, 8, 128))
    side = (COARSEN - 1) * REACH
    even = even_place()
    pay_even[...] = state[pl.ds(jnp.where(even, n - side, 0), side)]
    pay_odd[...] = state[pl.ds(jnp.where(even, 0, n - side), side)]


def put_block(dst, own, got, right, n):
    side = got.shape[0]
    dst[pl.ds(n, n)] = own[...]
    dst[pl.ds(jnp.where(right, 2 * n, n - side), side)] = got[...]
    dst[3 * n] = jnp.zeros((16, 128), BF16)


def second_early_kernel(idx, own, got, w, strip1, strip2, strip3, s0, s1, s2, s3):
    n = own.shape[0]
    full = 3 * n
    put_block(s0, own, got, even_place(), n)
    for state in (s1, s2, s3):
        state[full] = jnp.zeros((16, 128), BF16)
    for k, src, dst in ((1, s0, s1), (2, s1, s2), (3, s2, s3)):
        size = (8 - 2 * k) * REACH
        base = mirrored(k * REACH, size, full)
        dst[pl.ds(base, size)] = split(apply_phi(src, idx, w, base, size))
    put_strips((strip1, strip2, strip3), (s1, s2, s3), full)


def second_late_kernel(idx, own, got, strip1, strip2, strip3, w1, w, pk, res, end, total, s0, s1, s2, s3, y):
    n = own.shape[0]
    full = 3 * n
    put_block(s0, own, got, jnp.logical_not(even_place()), n)
    get_strips((strip1, strip2, strip3), (s1, s2, s3), full)
    count = 4 * REACH
    for k, src, dst in ((1, s0, s1), (2, s1, s2), (3, s2, s3)):
        base = mirrored((8 - k) * REACH, count, full)
        dst[pl.ds(base, count)] = split(apply_phi(src, idx, w, base, count))
    value = apply_phi(s3, idx, w, n, n)
    total[...] = value + w1[...]
    value = value - product(own[...].reshape(n * 16, 128), power(pk, 1))
    res[...] = value
    y[...] = value.reshape(n * 8, 128)
    end[...] = block_end(y, pk, n)


def write_out(out, k, value, begin, flip, sems):
    size = value.shape[0]
    for e in range(size):
        flip[pl.ds(e, 8, stride=size), :] = value[e]
    rows = pl.ds(pl.multiple_of(begin, REACH), size)
    copies = [
        pltpu.make_async_copy(flip.at[pl.ds(i * size, size)], out.at[i * COARSEN + k, rows], sems.at[k, i])
        for i in range(8)
    ]
    for copy in copies:
        copy.start()
    return copies


def third_early_kernel(
    idx, own, got, corr, total, fe, pay, w, pk, out, strip1, strip2, s0, s1, s2, force, flip0, flip1, flip2, flip3, sems
):
    n = own.shape[0]
    full = 3 * n
    even = even_place()
    points = product(split(corr[...]).reshape(-1, 128), power(pk, 1)) + total[...]
    copies = write_out(out, COARSEN - 1, points, 0, flip3, sems)
    put_block(s0, own, got, even, n)
    for state in (s1, s2):
        state[full] = jnp.zeros((16, 128), BF16)
    for k, src, dst, flip in ((0, s0, s1, flip0), (1, s1, s2, flip1), (2, s2, None, flip2)):
        put_force(force, fe, pay, even, k, n)
        size = (5 - 2 * k) * REACH
        base = mirrored((2 + k) * REACH, size, full)
        value = apply_phi(src, idx, w, base, size) + force_at(force, base, size)
        if dst is not None:
            dst[pl.ds(base, size)] = split(value)
        mine = (3 - k) * REACH
        skip = size - mine
        kept = jnp.where(even, value[:mine], value[skip:])
        copies += write_out(out, k, kept, jnp.where(even, n - mine, 0), flip, sems)
    put_strips((strip1, strip2), (s1, s2), full)
    for copy in copies:
        copy.wait()


def third_late_kernel(
    idx, own, got, strip1, strip2, fe, pay, w, partial, out, s0, s1, s2, force, flip0, flip1, flip2, sems
):
    n = own.shape[0]
    full = 3 * n
    even = even_place()
    odd = jnp.logical_not(even)
    put_block(s0, own, got, odd, n)
    get_strips((strip1, strip2), (s1, s2), full)
    copies = []
    size = 3 * REACH
    for k, src, dst, flip in ((0, s0, s1, flip0), (1, s1, s2, flip1), (2, s2, None, flip2)):
        put_force(force, fe, pay, odd, k, n)
        base = mirrored((7 - k) * REACH, size, full)
        value = apply_phi(src, idx, w, base, size) + force_at(force, base, size)
        if dst is not None:
            dst[pl.ds(base, size)] = split(value)
        mine = (k + 1) * REACH
        kept = jnp.where(even, value[size - mine :], value[:mine])
        copies += write_out(out, k, kept, jnp.where(even, 0, n - mine), flip, sems)
    for copy in copies:
        copy.wait()


def call(kernel, inputs, outs, scratch, spaces="", out_spaces="", aliases=None, flops=10**7, room=32):
    kinds = {"s": pltpu.SMEM, "h": pltpu.HBM, "v": pltpu.VMEM}

    def specs(arrays, letters):
        letters = letters.ljust(len(arrays), "v")
        return [pl.BlockSpec(memory_space=kinds[letter]) for letter in letters]

    moved = sum(a.size * a.dtype.itemsize for a in list(inputs) + list(outs))
    return pl.pallas_call(
        kernel,
        out_shape=outs,
        name=kernel.__name__,
        in_specs=specs(inputs, spaces),
        out_specs=specs(outs, out_spaces),
        scratch_shapes=scratch,
        input_output_aliases=aliases or {},
        compiler_params=pltpu.CompilerParams(vmem_limit_bytes=room * 1024 * 1024),
        cost_estimate=pl.CostEstimate(flops=flops, bytes_accessed=moved, transcendentals=0),
    )(*inputs)


def local(forcing, initial_state, connectivity, pattern, diag_block, face_blocks, coarse_block):
    n, width = initial_state.shape
    steps = forcing.shape[0]
    full = 3 * n
    tm = lax.axis_size("tm")
    shape = jax.ShapeDtypeStruct
    vmem = pltpu.VMEM
    dma = pltpu.SemaphoreType.DMA
    tiles = shape((n, 8, width), F32)
    state = shape((n, 16, width), BF16)
    ends = shape((n, width), F32)
    step_flops = 2 * 16 * 7 * width * 2 * width
    pay_rows = sum((COARSEN - 1 - k) * REACH * 8 for k in range(COARSEN)) + 2 * n + 16
    pay = shape((pay_rows, width), BF16)
    fe, tab, pay_even, pay_odd = call(
        pack_kernel,
        (forcing.reshape(steps // COARSEN, COARSEN, n, width), initial_state, connectivity.T, pattern.T),
        (shape((COARSEN, n * 8, width), BF16), shape((16, 128), BF16), pay, pay),
        [
            vmem((COARSEN, 8, n, width), BF16),
            vmem((8 * n, width), F32),
            vmem((n, width), F32),
            vmem((6, n), jnp.int32),
            vmem((6, n), jnp.int32),
            vmem((16, 128), F32),
            dma((COARSEN + 3,)),
        ],
        spaces="hhhh",
        room=62,
    )
    pay_odd, pay_even = swapped(pay_odd, 1), swapped(pay_even, 0)
    w, pk, we = call(
        weight_kernel,
        (diag_block, face_blocks, coarse_block),
        (
            shape((7 * width, 2 * width), BF16),
            shape((8 * width, 2 * width), BF16),
            shape(((tm - 1) * width, 2 * width), BF16),
        ),
        [],
        flops=10**9,
    )
    spaces = vmem((full + 1, 16, width), BF16)
    force = vmem((full * 8, width), BF16)
    rows = vmem((n * 8, width), F32)
    strip = shape((STRIP, 16, width), BF16)
    tables = [vmem((256, 256), BF16), vmem((256, 128), F32), vmem((128, 128), F32)]
    smem = pltpu.SMEM((8, 256), jnp.int32)
    strips = call(
        first_early_kernel,
        (fe, tab, initial_state, pay_even, w),
        (strip, strip, strip),
        [spaces] * 3 + [force, vmem((6 * REACH * 8, width), F32)] + tables + [vmem((8, 256), jnp.int32), smem, dma],
        flops=step_flops * 6 * REACH,
    )
    w1, end, idx = call(
        first_late_kernel,
        (fe, tab, initial_state, pay_even, pay_odd, *strips, w, pk),
        (tiles, ends, shape((8, 256), jnp.int32)),
        [spaces] * 3 + [force, rows] + tables + [smem, dma],
        flops=step_flops * 12 * REACH,
    )
    arrivals = earlier(end)
    (starts,) = call(scan_kernel, (w1, pk), (tiles,), [])
    (coarse,) = call(enter_first_kernel, (*arrivals, starts, we, pk), (state,), [rows])
    got_odd, got_even = swapped(coarse, 1), swapped(coarse, 0)
    strips = call(
        second_early_kernel,
        (idx, coarse, got_even, w),
        (strip, strip, strip),
        [spaces] * 4,
        spaces="s",
        flops=step_flops * 12 * REACH,
    )
    res, end, total = call(
        second_late_kernel,
        (idx, coarse, got_odd, *strips, w1, w, pk),
        (tiles, ends, tiles),
        [spaces] * 4 + [rows],
        spaces="s",
        flops=step_flops * 16 * REACH,
    )
    arrivals = earlier(end)
    (starts,) = call(scan_kernel, (res, pk), (tiles,), [])
    side = shape(((COARSEN - 1) * REACH, 16, width), BF16)
    coarse, end_even, end_odd, corr = call(
        enter_second_kernel,
        (*arrivals, starts, coarse, initial_state, we, pk),
        (state, side, side, tiles),
        [rows],
    )
    got_odd, got_even = swapped(end_odd, 1), swapped(end_even, 0)
    result = shape((steps, n, width), F32)
    flips = [vmem((8 * m * REACH, width), F32) for m in (3, 2, 1)]
    out, *strips = call(
        third_early_kernel,
        (idx, coarse, got_even, corr, total, fe, pay_even, w, pk),
        (result, strip, strip),
        [spaces] * 3 + [force] + flips + [rows, dma((COARSEN, 8))],
        spaces="s",
        out_spaces="h",
        flops=step_flops * 9 * REACH,
    )
    (out,) = call(
        third_late_kernel,
        (idx, coarse, got_odd, *strips, fe, pay_odd, w, out),
        (result,),
        [spaces] * 3 + [force] + flips[::-1] + [dma((COARSEN - 1, 8))],
        spaces="svvvvvvvh",
        out_spaces="h",
        aliases={8: 0},
        flops=step_flops * 9 * REACH,
    )
    return out


def solution(mesh):
    return jax.shard_map(
        local,
        mesh=mesh,
        in_specs=(
            P("tm", ("groups", "space"), None),
            P(("groups", "space"), None),
            P("space", None),
            P("space", None),
            P(),
            P(),
            P(),
        ),
        out_specs=P("tm", ("groups", "space"), None),
        check_vma=False,
    )
```

time: 67.7 us -> 61.5 us (0.908)
  waiting for transfers between devices: 9.54 us -> 0.84 us
  Pallas kernels: 24.9 us -> 30.4 us
  local copies, waits for them, and re-layouts: 3.19 us -> 0.65 us
    ppermute x6, waiting for transfers between devices: 8.96 us -> 0.26 us  [swapped(): return lax.ppermute(value, 'space', pairs)]
    pallas_call x10 -> x12, Pallas kernels: 24.9 us -> 30.4 us  [call(): pl.pallas_call(kernel, out_shape=outs, name=kernel.__name__, in_specs=spe...]
    unnamed x16 -> x12, local copies, waits for them, and re-layouts: 3.19 us -> 0.65 us
  transfers between devices with their start and end apart: 12 -> 12, of which waited for: 5 -> 3; matrix products, arithmetic and copies ran while one was open for 0% -> 0% of each run, Pallas kernels for 5% -> 23%
where the time goes in v2:
time: 61.5 us; the launch traced here: 61.1 us
  Pallas kernels  30.4 us (49%)
  starting transfers between devices  28.8 us (47%)
  waiting for transfers between devices  0.84 us (1%)
  local copies, waits for them, and re-layouts  0.65 us (1%)
    pallas_call x12, Pallas kernels, call(): pl.pallas_call(kernel, out_shape=outs, name=kernel.__name__, in_specs=spe...  30.4 us
    ppermute x6, starting transfers between devices, earlier(): lax.ppermute(value, 'tm', [(i, i + s) for i in range(count - s)])  15.1 us
    ppermute x6, starting transfers between devices, swapped(): return lax.ppermute(value, 'space', pairs)  13.7 us
  transfers between devices with their start and end apart: 12, of which 3 were waited for; matrix products, arithmetic and copies ran while one was open for 0% of the time, Pallas kernels for 23%

profile of v2, /device:TPU:1, one launch (start us, length us, event | category | flops | bytes accessed | tf_op | source)
XLA Modules:
  0.0 61.1 jit_solution(15700154970199507484)
XLA Ops:
  0.0 3.0 %pack_kernel.1 = (bf16[4,512,128]{2,1,0:T(8,128)(2,1)}, bf16[16,128]{1,0:T(8,128)(2,1)}, bf16[912,128]{1,0:T(8,128)(2,1)}, bf16[912,128]{1,0:T(8,128)(2,1)}) custom-call(bf16[8,4,64,128]{3,2,1,0:T(8,128)(2,1)} %bitcast.3, f32[64,128]{1,0:T(8,128)} %refs_5_.1, s32[6,64]{1,0:T(8,128)} %bitcast.4, s32[6,64]{1,0:T(8,128)} %bitcast.5), custom_call_target="tpu_custom_call" | custom-call | flops 10000000 | bytes 1555456 | tf_op jit(solution)/shard_map/pack_kernel/pallas_call | solution.py:451
  3.2 4.6 %collective-permute-start.1 = (bf16[912,128]{1,0:T(8,128)(2,1)}, bf16[912,128]{1,0:T(8,128)(2,1)S(1)}, u32[]{:S(2)}, u32[]{:S(2)}) collective-permute-start(bf16[912,128]{1,0:T(8,128)(2,1)} %get-tuple-element.34), channel_id=1, source_target_pairs={{1,2},{2,1},{5,6},{6,5},{9,10},{10,9},{13,14},{14,13},{17,18},{18,... | collective-permute-start | bytes 700424 | tf_op jit(solution)/shard_map/ppermute | solution.py:22
  7.8 1.5 %weight_kernel.1 = (bf16[896,256]{1,0:T(8,128)(2,1)S(1)}, bf16[1024,256]{1,0:T(8,128)(2,1)S(1)}, bf16[384,256]{1,0:T(8,128)(2,1)S(1)}) custom-call(f32[128,128]{1,0:T(8,128)S(1)} %copy-done.3, f32[6,128,128]{2,1,0:T(8,128)S(1)} %copy-done.2, f32[128,128]{1,0:T(8,128)S(1)} %copy-done.4), custom_call_target="tpu_custom_call" | custom-call | flops 1000000000 | bytes 1703936 | tf_op jit(solution)/shard_map/weight_kernel/pallas_call | solution.py:451
  9.4 0.6 %copy-done.5 = bf16[16,128]{1,0:T(8,128)(2,1)S(1)} copy-done((bf16[16,128]{1,0:T(8,128)(2,1)S(1)}, bf16[16,128]{1,0:T(8,128)(2,1)}, u32[]{:S(2)}) %copy-start.5) | copy-done | bytes 4120
  10.1 3.0 %first_early_kernel.1 = (bf16[32,16,128]{2,1,0:T(8,128)(2,1)S(1)}, bf16[32,16,128]{2,1,0:T(8,128)(2,1)S(1)}, bf16[32,16,128]{2,1,0:T(8,128)(2,1)S(1)}) custom-call(bf16[4,512,128]{2,1,0:T(8,128)(2,1)S(1)} %copy-done, bf16[16,128]{1,0:T(8,128)(2,1)S(1)} %copy-done.5, f32[64,128]{1,0:T(8,128)S(1)} %copy-done.1, ...), custom_call_target="tpu_custom_call" | custom-call | flops 704643072 | bytes 1646592 | tf_op jit(solution)/shard_map/first_early_kernel/pallas_call | solution.py:451
  13.0 3.6 %first_late_kernel.1 = (f32[64,8,128]{2,1,0:T(8,128)S(1)}, f32[64,128]{1,0:T(8,128)S(1)}, s32[8,256]{1,0:T(8,128)S(1)}) custom-call(bf16[4,512,128]{2,1,0:T(8,128)(2,1)S(1)} %copy-done, bf16[16,128]{1,0:T(8,128)(2,1)S(1)} %copy-done.5, f32[64,128]{1,0:T(8,128)S(1)} %copy-done.1, bf16[912,128]{1,0:T(8,128)(2,1)S(1)} %collective-permute-done.got.got_even.pay, ...), custom_call_target="tpu_custom_call" | custom-call | flops 1409286144 | bytes 2707456 | tf_op jit(solution)/shard_map/first_late_kernel/pallas_call | solution.py:451
  16.7 5.2 %collective-permute-start.4 = (f32[64,128]{1,0:T(8,128)S(1)}, f32[64,128]{1,0:T(8,128)S(1)}, u32[]{:S(2)}, u32[]{:S(2)}) collective-permute-start(f32[64,128]{1,0:T(8,128)S(1)} %get-tuple-element.41), channel_id=1, source_target_pairs={{0,12},{1,13},{2,14},{3,15},{16,28},{17,29},{18,30},{19,31}} | collective-permute-start | bytes 98312 | tf_op jit(solution)/shard_map/ppermute | solution.py:28
  21.9 1.3 %collective-permute-start.3 = (f32[64,128]{1,0:T(8,128)S(1)}, f32[64,128]{1,0:T(8,128)S(1)}, u32[]{:S(2)}, u32[]{:S(2)}) collective-permute-start(f32[64,128]{1,0:T(8,128)S(1)} %get-tuple-element.41), channel_id=1, source_target_pairs={{0,8},{4,12},{1,9},{5,13},{2,10},{6,14},{3,11},{7,15},{16,24},{20,... | collective-permute-start | bytes 98312 | tf_op jit(solution)/shard_map/ppermute | solution.py:28
  23.2 2.2 %collective-permute-start.2 = (f32[64,128]{1,0:T(8,128)S(1)}, f32[64,128]{1,0:T(8,128)S(1)}, u32[]{:S(2)}, u32[]{:S(2)}) collective-permute-start(f32[64,128]{1,0:T(8,128)S(1)} %get-tuple-element.41), channel_id=1, source_target_pairs={{0,4},{4,8},{8,12},{1,5},{5,9},{9,13},{2,6},{6,10},{10,14},{3,7},{... | collective-permute-start | bytes 98312 | tf_op jit(solution)/shard_map/ppermute | solution.py:28
  25.4 0.7 %scan_kernel.2.refs_3_ = f32[64,8,128]{2,1,0:T(8,128)S(1)} custom-call(f32[64,8,128]{2,1,0:T(8,128)S(1)} %get-tuple-element.42.values.w1, bf16[1024,256]{1,0:T(8,128)(2,1)S(1)} %get-tuple-element.39.pk.refs_5_.refs_7_), custom_call_target="tpu_custom_call" | custom-call | flops 10000000 | bytes 1048576 | tf_op jit(solution)/shard_map/scan_kernel/pallas_call | solution.py:451
  26.1 0.3 collective-permute-done.2.refs_0_
  26.4 0.5 enter_first_kernel.1.own.refs_4_
  27.0 3.8 %collective-permute-start.5 = (bf16[64,16,128]{2,1,0:T(8,128)(2,1)S(1)}, bf16[64,16,128]{2,1,0:T(8,128)(2,1)S(1)}, u32[]{:S(2)}, u32[]{:S(2)}) collective-permute-start(bf16[64,16,128]{2,1,0:T(8,128)(2,1)S(1)} %enter_first_kernel.1.own.refs_4_), channel_id=1, source_target_pairs={{1,2},{2,1},{5,6},{6,5},{9,10},{10,9},{13,14},{14,13},{17,18},{18,... | collective-permute-start | bytes 786440 | tf_op jit(solution)/shard_map/ppermute | solution.py:22
  30.9 3.6 %second_early_kernel.1 = (bf16[32,16,128]{2,1,0:T(8,128)(2,1)S(1)}, bf16[32,16,128]{2,1,0:T(8,128)(2,1)S(1)}, bf16[32,16,128]{2,1,0:T(8,128)(2,1)S(1)}) custom-call(s32[8,256]{1,0:T(8,128)S(1)} %get-tuple-element.40.idx, bf16[64,16,128]{2,1,0:T(8,128)(2,1)S(1)} %enter_first_kernel.1.own.refs_4_, bf16[64,16,128]{2,1,0:T(8,128)(2,1)S(1)} %collective-permute-done.6.got, ...), custom_call_target="tpu_custom_call" | custom-call | flops 1409286144 | bytes 1384448 | tf_op jit(solution)/shard_map/second_early_kernel/pallas_call | solution.py:451
  34.7 4.8 %second_late_kernel.1 = (f32[64,8,128]{2,1,0:T(8,128)S(1)}, f32[64,128]{1,0:T(8,128)S(1)}, f32[64,8,128]{2,1,0:T(8,128)S(1)}) custom-call(s32[8,256]{1,0:T(8,128)S(1)} %get-tuple-element.40.idx, bf16[64,16,128]{2,1,0:T(8,128)(2,1)S(1)} %enter_first_kernel.1.own.refs_4_, bf16[64,16,128]{2,1,0:T(8,128)(2,1)S(1)} %collective-permute-done.5.got, ...), custom_call_target="tpu_custom_call" | custom-call | flops 1879048192 | bytes 2727936 | tf_op jit(solution)/shard_map/second_late_kernel/pallas_call | solution.py:451
  39.6 2.9 %collective-permute-start.9 = (f32[64,128]{1,0:T(8,128)S(1)}, f32[64,128]{1,0:T(8,128)S(1)}, u32[]{:S(2)}, u32[]{:S(2)}) collective-permute-start(f32[64,128]{1,0:T(8,128)S(1)} %get-tuple-element.47), channel_id=1, source_target_pairs={{0,12},{1,13},{2,14},{3,15},{16,28},{17,29},{18,30},{19,31}} | collective-permute-start | bytes 98312 | tf_op jit(solution)/shard_map/ppermute | solution.py:28
  42.5 1.3 %collective-permute-start.8 = (f32[64,128]{1,0:T(8,128)S(1)}, f32[64,128]{1,0:T(8,128)S(1)}, u32[]{:S(2)}, u32[]{:S(2)}) collective-permute-start(f32[64,128]{1,0:T(8,128)S(1)} %get-tuple-element.47), channel_id=1, source_target_pairs={{0,8},{4,12},{1,9},{5,13},{2,10},{6,14},{3,11},{7,15},{16,24},{20,... | collective-permute-start | bytes 98312 | tf_op jit(solution)/shard_map/ppermute | solution.py:28
  43.8 2.2 %collective-permute-start.7 = (f32[64,128]{1,0:T(8,128)S(1)}, f32[64,128]{1,0:T(8,128)S(1)}, u32[]{:S(2)}, u32[]{:S(2)}) collective-permute-start(f32[64,128]{1,0:T(8,128)S(1)} %get-tuple-element.47), channel_id=1, source_target_pairs={{0,4},{4,8},{8,12},{1,5},{5,9},{9,13},{2,6},{6,10},{10,14},{3,7},{... | collective-permute-start | bytes 98312 | tf_op jit(solution)/shard_map/ppermute | solution.py:28
  46.0 0.7 %scan_kernel.3.refs_3_ = f32[64,8,128]{2,1,0:T(8,128)S(1)} custom-call(f32[64,8,128]{2,1,0:T(8,128)S(1)} %get-tuple-element.48.values, bf16[1024,256]{1,0:T(8,128)(2,1)S(1)} %get-tuple-element.39.pk.refs_5_.refs_7_), custom_call_target="tpu_custom_call" | custom-call | flops 10000000 | bytes 1048576 | tf_op jit(solution)/shard_map/scan_kernel/pallas_call | solution.py:451
  46.7 0.3 collective-permute-done.7.refs_0_
  47.0 0.6 %enter_second_kernel.1 = (bf16[64,16,128]{2,1,0:T(8,128)(2,1)S(1)}, bf16[48,16,128]{2,1,0:T(8,128)(2,1)S(1)}, bf16[48,16,128]{2,1,0:T(8,128)(2,1)S(1)}, f32[64,8,128]{2,1,0:T(8,128)S(1)}) custom-call(f32[64,128]{1,0:T(8,128)S(1)} %collective-permute-done.7.refs_0_, f32[64,128]{1,0:T(8,128)S(1)} %collective-permute-done.8.refs_1_, ...), custom_call_target="tpu_custom_call" | custom-call | flops 10000000 | bytes 2293760 | tf_op jit(solution)/shard_map/enter_second_kernel/pallas_call | solution.py:451
  47.7 5.0 %collective-permute-start.10 = (bf16[48,16,128]{2,1,0:T(8,128)(2,1)S(1)}, bf16[48,16,128]{2,1,0:T(8,128)(2,1)S(1)}, u32[]{:S(2)}, u32[]{:S(2)}) collective-permute-start(bf16[48,16,128]{2,1,0:T(8,128)(2,1)S(1)} %get-tuple-element.50), channel_id=1, source_target_pairs={{1,2},{2,1},{5,6},{6,5},{9,10},{10,9},{13,14},{14,13},{17,18},{18,... | collective-permute-start | bytes 589832 | tf_op jit(solution)/shard_map/ppermute | solution.py:22
  52.7 4.5 %third_early_kernel.1 = (f32[32,64,128]{2,1,0:T(8,128)}, bf16[32,16,128]{2,1,0:T(8,128)(2,1)S(1)}, bf16[32,16,128]{2,1,0:T(8,128)(2,1)S(1)}) custom-call(s32[8,256]{1,0:T(8,128)S(1)} %get-tuple-element.40.idx, bf16[64,16,128]{2,1,0:T(8,128)(2,1)S(1)} %get-tuple-element.49.own, bf16[48,16,128]{2,1,0:T(8,128)(2,1)S(1)} %collective-permute-done.11.got, ...), custom_call_target="tpu_custom_call" | custom-call | flops 1056964608 | bytes 4042752 | tf_op jit(solution)/shard_map/third_early_kernel/pallas_call | solution.py:451
  57.2 3.8 %third_late_kernel.1 = f32[32,64,128]{2,1,0:T(8,128)} custom-call(s32[8,256]{1,0:T(8,128)S(1)} %get-tuple-element.40.idx, bf16[64,16,128]{2,1,0:T(8,128)(2,1)S(1)} %get-tuple-element.49.own, bf16[48,16,128]{2,1,0:T(8,128)(2,1)S(1)} %collective-permute-done.10.got, bf16[32,16,128]{2,1,0:T(8,128)(2,1)S(1)} %get-tuple-element.54.strip1, ...), custom_call_target="tpu_custom_call", output_to_operand_aliasing={{}: (8, {})} | custom-call | flops 1056964608 | bytes 4042752 | tf_op jit(solution)/shard_map/third_late_kernel/pallas_call | solution.py:451
  (24 shorter events, 0.6 us)
Async XLA Ops:
  0.0 7.8 %copy-start.2 = (f32[6,128,128]{2,1,0:T(8,128)S(1)}, f32[6,128,128]{2,1,0:T(8,128)}, u32[]{:S(2)}) copy-start(f32[6,128,128]{2,1,0:T(8,128)} %faces.1) | copy-start | bytes 1179652
  0.0 7.8 %copy-start.3 = (f32[128,128]{1,0:T(8,128)S(1)}, f32[128,128]{1,0:T(8,128)}, u32[]{:S(2)}) copy-start(f32[128,128]{1,0:T(8,128)} %diag.1) | copy-start | bytes 196612
  0.0 7.8 %copy-start.4 = (f32[128,128]{1,0:T(8,128)S(1)}, f32[128,128]{1,0:T(8,128)}, u32[]{:S(2)}) copy-start(f32[128,128]{1,0:T(8,128)} %coarse.1) | copy-start | bytes 196612
  3.1 6.3 %collective-permute-start = (bf16[912,128]{1,0:T(8,128)(2,1)}, bf16[912,128]{1,0:T(8,128)(2,1)S(1)}, u32[]{:S(2)}, u32[]{:S(2)}) collective-permute-start(bf16[912,128]{1,0:T(8,128)(2,1)} %get-tuple-element.33), channel_id=1, source_target_pairs={{0,1},{1,0},{2,3},{3,2},{4,5},{5,4},{6,7},{7,6},{8,9},{9,8},{10,11... | collective-permute-start | bytes 700424 | tf_op jit(solution)/shard_map/ppermute | solution.py:22
  3.2 6.2 %copy-start = (bf16[4,512,128]{2,1,0:T(8,128)(2,1)S(1)}, bf16[4,512,128]{2,1,0:T(8,128)(2,1)}, u32[]{:S(2)}) copy-start(bf16[4,512,128]{2,1,0:T(8,128)(2,1)} %get-tuple-element.31.fe) | copy-start | bytes 1572868
  3.2 6.2 %copy-start.1 = (f32[64,128]{1,0:T(8,128)S(1)}, f32[64,128]{1,0:T(8,128)}, u32[]{:S(2)}) copy-start(f32[64,128]{1,0:T(8,128)} %refs_5_.1) | copy-start | bytes 98308
  3.2 9.9 %collective-permute-start.1 = (bf16[912,128]{1,0:T(8,128)(2,1)}, bf16[912,128]{1,0:T(8,128)(2,1)S(1)}, u32[]{:S(2)}, u32[]{:S(2)}) collective-permute-start(bf16[912,128]{1,0:T(8,128)(2,1)} %get-tuple-element.34), channel_id=1, source_target_pairs={{1,2},{2,1},{5,6},{6,5},{9,10},{10,9},{13,14},{14,13},{17,18},{18,... | collective-permute-start | bytes 700424 | tf_op jit(solution)/shard_map/ppermute | solution.py:22
  9.4 0.7 %copy-start.5 = (bf16[16,128]{1,0:T(8,128)(2,1)S(1)}, bf16[16,128]{1,0:T(8,128)(2,1)}, u32[]{:S(2)}) copy-start(bf16[16,128]{1,0:T(8,128)(2,1)} %get-tuple-element.32.tab) | copy-start | bytes 12292
  16.7 9.4 %collective-permute-start.4 = (f32[64,128]{1,0:T(8,128)S(1)}, f32[64,128]{1,0:T(8,128)S(1)}, u32[]{:S(2)}, u32[]{:S(2)}) collective-permute-start(f32[64,128]{1,0:T(8,128)S(1)} %get-tuple-element.41), channel_id=1, source_target_pairs={{0,12},{1,13},{2,14},{3,15},{16,28},{17,29},{18,30},{19,31}} | collective-permute-start | bytes 98312 | tf_op jit(solution)/shard_map/ppermute | solution.py:28
  21.9 4.2 %collective-permute-start.3 = (f32[64,128]{1,0:T(8,128)S(1)}, f32[64,128]{1,0:T(8,128)S(1)}, u32[]{:S(2)}, u32[]{:S(2)}) collective-permute-start(f32[64,128]{1,0:T(8,128)S(1)} %get-tuple-element.41), channel_id=1, source_target_pairs={{0,8},{4,12},{1,9},{5,13},{2,10},{6,14},{3,11},{7,15},{16,24},{20,... | collective-permute-start | bytes 98312 | tf_op jit(solution)/shard_map/ppermute | solution.py:28
  23.2 3.2 %collective-permute-start.2 = (f32[64,128]{1,0:T(8,128)S(1)}, f32[64,128]{1,0:T(8,128)S(1)}, u32[]{:S(2)}, u32[]{:S(2)}) collective-permute-start(f32[64,128]{1,0:T(8,128)S(1)} %get-tuple-element.41), channel_id=1, source_target_pairs={{0,4},{4,8},{8,12},{1,5},{5,9},{9,13},{2,6},{6,10},{10,14},{3,7},{... | collective-permute-start | bytes 98312 | tf_op jit(solution)/shard_map/ppermute | solution.py:28
  27.0 3.9 %collective-permute-start.6 = (bf16[64,16,128]{2,1,0:T(8,128)(2,1)S(1)}, bf16[64,16,128]{2,1,0:T(8,128)(2,1)S(1)}, u32[]{:S(2)}, u32[]{:S(2)}) collective-permute-start(bf16[64,16,128]{2,1,0:T(8,128)(2,1)S(1)} %enter_first_kernel.1.own.refs_4_), channel_id=1, source_target_pairs={{0,1},{1,0},{2,3},{3,2},{4,5},{5,4},{6,7},{7,6},{8,9},{9,8},{10,11... | collective-permute-start | bytes 786440 | tf_op jit(solution)/shard_map/ppermute | solution.py:22
  27.0 7.7 %collective-permute-start.5 = (bf16[64,16,128]{2,1,0:T(8,128)(2,1)S(1)}, bf16[64,16,128]{2,1,0:T(8,128)(2,1)S(1)}, u32[]{:S(2)}, u32[]{:S(2)}) collective-permute-start(bf16[64,16,128]{2,1,0:T(8,128)(2,1)S(1)} %enter_first_kernel.1.own.refs_4_), channel_id=1, source_target_pairs={{1,2},{2,1},{5,6},{6,5},{9,10},{10,9},{13,14},{14,13},{17,18},{18,... | collective-permute-start | bytes 786440 | tf_op jit(solution)/shard_map/ppermute | solution.py:22
  39.6 7.2 %collective-permute-start.9 = (f32[64,128]{1,0:T(8,128)S(1)}, f32[64,128]{1,0:T(8,128)S(1)}, u32[]{:S(2)}, u32[]{:S(2)}) collective-permute-start(f32[64,128]{1,0:T(8,128)S(1)} %get-tuple-element.47), channel_id=1, source_target_pairs={{0,12},{1,13},{2,14},{3,15},{16,28},{17,29},{18,30},{19,31}} | collective-permute-start | bytes 98312 | tf_op jit(solution)/shard_map/ppermute | solution.py:28
  42.5 4.2 %collective-permute-start.8 = (f32[64,128]{1,0:T(8,128)S(1)}, f32[64,128]{1,0:T(8,128)S(1)}, u32[]{:S(2)}, u32[]{:S(2)}) collective-permute-start(f32[64,128]{1,0:T(8,128)S(1)} %get-tuple-element.47), channel_id=1, source_target_pairs={{0,8},{4,12},{1,9},{5,13},{2,10},{6,14},{3,11},{7,15},{16,24},{20,... | collective-permute-start | bytes 98312 | tf_op jit(solution)/shard_map/ppermute | solution.py:28
  43.8 3.2 %collective-permute-start.7 = (f32[64,128]{1,0:T(8,128)S(1)}, f32[64,128]{1,0:T(8,128)S(1)}, u32[]{:S(2)}, u32[]{:S(2)}) collective-permute-start(f32[64,128]{1,0:T(8,128)S(1)} %get-tuple-element.47), channel_id=1, source_target_pairs={{0,4},{4,8},{8,12},{1,5},{5,9},{9,13},{2,6},{6,10},{10,14},{3,7},{... | collective-permute-start | bytes 98312 | tf_op jit(solution)/shard_map/ppermute | solution.py:28
  47.6 5.1 %collective-permute-start.11 = (bf16[48,16,128]{2,1,0:T(8,128)(2,1)S(1)}, bf16[48,16,128]{2,1,0:T(8,128)(2,1)S(1)}, u32[]{:S(2)}, u32[]{:S(2)}) collective-permute-start(bf16[48,16,128]{2,1,0:T(8,128)(2,1)S(1)} %get-tuple-element.51), channel_id=1, source_target_pairs={{0,1},{1,0},{2,3},{3,2},{4,5},{5,4},{6,7},{7,6},{8,9},{9,8},{10,11... | collective-permute-start | bytes 589832 | tf_op jit(solution)/shard_map/ppermute | solution.py:22
  47.7 9.5 %collective-permute-start.10 = (bf16[48,16,128]{2,1,0:T(8,128)(2,1)S(1)}, bf16[48,16,128]{2,1,0:T(8,128)(2,1)S(1)}, u32[]{:S(2)}, u32[]{:S(2)}) collective-permute-start(bf16[48,16,128]{2,1,0:T(8,128)(2,1)S(1)} %get-tuple-element.50), channel_id=1, source_target_pairs={{1,2},{2,1},{5,6},{6,5},{9,10},{10,9},{13,14},{14,13},{17,18},{18,... | collective-permute-start | bytes 589832 | tf_op jit(solution)/shard_map/ppermute | solution.py:22

commit v3 on v2

--- a/solution.py
+++ b/solution.py
@@ -22,14 +22,8 @@
     return lax.ppermute(value, "space", pairs)
 
 
-def earlier(value):
-    count = lax.axis_size("tm")
-    if count <= 8:
-        return [lax.ppermute(value, "tm", [(i, i + s) for i in range(count - s)]) for s in range(1, count)]
-    every = lax.all_gather(value, "tm")
-    at = lax.axis_index("tm") - jnp.arange(1, count)
-    picked = jnp.where((at >= 0)[:, None, None], jnp.take(every, jnp.maximum(at, 0), axis=0), 0.0)
-    return [picked[s] for s in range(count - 1)]
+def exchanged(ends):
+    return lax.all_to_all(ends, "tm", 0, 0)
 
 
 def split(u):
@@ -73,13 +67,15 @@
     return jnp.where(row >= 1, pltpu.roll(y, 1, axis=1), 0.0)
 
 
-def block_end(y, pk, n):
+def block_end(ends, y, pk, n):
     parts = [y[pl.ds(i, n, stride=8), :] for i in range(8)]
-    return product_rows(split_rows(jnp.concatenate(parts, axis=1)), pk[...])
-
-
-def enter(arrivals, we, pk, y, n):
-    value = jnp.concatenate([a[...] for a in arrivals], axis=1)
+    end = product_rows(split_rows(jnp.concatenate(parts, axis=1)), pk[...])
+    for i in range(ends.shape[0]):
+        ends[i] = end
+
+
+def enter(ends, we, pk, y, n):
+    value = jnp.concatenate([ends[i] for i in range(ends.shape[0])], axis=1)
     entry = product_rows(split_rows(value), we[...])
     y[pl.ds(0, n, stride=8), :] = entry
     rows = split_rows(entry)
@@ -88,11 +84,35 @@
     return y[...].reshape(n, 8, 128)
 
 
-def apply_phi(src, idx, w, base, size):
-    cols = [src[pl.ds(base, size)].reshape(size * 16, 128)]
-    for f in range(6):
-        cols.append(jnp.concatenate([src[idx[f, base + e]] for e in range(size)], axis=0))
-    return product(jnp.concatenate(cols, axis=1), w[...])
+def gathered(src, idx, base, size, f):
+    if f == 0:
+        return src[pl.ds(base, size)].reshape(size * 16, 128)
+    return jnp.concatenate([src[idx[f - 1, base + e]] for e in range(size)], axis=0)
+
+
+def phi_halves(src, idx, w, base, size):
+    size = size // 2
+    parts = []
+    for at in (base, base + size):
+        x = jnp.concatenate([gathered(src, idx, at, size, f) for f in range(7)], axis=1)
+        parts.append(product(x, w[...]))
+    return jnp.concatenate(parts, axis=0)
+
+
+def phi_pairs(src, idx, w, base, size):
+    total = None
+    for f in (0, 2, 4, 6):
+        x = jnp.concatenate([gathered(src, idx, base, size, f + j) for j in range(min(2, 7 - f))], axis=1)
+        r = jnp.dot(x, w[pl.ds(f * 128, x.shape[1]), :], preferred_element_type=F32)
+        total = r if total is None else total + r
+    r = total.reshape(size, 16, 256)
+    return r[:, :8, :128] + (r[:, 8:, :128] + r[:, :8, 128:])
+
+
+def phi_through(src, idx, w, base, size, lhs):
+    for f in range(7):
+        lhs[pl.ds(0, size * 16), f * 128 : (f + 1) * 128] = gathered(src, idx, base, size, f)
+    return product(lhs[pl.ds(0, size * 16), :], w[...])
 
 
 def even_place():
@@ -175,11 +195,14 @@
     for k in range(8):
         put_halves(pk.at[pl.ds(128 * (7 - k), 128)], powers[k])
 
+    t = lax.axis_index("tm")
+    we[...] = jnp.zeros_like(we)
+
     def body(k, current):
-        put_halves(we.at[pl.ds(pl.multiple_of(k * 128, 128), 128)], current)
+        put_halves(we.at[pl.ds(pl.multiple_of((t - 1 - k) * 128, 128), 128)], current)
         return mul(current, powers[8])
 
-    lax.fori_loop(0, we.shape[0] // 128, body, one)
+    lax.fori_loop(0, t, body, one)
 
 
 def put_force(dst, own, got, right, k, n):
@@ -277,12 +300,12 @@
         put_force(force, fe, got, even, k, n)
         size = (6 - 2 * k) * REACH
         base = mirrored((k + 1) * REACH, size, full)
-        dst[pl.ds(base, size)] = split(apply_phi(src, idx, w, base, size) + force_at(force, base, size))
+        dst[pl.ds(base, size)] = split(phi_halves(src, idx, w, base, size) + force_at(force, base, size))
     put_strips((strip1, strip2, strip3), (s1, s2, s3), full)
 
 
 def first_late_kernel(
-    fe, tab, init, got_even, got_odd, strip1, strip2, strip3, w, pk, w1, end, idx_out,
+    fe, tab, init, got_even, got_odd, strip1, strip2, strip3, w, pk, w1, ends, idx_out,
     s1, s2, s3, force, y, i16, columns, square, idx, sem
 ):
     n = init.shape[0]
@@ -303,29 +326,27 @@
     for k, src, dst in ((1, s1, s2), (2, s2, s3), (3, s3, None)):
         put_force(force, fe, got_odd, odd, k, n)
         base = mirrored((7 - k) * REACH, count, full)
-        value = apply_phi(src, idx, w, base, count) + force_at(force, base, count)
+        value = phi_halves(src, idx, w, base, count) + force_at(force, base, count)
         if dst is None:
             w1[...] = value
             y[...] = value.reshape(n * 8, 128)
         else:
             dst[pl.ds(base, count)] = split(value)
-    end[...] = block_end(y, pk, n)
+    block_end(ends, y, pk, n)
 
 
 def scan_kernel(values, pk, starts):
     starts[...] = scan_starts(values[...], pk)
 
 
-def enter_first_kernel(*refs):
-    *arrivals, starts, we, pk, state, y = refs
+def enter_first_kernel(ends, starts, we, pk, state, y):
     n = starts.shape[0]
-    state[...] = split(enter(arrivals, we, pk, y, n) + starts[...])
-
-
-def enter_second_kernel(*refs):
-    *arrivals, starts, before, init, we, pk, state, pay_even, pay_odd, corr, y = refs
+    state[...] = split(enter(ends, we, pk, y, n) + starts[...])
+
+
+def enter_second_kernel(ends, starts, before, init, we, pk, state, pay_even, pay_odd, corr, y):
     n = starts.shape[0]
-    value = enter(arrivals, we, pk, y, n) + starts[...]
+    value = enter(ends, we, pk, y, n) + starts[...]
     corr[...] = value
     old = before[...].astype(F32)
     y[...] = (value + (old[:, 0:8] + old[:, 8:16])).reshape(n * 8, 128)
@@ -354,11 +375,11 @@
     for k, src, dst in ((1, s0, s1), (2, s1, s2), (3, s2, s3)):
         size = (8 - 2 * k) * REACH
         base = mirrored(k * REACH, size, full)
-        dst[pl.ds(base, size)] = split(apply_phi(src, idx, w, base, size))
+        dst[pl.ds(base, size)] = split(phi_pairs(src, idx, w, base, size))
     put_strips((strip1, strip2, strip3), (s1, s2, s3), full)
 
 
-def second_late_kernel(idx, own, got, strip1, strip2, strip3, w1, w, pk, res, end, total, s0, s1, s2, s3, y):
+def second_late_kernel(idx, own, got, strip1, strip2, strip3, w1, w, pk, res, ends, total, s0, s1, s2, s3, y):
     n = own.shape[0]
     full = 3 * n
     put_block(s0, own, got, jnp.logical_not(even_place()), n)
@@ -366,13 +387,13 @@
     count = 4 * REACH
     for k, src, dst in ((1, s0, s1), (2, s1, s2), (3, s2, s3)):
         base = mirrored((8 - k) * REACH, count, full)
-        dst[pl.ds(base, count)] = split(apply_phi(src, idx, w, base, count))
-    value = apply_phi(s3, idx, w, n, n)
+        dst[pl.ds(base, count)] = split(phi_pairs(src, idx, w, base, count))
+    value = phi_pairs(s3, idx, w, n, n)
     total[...] = value + w1[...]
     value = value - product(own[...].reshape(n * 16, 128), power(pk, 1))
     res[...] = value
     y[...] = value.reshape(n * 8, 128)
-    end[...] = block_end(y, pk, n)
+    block_end(ends, y, pk, n)
 
 
 def write_out(out, k, value, begin, flip, sems):
@@ -390,7 +411,8 @@
 
 
 def third_early_kernel(
-    idx, own, got, corr, total, fe, pay, w, pk, out, strip1, strip2, s0, s1, s2, force, flip0, flip1, flip2, flip3, sems
+    idx, own, got, corr, total, fe, pay, w, pk, out, strip1, strip2,
+    s0, s1, s2, force, lhs, flip0, flip1, flip2, flip3, sems
 ):
     n = own.shape[0]
     full = 3 * n
@@ -404,7 +426,7 @@
         put_force(force, fe, pay, even, k, n)
         size = (5 - 2 * k) * REACH
         base = mirrored((2 + k) * REACH, size, full)
-        value = apply_phi(src, idx, w, base, size) + force_at(force, base, size)
+        value = phi_through(src, idx, w, base, size, lhs) + force_at(force, base, size)
         if dst is not None:
             dst[pl.ds(base, size)] = split(value)
         mine = (3 - k) * REACH
@@ -417,7 +439,7 @@
 
 
 def third_late_kernel(
-    idx, own, got, strip1, strip2, fe, pay, w, partial, out, s0, s1, s2, force, flip0, flip1, flip2, sems
+    idx, own, got, strip1, strip2, fe, pay, w, partial, out, s0, s1, s2, force, lhs, flip0, flip1, flip2, sems
 ):
     n = own.shape[0]
     full = 3 * n
@@ -430,7 +452,7 @@
     for k, src, dst, flip in ((0, s0, s1, flip0), (1, s1, s2, flip1), (2, s2, None, flip2)):
         put_force(force, fe, pay, odd, k, n)
         base = mirrored((7 - k) * REACH, size, full)
-        value = apply_phi(src, idx, w, base, size) + force_at(force, base, size)
+        value = phi_through(src, idx, w, base, size, lhs) + force_at(force, base, size)
         if dst is not None:
             dst[pl.ds(base, size)] = split(value)
         mine = (k + 1) * REACH
@@ -471,7 +493,7 @@
     dma = pltpu.SemaphoreType.DMA
     tiles = shape((n, 8, width), F32)
     state = shape((n, 16, width), BF16)
-    ends = shape((n, width), F32)
+    all_ends = shape((tm, n, width), F32)
     step_flops = 2 * 16 * 7 * width * 2 * width
     pay_rows = sum((COARSEN - 1 - k) * REACH * 8 for k in range(COARSEN)) + 2 * n + 16
     pay = shape((pay_rows, width), BF16)
@@ -498,7 +520,7 @@
         (
             shape((7 * width, 2 * width), BF16),
             shape((8 * width, 2 * width), BF16),
-            shape(((tm - 1) * width, 2 * width), BF16),
+            shape((tm * width, 2 * width), BF16),
         ),
         [],
         flops=10**9,
@@ -516,16 +538,16 @@
         [spaces] * 3 + [force, vmem((6 * REACH * 8, width), F32)] + tables + [vmem((8, 256), jnp.int32), smem, dma],
         flops=step_flops * 6 * REACH,
     )
-    w1, end, idx = call(
+    w1, ends, idx = call(
         first_late_kernel,
         (fe, tab, initial_state, pay_even, pay_odd, *strips, w, pk),
-        (tiles, ends, shape((8, 256), jnp.int32)),
+        (tiles, all_ends, shape((8, 256), jnp.int32)),
         [spaces] * 3 + [force, rows] + tables + [smem, dma],
         flops=step_flops * 12 * REACH,
     )
-    arrivals = earlier(end)
+    ends = exchanged(ends)
     (starts,) = call(scan_kernel, (w1, pk), (tiles,), [])
-    (coarse,) = call(enter_first_kernel, (*arrivals, starts, we, pk), (state,), [rows])
+    (coarse,) = call(enter_first_kernel, (ends, starts, we, pk), (state,), [rows])
     got_odd, got_even = swapped(coarse, 1), swapped(coarse, 0)
     strips = call(
         second_early_kernel,
@@ -535,31 +557,32 @@
         spaces="s",
         flops=step_flops * 12 * REACH,
     )
-    res, end, total = call(
+    res, ends, total = call(
         second_late_kernel,
         (idx, coarse, got_odd, *strips, w1, w, pk),
-        (tiles, ends, tiles),
+        (tiles, all_ends, tiles),
         [spaces] * 4 + [rows],
         spaces="s",
         flops=step_flops * 16 * REACH,
     )
-    arrivals = earlier(end)
+    ends = exchanged(ends)
     (starts,) = call(scan_kernel, (res, pk), (tiles,), [])
     side = shape(((COARSEN - 1) * REACH, 16, width), BF16)
     coarse, end_even, end_odd, corr = call(
         enter_second_kernel,
-        (*arrivals, starts, coarse, initial_state, we, pk),
+        (ends, starts, coarse, initial_state, we, pk),
         (state, side, side, tiles),
         [rows],
     )
     got_odd, got_even = swapped(end_odd, 1), swapped(end_even, 0)
     result = shape((steps, n, width), F32)
+    lhs = vmem((5 * REACH * 16, 7 * width), BF16)
     flips = [vmem((8 * m * REACH, width), F32) for m in (3, 2, 1)]
     out, *strips = call(
         third_early_kernel,
         (idx, coarse, got_even, corr, total, fe, pay_even, w, pk),
         (result, strip, strip),
-        [spaces] * 3 + [force] + flips + [rows, dma((COARSEN, 8))],
+        [spaces] * 3 + [force, lhs] + flips + [rows, dma((COARSEN, 8))],
         spaces="s",
         out_spaces="h",
         flops=step_flops * 9 * REACH,
@@ -568,7 +591,7 @@
         third_late_kernel,
         (idx, coarse, got_odd, *strips, fe, pay_odd, w, out),
         (result,),
-        [spaces] * 3 + [force] + flips[::-1] + [dma((COARSEN - 1, 8))],
+        [spaces] * 3 + [force, lhs] + flips[::-1] + [dma((COARSEN - 1, 8))],
         spaces="svvvvvvvh",
         out_spaces="h",
         aliases={8: 0},

time: 61.5 us -> 65.7 us (1.068)
  waiting for transfers between devices: 0.84 us -> 8.52 us
  starting transfers between devices: 28.8 us -> 22.4 us
  Pallas kernels: 30.4 us -> 32.6 us
  local copies, waits for them, and re-layouts: 0.65 us -> 1.36 us
    ppermute x6 -> x0, starting transfers between devices: 15.1 us -> none  [earlier(): lax.ppermute(value, 'tm', [(i, i + s) for i in range(count - s)])]
    all_to_all x0 -> x2, starting transfers between devices: none -> 8.55 us  [exchanged(): return lax.all_to_all(ends, 'tm', 0, 0)]
    all_to_all x0 -> x2, waiting for transfers between devices: none -> 8.26 us  [exchanged(): return lax.all_to_all(ends, 'tm', 0, 0)]
    pallas_call x12, Pallas kernels: 30.4 us -> 32.6 us  [call(): pl.pallas_call(kernel, out_shape=outs, name=kernel.__name__, in_specs=spe...]
    unnamed x12 -> x16, local copies, waits for them, and re-layouts: 0.65 us -> 1.36 us
  transfers between devices with their start and end apart: 12 -> 8, of which waited for: 3 -> 3; matrix products, arithmetic and copies ran while one was open for 0% -> 0% of each run, Pallas kernels for 23% -> 22%
where the time goes in v3:
time: 65.7 us; the launch traced here: 65.3 us
  Pallas kernels  32.6 us (50%)
  starting transfers between devices  22.4 us (34%)
  waiting for transfers between devices  8.52 us (13%)
  local copies, waits for them, and re-layouts  1.36 us (2%)
    pallas_call x12, Pallas kernels, call(): pl.pallas_call(kernel, out_shape=outs, name=kernel.__name__, in_specs=spe...  32.6 us
    ppermute x6, starting transfers between devices, swapped(): return lax.ppermute(value, 'space', pairs)  13.9 us
    all_to_all x2, starting transfers between devices, exchanged(): return lax.all_to_all(ends, 'tm', 0, 0)  8.55 us
    all_to_all x2, waiting for transfers between devices, exchanged(): return lax.all_to_all(ends, 'tm', 0, 0)  8.26 us
    unnamed x16, local copies, waits for them, and re-layouts  1.36 us
  transfers between devices with their start and end apart: 8, of which 3 were waited for; matrix products, arithmetic and copies ran while one was open for 0% of the time, Pallas kernels for 22%

profile of v3, /device:TPU:1, one launch (start us, length us, event | category | flops | bytes accessed | tf_op | source)
XLA Modules:
  0.0 65.3 jit_solution(16702918579044063353)
XLA Ops:
  0.0 3.0 %pack_kernel.1 = (bf16[4,512,128]{2,1,0:T(8,128)(2,1)}, bf16[16,128]{1,0:T(8,128)(2,1)}, bf16[912,128]{1,0:T(8,128)(2,1)}, bf16[912,128]{1,0:T(8,128)(2,1)}) custom-call(bf16[8,4,64,128]{3,2,1,0:T(8,128)(2,1)} %bitcast.3, f32[64,128]{1,0:T(8,128)} %init.7, s32[6,64]{1,0:T(8,128)} %bitcast.4, s32[6,64]{1,0:T(8,128)} %bitcast.5), custom_call_target="tpu_custom_call" | custom-call | flops 10000000 | bytes 1555456 | tf_op jit(solution)/shard_map/pack_kernel/pallas_call | solution.py:473
  3.1 0.1 collective-permute-start
  3.2 4.6 %collective-permute-start.1 = (bf16[912,128]{1,0:T(8,128)(2,1)}, bf16[912,128]{1,0:T(8,128)(2,1)S(1)}, u32[]{:S(2)}, u32[]{:S(2)}) collective-permute-start(bf16[912,128]{1,0:T(8,128)(2,1)} %get-tuple-element.34), channel_id=1, source_target_pairs={{1,2},{2,1},{5,6},{6,5},{9,10},{10,9},{13,14},{14,13},{17,18},{18,... | collective-permute-start | bytes 700424 | tf_op jit(solution)/shard_map/ppermute | solution.py:22
  7.8 0.9 %weight_kernel.1 = (bf16[896,256]{1,0:T(8,128)(2,1)S(1)}, bf16[1024,256]{1,0:T(8,128)(2,1)S(1)}, bf16[512,256]{1,0:T(8,128)(2,1)S(1)}) custom-call(f32[128,128]{1,0:T(8,128)S(1)} %copy-done.3, f32[6,128,128]{2,1,0:T(8,128)S(1)} %copy-done.2, f32[128,128]{1,0:T(8,128)S(1)} %copy-done.4), custom_call_target="tpu_custom_call" | custom-call | flops 1000000000 | bytes 1769472 | tf_op jit(solution)/shard_map/weight_kernel/pallas_call | solution.py:473
  8.8 0.6 copy-done.5
  9.4 2.9 %first_early_kernel.1 = (bf16[32,16,128]{2,1,0:T(8,128)(2,1)S(1)}, bf16[32,16,128]{2,1,0:T(8,128)(2,1)S(1)}, bf16[32,16,128]{2,1,0:T(8,128)(2,1)S(1)}) custom-call(bf16[4,512,128]{2,1,0:T(8,128)(2,1)S(1)} %copy-done, bf16[16,128]{1,0:T(8,128)(2,1)S(1)} %copy-done.5, f32[64,128]{1,0:T(8,128)S(1)} %copy-done.1, ...), custom_call_target="tpu_custom_call" | custom-call | flops 704643072 | bytes 1646592 | tf_op jit(solution)/shard_map/first_early_kernel/pallas_call | solution.py:473
  12.3 4.1 %first_late_kernel.1 = (f32[64,8,128]{2,1,0:T(8,128)S(1)}, f32[4,64,128]{2,1,0:T(8,128)}, s32[8,256]{1,0:T(8,128)S(1)}) custom-call(bf16[4,512,128]{2,1,0:T(8,128)(2,1)S(1)} %copy-done, bf16[16,128]{1,0:T(8,128)(2,1)S(1)} %copy-done.5, f32[64,128]{1,0:T(8,128)S(1)} %copy-done.1, bf16[912,128]{1,0:T(8,128)(2,1)S(1)} %collective-permute-done.got.got_even.pay, ...), custom_call_target="tpu_custom_call" | custom-call | flops 1409286144 | bytes 2805760 | tf_op jit(solution)/shard_map/first_late_kernel/pallas_call | solution.py:473
  16.4 5.2 %all-to-all-start = ((f32[4,64,128]{2,1,0:T(8,128)}), f32[4,64,128]{2,1,0:T(8,128)S(1)}, u32[]{:S(2)}, u32[]{:S(2)}) async-start(f32[4,64,128]{2,1,0:T(8,128)} %get-tuple-element.41), calls=%async_computation | async-start | bytes 262144 | tf_op jit(solution)/shard_map/all_to_all | solution.py:26
  21.7 0.7 %scan_kernel.2.starts = f32[64,8,128]{2,1,0:T(8,128)S(1)} custom-call(f32[64,8,128]{2,1,0:T(8,128)S(1)} %get-tuple-element.42.values.w1, bf16[1024,256]{1,0:T(8,128)(2,1)S(1)} %get-tuple-element.39.pk), custom_call_target="tpu_custom_call" | custom-call | flops 10000000 | bytes 1048576 | tf_op jit(solution)/shard_map/scan_kernel/pallas_call | solution.py:473
  22.4 4.2 %all-to-all-done.ends = f32[4,64,128]{2,1,0:T(8,128)S(1)} async-done(((f32[4,64,128]{2,1,0:T(8,128)}), f32[4,64,128]{2,1,0:T(8,128)S(1)}, u32[]{:S(2)}, u32[]{:S(2)}) %all-to-all-start) | async-done | bytes 131104 | tf_op jit(solution)/shard_map/all_to_all | solution.py:26
  26.6 0.5 enter_first_kernel.1.own.before
  27.2 0.1 collective-permute-start.3
  27.2 4.0 %collective-permute-start.2 = (bf16[64,16,128]{2,1,0:T(8,128)(2,1)S(1)}, bf16[64,16,128]{2,1,0:T(8,128)(2,1)S(1)}, u32[]{:S(2)}, u32[]{:S(2)}) collective-permute-start(bf16[64,16,128]{2,1,0:T(8,128)(2,1)S(1)} %enter_first_kernel.1.own.before), channel_id=1, source_target_pairs={{1,2},{2,1},{5,6},{6,5},{9,10},{10,9},{13,14},{14,13},{17,18},{18,... | collective-permute-start | bytes 786440 | tf_op jit(solution)/shard_map/ppermute | solution.py:22
  31.2 3.6 %second_early_kernel.1 = (bf16[32,16,128]{2,1,0:T(8,128)(2,1)S(1)}, bf16[32,16,128]{2,1,0:T(8,128)(2,1)S(1)}, bf16[32,16,128]{2,1,0:T(8,128)(2,1)S(1)}) custom-call(s32[8,256]{1,0:T(8,128)S(1)} %get-tuple-element.40.idx, bf16[64,16,128]{2,1,0:T(8,128)(2,1)S(1)} %enter_first_kernel.1.own.before, bf16[64,16,128]{2,1,0:T(8,128)(2,1)S(1)} %collective-permute-done.3.got, ...), custom_call_target="tpu_custom_call" | custom-call | flops 1409286144 | bytes 1384448 | tf_op jit(solution)/shard_map/second_early_kernel/pallas_call | solution.py:473
  34.8 0.3 collective-permute-done.2.got
  35.1 5.4 %second_late_kernel.1 = (f32[64,8,128]{2,1,0:T(8,128)S(1)}, f32[4,64,128]{2,1,0:T(8,128)}, f32[64,8,128]{2,1,0:T(8,128)S(1)}) custom-call(s32[8,256]{1,0:T(8,128)S(1)} %get-tuple-element.40.idx, bf16[64,16,128]{2,1,0:T(8,128)(2,1)S(1)} %enter_first_kernel.1.own.before, bf16[64,16,128]{2,1,0:T(8,128)(2,1)S(1)} %collective-permute-done.2.got, ...), custom_call_target="tpu_custom_call" | custom-call | flops 1879048192 | bytes 2826240 | tf_op jit(solution)/shard_map/second_late_kernel/pallas_call | solution.py:473
  40.5 0.7 %copy-done.6 = f32[64,8,128]{2,1,0:T(8,128)} copy-done((f32[64,8,128]{2,1,0:T(8,128)}, f32[64,8,128]{2,1,0:T(8,128)S(1)}, u32[]{:S(2)}) %copy-start.6) | copy-done | bytes 262168
  41.2 3.3 %all-to-all-start.1 = ((f32[4,64,128]{2,1,0:T(8,128)}), f32[4,64,128]{2,1,0:T(8,128)S(1)}, u32[]{:S(2)}, u32[]{:S(2)}) async-start(f32[4,64,128]{2,1,0:T(8,128)} %get-tuple-element.47), calls=%async_computation.1 | async-start | bytes 262144 | tf_op jit(solution)/shard_map/all_to_all | solution.py:26
  44.5 0.7 %scan_kernel.3.starts = f32[64,8,128]{2,1,0:T(8,128)S(1)} custom-call(f32[64,8,128]{2,1,0:T(8,128)S(1)} %get-tuple-element.48.values, bf16[1024,256]{1,0:T(8,128)(2,1)S(1)} %get-tuple-element.39.pk), custom_call_target="tpu_custom_call" | custom-call | flops 10000000 | bytes 1048576 | tf_op jit(solution)/shard_map/scan_kernel/pallas_call | solution.py:473
  45.3 4.0 %all-to-all-done.1.ends = f32[4,64,128]{2,1,0:T(8,128)S(1)} async-done(((f32[4,64,128]{2,1,0:T(8,128)}), f32[4,64,128]{2,1,0:T(8,128)S(1)}, u32[]{:S(2)}, u32[]{:S(2)}) %all-to-all-start.1) | async-done | bytes 131104 | tf_op jit(solution)/shard_map/all_to_all | solution.py:26
  49.3 0.6 enter_second_kernel.1
  50.0 5.0 %collective-permute-start.4 = (bf16[48,16,128]{2,1,0:T(8,128)(2,1)S(1)}, bf16[48,16,128]{2,1,0:T(8,128)(2,1)S(1)}, u32[]{:S(2)}, u32[]{:S(2)}) collective-permute-start(bf16[48,16,128]{2,1,0:T(8,128)(2,1)S(1)} %get-tuple-element.50), channel_id=1, source_target_pairs={{1,2},{2,1},{5,6},{6,5},{9,10},{10,9},{13,14},{14,13},{17,18},{18,... | collective-permute-start | bytes 589832 | tf_op jit(solution)/shard_map/ppermute | solution.py:22
  55.0 5.3 %third_early_kernel.1 = (f32[32,64,128]{2,1,0:T(8,128)}, bf16[32,16,128]{2,1,0:T(8,128)(2,1)S(1)}, bf16[32,16,128]{2,1,0:T(8,128)(2,1)S(1)}) custom-call(s32[8,256]{1,0:T(8,128)S(1)} %get-tuple-element.40.idx, bf16[64,16,128]{2,1,0:T(8,128)(2,1)S(1)} %get-tuple-element.49.own, bf16[48,16,128]{2,1,0:T(8,128)(2,1)S(1)} %collective-permute-done.5.got, ...), custom_call_target="tpu_custom_call" | custom-call | flops 1056964608 | bytes 4042752 | tf_op jit(solution)/shard_map/third_early_kernel/pallas_call | solution.py:473
  60.4 4.7 %third_late_kernel.1 = f32[32,64,128]{2,1,0:T(8,128)} custom-call(s32[8,256]{1,0:T(8,128)S(1)} %get-tuple-element.40.idx, bf16[64,16,128]{2,1,0:T(8,128)(2,1)S(1)} %get-tuple-element.49.own, bf16[48,16,128]{2,1,0:T(8,128)(2,1)S(1)} %collective-permute-done.4.got, bf16[32,16,128]{2,1,0:T(8,128)(2,1)S(1)} %get-tuple-element.54.strip1, ...), custom_call_target="tpu_custom_call", output_to_operand_aliasing={{}: (8, {})} | custom-call | flops 1056964608 | bytes 4042752 | tf_op jit(solution)/shard_map/third_late_kernel/pallas_call | solution.py:473
  (20 shorter events, 0.1 us)
Async XLA Ops:
  0.0 7.8 %copy-start.2 = (f32[6,128,128]{2,1,0:T(8,128)S(1)}, f32[6,128,128]{2,1,0:T(8,128)}, u32[]{:S(2)}) copy-start(f32[6,128,128]{2,1,0:T(8,128)} %faces.1) | copy-start | bytes 1179652
  0.0 7.8 %copy-start.3 = (f32[128,128]{1,0:T(8,128)S(1)}, f32[128,128]{1,0:T(8,128)}, u32[]{:S(2)}) copy-start(f32[128,128]{1,0:T(8,128)} %diag.1) | copy-start | bytes 196612
  0.0 7.8 %copy-start.4 = (f32[128,128]{1,0:T(8,128)S(1)}, f32[128,128]{1,0:T(8,128)}, u32[]{:S(2)}) copy-start(f32[128,128]{1,0:T(8,128)} %coarse.1) | copy-start | bytes 196612
  3.1 5.7 %collective-permute-start = (bf16[912,128]{1,0:T(8,128)(2,1)}, bf16[912,128]{1,0:T(8,128)(2,1)S(1)}, u32[]{:S(2)}, u32[]{:S(2)}) collective-permute-start(bf16[912,128]{1,0:T(8,128)(2,1)} %get-tuple-element.33), channel_id=1, source_target_pairs={{0,1},{1,0},{2,3},{3,2},{4,5},{5,4},{6,7},{7,6},{8,9},{9,8},{10,11... | collective-permute-start | bytes 700424 | tf_op jit(solution)/shard_map/ppermute | solution.py:22
  3.2 5.6 %copy-start = (bf16[4,512,128]{2,1,0:T(8,128)(2,1)S(1)}, bf16[4,512,128]{2,1,0:T(8,128)(2,1)}, u32[]{:S(2)}) copy-start(bf16[4,512,128]{2,1,0:T(8,128)(2,1)} %get-tuple-element.31.fe) | copy-start | bytes 1572868
  3.2 5.6 %copy-start.1 = (f32[64,128]{1,0:T(8,128)S(1)}, f32[64,128]{1,0:T(8,128)}, u32[]{:S(2)}) copy-start(f32[64,128]{1,0:T(8,128)} %init.7) | copy-start | bytes 98308
  3.2 9.1 %collective-permute-start.1 = (bf16[912,128]{1,0:T(8,128)(2,1)}, bf16[912,128]{1,0:T(8,128)(2,1)S(1)}, u32[]{:S(2)}, u32[]{:S(2)}) collective-permute-start(bf16[912,128]{1,0:T(8,128)(2,1)} %get-tuple-element.34), channel_id=1, source_target_pairs={{1,2},{2,1},{5,6},{6,5},{9,10},{10,9},{13,14},{14,13},{17,18},{18,... | collective-permute-start | bytes 700424 | tf_op jit(solution)/shard_map/ppermute | solution.py:22
  8.8 0.7 %copy-start.5 = (bf16[16,128]{1,0:T(8,128)(2,1)S(1)}, bf16[16,128]{1,0:T(8,128)(2,1)}, u32[]{:S(2)}) copy-start(bf16[16,128]{1,0:T(8,128)(2,1)} %get-tuple-element.32.tab) | copy-start | bytes 12292
  16.4 10.2 %all-to-all-start = ((f32[4,64,128]{2,1,0:T(8,128)}), f32[4,64,128]{2,1,0:T(8,128)S(1)}, u32[]{:S(2)}, u32[]{:S(2)}) async-start(f32[4,64,128]{2,1,0:T(8,128)} %get-tuple-element.41), calls=%async_computation | async-start | bytes 262144 | tf_op jit(solution)/shard_map/all_to_all | solution.py:26
  27.2 4.1 %collective-permute-start.3 = (bf16[64,16,128]{2,1,0:T(8,128)(2,1)S(1)}, bf16[64,16,128]{2,1,0:T(8,128)(2,1)S(1)}, u32[]{:S(2)}, u32[]{:S(2)}) collective-permute-start(bf16[64,16,128]{2,1,0:T(8,128)(2,1)S(1)} %enter_first_kernel.1.own.before), channel_id=1, source_target_pairs={{0,1},{1,0},{2,3},{3,2},{4,5},{5,4},{6,7},{7,6},{8,9},{9,8},{10,11... | collective-permute-start | bytes 786440 | tf_op jit(solution)/shard_map/ppermute | solution.py:22
  27.2 7.8 %collective-permute-start.2 = (bf16[64,16,128]{2,1,0:T(8,128)(2,1)S(1)}, bf16[64,16,128]{2,1,0:T(8,128)(2,1)S(1)}, u32[]{:S(2)}, u32[]{:S(2)}) collective-permute-start(bf16[64,16,128]{2,1,0:T(8,128)(2,1)S(1)} %enter_first_kernel.1.own.before), channel_id=1, source_target_pairs={{1,2},{2,1},{5,6},{6,5},{9,10},{10,9},{13,14},{14,13},{17,18},{18,... | collective-permute-start | bytes 786440 | tf_op jit(solution)/shard_map/ppermute | solution.py:22
  40.5 0.7 %copy-start.6 = (f32[64,8,128]{2,1,0:T(8,128)}, f32[64,8,128]{2,1,0:T(8,128)S(1)}, u32[]{:S(2)}) copy-start(f32[64,8,128]{2,1,0:T(8,128)S(1)} %get-tuple-element.53.total) | copy-start | bytes 786436
  41.2 8.1 %all-to-all-start.1 = ((f32[4,64,128]{2,1,0:T(8,128)}), f32[4,64,128]{2,1,0:T(8,128)S(1)}, u32[]{:S(2)}, u32[]{:S(2)}) async-start(f32[4,64,128]{2,1,0:T(8,128)} %get-tuple-element.47), calls=%async_computation.1 | async-start | bytes 262144 | tf_op jit(solution)/shard_map/all_to_all | solution.py:26
  49.3 5.7 %copy-start.7 = (f32[64,8,128]{2,1,0:T(8,128)S(1)}, f32[64,8,128]{2,1,0:T(8,128)}, u32[]{:S(2)}) copy-start(f32[64,8,128]{2,1,0:T(8,128)} %copy-done.6) | copy-start | bytes 786436
  49.9 5.1 %collective-permute-start.5 = (bf16[48,16,128]{2,1,0:T(8,128)(2,1)S(1)}, bf16[48,16,128]{2,1,0:T(8,128)(2,1)S(1)}, u32[]{:S(2)}, u32[]{:S(2)}) collective-permute-start(bf16[48,16,128]{2,1,0:T(8,128)(2,1)S(1)} %get-tuple-element.51), channel_id=1, source_target_pairs={{0,1},{1,0},{2,3},{3,2},{4,5},{5,4},{6,7},{7,6},{8,9},{9,8},{10,11... | collective-permute-start | bytes 589832 | tf_op jit(solution)/shard_map/ppermute | solution.py:22
  50.0 10.4 %collective-permute-start.4 = (bf16[48,16,128]{2,1,0:T(8,128)(2,1)S(1)}, bf16[48,16,128]{2,1,0:T(8,128)(2,1)S(1)}, u32[]{:S(2)}, u32[]{:S(2)}) collective-permute-start(bf16[48,16,128]{2,1,0:T(8,128)(2,1)S(1)} %get-tuple-element.50), channel_id=1, source_target_pairs={{1,2},{2,1},{5,6},{6,5},{9,10},{10,9},{13,14},{14,13},{17,18},{18,... | collective-permute-start | bytes 589832 | tf_op jit(solution)/shard_map/ppermute | solution.py:22

commit v4 on v2

--- a/solution.py
+++ b/solution.py
@@ -99,8 +99,14 @@
     return lax.rem(lax.axis_index("space"), 2) == 0
 
 
-def mirrored(low, size, full):
-    return jnp.where(even_place(), full - low - size, low)
+def by_parity(body):
+    even = even_place()
+    pl.when(even)(lambda: body(True))
+    pl.when(jnp.logical_not(even))(lambda: body(False))
+
+
+def mirrored(low, size, full, even):
+    return full - low - size if even else low
 
 
 def pack_kernel(
@@ -187,25 +193,23 @@
     width = (COARSEN - 1 - k) * REACH * 8
     dst[pl.ds(n * 8, n * 8), :] = own[k]
     if width:
-        to = pl.multiple_of(jnp.where(right, 2 * n * 8, n * 8 - width), 128)
+        to = 2 * n * 8 if right else n * 8 - width
         dst[pl.ds(to, width), :] = got[pl.ds(at, width), :]
 
 
 def force_at(src, base, size):
-    at = pl.multiple_of(base * 8, 128)
-    return src[pl.ds(at, size * 8), :].astype(F32).reshape(size, 8, 128)
-
-
-def put_tables(tab, got_even, got_odd, idx_v, columns, square, full, n):
-    even = even_place()
+    return src[pl.ds(base * 8, size * 8), :].astype(F32).reshape(size, 8, 128)
+
+
+def put_tables(tab, got_even, got_odd, idx_v, columns, square, full, n, even):
     lane = lax.broadcasted_iota(jnp.int32, (8, 128), 1)
 
     def table(ref):
         return 0.0 if ref is None else ref[pl.ds(ref.shape[0] - 16, 16), :].astype(F32)[0:8]
 
     from_even, from_odd = table(got_even), table(got_odd)
-    low = jnp.where(lane < n, jnp.where(even, from_odd, from_even), table(tab))
-    high = jnp.where(lane < n, jnp.where(even, from_even, from_odd), 0.0)
+    low = jnp.where(lane < n, from_odd if even else from_even, table(tab))
+    high = jnp.where(lane < n, from_even if even else from_odd, 0.0)
     for at, offs in ((0, low), (128, high)):
         value = jnp.where(offs != 0.0, lane + at + offs.astype(jnp.int32), full)
         idx_v[:, pl.ds(at, 128)] = value
@@ -214,19 +218,18 @@
         columns[pl.ds(at, 128), :] = square[...].T
 
 
-def push_init(init, got_even, got_odd, w, columns, i16, base, count, n):
-    even = even_place()
+def push_init(init, got_even, got_odd, w, columns, i16, base, count, n, even):
     i16[...] = jnp.zeros_like(i16)
     lead = init[...].astype(BF16)
     i16[pl.ds(n, n), 0:128] = lead
     i16[pl.ds(n, n), 128:256] = (init[...] - lead.astype(F32)).astype(BF16)
-    for ref, right in ((got_even, even), (got_odd, jnp.logical_not(even))):
+    for ref, right in ((got_even, even), (got_odd, not even)):
         if ref is not None:
             at = ref.shape[0] - 16
-            to = pl.multiple_of(jnp.where(right, 2 * n, 0), n)
+            to = 2 * n if right else 0
             i16[pl.ds(to, n), 0:128] = ref[pl.ds(at - 2 * n, n), :]
             i16[pl.ds(to, n), 128:256] = ref[pl.ds(at - n, n), :]
-    rows = pl.ds(pl.multiple_of(base, REACH), count)
+    rows = pl.ds(base, count)
     place = columns[rows, :]
     spot = lax.broadcasted_iota(jnp.int32, (count, 256), 1).astype(F32)
     cols = [i16[rows, :]]
@@ -243,77 +246,86 @@
 STRIP = 2 * REACH
 
 
-def put_strips(strips, states, full):
+def put_strips(strips, states, full, even):
     for strip, state, low in zip(strips, states, STRIPS):
-        strip[...] = state[pl.ds(mirrored(low, STRIP, full), STRIP)]
-
-
-def get_strips(strips, states, full):
+        strip[...] = state[pl.ds(mirrored(low, STRIP, full, even), STRIP)]
+
+
+def get_strips(strips, states, full, even):
     for strip, state, low in zip(strips, states, STRIPS):
-        state[pl.ds(mirrored(low, STRIP, full), STRIP)] = strip[...]
+        state[pl.ds(mirrored(low, STRIP, full, even), STRIP)] = strip[...]
         state[full] = jnp.zeros((16, 128), BF16)
 
 
 def first_early_kernel(
     fe, tab, init, got, w, strip1, strip2, strip3, s1, s2, s3, force, y, i16, columns, square, idx_v, idx, sem
 ):
-    n = init.shape[0]
-    full = 3 * n
-    even = even_place()
-    put_tables(tab, got, None, idx_v, columns, square, full, n)
-    copy = pltpu.make_async_copy(idx_v, idx, sem)
-    copy.start()
-    count = 6 * REACH
-    base = mirrored(REACH, count, full)
-    pushed = push_init(init, got, None, w, columns, i16, base, count, n)
-    put_force(force, fe, got, even, 0, n)
-    y[pl.ds(0, count * 8), :] = force[pl.ds(pl.multiple_of(base * 8, 128), count * 8), :].astype(F32)
-    y[pl.ds(0, count, stride=8), :] = y[pl.ds(0, count, stride=8), :] + pushed
-    s1[pl.ds(base, count)] = split(y[pl.ds(0, count * 8), :].reshape(count, 8, 128))
-    for state in (s1, s2, s3):
-        state[full] = jnp.zeros((16, 128), BF16)
-    copy.wait()
-    for k, src, dst in ((1, s1, s2), (2, s2, s3)):
-        put_force(force, fe, got, even, k, n)
-        size = (6 - 2 * k) * REACH
-        base = mirrored((k + 1) * REACH, size, full)
-        dst[pl.ds(base, size)] = split(apply_phi(src, idx, w, base, size) + force_at(force, base, size))
-    put_strips((strip1, strip2, strip3), (s1, s2, s3), full)
+    def body(even):
+        n = init.shape[0]
+        full = 3 * n
+        put_tables(tab, got, None, idx_v, columns, square, full, n, even)
+        copy = pltpu.make_async_copy(idx_v, idx, sem)
+        copy.start()
+        count = 6 * REACH
+        base = mirrored(REACH, count, full, even)
+        pushed = push_init(init, got, None, w, columns, i16, base, count, n, even)
+        put_force(force, fe, got, even, 0, n)
+        y[pl.ds(0, count * 8), :] = force[pl.ds(base * 8, count * 8), :].astype(F32)
+        y[pl.ds(0, count, stride=8), :] = y[pl.ds(0, count, stride=8), :] + pushed
+        s1[pl.ds(base, count)] = split(y[pl.ds(0, count * 8), :].reshape(count, 8, 128))
+        for state in (s1, s2, s3):
+            state[full] = jnp.zeros((16, 128), BF16)
+        copy.wait()
+        for k, src, dst in ((1, s1, s2), (2, s2, s3)):
+            put_force(force, fe, got, even, k, n)
+            size = (6 - 2 * k) * REACH
+            base = mirrored((k + 1) * REACH, size, full, even)
+            dst[pl.ds(base, size)] = split(apply_phi(src, idx, w, base, size) + force_at(force, base, size))
+        put_strips((strip1, strip2, strip3), (s1, s2, s3), full, even)
+
+    by_parity(body)
 
 
 def first_late_kernel(
     fe, tab, init, got_even, got_odd, strip1, strip2, strip3, w, pk, w1, end, idx_out,
     s1, s2, s3, force, y, i16, columns, square, idx, sem
 ):
-    n = init.shape[0]
-    full = 3 * n
-    odd = jnp.logical_not(even_place())
-    put_tables(tab, got_even, got_odd, idx_out, columns, square, full, n)
-    copy = pltpu.make_async_copy(idx_out, idx, sem)
-    copy.start()
-    count = 4 * REACH
-    base = mirrored(7 * REACH, count, full)
-    pushed = push_init(init, got_even, got_odd, w, columns, i16, base, count, n)
-    put_force(force, fe, got_odd, odd, 0, n)
-    y[...] = force[pl.ds(pl.multiple_of(base * 8, 128), count * 8), :].astype(F32)
-    y[pl.ds(0, count, stride=8), :] = y[pl.ds(0, count, stride=8), :] + pushed
-    s1[pl.ds(base, count)] = split(y[...].reshape(count, 8, 128))
-    get_strips((strip1, strip2, strip3), (s1, s2, s3), full)
-    copy.wait()
-    for k, src, dst in ((1, s1, s2), (2, s2, s3), (3, s3, None)):
-        put_force(force, fe, got_odd, odd, k, n)
-        base = mirrored((7 - k) * REACH, count, full)
-        value = apply_phi(src, idx, w, base, count) + force_at(force, base, count)
-        if dst is None:
-            w1[...] = value
-            y[...] = value.reshape(n * 8, 128)
-        else:
-            dst[pl.ds(base, count)] = split(value)
-    end[...] = block_end(y, pk, n)
+    def body(even):
+        n = init.shape[0]
+        full = 3 * n
+        put_tables(tab, got_even, got_odd, idx_out, columns, square, full, n, even)
+        copy = pltpu.make_async_copy(idx_out, idx, sem)
+        copy.start()
+        count = 4 * REACH
+        base = mirrored(7 * REACH, count, full, even)
+        pushed = push_init(init, got_even, got_odd, w, columns, i16, base, count, n, even)
+        put_force(force, fe, got_odd, not even, 0, n)
+        y[...] = force[pl.ds(base * 8, count * 8), :].astype(F32)
+        y[pl.ds(0, count, stride=8), :] = y[pl.ds(0, count, stride=8), :] + pushed
+        s1[pl.ds(base, count)] = split(y[...].reshape(count, 8, 128))
+        get_strips((strip1, strip2, strip3), (s1, s2, s3), full, even)
+        copy.wait()
+        for k, src, dst in ((1, s1, s2), (2, s2, s3), (3, s3, None)):
+            put_force(force, fe, got_odd, not even, k, n)
+            base = mirrored((7 - k) * REACH, count, full, even)
+            value = apply_phi(src, idx, w, base, count) + force_at(force, base, count)
+            if dst is None:
+                w1[...] = value
+                y[...] = value.reshape(n * 8, 128)
+            else:
+                dst[pl.ds(base, count)] = split(value)
+        end[...] = block_end(y, pk, n)
+
+    by_parity(body)
 
 
 def scan_kernel(values, pk, starts):
     starts[...] = scan_starts(values[...], pk)
+
+
+def scan_sum_kernel(values, w1, coarse, pk, starts, total):
+    starts[...] = scan_starts(values[...], pk)
+    total[...] = values[...] + (w1[...] + coarse[...])
 
 
 def enter_first_kernel(*refs):
@@ -341,45 +353,51 @@
 def put_block(dst, own, got, right, n):
     side = got.shape[0]
     dst[pl.ds(n, n)] = own[...]
-    dst[pl.ds(jnp.where(right, 2 * n, n - side), side)] = got[...]
+    dst[pl.ds(2 * n if right else n - side, side)] = got[...]
     dst[3 * n] = jnp.zeros((16, 128), BF16)
 
 
-def second_early_kernel(idx, own, got, w, strip1, strip2, strip3, s0, s1, s2, s3):
-    n = own.shape[0]
-    full = 3 * n
-    put_block(s0, own, got, even_place(), n)
-    for state in (s1, s2, s3):
-        state[full] = jnp.zeros((16, 128), BF16)
-    for k, src, dst in ((1, s0, s1), (2, s1, s2), (3, s2, s3)):
-        size = (8 - 2 * k) * REACH
-        base = mirrored(k * REACH, size, full)
-        dst[pl.ds(base, size)] = split(apply_phi(src, idx, w, base, size))
-    put_strips((strip1, strip2, strip3), (s1, s2, s3), full)
-
-
-def second_late_kernel(idx, own, got, strip1, strip2, strip3, w1, w, pk, res, end, total, s0, s1, s2, s3, y):
-    n = own.shape[0]
-    full = 3 * n
-    put_block(s0, own, got, jnp.logical_not(even_place()), n)
-    get_strips((strip1, strip2, strip3), (s1, s2, s3), full)
-    count = 4 * REACH
-    for k, src, dst in ((1, s0, s1), (2, s1, s2), (3, s2, s3)):
-        base = mirrored((8 - k) * REACH, count, full)
-        dst[pl.ds(base, count)] = split(apply_phi(src, idx, w, base, count))
-    value = apply_phi(s3, idx, w, n, n)
-    total[...] = value + w1[...]
-    value = value - product(own[...].reshape(n * 16, 128), power(pk, 1))
-    res[...] = value
-    y[...] = value.reshape(n * 8, 128)
-    end[...] = block_end(y, pk, n)
+def second_early_kernel(idx, own, got, w, pk, strip1, strip2, strip3, coarse, s0, s1, s2, s3):
+    def body(even):
+        n = own.shape[0]
+        full = 3 * n
+        coarse[...] = product(own[...].reshape(n * 16, 128), power(pk, 1))
+        put_block(s0, own, got, even, n)
+        for state in (s1, s2, s3):
+            state[full] = jnp.zeros((16, 128), BF16)
+        for k, src, dst in ((1, s0, s1), (2, s1, s2), (3, s2, s3)):
+            size = (8 - 2 * k) * REACH
+            base = mirrored(k * REACH, size, full, even)
+            dst[pl.ds(base, size)] = split(apply_phi(src, idx, w, base, size))
+        put_strips((strip1, strip2, strip3), (s1, s2, s3), full, even)
+
+    by_parity(body)
+
+
+def second_late_kernel(idx, own, got, strip1, strip2, strip3, coarse, w, pk, res, end, s0, s1, s2, s3, y):
+    def body(even):
+        n = own.shape[0]
+        full = 3 * n
+        put_block(s0, own, got, not even, n)
+        get_strips((strip1, strip2, strip3), (s1, s2, s3), full, even)
+        count = 4 * REACH
+        for k, src, dst in ((1, s0, s1), (2, s1, s2), (3, s2, s3)):
+            base = mirrored((8 - k) * REACH, count, full, even)
+            dst[pl.ds(base, count)] = split(apply_phi(src, idx, w, base, count))
+        value = apply_phi(s3, idx, w, n, n)
+        value = value - coarse[...]
+        res[...] = value
+        y[...] = value.reshape(n * 8, 128)
+        end[...] = block_end(y, pk, n)
+
+    by_parity(body)
 
 
 def write_out(out, k, value, begin, flip, sems):
     size = value.shape[0]
     for e in range(size):
         flip[pl.ds(e, 8, stride=size), :] = value[e]
-    rows = pl.ds(pl.multiple_of(begin, REACH), size)
+    rows = pl.ds(begin, size)
     copies = [
         pltpu.make_async_copy(flip.at[pl.ds(i * size, size)], out.at[i * COARSEN + k, rows], sems.at[k, i])
         for i in range(8)
@@ -392,52 +410,55 @@
 def third_early_kernel(
     idx, own, got, corr, total, fe, pay, w, pk, out, strip1, strip2, s0, s1, s2, force, flip0, flip1, flip2, flip3, sems
 ):
-    n = own.shape[0]
-    full = 3 * n
-    even = even_place()
-    points = product(split(corr[...]).reshape(-1, 128), power(pk, 1)) + total[...]
-    copies = write_out(out, COARSEN - 1, points, 0, flip3, sems)
-    put_block(s0, own, got, even, n)
-    for state in (s1, s2):
-        state[full] = jnp.zeros((16, 128), BF16)
-    for k, src, dst, flip in ((0, s0, s1, flip0), (1, s1, s2, flip1), (2, s2, None, flip2)):
-        put_force(force, fe, pay, even, k, n)
-        size = (5 - 2 * k) * REACH
-        base = mirrored((2 + k) * REACH, size, full)
-        value = apply_phi(src, idx, w, base, size) + force_at(force, base, size)
-        if dst is not None:
-            dst[pl.ds(base, size)] = split(value)
-        mine = (3 - k) * REACH
-        skip = size - mine
-        kept = jnp.where(even, value[:mine], value[skip:])
-        copies += write_out(out, k, kept, jnp.where(even, n - mine, 0), flip, sems)
-    put_strips((strip1, strip2), (s1, s2), full)
-    for copy in copies:
-        copy.wait()
+    def body(even):
+        n = own.shape[0]
+        full = 3 * n
+        points = product(split(corr[...]).reshape(-1, 128), power(pk, 1)) + total[...]
+        copies = write_out(out, COARSEN - 1, points, 0, flip3, sems)
+        put_block(s0, own, got, even, n)
+        for state in (s1, s2):
+            state[full] = jnp.zeros((16, 128), BF16)
+        for k, src, dst, flip in ((0, s0, s1, flip0), (1, s1, s2, flip1), (2, s2, None, flip2)):
+            put_force(force, fe, pay, even, k, n)
+            size = (5 - 2 * k) * REACH
+            base = mirrored((2 + k) * REACH, size, full, even)
+            value = apply_phi(src, idx, w, base, size) + force_at(force, base, size)
+            if dst is not None:
+                dst[pl.ds(base, size)] = split(value)
+            mine = (3 - k) * REACH
+            skip = size - mine
+            kept = value[:mine] if even else value[skip:]
+            copies += write_out(out, k, kept, n - mine if even else 0, flip, sems)
+        put_strips((strip1, strip2), (s1, s2), full, even)
+        for copy in copies:
+            copy.wait()
+
+    by_parity(body)
 
 
 def third_late_kernel(
     idx, own, got, strip1, strip2, fe, pay, w, partial, out, s0, s1, s2, force, flip0, flip1, flip2, sems
 ):
-    n = own.shape[0]
-    full = 3 * n
-    even = even_place()
-    odd = jnp.logical_not(even)
-    put_block(s0, own, got, odd, n)
-    get_strips((strip1, strip2), (s1, s2), full)
-    copies = []
-    size = 3 * REACH
-    for k, src, dst, flip in ((0, s0, s1, flip0), (1, s1, s2, flip1), (2, s2, None, flip2)):
-        put_force(force, fe, pay, odd, k, n)
-        base = mirrored((7 - k) * REACH, size, full)
-        value = apply_phi(src, idx, w, base, size) + force_at(force, base, size)
-        if dst is not None:
-            dst[pl.ds(base, size)] = split(value)
-        mine = (k + 1) * REACH
-        kept = jnp.where(even, value[size - mine :], value[:mine])
-        copies += write_out(out, k, kept, jnp.where(even, 0, n - mine), flip, sems)
-    for copy in copies:
-        copy.wait()
+    def body(even):
+        n = own.shape[0]
+        full = 3 * n
+        put_block(s0, own, got, not even, n)
+        get_strips((strip1, strip2), (s1, s2), full, even)
+        copies = []
+        size = 3 * REACH
+        for k, src, dst, flip in ((0, s0, s1, flip0), (1, s1, s2, flip1), (2, s2, None, flip2)):
+            put_force(force, fe, pay, not even, k, n)
+            base = mirrored((7 - k) * REACH, size, full, even)
+            value = apply_phi(src, idx, w, base, size) + force_at(force, base, size)
+            if dst is not None:
+                dst[pl.ds(base, size)] = split(value)
+            mine = (k + 1) * REACH
+            kept = value[size - mine :] if even else value[:mine]
+            copies += write_out(out, k, kept, 0 if even else n - mine, flip, sems)
+        for copy in copies:
+            copy.wait()
+
+    by_parity(body)
 
 
 def call(kernel, inputs, outs, scratch, spaces="", out_spaces="", aliases=None, flops=10**7, room=32):
@@ -527,24 +548,24 @@
     (starts,) = call(scan_kernel, (w1, pk), (tiles,), [])
     (coarse,) = call(enter_first_kernel, (*arrivals, starts, we, pk), (state,), [rows])
     got_odd, got_even = swapped(coarse, 1), swapped(coarse, 0)
-    strips = call(
+    *strips, moved = call(
         second_early_kernel,
-        (idx, coarse, got_even, w),
-        (strip, strip, strip),
+        (idx, coarse, got_even, w, pk),
+        (strip, strip, strip, tiles),
         [spaces] * 4,
         spaces="s",
         flops=step_flops * 12 * REACH,
     )
-    res, end, total = call(
+    res, end = call(
         second_late_kernel,
-        (idx, coarse, got_odd, *strips, w1, w, pk),
-        (tiles, ends, tiles),
+        (idx, coarse, got_odd, *strips, moved, w, pk),
+        (tiles, ends),
         [spaces] * 4 + [rows],
         spaces="s",
         flops=step_flops * 16 * REACH,
     )
     arrivals = earlier(end)
-    (starts,) = call(scan_kernel, (res, pk), (tiles,), [])
+    starts, total = call(scan_sum_kernel, (res, w1, moved, pk), (tiles, tiles), [])
     side = shape(((COARSEN - 1) * REACH, 16, width), BF16)
     coarse, end_even, end_odd, corr = call(
         enter_second_kernel,

time: 61.5 us -> 58.6 us (0.953)
  Pallas kernels: 30.4 us -> 27.5 us
    pallas_call x12, Pallas kernels: 30.4 us -> 27.5 us  [call(): pl.pallas_call(kernel, out_shape=outs, name=kernel.__name__, in_specs=spe...]
  transfers between devices with their start and end apart: 12 -> 12, of which waited for: 3 -> 3; matrix products, arithmetic and copies ran while one was open for 0% -> 0% of each run, Pallas kernels for 23% -> 22%
where the time goes in v4:
time: 58.6 us; the launch traced here: 58.3 us
  starting transfers between devices  28.7 us (49%)
  Pallas kernels  27.5 us (47%)
  waiting for transfers between devices  0.94 us (2%)
  local copies, waits for them, and re-layouts  0.66 us (1%)
    pallas_call x12, Pallas kernels, call(): pl.pallas_call(kernel, out_shape=outs, name=kernel.__name__, in_specs=spe...  27.5 us
    ppermute x6, starting transfers between devices, earlier(): lax.ppermute(value, 'tm', [(i, i + s) for i in range(count - s)])  15.2 us
    ppermute x6, starting transfers between devices, swapped(): return lax.ppermute(value, 'space', pairs)  13.5 us
  transfers between devices with their start and end apart: 12, of which 3 were waited for; matrix products, arithmetic and copies ran while one was open for 0% of the time, Pallas kernels for 22%

profile of v4, /device:TPU:1, one launch (start us, length us, event | category | flops | bytes accessed | tf_op | source)
XLA Modules:
  0.0 58.3 jit_solution(5081242541632824406)
XLA Ops:
  0.0 3.0 %pack_kernel.1 = (bf16[4,512,128]{2,1,0:T(8,128)(2,1)}, bf16[16,128]{1,0:T(8,128)(2,1)}, bf16[912,128]{1,0:T(8,128)(2,1)}, bf16[912,128]{1,0:T(8,128)(2,1)}) custom-call(bf16[8,4,64,128]{3,2,1,0:T(8,128)(2,1)} %bitcast.3, f32[64,128]{1,0:T(8,128)} %refs_5_.1, s32[6,64]{1,0:T(8,128)} %bitcast.4, s32[6,64]{1,0:T(8,128)} %bitcast.5), custom_call_target="tpu_custom_call" | custom-call | flops 10000000 | bytes 1555456 | tf_op jit(solution)/shard_map/pack_kernel/pallas_call | solution.py:472
  3.2 4.6 %collective-permute-start.1 = (bf16[912,128]{1,0:T(8,128)(2,1)}, bf16[912,128]{1,0:T(8,128)(2,1)S(1)}, u32[]{:S(2)}, u32[]{:S(2)}) collective-permute-start(bf16[912,128]{1,0:T(8,128)(2,1)} %get-tuple-element.36), channel_id=1, source_target_pairs={{1,2},{2,1},{5,6},{6,5},{9,10},{10,9},{13,14},{14,13},{17,18},{18,... | collective-permute-start | bytes 700424 | tf_op jit(solution)/shard_map/ppermute | solution.py:22
  7.8 1.5 %weight_kernel.1 = (bf16[896,256]{1,0:T(8,128)(2,1)S(1)}, bf16[1024,256]{1,0:T(8,128)(2,1)S(1)}, bf16[384,256]{1,0:T(8,128)(2,1)S(1)}) custom-call(f32[128,128]{1,0:T(8,128)S(1)} %copy-done.3, f32[6,128,128]{2,1,0:T(8,128)S(1)} %copy-done.2, f32[128,128]{1,0:T(8,128)S(1)} %copy-done.4), custom_call_target="tpu_custom_call" | custom-call | flops 1000000000 | bytes 1703936 | tf_op jit(solution)/shard_map/weight_kernel/pallas_call | solution.py:472
  9.4 0.6 %copy-done.5 = bf16[16,128]{1,0:T(8,128)(2,1)S(1)} copy-done((bf16[16,128]{1,0:T(8,128)(2,1)S(1)}, bf16[16,128]{1,0:T(8,128)(2,1)}, u32[]{:S(2)}) %copy-start.5) | copy-done | bytes 4120
  10.1 2.6 %first_early_kernel.1 = (bf16[32,16,128]{2,1,0:T(8,128)(2,1)S(1)}, bf16[32,16,128]{2,1,0:T(8,128)(2,1)S(1)}, bf16[32,16,128]{2,1,0:T(8,128)(2,1)S(1)}) custom-call(bf16[4,512,128]{2,1,0:T(8,128)(2,1)S(1)} %copy-done, bf16[16,128]{1,0:T(8,128)(2,1)S(1)} %copy-done.5, f32[64,128]{1,0:T(8,128)S(1)} %copy-done.1, ...), custom_call_target="tpu_custom_call" | custom-call | flops 704643072 | bytes 1646592 | tf_op jit(solution)/shard_map/first_early_kernel/pallas_call | solution.py:472
  12.6 3.1 %first_late_kernel.1 = (f32[64,8,128]{2,1,0:T(8,128)S(1)}, f32[64,128]{1,0:T(8,128)S(1)}, s32[8,256]{1,0:T(8,128)S(1)}) custom-call(bf16[4,512,128]{2,1,0:T(8,128)(2,1)S(1)} %copy-done, bf16[16,128]{1,0:T(8,128)(2,1)S(1)} %copy-done.5, f32[64,128]{1,0:T(8,128)S(1)} %copy-done.1, bf16[912,128]{1,0:T(8,128)(2,1)S(1)} %collective-permute-done.got.got_even.pay, ...), custom_call_target="tpu_custom_call" | custom-call | flops 1409286144 | bytes 2707456 | tf_op jit(solution)/shard_map/first_late_kernel/pallas_call | solution.py:472
  15.8 5.2 %collective-permute-start.4 = (f32[64,128]{1,0:T(8,128)S(1)}, f32[64,128]{1,0:T(8,128)S(1)}, u32[]{:S(2)}, u32[]{:S(2)}) collective-permute-start(f32[64,128]{1,0:T(8,128)S(1)} %get-tuple-element.43), channel_id=1, source_target_pairs={{0,12},{1,13},{2,14},{3,15},{16,28},{17,29},{18,30},{19,31}} | collective-permute-start | bytes 98312 | tf_op jit(solution)/shard_map/ppermute | solution.py:28
  21.0 1.3 %collective-permute-start.3 = (f32[64,128]{1,0:T(8,128)S(1)}, f32[64,128]{1,0:T(8,128)S(1)}, u32[]{:S(2)}, u32[]{:S(2)}) collective-permute-start(f32[64,128]{1,0:T(8,128)S(1)} %get-tuple-element.43), channel_id=1, source_target_pairs={{0,8},{4,12},{1,9},{5,13},{2,10},{6,14},{3,11},{7,15},{16,24},{20,... | collective-permute-start | bytes 98312 | tf_op jit(solution)/shard_map/ppermute | solution.py:28
  22.3 2.2 %collective-permute-start.2 = (f32[64,128]{1,0:T(8,128)S(1)}, f32[64,128]{1,0:T(8,128)S(1)}, u32[]{:S(2)}, u32[]{:S(2)}) collective-permute-start(f32[64,128]{1,0:T(8,128)S(1)} %get-tuple-element.43), channel_id=1, source_target_pairs={{0,4},{4,8},{8,12},{1,5},{5,9},{9,13},{2,6},{6,10},{10,14},{3,7},{... | collective-permute-start | bytes 98312 | tf_op jit(solution)/shard_map/ppermute | solution.py:28
  24.5 0.7 %scan_kernel.1.refs_3_ = f32[64,8,128]{2,1,0:T(8,128)S(1)} custom-call(f32[64,8,128]{2,1,0:T(8,128)S(1)} %get-tuple-element.44.values.w1, bf16[1024,256]{1,0:T(8,128)(2,1)S(1)} %get-tuple-element.41.pk.refs_5_.refs_7_), custom_call_target="tpu_custom_call" | custom-call | flops 10000000 | bytes 1048576 | tf_op jit(solution)/shard_map/scan_kernel/pallas_call | solution.py:472
  25.2 0.3 collective-permute-done.2.refs_0_
  25.5 0.5 enter_first_kernel.1.own.refs_4_
  26.2 3.8 %collective-permute-start.5 = (bf16[64,16,128]{2,1,0:T(8,128)(2,1)S(1)}, bf16[64,16,128]{2,1,0:T(8,128)(2,1)S(1)}, u32[]{:S(2)}, u32[]{:S(2)}) collective-permute-start(bf16[64,16,128]{2,1,0:T(8,128)(2,1)S(1)} %enter_first_kernel.1.own.refs_4_), channel_id=1, source_target_pairs={{1,2},{2,1},{5,6},{6,5},{9,10},{10,9},{13,14},{14,13},{17,18},{18,... | collective-permute-start | bytes 786440 | tf_op jit(solution)/shard_map/ppermute | solution.py:22
  30.0 3.4 %second_early_kernel.1 = (bf16[32,16,128]{2,1,0:T(8,128)(2,1)S(1)}, bf16[32,16,128]{2,1,0:T(8,128)(2,1)S(1)}, bf16[32,16,128]{2,1,0:T(8,128)(2,1)S(1)}, f32[64,8,128]{2,1,0:T(8,128)S(1)}) custom-call(s32[8,256]{1,0:T(8,128)S(1)} %get-tuple-element.42.idx, bf16[64,16,128]{2,1,0:T(8,128)(2,1)S(1)} %enter_first_kernel.1.own.refs_4_, ...), custom_call_target="tpu_custom_call" | custom-call | flops 1409286144 | bytes 2170880 | tf_op jit(solution)/shard_map/second_early_kernel/pallas_call | solution.py:472
  33.5 0.6 collective-permute-done.5.got
  34.0 3.9 %second_late_kernel.1 = (f32[64,8,128]{2,1,0:T(8,128)S(1)}, f32[64,128]{1,0:T(8,128)S(1)}) custom-call(s32[8,256]{1,0:T(8,128)S(1)} %get-tuple-element.42.idx, bf16[64,16,128]{2,1,0:T(8,128)(2,1)S(1)} %enter_first_kernel.1.own.refs_4_, bf16[64,16,128]{2,1,0:T(8,128)(2,1)S(1)} %collective-permute-done.5.got, ...), custom_call_target="tpu_custom_call" | custom-call | flops 1879048192 | bytes 2465792 | tf_op jit(solution)/shard_map/second_late_kernel/pallas_call | solution.py:472
  37.9 2.8 %collective-permute-start.9 = (f32[64,128]{1,0:T(8,128)S(1)}, f32[64,128]{1,0:T(8,128)S(1)}, u32[]{:S(2)}, u32[]{:S(2)}) collective-permute-start(f32[64,128]{1,0:T(8,128)S(1)} %get-tuple-element.50), channel_id=1, source_target_pairs={{0,12},{1,13},{2,14},{3,15},{16,28},{17,29},{18,30},{19,31}} | collective-permute-start | bytes 98312 | tf_op jit(solution)/shard_map/ppermute | solution.py:28
  40.7 1.3 %collective-permute-start.8 = (f32[64,128]{1,0:T(8,128)S(1)}, f32[64,128]{1,0:T(8,128)S(1)}, u32[]{:S(2)}, u32[]{:S(2)}) collective-permute-start(f32[64,128]{1,0:T(8,128)S(1)} %get-tuple-element.50), channel_id=1, source_target_pairs={{0,8},{4,12},{1,9},{5,13},{2,10},{6,14},{3,11},{7,15},{16,24},{20,... | collective-permute-start | bytes 98312 | tf_op jit(solution)/shard_map/ppermute | solution.py:28
  42.0 2.4 %collective-permute-start.7 = (f32[64,128]{1,0:T(8,128)S(1)}, f32[64,128]{1,0:T(8,128)S(1)}, u32[]{:S(2)}, u32[]{:S(2)}) collective-permute-start(f32[64,128]{1,0:T(8,128)S(1)} %get-tuple-element.50), channel_id=1, source_target_pairs={{0,4},{4,8},{8,12},{1,5},{5,9},{9,13},{2,6},{6,10},{10,14},{3,7},{... | collective-permute-start | bytes 98312 | tf_op jit(solution)/shard_map/ppermute | solution.py:28
  44.4 0.7 %scan_sum_kernel.1 = (f32[64,8,128]{2,1,0:T(8,128)S(1)}, f32[64,8,128]{2,1,0:T(8,128)S(1)}) custom-call(f32[64,8,128]{2,1,0:T(8,128)S(1)} %get-tuple-element.51.values, f32[64,8,128]{2,1,0:T(8,128)S(1)} %get-tuple-element.44.values.w1, f32[64,8,128]{2,1,0:T(8,128)S(1)} %get-tuple-element.49.coarse, bf16[1024,256]{1,0:T(8,128)(2,1)S(1)} %get-tuple-element.41.pk.refs_5_.refs_7_), custom_call_target="tpu_custom_call" | custom-call | flops 10000000 | bytes 1835008 | tf_op jit(solution)/shard_map/scan_sum_kernel/pallas_call | solution.py:472
  45.2 0.6 %enter_second_kernel.1 = (bf16[64,16,128]{2,1,0:T(8,128)(2,1)S(1)}, bf16[48,16,128]{2,1,0:T(8,128)(2,1)S(1)}, bf16[48,16,128]{2,1,0:T(8,128)(2,1)S(1)}, f32[64,8,128]{2,1,0:T(8,128)S(1)}) custom-call(f32[64,128]{1,0:T(8,128)S(1)} %collective-permute-done.7.refs_0_, f32[64,128]{1,0:T(8,128)S(1)} %collective-permute-done.8.refs_1_, ...), custom_call_target="tpu_custom_call" | custom-call | flops 10000000 | bytes 2293760 | tf_op jit(solution)/shard_map/enter_second_kernel/pallas_call | solution.py:472
  45.9 4.8 %collective-permute-start.10 = (bf16[48,16,128]{2,1,0:T(8,128)(2,1)S(1)}, bf16[48,16,128]{2,1,0:T(8,128)(2,1)S(1)}, u32[]{:S(2)}, u32[]{:S(2)}) collective-permute-start(bf16[48,16,128]{2,1,0:T(8,128)(2,1)S(1)} %get-tuple-element.54), channel_id=1, source_target_pairs={{1,2},{2,1},{5,6},{6,5},{9,10},{10,9},{13,14},{14,13},{17,18},{18,... | collective-permute-start | bytes 589832 | tf_op jit(solution)/shard_map/ppermute | solution.py:22
  50.7 4.0 %third_early_kernel.1 = (f32[32,64,128]{2,1,0:T(8,128)}, bf16[32,16,128]{2,1,0:T(8,128)(2,1)S(1)}, bf16[32,16,128]{2,1,0:T(8,128)(2,1)S(1)}) custom-call(s32[8,256]{1,0:T(8,128)S(1)} %get-tuple-element.42.idx, bf16[64,16,128]{2,1,0:T(8,128)(2,1)S(1)} %get-tuple-element.53.own, bf16[48,16,128]{2,1,0:T(8,128)(2,1)S(1)} %collective-permute-done.11.got, ...), custom_call_target="tpu_custom_call" | custom-call | flops 1056964608 | bytes 4042752 | tf_op jit(solution)/shard_map/third_early_kernel/pallas_call | solution.py:472
  54.8 3.4 %third_late_kernel.1 = f32[32,64,128]{2,1,0:T(8,128)} custom-call(s32[8,256]{1,0:T(8,128)S(1)} %get-tuple-element.42.idx, bf16[64,16,128]{2,1,0:T(8,128)(2,1)S(1)} %get-tuple-element.53.own, bf16[48,16,128]{2,1,0:T(8,128)(2,1)S(1)} %collective-permute-done.10.got, bf16[32,16,128]{2,1,0:T(8,128)(2,1)S(1)} %get-tuple-element.58.strip1, ...), custom_call_target="tpu_custom_call", output_to_operand_aliasing={{}: (8, {})} | custom-call | flops 1056964608 | bytes 4042752 | tf_op jit(solution)/shard_map/third_late_kernel/pallas_call | solution.py:472
  (24 shorter events, 0.4 us)
Async XLA Ops:
  0.0 7.8 %copy-start.2 = (f32[6,128,128]{2,1,0:T(8,128)S(1)}, f32[6,128,128]{2,1,0:T(8,128)}, u32[]{:S(2)}) copy-start(f32[6,128,128]{2,1,0:T(8,128)} %faces.1) | copy-start | bytes 1179652
  0.0 7.8 %copy-start.3 = (f32[128,128]{1,0:T(8,128)S(1)}, f32[128,128]{1,0:T(8,128)}, u32[]{:S(2)}) copy-start(f32[128,128]{1,0:T(8,128)} %diag.1) | copy-start | bytes 196612
  0.0 7.8 %copy-start.4 = (f32[128,128]{1,0:T(8,128)S(1)}, f32[128,128]{1,0:T(8,128)}, u32[]{:S(2)}) copy-start(f32[128,128]{1,0:T(8,128)} %coarse.1) | copy-start | bytes 196612
  3.1 6.3 %collective-permute-start = (bf16[912,128]{1,0:T(8,128)(2,1)}, bf16[912,128]{1,0:T(8,128)(2,1)S(1)}, u32[]{:S(2)}, u32[]{:S(2)}) collective-permute-start(bf16[912,128]{1,0:T(8,128)(2,1)} %get-tuple-element.35), channel_id=1, source_target_pairs={{0,1},{1,0},{2,3},{3,2},{4,5},{5,4},{6,7},{7,6},{8,9},{9,8},{10,11... | collective-permute-start | bytes 700424 | tf_op jit(solution)/shard_map/ppermute | solution.py:22
  3.2 6.2 %copy-start = (bf16[4,512,128]{2,1,0:T(8,128)(2,1)S(1)}, bf16[4,512,128]{2,1,0:T(8,128)(2,1)}, u32[]{:S(2)}) copy-start(bf16[4,512,128]{2,1,0:T(8,128)(2,1)} %get-tuple-element.33.fe) | copy-start | bytes 1572868
  3.2 6.2 %copy-start.1 = (f32[64,128]{1,0:T(8,128)S(1)}, f32[64,128]{1,0:T(8,128)}, u32[]{:S(2)}) copy-start(f32[64,128]{1,0:T(8,128)} %refs_5_.1) | copy-start | bytes 98308
  3.2 9.5 %collective-permute-start.1 = (bf16[912,128]{1,0:T(8,128)(2,1)}, bf16[912,128]{1,0:T(8,128)(2,1)S(1)}, u32[]{:S(2)}, u32[]{:S(2)}) collective-permute-start(bf16[912,128]{1,0:T(8,128)(2,1)} %get-tuple-element.36), channel_id=1, source_target_pairs={{1,2},{2,1},{5,6},{6,5},{9,10},{10,9},{13,14},{14,13},{17,18},{18,... | collective-permute-start | bytes 700424 | tf_op jit(solution)/shard_map/ppermute | solution.py:22
  9.4 0.7 %copy-start.5 = (bf16[16,128]{1,0:T(8,128)(2,1)S(1)}, bf16[16,128]{1,0:T(8,128)(2,1)}, u32[]{:S(2)}) copy-start(bf16[16,128]{1,0:T(8,128)(2,1)} %get-tuple-element.34.tab) | copy-start | bytes 12292
  15.8 9.4 %collective-permute-start.4 = (f32[64,128]{1,0:T(8,128)S(1)}, f32[64,128]{1,0:T(8,128)S(1)}, u32[]{:S(2)}, u32[]{:S(2)}) collective-permute-start(f32[64,128]{1,0:T(8,128)S(1)} %get-tuple-element.43), channel_id=1, source_target_pairs={{0,12},{1,13},{2,14},{3,15},{16,28},{17,29},{18,30},{19,31}} | collective-permute-start | bytes 98312 | tf_op jit(solution)/shard_map/ppermute | solution.py:28
  21.0 4.2 %collective-permute-start.3 = (f32[64,128]{1,0:T(8,128)S(1)}, f32[64,128]{1,0:T(8,128)S(1)}, u32[]{:S(2)}, u32[]{:S(2)}) collective-permute-start(f32[64,128]{1,0:T(8,128)S(1)} %get-tuple-element.43), channel_id=1, source_target_pairs={{0,8},{4,12},{1,9},{5,13},{2,10},{6,14},{3,11},{7,15},{16,24},{20,... | collective-permute-start | bytes 98312 | tf_op jit(solution)/shard_map/ppermute | solution.py:28
  22.3 3.2 %collective-permute-start.2 = (f32[64,128]{1,0:T(8,128)S(1)}, f32[64,128]{1,0:T(8,128)S(1)}, u32[]{:S(2)}, u32[]{:S(2)}) collective-permute-start(f32[64,128]{1,0:T(8,128)S(1)} %get-tuple-element.43), channel_id=1, source_target_pairs={{0,4},{4,8},{8,12},{1,5},{5,9},{9,13},{2,6},{6,10},{10,14},{3,7},{... | collective-permute-start | bytes 98312 | tf_op jit(solution)/shard_map/ppermute | solution.py:28
  26.1 3.9 %collective-permute-start.6 = (bf16[64,16,128]{2,1,0:T(8,128)(2,1)S(1)}, bf16[64,16,128]{2,1,0:T(8,128)(2,1)S(1)}, u32[]{:S(2)}, u32[]{:S(2)}) collective-permute-start(bf16[64,16,128]{2,1,0:T(8,128)(2,1)S(1)} %enter_first_kernel.1.own.refs_4_), channel_id=1, source_target_pairs={{0,1},{1,0},{2,3},{3,2},{4,5},{5,4},{6,7},{7,6},{8,9},{9,8},{10,11... | collective-permute-start | bytes 786440 | tf_op jit(solution)/shard_map/ppermute | solution.py:22
  26.2 7.9 %collective-permute-start.5 = (bf16[64,16,128]{2,1,0:T(8,128)(2,1)S(1)}, bf16[64,16,128]{2,1,0:T(8,128)(2,1)S(1)}, u32[]{:S(2)}, u32[]{:S(2)}) collective-permute-start(bf16[64,16,128]{2,1,0:T(8,128)(2,1)S(1)} %enter_first_kernel.1.own.refs_4_), channel_id=1, source_target_pairs={{1,2},{2,1},{5,6},{6,5},{9,10},{10,9},{13,14},{14,13},{17,18},{18,... | collective-permute-start | bytes 786440 | tf_op jit(solution)/shard_map/ppermute | solution.py:22
  37.9 7.2 %collective-permute-start.9 = (f32[64,128]{1,0:T(8,128)S(1)}, f32[64,128]{1,0:T(8,128)S(1)}, u32[]{:S(2)}, u32[]{:S(2)}) collective-permute-start(f32[64,128]{1,0:T(8,128)S(1)} %get-tuple-element.50), channel_id=1, source_target_pairs={{0,12},{1,13},{2,14},{3,15},{16,28},{17,29},{18,30},{19,31}} | collective-permute-start | bytes 98312 | tf_op jit(solution)/shard_map/ppermute | solution.py:28
  40.7 4.4 %collective-permute-start.8 = (f32[64,128]{1,0:T(8,128)S(1)}, f32[64,128]{1,0:T(8,128)S(1)}, u32[]{:S(2)}, u32[]{:S(2)}) collective-permute-start(f32[64,128]{1,0:T(8,128)S(1)} %get-tuple-element.50), channel_id=1, source_target_pairs={{0,8},{4,12},{1,9},{5,13},{2,10},{6,14},{3,11},{7,15},{16,24},{20,... | collective-permute-start | bytes 98312 | tf_op jit(solution)/shard_map/ppermute | solution.py:28
  42.0 3.2 %collective-permute-start.7 = (f32[64,128]{1,0:T(8,128)S(1)}, f32[64,128]{1,0:T(8,128)S(1)}, u32[]{:S(2)}, u32[]{:S(2)}) collective-permute-start(f32[64,128]{1,0:T(8,128)S(1)} %get-tuple-element.50), channel_id=1, source_target_pairs={{0,4},{4,8},{8,12},{1,5},{5,9},{9,13},{2,6},{6,10},{10,14},{3,7},{... | collective-permute-start | bytes 98312 | tf_op jit(solution)/shard_map/ppermute | solution.py:28
  45.8 4.9 %collective-permute-start.11 = (bf16[48,16,128]{2,1,0:T(8,128)(2,1)S(1)}, bf16[48,16,128]{2,1,0:T(8,128)(2,1)S(1)}, u32[]{:S(2)}, u32[]{:S(2)}) collective-permute-start(bf16[48,16,128]{2,1,0:T(8,128)(2,1)S(1)} %get-tuple-element.55), channel_id=1, source_target_pairs={{0,1},{1,0},{2,3},{3,2},{4,5},{5,4},{6,7},{7,6},{8,9},{9,8},{10,11... | collective-permute-start | bytes 589832 | tf_op jit(solution)/shard_map/ppermute | solution.py:22
  45.9 8.8 %collective-permute-start.10 = (bf16[48,16,128]{2,1,0:T(8,128)(2,1)S(1)}, bf16[48,16,128]{2,1,0:T(8,128)(2,1)S(1)}, u32[]{:S(2)}, u32[]{:S(2)}) collective-permute-start(bf16[48,16,128]{2,1,0:T(8,128)(2,1)S(1)} %get-tuple-element.54), channel_id=1, source_target_pairs={{1,2},{2,1},{5,6},{6,5},{9,10},{10,9},{13,14},{14,13},{17,18},{18,... | collective-permute-start | bytes 589832 | tf_op jit(solution)/shard_map/ppermute | solution.py:22

commit v5 on v4

--- a/solution.py
+++ b/solution.py
@@ -88,10 +88,17 @@
     return y[...].reshape(n, 8, 128)
 
 
-def apply_phi(src, idx, w, base, size):
+FIXED = {0: -1, 2: -REACH, 3: 1, 5: REACH}
+
+
+def apply_phi(src, idx, masks, w, base, size):
     cols = [src[pl.ds(base, size)].reshape(size * 16, 128)]
     for f in range(6):
-        cols.append(jnp.concatenate([src[idx[f, base + e]] for e in range(size)], axis=0))
+        if masks is not None and f in FIXED:
+            near = src[pl.ds(base + FIXED[f], size)] * masks[list(FIXED).index(f), pl.ds(base, size)]
+            cols.append(near.reshape(size * 16, 128))
+        else:
+            cols.append(jnp.concatenate([src[idx[f, base + e]] for e in range(size)], axis=0))
     return product(jnp.concatenate(cols, axis=1), w[...])
 
 
@@ -110,9 +117,11 @@
 
 
 def pack_kernel(
-    forcing, init, conn, pattern, fe, tab, pay_even, pay_odd, landed, rows, init_v, conn_v, pattern_v, offs, sems
+    forcing, init, conn, pattern, fe_out, even_out, odd_out,
+    landed, rows, init_v, conn_v, pattern_v, offs, fe, pay_even, pay_odd, sems, out_sems
 ):
     n = init_v.shape[0]
+    pitch = n + 8
     copies = [pltpu.make_async_copy(forcing.at[:, k], landed.at[k], sems.at[k]) for k in range(COARSEN)]
     small = ((conn, conn_v), (pattern, pattern_v), (init, init_v))
     copies += [pltpu.make_async_copy(src, dst, sems.at[COARSEN + i]) for i, (src, dst) in enumerate(small)]
@@ -125,7 +134,8 @@
     offs[...] = jnp.zeros_like(offs)
     offs[0:6, 0:n] = value
     offs[0:6, n : 2 * n] = value
-    tab[...] = offs[...].astype(BF16)
+    tab = offs[...].astype(BF16)
+    fe[pl.ds(COARSEN * n * 8, 16), :] = tab
     lead = init_v[...].astype(BF16)
     rest = (init_v[...] - lead.astype(F32)).astype(BF16)
     even = even_place()
@@ -133,26 +143,36 @@
     for pay in (pay_even, pay_odd):
         pay[pl.ds(at, n), :] = lead
         pay[pl.ds(at + n, n), :] = rest
-        pay[pl.ds(at + 2 * n, 16), :] = tab[...]
+        pay[pl.ds(at + 2 * n, 16), :] = tab
     at = 0
+    results = []
     for k in range(COARSEN):
         copies[k].wait()
         for i in range(8):
-            rows[pl.ds(i * n, n), :] = landed[k, i].astype(F32)
+            rows[pl.ds(i * pitch, n), :] = landed[k, i].astype(F32)
 
         def body(pair, carry, k=k):
             e = pair * 2
-            two = [rows[pl.ds(e + j, 8, stride=n), :] for j in range(2)]
-            fe[k, pl.ds(pl.multiple_of(e * 8, 16), 16), :] = jnp.concatenate(two, axis=0).astype(BF16)
+            two = [rows[pl.ds(e + j, 8, stride=pitch), :] for j in range(2)]
+            fe[pl.ds(pl.multiple_of((k * n + e) * 8, 16), 16), :] = jnp.concatenate(two, axis=0).astype(BF16)
             return carry
 
         lax.fori_loop(0, n // 2, body, 0, unroll=8)
         width = (COARSEN - 1 - k) * REACH * 8
         if width:
             for pay, right in ((pay_even, even), (pay_odd, jnp.logical_not(even))):
-                begin = pl.multiple_of(jnp.where(right, n * 8 - width, 0), 128)
-                pay[pl.ds(at, width), :] = fe[k, pl.ds(begin, width), :]
+                begin = pl.multiple_of(k * n * 8 + jnp.where(right, n * 8 - width, 0), 128)
+                pay[pl.ds(at, width), :] = fe[pl.ds(begin, width), :]
         at += width
+        if k == COARSEN - 2:
+            results.append(pltpu.make_async_copy(pay_odd, odd_out, out_sems.at[0]))
+            results.append(pltpu.make_async_copy(pay_even, even_out, out_sems.at[1]))
+            results[0].start()
+            results[1].start()
+    results.append(pltpu.make_async_copy(fe, fe_out, out_sems.at[2]))
+    results[2].start()
+    for result in results:
+        result.wait()
 
 
 def weight_kernel(diag, faces, coarse, w, pk, we):
@@ -191,7 +211,7 @@
 def put_force(dst, own, got, right, k, n):
     at = sum((COARSEN - 1 - j) * REACH * 8 for j in range(k))
     width = (COARSEN - 1 - k) * REACH * 8
-    dst[pl.ds(n * 8, n * 8), :] = own[k]
+    dst[pl.ds(n * 8, n * 8), :] = own[pl.ds(k * n * 8, n * 8), :]
     if width:
         to = 2 * n * 8 if right else n * 8 - width
         dst[pl.ds(to, width), :] = got[pl.ds(at, width), :]
@@ -201,14 +221,14 @@
     return src[pl.ds(base * 8, size * 8), :].astype(F32).reshape(size, 8, 128)
 
 
-def put_tables(tab, got_even, got_odd, idx_v, columns, square, full, n, even):
+def put_tables(fe, got_even, got_odd, idx_v, columns, square, full, n, even):
     lane = lax.broadcasted_iota(jnp.int32, (8, 128), 1)
 
     def table(ref):
         return 0.0 if ref is None else ref[pl.ds(ref.shape[0] - 16, 16), :].astype(F32)[0:8]
 
     from_even, from_odd = table(got_even), table(got_odd)
-    low = jnp.where(lane < n, from_odd if even else from_even, table(tab))
+    low = jnp.where(lane < n, from_odd if even else from_even, table(fe))
     high = jnp.where(lane < n, from_even if even else from_odd, 0.0)
     for at, offs in ((0, low), (128, high)):
         value = jnp.where(offs != 0.0, lane + at + offs.astype(jnp.int32), full)
@@ -258,12 +278,12 @@
 
 
 def first_early_kernel(
-    fe, tab, init, got, w, strip1, strip2, strip3, s1, s2, s3, force, y, i16, columns, square, idx_v, idx, sem
+    fe, init, got, w, strip1, strip2, strip3, s1, s2, s3, force, y, i16, columns, square, idx_v, idx, sem
 ):
     def body(even):
         n = init.shape[0]
         full = 3 * n
-        put_tables(tab, got, None, idx_v, columns, square, full, n, even)
+        put_tables(fe, got, None, idx_v, columns, square, full, n, even)
         copy = pltpu.make_async_copy(idx_v, idx, sem)
         copy.start()
         count = 6 * REACH
@@ -280,20 +300,20 @@
             put_force(force, fe, got, even, k, n)
             size = (6 - 2 * k) * REACH
             base = mirrored((k + 1) * REACH, size, full, even)
-            dst[pl.ds(base, size)] = split(apply_phi(src, idx, w, base, size) + force_at(force, base, size))
+            dst[pl.ds(base, size)] = split(apply_phi(src, idx, None, w, base, size) + force_at(force, base, size))
         put_strips((strip1, strip2, strip3), (s1, s2, s3), full, even)
 
     by_parity(body)
 
 
 def first_late_kernel(
-    fe, tab, init, got_even, got_odd, strip1, strip2, strip3, w, pk, w1, end, idx_out,
+    fe, init, got_even, got_odd, strip1, strip2, strip3, w, pk, w1, end, idx_out,
     s1, s2, s3, force, y, i16, columns, square, idx, sem
 ):
     def body(even):
         n = init.shape[0]
         full = 3 * n
-        put_tables(tab, got_even, got_odd, idx_out, columns, square, full, n, even)
+        put_tables(fe, got_even, got_odd, idx_out, columns, square, full, n, even)
         copy = pltpu.make_async_copy(idx_out, idx, sem)
         copy.start()
         count = 4 * REACH
@@ -308,7 +328,7 @@
         for k, src, dst in ((1, s1, s2), (2, s2, s3), (3, s3, None)):
             put_force(force, fe, got_odd, not even, k, n)
             base = mirrored((7 - k) * REACH, count, full, even)
-            value = apply_phi(src, idx, w, base, count) + force_at(force, base, count)
+            value = apply_phi(src, idx, None, w, base, count) + force_at(force, base, count)
             if dst is None:
                 w1[...] = value
                 y[...] = value.reshape(n * 8, 128)
@@ -319,8 +339,23 @@
     by_parity(body)
 
 
-def scan_kernel(values, pk, starts):
+def scan_kernel(values, pk, idx, starts, masks, square, there):
     starts[...] = scan_starts(values[...], pk)
+    full = masks.shape[1]
+    for at in range(0, full, 128):
+        square[...] = jnp.zeros_like(square)
+        square[0:8, :] = (idx[:, pl.ds(at, 128)] != full).astype(F32)
+        count = min(128, full - at)
+        turned = square[...].T
+        for m, f in enumerate(FIXED):
+            there[m, pl.ds(at, count), :] = jnp.broadcast_to(turned[:count, f : f + 1], (count, 128))
+
+    def body(e, carry):
+        for m in range(len(FIXED)):
+            masks[m, e] = jnp.broadcast_to(there[m, pl.ds(e, 1), :], (16, 128)).astype(BF16)
+        return carry
+
+    lax.fori_loop(REACH, full - REACH, body, 0, unroll=8)
 
 
 def scan_sum_kernel(values, w1, coarse, pk, starts, total):
@@ -357,7 +392,7 @@
     dst[3 * n] = jnp.zeros((16, 128), BF16)
 
 
-def second_early_kernel(idx, own, got, w, pk, strip1, strip2, strip3, coarse, s0, s1, s2, s3):
+def second_early_kernel(idx, own, got, masks, w, pk, strip1, strip2, strip3, coarse, s0, s1, s2, s3):
     def body(even):
         n = own.shape[0]
         full = 3 * n
@@ -368,13 +403,13 @@
         for k, src, dst in ((1, s0, s1), (2, s1, s2), (3, s2, s3)):
             size = (8 - 2 * k) * REACH
             base = mirrored(k * REACH, size, full, even)
-            dst[pl.ds(base, size)] = split(apply_phi(src, idx, w, base, size))
+            dst[pl.ds(base, size)] = split(apply_phi(src, idx, masks, w, base, size))
         put_strips((strip1, strip2, strip3), (s1, s2, s3), full, even)
 
     by_parity(body)
 
 
-def second_late_kernel(idx, own, got, strip1, strip2, strip3, coarse, w, pk, res, end, s0, s1, s2, s3, y):
+def second_late_kernel(idx, own, got, strip1, strip2, strip3, coarse, masks, w, pk, res, end, s0, s1, s2, s3, y):
     def body(even):
         n = own.shape[0]
         full = 3 * n
@@ -383,8 +418,8 @@
         count = 4 * REACH
         for k, src, dst in ((1, s0, s1), (2, s1, s2), (3, s2, s3)):
             base = mirrored((8 - k) * REACH, count, full, even)
-            dst[pl.ds(base, count)] = split(apply_phi(src, idx, w, base, count))
-        value = apply_phi(s3, idx, w, n, n)
+            dst[pl.ds(base, count)] = split(apply_phi(src, idx, masks, w, base, count))
+        value = apply_phi(s3, idx, masks, w, n, n)
         value = value - coarse[...]
         res[...] = value
         y[...] = value.reshape(n * 8, 128)
@@ -395,11 +430,12 @@
 
 def write_out(out, k, value, begin, flip, sems):
     size = value.shape[0]
+    pitch = size + 8
     for e in range(size):
-        flip[pl.ds(e, 8, stride=size), :] = value[e]
+        flip[pl.ds(e, 8, stride=pitch), :] = value[e]
     rows = pl.ds(begin, size)
     copies = [
-        pltpu.make_async_copy(flip.at[pl.ds(i * size, size)], out.at[i * COARSEN + k, rows], sems.at[k, i])
+        pltpu.make_async_copy(flip.at[pl.ds(i * pitch, size)], out.at[i * COARSEN + k, rows], sems.at[k, i])
         for i in range(8)
     ]
     for copy in copies:
@@ -408,7 +444,7 @@
 
 
 def third_early_kernel(
-    idx, own, got, corr, total, fe, pay, w, pk, out, strip1, strip2, s0, s1, s2, force, flip0, flip1, flip2, flip3, sems
+    idx, own, got, corr, total, fe, pay, masks, w, pk, out, strip1, strip2, s0, s1, s2, force, flip0, flip1, flip2, flip3, sems
 ):
     def body(even):
         n = own.shape[0]
@@ -422,7 +458,7 @@
             put_force(force, fe, pay, even, k, n)
             size = (5 - 2 * k) * REACH
             base = mirrored((2 + k) * REACH, size, full, even)
-            value = apply_phi(src, idx, w, base, size) + force_at(force, base, size)
+            value = apply_phi(src, idx, masks, w, base, size) + force_at(force, base, size)
             if dst is not None:
                 dst[pl.ds(base, size)] = split(value)
             mine = (3 - k) * REACH
@@ -437,7 +473,7 @@
 
 
 def third_late_kernel(
-    idx, own, got, strip1, strip2, fe, pay, w, partial, out, s0, s1, s2, force, flip0, flip1, flip2, sems
+    idx, own, got, strip1, strip2, fe, pay, masks, w, partial, out, s0, s1, s2, force, flip0, flip1, flip2, sems
 ):
     def body(even):
         n = own.shape[0]
@@ -449,7 +485,7 @@
         for k, src, dst, flip in ((0, s0, s1, flip0), (1, s1, s2, flip1), (2, s2, None, flip2)):
             put_force(force, fe, pay, not even, k, n)
             base = mirrored((7 - k) * REACH, size, full, even)
-            value = apply_phi(src, idx, w, base, size) + force_at(force, base, size)
+            value = apply_phi(src, idx, masks, w, base, size) + force_at(force, base, size)
             if dst is not None:
                 dst[pl.ds(base, size)] = split(value)
             mine = (k + 1) * REACH
@@ -496,20 +532,26 @@
     step_flops = 2 * 16 * 7 * width * 2 * width
     pay_rows = sum((COARSEN - 1 - k) * REACH * 8 for k in range(COARSEN)) + 2 * n + 16
     pay = shape((pay_rows, width), BF16)
-    fe, tab, pay_even, pay_odd = call(
+    all_force = ((COARSEN * n * 8 + 16), width)
+    fe, pay_even, pay_odd = call(
         pack_kernel,
         (forcing.reshape(steps // COARSEN, COARSEN, n, width), initial_state, connectivity.T, pattern.T),
-        (shape((COARSEN, n * 8, width), BF16), shape((16, 128), BF16), pay, pay),
+        (shape(all_force, BF16), pay, pay),
         [
             vmem((COARSEN, 8, n, width), BF16),
-            vmem((8 * n, width), F32),
+            vmem((8 * (n + 8), width), F32),
             vmem((n, width), F32),
             vmem((6, n), jnp.int32),
             vmem((6, n), jnp.int32),
             vmem((16, 128), F32),
+            vmem(all_force, BF16),
+            vmem((pay_rows, width), BF16),
+            vmem((pay_rows, width), BF16),
             dma((COARSEN + 3,)),
+            dma((3,)),
         ],
         spaces="hhhh",
+        out_spaces="hhh",
         room=62,
     )
     pay_odd, pay_even = swapped(pay_odd, 1), swapped(pay_even, 0)
@@ -532,25 +574,30 @@
     smem = pltpu.SMEM((8, 256), jnp.int32)
     strips = call(
         first_early_kernel,
-        (fe, tab, initial_state, pay_even, w),
+        (fe, initial_state, pay_even, w),
         (strip, strip, strip),
         [spaces] * 3 + [force, vmem((6 * REACH * 8, width), F32)] + tables + [vmem((8, 256), jnp.int32), smem, dma],
         flops=step_flops * 6 * REACH,
     )
     w1, end, idx = call(
         first_late_kernel,
-        (fe, tab, initial_state, pay_even, pay_odd, *strips, w, pk),
+        (fe, initial_state, pay_even, pay_odd, *strips, w, pk),
         (tiles, ends, shape((8, 256), jnp.int32)),
         [spaces] * 3 + [force, rows] + tables + [smem, dma],
         flops=step_flops * 12 * REACH,
     )
     arrivals = earlier(end)
-    (starts,) = call(scan_kernel, (w1, pk), (tiles,), [])
+    starts, masks = call(
+        scan_kernel,
+        (w1, pk, idx),
+        (tiles, shape((len(FIXED), full, 16, width), BF16)),
+        [vmem((128, 128), F32), vmem((len(FIXED), full, width), F32)],
+    )
     (coarse,) = call(enter_first_kernel, (*arrivals, starts, we, pk), (state,), [rows])
     got_odd, got_even = swapped(coarse, 1), swapped(coarse, 0)
     *strips, moved = call(
         second_early_kernel,
-        (idx, coarse, got_even, w, pk),
+        (idx, coarse, got_even, masks, w, pk),
         (strip, strip, strip, tiles),
         [spaces] * 4,
         spaces="s",
@@ -558,7 +605,7 @@
     )
     res, end = call(
         second_late_kernel,
-        (idx, coarse, got_odd, *strips, moved, w, pk),
+        (idx, coarse, got_odd, *strips, moved, masks, w, pk),
         (tiles, ends),
         [spaces] * 4 + [rows],
         spaces="s",
@@ -575,24 +622,24 @@
     )
     got_odd, got_even = swapped(end_odd, 1), swapped(end_even, 0)
     result = shape((steps, n, width), F32)
-    flips = [vmem((8 * m * REACH, width), F32) for m in (3, 2, 1)]
+    flips = [vmem((8 * (m * REACH + 8), width), F32) for m in (3, 2, 1)]
     out, *strips = call(
         third_early_kernel,
-        (idx, coarse, got_even, corr, total, fe, pay_even, w, pk),
+        (idx, coarse, got_even, corr, total, fe, pay_even, masks, w, pk),
         (result, strip, strip),
-        [spaces] * 3 + [force] + flips + [rows, dma((COARSEN, 8))],
+        [spaces] * 3 + [force] + flips + [vmem((8 * (n + 8), width), F32), dma((COARSEN, 8))],
         spaces="s",
         out_spaces="h",
         flops=step_flops * 9 * REACH,
     )
     (out,) = call(
         third_late_kernel,
-        (idx, coarse, got_odd, *strips, fe, pay_odd, w, out),
+        (idx, coarse, got_odd, *strips, fe, pay_odd, masks, w, out),
         (result,),
         [spaces] * 3 + [force] + flips[::-1] + [dma((COARSEN - 1, 8))],
-        spaces="svvvvvvvh",
+        spaces="svvvvvvvvh",
         out_spaces="h",
-        aliases={8: 0},
+        aliases={9: 0},
         flops=step_flops * 9 * REACH,
     )
     return out

time: 58.6 us -> 59.6 us (1.017)
  local copies, waits for them, and re-layouts: 0.66 us -> 2.68 us
  starting transfers between devices: 28.7 us -> 27 us
    unnamed x12 -> x10, local copies, waits for them, and re-layouts: 0.66 us -> 2.68 us
    ppermute x6, starting transfers between devices: 13.5 us -> 12 us  [swapped(): return lax.ppermute(value, 'space', pairs)]
    ppermute x6, waiting for transfers between devices: 0.59 us -> 1.22 us  [swapped(): return lax.ppermute(value, 'space', pairs)]
  transfers between devices with their start and end apart: 12 -> 12, of which waited for: 3 -> 2; matrix products, arithmetic and copies ran while one was open for 0% -> 0% of each run, Pallas kernels for 22% -> 23%
where the time goes in v5:
time: 59.6 us; the launch traced here: 59.2 us
  Pallas kernels  27.5 us (46%)
  starting transfers between devices  27 us (45%)
  local copies, waits for them, and re-layouts  2.68 us (4%)
  waiting for transfers between devices  1.51 us (3%)
    pallas_call x12, Pallas kernels, call(): pl.pallas_call(kernel, out_shape=outs, name=kernel.__name__, in_specs=spe...  27.5 us
    ppermute x6, starting transfers between devices, earlier(): lax.ppermute(value, 'tm', [(i, i + s) for i in range(count - s)])  15.1 us
    ppermute x6, starting transfers between devices, swapped(): return lax.ppermute(value, 'space', pairs)  12 us
    unnamed x10, local copies, waits for them, and re-layouts  2.68 us
    ppermute x6, waiting for transfers between devices, swapped(): return lax.ppermute(value, 'space', pairs)  1.22 us
  transfers between devices with their start and end apart: 12, of which 2 were waited for; matrix products, arithmetic and copies ran while one was open for 0% of the time, Pallas kernels for 23%

profile of v5, /device:TPU:1, one launch (start us, length us, event | category | flops | bytes accessed | tf_op | source)
XLA Modules:
  0.0 59.2 jit_solution(12216626151998097336)
XLA Ops:
  0.0 2.5 %pack_kernel.1 = (bf16[2064,128]{1,0:T(8,128)(2,1)}, bf16[912,128]{1,0:T(8,128)(2,1)}, bf16[912,128]{1,0:T(8,128)(2,1)}) custom-call(bf16[8,4,64,128]{3,2,1,0:T(8,128)(2,1)} %bitcast.3, f32[64,128]{1,0:T(8,128)} %refs_5_.1, s32[6,64]{1,0:T(8,128)} %bitcast.4, s32[6,64]{1,0:T(8,128)} %bitcast.5), custom_call_target="tpu_custom_call" | custom-call | flops 10000000 | bytes 1555456 | tf_op jit(solution)/shard_map/pack_kernel/pallas_call | solution.py:508
  2.6 4.6 %collective-permute-start.1 = (bf16[912,128]{1,0:T(8,128)(2,1)}, bf16[912,128]{1,0:T(8,128)(2,1)S(1)}, u32[]{:S(2)}, u32[]{:S(2)}) collective-permute-start(bf16[912,128]{1,0:T(8,128)(2,1)} %get-tuple-element.36), channel_id=1, source_target_pairs={{1,2},{2,1},{5,6},{6,5},{9,10},{10,9},{13,14},{14,13},{17,18},{18,... | collective-permute-start | bytes 700424 | tf_op jit(solution)/shard_map/ppermute | solution.py:22
  7.2 1.0 %copy-done.2 = f32[6,128,128]{2,1,0:T(8,128)S(1)} copy-done((f32[6,128,128]{2,1,0:T(8,128)S(1)}, f32[6,128,128]{2,1,0:T(8,128)}, u32[]{:S(2)}) %copy-start.2) | copy-done | bytes 393240
  8.2 0.8 %copy-done.3 = f32[128,128]{1,0:T(8,128)S(1)} copy-done((f32[128,128]{1,0:T(8,128)S(1)}, f32[128,128]{1,0:T(8,128)}, u32[]{:S(2)}) %copy-start.3) | copy-done | bytes 65560
  9.1 0.8 %copy-done.4 = f32[128,128]{1,0:T(8,128)S(1)} copy-done((f32[128,128]{1,0:T(8,128)S(1)}, f32[128,128]{1,0:T(8,128)}, u32[]{:S(2)}) %copy-start.4) | copy-done | bytes 65560
  9.9 1.5 %weight_kernel.1 = (bf16[896,256]{1,0:T(8,128)(2,1)S(1)}, bf16[1024,256]{1,0:T(8,128)(2,1)S(1)}, bf16[384,256]{1,0:T(8,128)(2,1)S(1)}) custom-call(f32[128,128]{1,0:T(8,128)S(1)} %copy-done.3, f32[6,128,128]{2,1,0:T(8,128)S(1)} %copy-done.2, f32[128,128]{1,0:T(8,128)S(1)} %copy-done.4), custom_call_target="tpu_custom_call" | custom-call | flops 1000000000 | bytes 1703936 | tf_op jit(solution)/shard_map/weight_kernel/pallas_call | solution.py:508
  11.5 2.6 %first_early_kernel.1 = (bf16[32,16,128]{2,1,0:T(8,128)(2,1)S(1)}, bf16[32,16,128]{2,1,0:T(8,128)(2,1)S(1)}, bf16[32,16,128]{2,1,0:T(8,128)(2,1)S(1)}) custom-call(bf16[2064,128]{1,0:T(8,128)(2,1)S(1)} %copy-done, f32[64,128]{1,0:T(8,128)S(1)} %copy-done.1, bf16[912,128]{1,0:T(8,128)(2,1)S(1)} %collective-permute-done.got.got_even.pay, ...), custom_call_target="tpu_custom_call" | custom-call | flops 704643072 | bytes 1646592 | tf_op jit(solution)/shard_map/first_early_kernel/pallas_call | solution.py:508
  14.1 3.1 %first_late_kernel.1 = (f32[64,8,128]{2,1,0:T(8,128)S(1)}, f32[64,128]{1,0:T(8,128)S(1)}, s32[8,256]{1,0:T(8,128)S(1)}) custom-call(bf16[2064,128]{1,0:T(8,128)(2,1)S(1)} %copy-done, f32[64,128]{1,0:T(8,128)S(1)} %copy-done.1, bf16[912,128]{1,0:T(8,128)(2,1)S(1)} %collective-permute-done.got.got_even.pay, ...), custom_call_target="tpu_custom_call" | custom-call | flops 1409286144 | bytes 2707456 | tf_op jit(solution)/shard_map/first_late_kernel/pallas_call | solution.py:508
  17.2 5.2 %collective-permute-start.4 = (f32[64,128]{1,0:T(8,128)S(1)}, f32[64,128]{1,0:T(8,128)S(1)}, u32[]{:S(2)}, u32[]{:S(2)}) collective-permute-start(f32[64,128]{1,0:T(8,128)S(1)} %get-tuple-element.43), channel_id=1, source_target_pairs={{0,12},{1,13},{2,14},{3,15},{16,28},{17,29},{18,30},{19,31}} | collective-permute-start | bytes 98312 | tf_op jit(solution)/shard_map/ppermute | solution.py:28
  22.5 1.3 %collective-permute-start.3 = (f32[64,128]{1,0:T(8,128)S(1)}, f32[64,128]{1,0:T(8,128)S(1)}, u32[]{:S(2)}, u32[]{:S(2)}) collective-permute-start(f32[64,128]{1,0:T(8,128)S(1)} %get-tuple-element.43), channel_id=1, source_target_pairs={{0,8},{4,12},{1,9},{5,13},{2,10},{6,14},{3,11},{7,15},{16,24},{20,... | collective-permute-start | bytes 98312 | tf_op jit(solution)/shard_map/ppermute | solution.py:28
  23.8 2.2 %collective-permute-start.2 = (f32[64,128]{1,0:T(8,128)S(1)}, f32[64,128]{1,0:T(8,128)S(1)}, u32[]{:S(2)}, u32[]{:S(2)}) collective-permute-start(f32[64,128]{1,0:T(8,128)S(1)} %get-tuple-element.43), channel_id=1, source_target_pairs={{0,4},{4,8},{8,12},{1,5},{5,9},{9,13},{2,6},{6,10},{10,14},{3,7},{... | collective-permute-start | bytes 98312 | tf_op jit(solution)/shard_map/ppermute | solution.py:28
  26.0 1.0 %scan_kernel.1 = (f32[64,8,128]{2,1,0:T(8,128)S(1)}, bf16[4,192,16,128]{3,2,1,0:T(8,128)(2,1)S(1)}) custom-call(f32[64,8,128]{2,1,0:T(8,128)S(1)} %get-tuple-element.44.values.w1, bf16[1024,256]{1,0:T(8,128)(2,1)S(1)} %get-tuple-element.41.pk.refs_5_.refs_7_, s32[8,256]{1,0:T(8,128)S(1)} %get-tuple-element.42.idx), custom_call_target="tpu_custom_call" | custom-call | flops 10000000 | bytes 4202496 | tf_op jit(solution)/shard_map/scan_kernel/pallas_call | solution.py:508
  27.6 3.0 %collective-permute-start.5 = (bf16[64,16,128]{2,1,0:T(8,128)(2,1)S(1)}, bf16[64,16,128]{2,1,0:T(8,128)(2,1)S(1)}, u32[]{:S(2)}, u32[]{:S(2)}) collective-permute-start(bf16[64,16,128]{2,1,0:T(8,128)(2,1)S(1)} %enter_first_kernel.1.own.refs_4_), channel_id=1, source_target_pairs={{1,2},{2,1},{5,6},{6,5},{9,10},{10,9},{13,14},{14,13},{17,18},{18,... | collective-permute-start | bytes 786440 | tf_op jit(solution)/shard_map/ppermute | solution.py:22
  30.6 3.5 %second_early_kernel.1 = (bf16[32,16,128]{2,1,0:T(8,128)(2,1)S(1)}, bf16[32,16,128]{2,1,0:T(8,128)(2,1)S(1)}, bf16[32,16,128]{2,1,0:T(8,128)(2,1)S(1)}, f32[64,8,128]{2,1,0:T(8,128)S(1)}) custom-call(s32[8,256]{1,0:T(8,128)S(1)} %get-tuple-element.42.idx, bf16[64,16,128]{2,1,0:T(8,128)(2,1)S(1)} %enter_first_kernel.1.own.refs_4_, ...), custom_call_target="tpu_custom_call" | custom-call | flops 1409286144 | bytes 5316608 | tf_op jit(solution)/shard_map/second_early_kernel/pallas_call | solution.py:508
  34.1 1.2 %collective-permute-done.5.got = bf16[64,16,128]{2,1,0:T(8,128)(2,1)S(1)} collective-permute-done((bf16[64,16,128]{2,1,0:T(8,128)(2,1)S(1)}, bf16[64,16,128]{2,1,0:T(8,128)(2,1)S(1)}, u32[]{:S(2)}, u32[]{:S(2)}) %collective-permute-start.5) | collective-permute-done | bytes 262176 | tf_op jit(solution)/shard_map/ppermute | solution.py:22
  35.3 4.0 %second_late_kernel.1 = (f32[64,8,128]{2,1,0:T(8,128)S(1)}, f32[64,128]{1,0:T(8,128)S(1)}) custom-call(s32[8,256]{1,0:T(8,128)S(1)} %get-tuple-element.42.idx, bf16[64,16,128]{2,1,0:T(8,128)(2,1)S(1)} %enter_first_kernel.1.own.refs_4_, bf16[64,16,128]{2,1,0:T(8,128)(2,1)S(1)} %collective-permute-done.5.got, ...), custom_call_target="tpu_custom_call" | custom-call | flops 1879048192 | bytes 5611520 | tf_op jit(solution)/shard_map/second_late_kernel/pallas_call | solution.py:508
  39.4 2.9 %collective-permute-start.9 = (f32[64,128]{1,0:T(8,128)S(1)}, f32[64,128]{1,0:T(8,128)S(1)}, u32[]{:S(2)}, u32[]{:S(2)}) collective-permute-start(f32[64,128]{1,0:T(8,128)S(1)} %get-tuple-element.52), channel_id=1, source_target_pairs={{0,12},{1,13},{2,14},{3,15},{16,28},{17,29},{18,30},{19,31}} | collective-permute-start | bytes 98312 | tf_op jit(solution)/shard_map/ppermute | solution.py:28
  42.3 1.3 %collective-permute-start.8 = (f32[64,128]{1,0:T(8,128)S(1)}, f32[64,128]{1,0:T(8,128)S(1)}, u32[]{:S(2)}, u32[]{:S(2)}) collective-permute-start(f32[64,128]{1,0:T(8,128)S(1)} %get-tuple-element.52), channel_id=1, source_target_pairs={{0,8},{4,12},{1,9},{5,13},{2,10},{6,14},{3,11},{7,15},{16,24},{20,... | collective-permute-start | bytes 98312 | tf_op jit(solution)/shard_map/ppermute | solution.py:28
  43.6 2.2 %collective-permute-start.7 = (f32[64,128]{1,0:T(8,128)S(1)}, f32[64,128]{1,0:T(8,128)S(1)}, u32[]{:S(2)}, u32[]{:S(2)}) collective-permute-start(f32[64,128]{1,0:T(8,128)S(1)} %get-tuple-element.52), channel_id=1, source_target_pairs={{0,4},{4,8},{8,12},{1,5},{5,9},{9,13},{2,6},{6,10},{10,14},{3,7},{... | collective-permute-start | bytes 98312 | tf_op jit(solution)/shard_map/ppermute | solution.py:28
  45.8 0.7 %scan_sum_kernel.1 = (f32[64,8,128]{2,1,0:T(8,128)S(1)}, f32[64,8,128]{2,1,0:T(8,128)S(1)}) custom-call(f32[64,8,128]{2,1,0:T(8,128)S(1)} %get-tuple-element.53.values, f32[64,8,128]{2,1,0:T(8,128)S(1)} %get-tuple-element.44.values.w1, f32[64,8,128]{2,1,0:T(8,128)S(1)} %get-tuple-element.51.coarse, bf16[1024,256]{1,0:T(8,128)(2,1)S(1)} %get-tuple-element.41.pk.refs_5_.refs_7_), custom_call_target="tpu_custom_call" | custom-call | flops 10000000 | bytes 1835008 | tf_op jit(solution)/shard_map/scan_sum_kernel/pallas_call | solution.py:508
  46.8 0.6 %enter_second_kernel.1 = (bf16[64,16,128]{2,1,0:T(8,128)(2,1)S(1)}, bf16[48,16,128]{2,1,0:T(8,128)(2,1)S(1)}, bf16[48,16,128]{2,1,0:T(8,128)(2,1)S(1)}, f32[64,8,128]{2,1,0:T(8,128)S(1)}) custom-call(f32[64,128]{1,0:T(8,128)S(1)} %collective-permute-done.7.refs_0_, f32[64,128]{1,0:T(8,128)S(1)} %collective-permute-done.8.refs_1_, ...), custom_call_target="tpu_custom_call" | custom-call | flops 10000000 | bytes 2293760 | tf_op jit(solution)/shard_map/enter_second_kernel/pallas_call | solution.py:508
  47.5 4.1 %collective-permute-start.10 = (bf16[48,16,128]{2,1,0:T(8,128)(2,1)S(1)}, bf16[48,16,128]{2,1,0:T(8,128)(2,1)S(1)}, u32[]{:S(2)}, u32[]{:S(2)}) collective-permute-start(bf16[48,16,128]{2,1,0:T(8,128)(2,1)S(1)} %get-tuple-element.56), channel_id=1, source_target_pairs={{1,2},{2,1},{5,6},{6,5},{9,10},{10,9},{13,14},{14,13},{17,18},{18,... | collective-permute-start | bytes 589832 | tf_op jit(solution)/shard_map/ppermute | solution.py:22
  51.6 4.0 %third_early_kernel.1 = (f32[32,64,128]{2,1,0:T(8,128)}, bf16[32,16,128]{2,1,0:T(8,128)(2,1)S(1)}, bf16[32,16,128]{2,1,0:T(8,128)(2,1)S(1)}) custom-call(s32[8,256]{1,0:T(8,128)S(1)} %get-tuple-element.42.idx, bf16[64,16,128]{2,1,0:T(8,128)(2,1)S(1)} %get-tuple-element.55.own, bf16[48,16,128]{2,1,0:T(8,128)(2,1)S(1)} %collective-permute-done.11.got, ...), custom_call_target="tpu_custom_call" | custom-call | flops 1056964608 | bytes 7192576 | tf_op jit(solution)/shard_map/third_early_kernel/pallas_call | solution.py:508
  55.6 3.4 %third_late_kernel.1 = f32[32,64,128]{2,1,0:T(8,128)} custom-call(s32[8,256]{1,0:T(8,128)S(1)} %get-tuple-element.42.idx, bf16[64,16,128]{2,1,0:T(8,128)(2,1)S(1)} %get-tuple-element.55.own, bf16[48,16,128]{2,1,0:T(8,128)(2,1)S(1)} %collective-permute-done.10.got, bf16[32,16,128]{2,1,0:T(8,128)(2,1)S(1)} %get-tuple-element.60.strip1, ...), custom_call_target="tpu_custom_call", output_to_operand_aliasing={{}: (9, {})} | custom-call | flops 1056964608 | bytes 7192576 | tf_op jit(solution)/shard_map/third_late_kernel/pallas_call | solution.py:508
  (22 shorter events, 1.1 us)
Async XLA Ops:
  0.0 11.5 %copy-start.1 = (f32[64,128]{1,0:T(8,128)S(1)}, f32[64,128]{1,0:T(8,128)}, u32[]{:S(2)}) copy-start(f32[64,128]{1,0:T(8,128)} %refs_5_.1) | copy-start | bytes 98308
  2.5 9.0 %copy-start = (bf16[2064,128]{1,0:T(8,128)(2,1)S(1)}, bf16[2064,128]{1,0:T(8,128)(2,1)}, u32[]{:S(2)}) copy-start(bf16[2064,128]{1,0:T(8,128)(2,1)} %get-tuple-element.34.fe) | copy-start | bytes 1585156
  2.5 9.0 %collective-permute-start = (bf16[912,128]{1,0:T(8,128)(2,1)}, bf16[912,128]{1,0:T(8,128)(2,1)S(1)}, u32[]{:S(2)}, u32[]{:S(2)}) collective-permute-start(bf16[912,128]{1,0:T(8,128)(2,1)} %get-tuple-element.35), channel_id=1, source_target_pairs={{0,1},{1,0},{2,3},{3,2},{4,5},{5,4},{6,7},{7,6},{8,9},{9,8},{10,11... | collective-permute-start | bytes 700424 | tf_op jit(solution)/shard_map/ppermute | solution.py:22
  2.6 11.4 %collective-permute-start.1 = (bf16[912,128]{1,0:T(8,128)(2,1)}, bf16[912,128]{1,0:T(8,128)(2,1)S(1)}, u32[]{:S(2)}, u32[]{:S(2)}) collective-permute-start(bf16[912,128]{1,0:T(8,128)(2,1)} %get-tuple-element.36), channel_id=1, source_target_pairs={{1,2},{2,1},{5,6},{6,5},{9,10},{10,9},{13,14},{14,13},{17,18},{18,... | collective-permute-start | bytes 700424 | tf_op jit(solution)/shard_map/ppermute | solution.py:22
  7.2 1.0 %copy-start.2 = (f32[6,128,128]{2,1,0:T(8,128)S(1)}, f32[6,128,128]{2,1,0:T(8,128)}, u32[]{:S(2)}) copy-start(f32[6,128,128]{2,1,0:T(8,128)} %faces.1) | copy-start | bytes 1179652
  8.2 0.8 %copy-start.3 = (f32[128,128]{1,0:T(8,128)S(1)}, f32[128,128]{1,0:T(8,128)}, u32[]{:S(2)}) copy-start(f32[128,128]{1,0:T(8,128)} %diag.1) | copy-start | bytes 196612
  9.1 0.8 %copy-start.4 = (f32[128,128]{1,0:T(8,128)S(1)}, f32[128,128]{1,0:T(8,128)}, u32[]{:S(2)}) copy-start(f32[128,128]{1,0:T(8,128)} %coarse.1) | copy-start | bytes 196612
  17.2 9.7 %collective-permute-start.4 = (f32[64,128]{1,0:T(8,128)S(1)}, f32[64,128]{1,0:T(8,128)S(1)}, u32[]{:S(2)}, u32[]{:S(2)}) collective-permute-start(f32[64,128]{1,0:T(8,128)S(1)} %get-tuple-element.43), channel_id=1, source_target_pairs={{0,12},{1,13},{2,14},{3,15},{16,28},{17,29},{18,30},{19,31}} | collective-permute-start | bytes 98312 | tf_op jit(solution)/shard_map/ppermute | solution.py:28
  22.5 4.5 %collective-permute-start.3 = (f32[64,128]{1,0:T(8,128)S(1)}, f32[64,128]{1,0:T(8,128)S(1)}, u32[]{:S(2)}, u32[]{:S(2)}) collective-permute-start(f32[64,128]{1,0:T(8,128)S(1)} %get-tuple-element.43), channel_id=1, source_target_pairs={{0,8},{4,12},{1,9},{5,13},{2,10},{6,14},{3,11},{7,15},{16,24},{20,... | collective-permute-start | bytes 98312 | tf_op jit(solution)/shard_map/ppermute | solution.py:28
  23.8 3.2 %collective-permute-start.2 = (f32[64,128]{1,0:T(8,128)S(1)}, f32[64,128]{1,0:T(8,128)S(1)}, u32[]{:S(2)}, u32[]{:S(2)}) collective-permute-start(f32[64,128]{1,0:T(8,128)S(1)} %get-tuple-element.43), channel_id=1, source_target_pairs={{0,4},{4,8},{8,12},{1,5},{5,9},{9,13},{2,6},{6,10},{10,14},{3,7},{... | collective-permute-start | bytes 98312 | tf_op jit(solution)/shard_map/ppermute | solution.py:28
  27.6 3.1 %collective-permute-start.6 = (bf16[64,16,128]{2,1,0:T(8,128)(2,1)S(1)}, bf16[64,16,128]{2,1,0:T(8,128)(2,1)S(1)}, u32[]{:S(2)}, u32[]{:S(2)}) collective-permute-start(bf16[64,16,128]{2,1,0:T(8,128)(2,1)S(1)} %enter_first_kernel.1.own.refs_4_), channel_id=1, source_target_pairs={{0,1},{1,0},{2,3},{3,2},{4,5},{5,4},{6,7},{7,6},{8,9},{9,8},{10,11... | collective-permute-start | bytes 786440 | tf_op jit(solution)/shard_map/ppermute | solution.py:22
  27.6 7.7 %collective-permute-start.5 = (bf16[64,16,128]{2,1,0:T(8,128)(2,1)S(1)}, bf16[64,16,128]{2,1,0:T(8,128)(2,1)S(1)}, u32[]{:S(2)}, u32[]{:S(2)}) collective-permute-start(bf16[64,16,128]{2,1,0:T(8,128)(2,1)S(1)} %enter_first_kernel.1.own.refs_4_), channel_id=1, source_target_pairs={{1,2},{2,1},{5,6},{6,5},{9,10},{10,9},{13,14},{14,13},{17,18},{18,... | collective-permute-start | bytes 786440 | tf_op jit(solution)/shard_map/ppermute | solution.py:22
  39.4 7.1 %collective-permute-start.9 = (f32[64,128]{1,0:T(8,128)S(1)}, f32[64,128]{1,0:T(8,128)S(1)}, u32[]{:S(2)}, u32[]{:S(2)}) collective-permute-start(f32[64,128]{1,0:T(8,128)S(1)} %get-tuple-element.52), channel_id=1, source_target_pairs={{0,12},{1,13},{2,14},{3,15},{16,28},{17,29},{18,30},{19,31}} | collective-permute-start | bytes 98312 | tf_op jit(solution)/shard_map/ppermute | solution.py:28
  42.3 4.2 %collective-permute-start.8 = (f32[64,128]{1,0:T(8,128)S(1)}, f32[64,128]{1,0:T(8,128)S(1)}, u32[]{:S(2)}, u32[]{:S(2)}) collective-permute-start(f32[64,128]{1,0:T(8,128)S(1)} %get-tuple-element.52), channel_id=1, source_target_pairs={{0,8},{4,12},{1,9},{5,13},{2,10},{6,14},{3,11},{7,15},{16,24},{20,... | collective-permute-start | bytes 98312 | tf_op jit(solution)/shard_map/ppermute | solution.py:28
  43.6 3.2 %collective-permute-start.7 = (f32[64,128]{1,0:T(8,128)S(1)}, f32[64,128]{1,0:T(8,128)S(1)}, u32[]{:S(2)}, u32[]{:S(2)}) collective-permute-start(f32[64,128]{1,0:T(8,128)S(1)} %get-tuple-element.52), channel_id=1, source_target_pairs={{0,4},{4,8},{8,12},{1,5},{5,9},{9,13},{2,6},{6,10},{10,14},{3,7},{... | collective-permute-start | bytes 98312 | tf_op jit(solution)/shard_map/ppermute | solution.py:28
  47.4 4.2 %collective-permute-start.11 = (bf16[48,16,128]{2,1,0:T(8,128)(2,1)S(1)}, bf16[48,16,128]{2,1,0:T(8,128)(2,1)S(1)}, u32[]{:S(2)}, u32[]{:S(2)}) collective-permute-start(bf16[48,16,128]{2,1,0:T(8,128)(2,1)S(1)} %get-tuple-element.57), channel_id=1, source_target_pairs={{0,1},{1,0},{2,3},{3,2},{4,5},{5,4},{6,7},{7,6},{8,9},{9,8},{10,11... | collective-permute-start | bytes 589832 | tf_op jit(solution)/shard_map/ppermute | solution.py:22
  47.5 8.2 %collective-permute-start.10 = (bf16[48,16,128]{2,1,0:T(8,128)(2,1)S(1)}, bf16[48,16,128]{2,1,0:T(8,128)(2,1)S(1)}, u32[]{:S(2)}, u32[]{:S(2)}) collective-permute-start(bf16[48,16,128]{2,1,0:T(8,128)(2,1)S(1)} %get-tuple-element.56), channel_id=1, source_target_pairs={{1,2},{2,1},{5,6},{6,5},{9,10},{10,9},{13,14},{14,13},{17,18},{18,... | collective-permute-start | bytes 589832 | tf_op jit(solution)/shard_map/ppermute | solution.py:22

commit v6 on v5

--- a/solution.py
+++ b/solution.py
@@ -22,12 +22,17 @@
     return lax.ppermute(value, "space", pairs)
 
 
+def shift_order(count):
+    return (2, 3, 1) if count == 4 else tuple(range(1, count))
+
+
 def earlier(value):
     count = lax.axis_size("tm")
+    shifts = shift_order(count)
     if count <= 8:
-        return [lax.ppermute(value, "tm", [(i, i + s) for i in range(count - s)]) for s in range(1, count)]
+        return [lax.ppermute(value, "tm", [(i, i + s) for i in range(count - s)]) for s in shifts]
     every = lax.all_gather(value, "tm")
-    at = lax.axis_index("tm") - jnp.arange(1, count)
+    at = lax.axis_index("tm") - jnp.array(shifts)
     picked = jnp.where((at >= 0)[:, None, None], jnp.take(every, jnp.maximum(at, 0), axis=0), 0.0)
     return [picked[s] for s in range(count - 1)]
 
@@ -79,7 +84,8 @@
 
 
 def enter(arrivals, we, pk, y, n):
-    value = jnp.concatenate([a[...] for a in arrivals], axis=1)
+    by_shift = dict(zip(shift_order(len(arrivals) + 1), arrivals))
+    value = jnp.concatenate([by_shift[shift][...] for shift in sorted(by_shift)], axis=1)
     entry = product_rows(split_rows(value), we[...])
     y[pl.ds(0, n, stride=8), :] = entry
     rows = split_rows(entry)
@@ -88,17 +94,10 @@
     return y[...].reshape(n, 8, 128)
 
 
-FIXED = {0: -1, 2: -REACH, 3: 1, 5: REACH}
-
-
-def apply_phi(src, idx, masks, w, base, size):
+def apply_phi(src, idx, w, base, size):
     cols = [src[pl.ds(base, size)].reshape(size * 16, 128)]
     for f in range(6):
-        if masks is not None and f in FIXED:
-            near = src[pl.ds(base + FIXED[f], size)] * masks[list(FIXED).index(f), pl.ds(base, size)]
-            cols.append(near.reshape(size * 16, 128))
-        else:
-            cols.append(jnp.concatenate([src[idx[f, base + e]] for e in range(size)], axis=0))
+        cols.append(jnp.concatenate([src[idx[f, base + e]] for e in range(size)], axis=0))
     return product(jnp.concatenate(cols, axis=1), w[...])
 
 
@@ -300,7 +299,7 @@
             put_force(force, fe, got, even, k, n)
             size = (6 - 2 * k) * REACH
             base = mirrored((k + 1) * REACH, size, full, even)
-            dst[pl.ds(base, size)] = split(apply_phi(src, idx, None, w, base, size) + force_at(force, base, size))
+            dst[pl.ds(base, size)] = split(apply_phi(src, idx, w, base, size) + force_at(force, base, size))
         put_strips((strip1, strip2, strip3), (s1, s2, s3), full, even)
 
     by_parity(body)
@@ -328,7 +327,7 @@
         for k, src, dst in ((1, s1, s2), (2, s2, s3), (3, s3, None)):
             put_force(force, fe, got_odd, not even, k, n)
             base = mirrored((7 - k) * REACH, count, full, even)
-            value = apply_phi(src, idx, None, w, base, count) + force_at(force, base, count)
+            value = apply_phi(src, idx, w, base, count) + force_at(force, base, count)
             if dst is None:
                 w1[...] = value
                 y[...] = value.reshape(n * 8, 128)
@@ -339,23 +338,8 @@
     by_parity(body)
 
 
-def scan_kernel(values, pk, idx, starts, masks, square, there):
+def scan_kernel(values, pk, starts):
     starts[...] = scan_starts(values[...], pk)
-    full = masks.shape[1]
-    for at in range(0, full, 128):
-        square[...] = jnp.zeros_like(square)
-        square[0:8, :] = (idx[:, pl.ds(at, 128)] != full).astype(F32)
-        count = min(128, full - at)
-        turned = square[...].T
-        for m, f in enumerate(FIXED):
-            there[m, pl.ds(at, count), :] = jnp.broadcast_to(turned[:count, f : f + 1], (count, 128))
-
-    def body(e, carry):
-        for m in range(len(FIXED)):
-            masks[m, e] = jnp.broadcast_to(there[m, pl.ds(e, 1), :], (16, 128)).astype(BF16)
-        return carry
-
-    lax.fori_loop(REACH, full - REACH, body, 0, unroll=8)
 
 
 def scan_sum_kernel(values, w1, coarse, pk, starts, total):
@@ -392,7 +376,7 @@
     dst[3 * n] = jnp.zeros((16, 128), BF16)
 
 
-def second_early_kernel(idx, own, got, masks, w, pk, strip1, strip2, strip3, coarse, s0, s1, s2, s3):
+def second_early_kernel(idx, own, got, w, pk, strip1, strip2, strip3, coarse, s0, s1, s2, s3):
     def body(even):
         n = own.shape[0]
         full = 3 * n
@@ -403,13 +387,13 @@
         for k, src, dst in ((1, s0, s1), (2, s1, s2), (3, s2, s3)):
             size = (8 - 2 * k) * REACH
             base = mirrored(k * REACH, size, full, even)
-            dst[pl.ds(base, size)] = split(apply_phi(src, idx, masks, w, base, size))
+            dst[pl.ds(base, size)] = split(apply_phi(src, idx, w, base, size))
         put_strips((strip1, strip2, strip3), (s1, s2, s3), full, even)
 
     by_parity(body)
 
 
-def second_late_kernel(idx, own, got, strip1, strip2, strip3, coarse, masks, w, pk, res, end, s0, s1, s2, s3, y):
+def second_late_kernel(idx, own, got, strip1, strip2, strip3, coarse, w, pk, res, end, s0, s1, s2, s3, y):
     def body(even):
         n = own.shape[0]
         full = 3 * n
@@ -418,8 +402,8 @@
         count = 4 * REACH
         for k, src, dst in ((1, s0, s1), (2, s1, s2), (3, s2, s3)):
             base = mirrored((8 - k) * REACH, count, full, even)
-            dst[pl.ds(base, count)] = split(apply_phi(src, idx, masks, w, base, count))
-        value = apply_phi(s3, idx, masks, w, n, n)
+            dst[pl.ds(base, count)] = split(apply_phi(src, idx, w, base, count))
+        value = apply_phi(s3, idx, w, n, n)
         value = value - coarse[...]
         res[...] = value
         y[...] = value.reshape(n * 8, 128)
@@ -444,7 +428,7 @@
 
 
 def third_early_kernel(
-    idx, own, got, corr, total, fe, pay, masks, w, pk, out, strip1, strip2, s0, s1, s2, force, flip0, flip1, flip2, flip3, sems
+    idx, own, got, corr, total, fe, pay, w, pk, out, strip1, strip2, s0, s1, s2, force, flip0, flip1, flip2, flip3, sems
 ):
     def body(even):
         n = own.shape[0]
@@ -458,7 +442,7 @@
             put_force(force, fe, pay, even, k, n)
             size = (5 - 2 * k) * REACH
             base = mirrored((2 + k) * REACH, size, full, even)
-            value = apply_phi(src, idx, masks, w, base, size) + force_at(force, base, size)
+            value = apply_phi(src, idx, w, base, size) + force_at(force, base, size)
             if dst is not None:
                 dst[pl.ds(base, size)] = split(value)
             mine = (3 - k) * REACH
@@ -473,7 +457,7 @@
 
 
 def third_late_kernel(
-    idx, own, got, strip1, strip2, fe, pay, masks, w, partial, out, s0, s1, s2, force, flip0, flip1, flip2, sems
+    idx, own, got, strip1, strip2, fe, pay, w, partial, out, s0, s1, s2, force, flip0, flip1, flip2, sems
 ):
     def body(even):
         n = own.shape[0]
@@ -485,7 +469,7 @@
         for k, src, dst, flip in ((0, s0, s1, flip0), (1, s1, s2, flip1), (2, s2, None, flip2)):
             put_force(force, fe, pay, not even, k, n)
             base = mirrored((7 - k) * REACH, size, full, even)
-            value = apply_phi(src, idx, masks, w, base, size) + force_at(force, base, size)
+            value = apply_phi(src, idx, w, base, size) + force_at(force, base, size)
             if dst is not None:
                 dst[pl.ds(base, size)] = split(value)
             mine = (k + 1) * REACH
@@ -551,6 +535,7 @@
             dma((3,)),
         ],
         spaces="hhhh",
+        flops=3 * 10**9,
         out_spaces="hhh",
         room=62,
     )
@@ -587,17 +572,12 @@
         flops=step_flops * 12 * REACH,
     )
     arrivals = earlier(end)
-    starts, masks = call(
-        scan_kernel,
-        (w1, pk, idx),
-        (tiles, shape((len(FIXED), full, 16, width), BF16)),
-        [vmem((128, 128), F32), vmem((len(FIXED), full, width), F32)],
-    )
+    (starts,) = call(scan_kernel, (w1, pk), (tiles,), [])
     (coarse,) = call(enter_first_kernel, (*arrivals, starts, we, pk), (state,), [rows])
     got_odd, got_even = swapped(coarse, 1), swapped(coarse, 0)
     *strips, moved = call(
         second_early_kernel,
-        (idx, coarse, got_even, masks, w, pk),
+        (idx, coarse, got_even, w, pk),
         (strip, strip, strip, tiles),
         [spaces] * 4,
         spaces="s",
@@ -605,7 +585,7 @@
     )
     res, end = call(
         second_late_kernel,
-        (idx, coarse, got_odd, *strips, moved, masks, w, pk),
+        (idx, coarse, got_odd, *strips, moved, w, pk),
         (tiles, ends),
         [spaces] * 4 + [rows],
         spaces="s",
@@ -625,7 +605,7 @@
     flips = [vmem((8 * (m * REACH + 8), width), F32) for m in (3, 2, 1)]
     out, *strips = call(
         third_early_kernel,
-        (idx, coarse, got_even, corr, total, fe, pay_even, masks, w, pk),
+        (idx, coarse, got_even, corr, total, fe, pay_even, w, pk),
         (result, strip, strip),
         [spaces] * 3 + [force] + flips + [vmem((8 * (n + 8), width), F32), dma((COARSEN, 8))],
         spaces="s",
@@ -634,12 +614,12 @@
     )
     (out,) = call(
         third_late_kernel,
-        (idx, coarse, got_odd, *strips, fe, pay_odd, masks, w, out),
+        (idx, coarse, got_odd, *strips, fe, pay_odd, w, out),
         (result,),
         [spaces] * 3 + [force] + flips[::-1] + [dma((COARSEN - 1, 8))],
-        spaces="svvvvvvvvh",
+        spaces="svvvvvvvh",
         out_spaces="h",
-        aliases={9: 0},
+        aliases={8: 0},
         flops=step_flops * 9 * REACH,
     )
     return out

time: 59.6 us -> 58.2 us (0.977)
  local copies, waits for them, and re-layouts: 2.68 us -> 0.02 us
  starting transfers between devices: 27 us -> 29.6 us
  Pallas kernels: 27.5 us -> 26.9 us
    unnamed x10, local copies, waits for them, and re-layouts: 2.68 us -> 0.02 us
    ppermute x6, starting transfers between devices: 12 us -> 13.5 us  [swapped(): return lax.ppermute(value, 'space', pairs)]
    ppermute x6, starting transfers between devices: 15.1 us -> 16.1 us  [earlier(): lax.ppermute(value, 'tm', [(i, i + s) for i in range(count - s)])]
    ppermute x6, waiting for transfers between devices: 1.22 us -> 0.59 us  [swapped(): return lax.ppermute(value, 'space', pairs)]
  transfers between devices with their start and end apart: 12 -> 12, of which waited for: 2 -> 3; matrix products, arithmetic and copies ran while one was open for 0% -> 0% of each run, Pallas kernels for 23% -> 22%
where the time goes in v6:
time: 58.2 us; the launch traced here: 57.9 us
  starting transfers between devices  29.6 us (51%)
  Pallas kernels  26.9 us (46%)
  waiting for transfers between devices  0.94 us (2%)
    pallas_call x12, Pallas kernels, call(): pl.pallas_call(kernel, out_shape=outs, name=kernel.__name__, in_specs=spe...  26.9 us
    ppermute x6, starting transfers between devices, earlier(): lax.ppermute(value, 'tm', [(i, i + s) for i in range(count - s)])  16.1 us
    ppermute x6, starting transfers between devices, swapped(): return lax.ppermute(value, 'space', pairs)  13.5 us
  transfers between devices with their start and end apart: 12, of which 3 were waited for; matrix products, arithmetic and copies ran while one was open for 0% of the time, Pallas kernels for 22%

profile of v6, /device:TPU:1, one launch (start us, length us, event | category | flops | bytes accessed | tf_op | source)
XLA Modules:
  0.0 57.9 jit_solution(351953936177777343)
XLA Ops:
  0.0 2.5 %pack_kernel.1 = (bf16[2064,128]{1,0:T(8,128)(2,1)}, bf16[912,128]{1,0:T(8,128)(2,1)}, bf16[912,128]{1,0:T(8,128)(2,1)}) custom-call(bf16[8,4,64,128]{3,2,1,0:T(8,128)(2,1)} %bitcast.3, f32[64,128]{1,0:T(8,128)} %refs_5_.1, s32[6,64]{1,0:T(8,128)} %bitcast.4, s32[6,64]{1,0:T(8,128)} %bitcast.5), custom_call_target="tpu_custom_call" | custom-call | flops 3000000000 | bytes 1555456 | tf_op jit(solution)/shard_map/pack_kernel/pallas_call | solution.py:492
  2.5 0.1 collective-permute-start
  2.7 4.6 %collective-permute-start.1 = (bf16[912,128]{1,0:T(8,128)(2,1)}, bf16[912,128]{1,0:T(8,128)(2,1)S(1)}, u32[]{:S(2)}, u32[]{:S(2)}) collective-permute-start(bf16[912,128]{1,0:T(8,128)(2,1)} %get-tuple-element.34), channel_id=1, source_target_pairs={{1,2},{2,1},{5,6},{6,5},{9,10},{10,9},{13,14},{14,13},{17,18},{18,... | collective-permute-start | bytes 700424 | tf_op jit(solution)/shard_map/ppermute | solution.py:22
  7.3 1.5 %weight_kernel.1 = (bf16[896,256]{1,0:T(8,128)(2,1)S(1)}, bf16[1024,256]{1,0:T(8,128)(2,1)S(1)}, bf16[384,256]{1,0:T(8,128)(2,1)S(1)}) custom-call(f32[128,128]{1,0:T(8,128)S(1)} %copy-done.3, f32[6,128,128]{2,1,0:T(8,128)S(1)} %copy-done.2, f32[128,128]{1,0:T(8,128)S(1)} %copy-done.4), custom_call_target="tpu_custom_call" | custom-call | flops 1000000000 | bytes 1703936 | tf_op jit(solution)/shard_map/weight_kernel/pallas_call | solution.py:492
  8.9 2.6 %first_early_kernel.1 = (bf16[32,16,128]{2,1,0:T(8,128)(2,1)S(1)}, bf16[32,16,128]{2,1,0:T(8,128)(2,1)S(1)}, bf16[32,16,128]{2,1,0:T(8,128)(2,1)S(1)}) custom-call(bf16[2064,128]{1,0:T(8,128)(2,1)S(1)} %copy-done, f32[64,128]{1,0:T(8,128)S(1)} %copy-done.1, bf16[912,128]{1,0:T(8,128)(2,1)S(1)} %collective-permute-done.got.got_even.pay, ...), custom_call_target="tpu_custom_call" | custom-call | flops 704643072 | bytes 1646592 | tf_op jit(solution)/shard_map/first_early_kernel/pallas_call | solution.py:492
  11.5 3.1 %first_late_kernel.1 = (f32[64,8,128]{2,1,0:T(8,128)S(1)}, f32[64,128]{1,0:T(8,128)S(1)}, s32[8,256]{1,0:T(8,128)S(1)}) custom-call(bf16[2064,128]{1,0:T(8,128)(2,1)S(1)} %copy-done, f32[64,128]{1,0:T(8,128)S(1)} %copy-done.1, bf16[912,128]{1,0:T(8,128)(2,1)S(1)} %collective-permute-done.got.got_even.pay, ...), custom_call_target="tpu_custom_call" | custom-call | flops 1409286144 | bytes 2707456 | tf_op jit(solution)/shard_map/first_late_kernel/pallas_call | solution.py:492
  14.6 3.5 %collective-permute-start.4 = (f32[64,128]{1,0:T(8,128)S(1)}, f32[64,128]{1,0:T(8,128)S(1)}, u32[]{:S(2)}, u32[]{:S(2)}) collective-permute-start(f32[64,128]{1,0:T(8,128)S(1)} %get-tuple-element.41), channel_id=1, source_target_pairs={{0,4},{4,8},{8,12},{1,5},{5,9},{9,13},{2,6},{6,10},{10,14},{3,7},{... | collective-permute-start | bytes 98312 | tf_op jit(solution)/shard_map/ppermute | solution.py:33
  18.2 3.3 %collective-permute-start.3 = (f32[64,128]{1,0:T(8,128)S(1)}, f32[64,128]{1,0:T(8,128)S(1)}, u32[]{:S(2)}, u32[]{:S(2)}) collective-permute-start(f32[64,128]{1,0:T(8,128)S(1)} %get-tuple-element.41), channel_id=1, source_target_pairs={{0,12},{1,13},{2,14},{3,15},{16,28},{17,29},{18,30},{19,31}} | collective-permute-start | bytes 98312 | tf_op jit(solution)/shard_map/ppermute | solution.py:33
  21.5 1.6 %collective-permute-start.2 = (f32[64,128]{1,0:T(8,128)S(1)}, f32[64,128]{1,0:T(8,128)S(1)}, u32[]{:S(2)}, u32[]{:S(2)}) collective-permute-start(f32[64,128]{1,0:T(8,128)S(1)} %get-tuple-element.41), channel_id=1, source_target_pairs={{0,8},{4,12},{1,9},{5,13},{2,10},{6,14},{3,11},{7,15},{16,24},{20,... | collective-permute-start | bytes 98312 | tf_op jit(solution)/shard_map/ppermute | solution.py:33
  23.1 0.7 %scan_kernel.1.refs_3_ = f32[64,8,128]{2,1,0:T(8,128)S(1)} custom-call(f32[64,8,128]{2,1,0:T(8,128)S(1)} %get-tuple-element.42.values.w1, bf16[1024,256]{1,0:T(8,128)(2,1)S(1)} %get-tuple-element.39.pk.refs_5_.refs_7_), custom_call_target="tpu_custom_call" | custom-call | flops 10000000 | bytes 1048576 | tf_op jit(solution)/shard_map/scan_kernel/pallas_call | solution.py:492
  23.8 0.3 collective-permute-done.2.refs_0_
  24.1 0.5 enter_first_kernel.1.own.refs_4_
  24.7 4.1 %collective-permute-start.5 = (bf16[64,16,128]{2,1,0:T(8,128)(2,1)S(1)}, bf16[64,16,128]{2,1,0:T(8,128)(2,1)S(1)}, u32[]{:S(2)}, u32[]{:S(2)}) collective-permute-start(bf16[64,16,128]{2,1,0:T(8,128)(2,1)S(1)} %enter_first_kernel.1.own.refs_4_), channel_id=1, source_target_pairs={{1,2},{2,1},{5,6},{6,5},{9,10},{10,9},{13,14},{14,13},{17,18},{18,... | collective-permute-start | bytes 786440 | tf_op jit(solution)/shard_map/ppermute | solution.py:22
  28.9 3.5 %second_early_kernel.1 = (bf16[32,16,128]{2,1,0:T(8,128)(2,1)S(1)}, bf16[32,16,128]{2,1,0:T(8,128)(2,1)S(1)}, bf16[32,16,128]{2,1,0:T(8,128)(2,1)S(1)}, f32[64,8,128]{2,1,0:T(8,128)S(1)}) custom-call(s32[8,256]{1,0:T(8,128)S(1)} %get-tuple-element.40.idx, bf16[64,16,128]{2,1,0:T(8,128)(2,1)S(1)} %enter_first_kernel.1.own.refs_4_, ...), custom_call_target="tpu_custom_call" | custom-call | flops 1409286144 | bytes 2170880 | tf_op jit(solution)/shard_map/second_early_kernel/pallas_call | solution.py:492
  32.3 0.6 collective-permute-done.5.got
  32.9 3.9 %second_late_kernel.1 = (f32[64,8,128]{2,1,0:T(8,128)S(1)}, f32[64,128]{1,0:T(8,128)S(1)}) custom-call(s32[8,256]{1,0:T(8,128)S(1)} %get-tuple-element.40.idx, bf16[64,16,128]{2,1,0:T(8,128)(2,1)S(1)} %enter_first_kernel.1.own.refs_4_, bf16[64,16,128]{2,1,0:T(8,128)(2,1)S(1)} %collective-permute-done.5.got, ...), custom_call_target="tpu_custom_call" | custom-call | flops 1879048192 | bytes 2465792 | tf_op jit(solution)/shard_map/second_late_kernel/pallas_call | solution.py:492
  36.8 1.7 %collective-permute-start.9 = (f32[64,128]{1,0:T(8,128)S(1)}, f32[64,128]{1,0:T(8,128)S(1)}, u32[]{:S(2)}, u32[]{:S(2)}) collective-permute-start(f32[64,128]{1,0:T(8,128)S(1)} %get-tuple-element.48), channel_id=1, source_target_pairs={{0,4},{4,8},{8,12},{1,5},{5,9},{9,13},{2,6},{6,10},{10,14},{3,7},{... | collective-permute-start | bytes 98312 | tf_op jit(solution)/shard_map/ppermute | solution.py:33
  38.4 3.9 %collective-permute-start.8 = (f32[64,128]{1,0:T(8,128)S(1)}, f32[64,128]{1,0:T(8,128)S(1)}, u32[]{:S(2)}, u32[]{:S(2)}) collective-permute-start(f32[64,128]{1,0:T(8,128)S(1)} %get-tuple-element.48), channel_id=1, source_target_pairs={{0,12},{1,13},{2,14},{3,15},{16,28},{17,29},{18,30},{19,31}} | collective-permute-start | bytes 98312 | tf_op jit(solution)/shard_map/ppermute | solution.py:33
  42.4 2.1 %collective-permute-start.7 = (f32[64,128]{1,0:T(8,128)S(1)}, f32[64,128]{1,0:T(8,128)S(1)}, u32[]{:S(2)}, u32[]{:S(2)}) collective-permute-start(f32[64,128]{1,0:T(8,128)S(1)} %get-tuple-element.48), channel_id=1, source_target_pairs={{0,8},{4,12},{1,9},{5,13},{2,10},{6,14},{3,11},{7,15},{16,24},{20,... | collective-permute-start | bytes 98312 | tf_op jit(solution)/shard_map/ppermute | solution.py:33
  44.4 0.7 %scan_sum_kernel.1 = (f32[64,8,128]{2,1,0:T(8,128)S(1)}, f32[64,8,128]{2,1,0:T(8,128)S(1)}) custom-call(f32[64,8,128]{2,1,0:T(8,128)S(1)} %get-tuple-element.49.values, f32[64,8,128]{2,1,0:T(8,128)S(1)} %get-tuple-element.42.values.w1, f32[64,8,128]{2,1,0:T(8,128)S(1)} %get-tuple-element.47.coarse, bf16[1024,256]{1,0:T(8,128)(2,1)S(1)} %get-tuple-element.39.pk.refs_5_.refs_7_), custom_call_target="tpu_custom_call" | custom-call | flops 10000000 | bytes 1835008 | tf_op jit(solution)/shard_map/scan_sum_kernel/pallas_call | solution.py:492
  45.2 0.6 %enter_second_kernel.1 = (bf16[64,16,128]{2,1,0:T(8,128)(2,1)S(1)}, bf16[48,16,128]{2,1,0:T(8,128)(2,1)S(1)}, bf16[48,16,128]{2,1,0:T(8,128)(2,1)S(1)}, f32[64,8,128]{2,1,0:T(8,128)S(1)}) custom-call(f32[64,128]{1,0:T(8,128)S(1)} %collective-permute-done.7.refs_0_, f32[64,128]{1,0:T(8,128)S(1)} %collective-permute-done.8.refs_1_, ...), custom_call_target="tpu_custom_call" | custom-call | flops 10000000 | bytes 2293760 | tf_op jit(solution)/shard_map/enter_second_kernel/pallas_call | solution.py:492
  45.9 4.5 %collective-permute-start.10 = (bf16[48,16,128]{2,1,0:T(8,128)(2,1)S(1)}, bf16[48,16,128]{2,1,0:T(8,128)(2,1)S(1)}, u32[]{:S(2)}, u32[]{:S(2)}) collective-permute-start(bf16[48,16,128]{2,1,0:T(8,128)(2,1)S(1)} %get-tuple-element.52), channel_id=1, source_target_pairs={{1,2},{2,1},{5,6},{6,5},{9,10},{10,9},{13,14},{14,13},{17,18},{18,... | collective-permute-start | bytes 589832 | tf_op jit(solution)/shard_map/ppermute | solution.py:22
  50.4 4.0 %third_early_kernel.1 = (f32[32,64,128]{2,1,0:T(8,128)}, bf16[32,16,128]{2,1,0:T(8,128)(2,1)S(1)}, bf16[32,16,128]{2,1,0:T(8,128)(2,1)S(1)}) custom-call(s32[8,256]{1,0:T(8,128)S(1)} %get-tuple-element.40.idx, bf16[64,16,128]{2,1,0:T(8,128)(2,1)S(1)} %get-tuple-element.51.own, bf16[48,16,128]{2,1,0:T(8,128)(2,1)S(1)} %collective-permute-done.11.got, ...), custom_call_target="tpu_custom_call" | custom-call | flops 1056964608 | bytes 4046848 | tf_op jit(solution)/shard_map/third_early_kernel/pallas_call | solution.py:492
  54.4 3.3 %third_late_kernel.1 = f32[32,64,128]{2,1,0:T(8,128)} custom-call(s32[8,256]{1,0:T(8,128)S(1)} %get-tuple-element.40.idx, bf16[64,16,128]{2,1,0:T(8,128)(2,1)S(1)} %get-tuple-element.51.own, bf16[48,16,128]{2,1,0:T(8,128)(2,1)S(1)} %collective-permute-done.10.got, bf16[32,16,128]{2,1,0:T(8,128)(2,1)S(1)} %get-tuple-element.56.strip1, ...), custom_call_target="tpu_custom_call", output_to_operand_aliasing={{}: (8, {})} | custom-call | flops 1056964608 | bytes 4046848 | tf_op jit(solution)/shard_map/third_late_kernel/pallas_call | solution.py:492
  (22 shorter events, 0.2 us)
Async XLA Ops:
  0.0 7.3 %copy-start.2 = (f32[6,128,128]{2,1,0:T(8,128)S(1)}, f32[6,128,128]{2,1,0:T(8,128)}, u32[]{:S(2)}) copy-start(f32[6,128,128]{2,1,0:T(8,128)} %faces.1) | copy-start | bytes 1179652
  0.0 7.3 %copy-start.3 = (f32[128,128]{1,0:T(8,128)S(1)}, f32[128,128]{1,0:T(8,128)}, u32[]{:S(2)}) copy-start(f32[128,128]{1,0:T(8,128)} %diag.1) | copy-start | bytes 196612
  0.0 7.3 %copy-start.4 = (f32[128,128]{1,0:T(8,128)S(1)}, f32[128,128]{1,0:T(8,128)}, u32[]{:S(2)}) copy-start(f32[128,128]{1,0:T(8,128)} %coarse.1) | copy-start | bytes 196612
  2.5 6.3 %collective-permute-start = (bf16[912,128]{1,0:T(8,128)(2,1)}, bf16[912,128]{1,0:T(8,128)(2,1)S(1)}, u32[]{:S(2)}, u32[]{:S(2)}) collective-permute-start(bf16[912,128]{1,0:T(8,128)(2,1)} %get-tuple-element.33), channel_id=1, source_target_pairs={{0,1},{1,0},{2,3},{3,2},{4,5},{5,4},{6,7},{7,6},{8,9},{9,8},{10,11... | collective-permute-start | bytes 700424 | tf_op jit(solution)/shard_map/ppermute | solution.py:22
  2.7 6.2 %copy-start = (bf16[2064,128]{1,0:T(8,128)(2,1)S(1)}, bf16[2064,128]{1,0:T(8,128)(2,1)}, u32[]{:S(2)}) copy-start(bf16[2064,128]{1,0:T(8,128)(2,1)} %get-tuple-element.32.fe) | copy-start | bytes 1585156
  2.7 6.2 %copy-start.1 = (f32[64,128]{1,0:T(8,128)S(1)}, f32[64,128]{1,0:T(8,128)}, u32[]{:S(2)}) copy-start(f32[64,128]{1,0:T(8,128)} %refs_5_.1) | copy-start | bytes 98308
  2.7 8.8 %collective-permute-start.1 = (bf16[912,128]{1,0:T(8,128)(2,1)}, bf16[912,128]{1,0:T(8,128)(2,1)S(1)}, u32[]{:S(2)}, u32[]{:S(2)}) collective-permute-start(bf16[912,128]{1,0:T(8,128)(2,1)} %get-tuple-element.34), channel_id=1, source_target_pairs={{1,2},{2,1},{5,6},{6,5},{9,10},{10,9},{13,14},{14,13},{17,18},{18,... | collective-permute-start | bytes 700424 | tf_op jit(solution)/shard_map/ppermute | solution.py:22
  14.6 9.1 %collective-permute-start.4 = (f32[64,128]{1,0:T(8,128)S(1)}, f32[64,128]{1,0:T(8,128)S(1)}, u32[]{:S(2)}, u32[]{:S(2)}) collective-permute-start(f32[64,128]{1,0:T(8,128)S(1)} %get-tuple-element.41), channel_id=1, source_target_pairs={{0,4},{4,8},{8,12},{1,5},{5,9},{9,13},{2,6},{6,10},{10,14},{3,7},{... | collective-permute-start | bytes 98312 | tf_op jit(solution)/shard_map/ppermute | solution.py:33
  18.2 5.6 %collective-permute-start.3 = (f32[64,128]{1,0:T(8,128)S(1)}, f32[64,128]{1,0:T(8,128)S(1)}, u32[]{:S(2)}, u32[]{:S(2)}) collective-permute-start(f32[64,128]{1,0:T(8,128)S(1)} %get-tuple-element.41), channel_id=1, source_target_pairs={{0,12},{1,13},{2,14},{3,15},{16,28},{17,29},{18,30},{19,31}} | collective-permute-start | bytes 98312 | tf_op jit(solution)/shard_map/ppermute | solution.py:33
  21.5 2.6 %collective-permute-start.2 = (f32[64,128]{1,0:T(8,128)S(1)}, f32[64,128]{1,0:T(8,128)S(1)}, u32[]{:S(2)}, u32[]{:S(2)}) collective-permute-start(f32[64,128]{1,0:T(8,128)S(1)} %get-tuple-element.41), channel_id=1, source_target_pairs={{0,8},{4,12},{1,9},{5,13},{2,10},{6,14},{3,11},{7,15},{16,24},{20,... | collective-permute-start | bytes 98312 | tf_op jit(solution)/shard_map/ppermute | solution.py:33
  24.6 4.2 %collective-permute-start.6 = (bf16[64,16,128]{2,1,0:T(8,128)(2,1)S(1)}, bf16[64,16,128]{2,1,0:T(8,128)(2,1)S(1)}, u32[]{:S(2)}, u32[]{:S(2)}) collective-permute-start(bf16[64,16,128]{2,1,0:T(8,128)(2,1)S(1)} %enter_first_kernel.1.own.refs_4_), channel_id=1, source_target_pairs={{0,1},{1,0},{2,3},{3,2},{4,5},{5,4},{6,7},{7,6},{8,9},{9,8},{10,11... | collective-permute-start | bytes 786440 | tf_op jit(solution)/shard_map/ppermute | solution.py:22
  24.7 8.2 %collective-permute-start.5 = (bf16[64,16,128]{2,1,0:T(8,128)(2,1)S(1)}, bf16[64,16,128]{2,1,0:T(8,128)(2,1)S(1)}, u32[]{:S(2)}, u32[]{:S(2)}) collective-permute-start(bf16[64,16,128]{2,1,0:T(8,128)(2,1)S(1)} %enter_first_kernel.1.own.refs_4_), channel_id=1, source_target_pairs={{1,2},{2,1},{5,6},{6,5},{9,10},{10,9},{13,14},{14,13},{17,18},{18,... | collective-permute-start | bytes 786440 | tf_op jit(solution)/shard_map/ppermute | solution.py:22
  36.8 8.4 %collective-permute-start.9 = (f32[64,128]{1,0:T(8,128)S(1)}, f32[64,128]{1,0:T(8,128)S(1)}, u32[]{:S(2)}, u32[]{:S(2)}) collective-permute-start(f32[64,128]{1,0:T(8,128)S(1)} %get-tuple-element.48), channel_id=1, source_target_pairs={{0,4},{4,8},{8,12},{1,5},{5,9},{9,13},{2,6},{6,10},{10,14},{3,7},{... | collective-permute-start | bytes 98312 | tf_op jit(solution)/shard_map/ppermute | solution.py:33
  38.4 6.7 %collective-permute-start.8 = (f32[64,128]{1,0:T(8,128)S(1)}, f32[64,128]{1,0:T(8,128)S(1)}, u32[]{:S(2)}, u32[]{:S(2)}) collective-permute-start(f32[64,128]{1,0:T(8,128)S(1)} %get-tuple-element.48), channel_id=1, source_target_pairs={{0,12},{1,13},{2,14},{3,15},{16,28},{17,29},{18,30},{19,31}} | collective-permute-start | bytes 98312 | tf_op jit(solution)/shard_map/ppermute | solution.py:33
  42.4 2.9 %collective-permute-start.7 = (f32[64,128]{1,0:T(8,128)S(1)}, f32[64,128]{1,0:T(8,128)S(1)}, u32[]{:S(2)}, u32[]{:S(2)}) collective-permute-start(f32[64,128]{1,0:T(8,128)S(1)} %get-tuple-element.48), channel_id=1, source_target_pairs={{0,8},{4,12},{1,9},{5,13},{2,10},{6,14},{3,11},{7,15},{16,24},{20,... | collective-permute-start | bytes 98312 | tf_op jit(solution)/shard_map/ppermute | solution.py:33
  45.8 4.6 %collective-permute-start.11 = (bf16[48,16,128]{2,1,0:T(8,128)(2,1)S(1)}, bf16[48,16,128]{2,1,0:T(8,128)(2,1)S(1)}, u32[]{:S(2)}, u32[]{:S(2)}) collective-permute-start(bf16[48,16,128]{2,1,0:T(8,128)(2,1)S(1)} %get-tuple-element.53), channel_id=1, source_target_pairs={{0,1},{1,0},{2,3},{3,2},{4,5},{5,4},{6,7},{7,6},{8,9},{9,8},{10,11... | collective-permute-start | bytes 589832 | tf_op jit(solution)/shard_map/ppermute | solution.py:22
  45.9 8.5 %collective-permute-start.10 = (bf16[48,16,128]{2,1,0:T(8,128)(2,1)S(1)}, bf16[48,16,128]{2,1,0:T(8,128)(2,1)S(1)}, u32[]{:S(2)}, u32[]{:S(2)}) collective-permute-start(bf16[48,16,128]{2,1,0:T(8,128)(2,1)S(1)} %get-tuple-element.52), channel_id=1, source_target_pairs={{1,2},{2,1},{5,6},{6,5},{9,10},{10,9},{13,14},{14,13},{17,18},{18,... | collective-permute-start | bytes 589832 | tf_op jit(solution)/shard_map/ppermute | solution.py:22

commit v7 on v6

--- a/solution.py
+++ b/solution.py
@@ -23,7 +23,7 @@
 
 
 def shift_order(count):
-    return (2, 3, 1) if count == 4 else tuple(range(1, count))
+    return (2, 1, 3) if count == 4 else tuple(range(1, count))
 
 
 def earlier(value):

time: 58.2 us -> 58.8 us (1.010)
  starting transfers between devices: 29.6 us -> 30.2 us
    ppermute x6, starting transfers between devices: 16.1 us -> 16.7 us  [earlier(): lax.ppermute(value, 'tm', [(i, i + s) for i in range(count - s)])]
where the time goes in v7:
time: 58.8 us; the launch traced here: 58.6 us
  starting transfers between devices  30.2 us (51%)
  Pallas kernels  26.9 us (46%)
  waiting for transfers between devices  0.94 us (2%)
    pallas_call x12, Pallas kernels, call(): pl.pallas_call(kernel, out_shape=outs, name=kernel.__name__, in_specs=spe...  26.9 us
    ppermute x6, starting transfers between devices, earlier(): lax.ppermute(value, 'tm', [(i, i + s) for i in range(count - s)])  16.7 us
    ppermute x6, starting transfers between devices, swapped(): return lax.ppermute(value, 'space', pairs)  13.5 us
  transfers between devices with their start and end apart: 12, of which 3 were waited for; matrix products, arithmetic and copies ran while one was open for 0% of the time, Pallas kernels for 22%

profile of v7, /device:TPU:1, one launch (start us, length us, event | category | flops | bytes accessed | tf_op | source)
XLA Modules:
  0.0 58.6 jit_solution(8420083559637744834)
XLA Ops:
  0.0 2.5 %pack_kernel.1 = (bf16[2064,128]{1,0:T(8,128)(2,1)}, bf16[912,128]{1,0:T(8,128)(2,1)}, bf16[912,128]{1,0:T(8,128)(2,1)}) custom-call(bf16[8,4,64,128]{3,2,1,0:T(8,128)(2,1)} %bitcast.3, f32[64,128]{1,0:T(8,128)} %refs_5_.1, s32[6,64]{1,0:T(8,128)} %bitcast.4, s32[6,64]{1,0:T(8,128)} %bitcast.5), custom_call_target="tpu_custom_call" | custom-call | flops 3000000000 | bytes 1555456 | tf_op jit(solution)/shard_map/pack_kernel/pallas_call | solution.py:492
  2.5 0.1 collective-permute-start
  2.7 4.6 %collective-permute-start.1 = (bf16[912,128]{1,0:T(8,128)(2,1)}, bf16[912,128]{1,0:T(8,128)(2,1)S(1)}, u32[]{:S(2)}, u32[]{:S(2)}) collective-permute-start(bf16[912,128]{1,0:T(8,128)(2,1)} %get-tuple-element.34), channel_id=1, source_target_pairs={{1,2},{2,1},{5,6},{6,5},{9,10},{10,9},{13,14},{14,13},{17,18},{18,... | collective-permute-start | bytes 700424 | tf_op jit(solution)/shard_map/ppermute | solution.py:22
  7.3 1.5 %weight_kernel.1 = (bf16[896,256]{1,0:T(8,128)(2,1)S(1)}, bf16[1024,256]{1,0:T(8,128)(2,1)S(1)}, bf16[384,256]{1,0:T(8,128)(2,1)S(1)}) custom-call(f32[128,128]{1,0:T(8,128)S(1)} %copy-done.3, f32[6,128,128]{2,1,0:T(8,128)S(1)} %copy-done.2, f32[128,128]{1,0:T(8,128)S(1)} %copy-done.4), custom_call_target="tpu_custom_call" | custom-call | flops 1000000000 | bytes 1703936 | tf_op jit(solution)/shard_map/weight_kernel/pallas_call | solution.py:492
  8.9 2.6 %first_early_kernel.1 = (bf16[32,16,128]{2,1,0:T(8,128)(2,1)S(1)}, bf16[32,16,128]{2,1,0:T(8,128)(2,1)S(1)}, bf16[32,16,128]{2,1,0:T(8,128)(2,1)S(1)}) custom-call(bf16[2064,128]{1,0:T(8,128)(2,1)S(1)} %copy-done, f32[64,128]{1,0:T(8,128)S(1)} %copy-done.1, bf16[912,128]{1,0:T(8,128)(2,1)S(1)} %collective-permute-done.got.got_even.pay, ...), custom_call_target="tpu_custom_call" | custom-call | flops 704643072 | bytes 1646592 | tf_op jit(solution)/shard_map/first_early_kernel/pallas_call | solution.py:492
  11.5 3.1 %first_late_kernel.1 = (f32[64,8,128]{2,1,0:T(8,128)S(1)}, f32[64,128]{1,0:T(8,128)S(1)}, s32[8,256]{1,0:T(8,128)S(1)}) custom-call(bf16[2064,128]{1,0:T(8,128)(2,1)S(1)} %copy-done, f32[64,128]{1,0:T(8,128)S(1)} %copy-done.1, bf16[912,128]{1,0:T(8,128)(2,1)S(1)} %collective-permute-done.got.got_even.pay, ...), custom_call_target="tpu_custom_call" | custom-call | flops 1409286144 | bytes 2707456 | tf_op jit(solution)/shard_map/first_late_kernel/pallas_call | solution.py:492
  14.6 5.5 %collective-permute-start.4 = (f32[64,128]{1,0:T(8,128)S(1)}, f32[64,128]{1,0:T(8,128)S(1)}, u32[]{:S(2)}, u32[]{:S(2)}) collective-permute-start(f32[64,128]{1,0:T(8,128)S(1)} %get-tuple-element.41), channel_id=1, source_target_pairs={{0,12},{1,13},{2,14},{3,15},{16,28},{17,29},{18,30},{19,31}} | collective-permute-start | bytes 98312 | tf_op jit(solution)/shard_map/ppermute | solution.py:33
  20.2 1.3 %collective-permute-start.3 = (f32[64,128]{1,0:T(8,128)S(1)}, f32[64,128]{1,0:T(8,128)S(1)}, u32[]{:S(2)}, u32[]{:S(2)}) collective-permute-start(f32[64,128]{1,0:T(8,128)S(1)} %get-tuple-element.41), channel_id=1, source_target_pairs={{0,4},{4,8},{8,12},{1,5},{5,9},{9,13},{2,6},{6,10},{10,14},{3,7},{... | collective-permute-start | bytes 98312 | tf_op jit(solution)/shard_map/ppermute | solution.py:33
  21.5 2.2 %collective-permute-start.2 = (f32[64,128]{1,0:T(8,128)S(1)}, f32[64,128]{1,0:T(8,128)S(1)}, u32[]{:S(2)}, u32[]{:S(2)}) collective-permute-start(f32[64,128]{1,0:T(8,128)S(1)} %get-tuple-element.41), channel_id=1, source_target_pairs={{0,8},{4,12},{1,9},{5,13},{2,10},{6,14},{3,11},{7,15},{16,24},{20,... | collective-permute-start | bytes 98312 | tf_op jit(solution)/shard_map/ppermute | solution.py:33
  23.7 0.7 %scan_kernel.1.refs_3_ = f32[64,8,128]{2,1,0:T(8,128)S(1)} custom-call(f32[64,8,128]{2,1,0:T(8,128)S(1)} %get-tuple-element.42.values.w1, bf16[1024,256]{1,0:T(8,128)(2,1)S(1)} %get-tuple-element.39.pk.refs_5_.refs_7_), custom_call_target="tpu_custom_call" | custom-call | flops 10000000 | bytes 1048576 | tf_op jit(solution)/shard_map/scan_kernel/pallas_call | solution.py:492
  24.4 0.3 collective-permute-done.2.refs_0_
  24.7 0.5 enter_first_kernel.1.own.refs_4_
  25.3 4.1 %collective-permute-start.5 = (bf16[64,16,128]{2,1,0:T(8,128)(2,1)S(1)}, bf16[64,16,128]{2,1,0:T(8,128)(2,1)S(1)}, u32[]{:S(2)}, u32[]{:S(2)}) collective-permute-start(bf16[64,16,128]{2,1,0:T(8,128)(2,1)S(1)} %enter_first_kernel.1.own.refs_4_), channel_id=1, source_target_pairs={{1,2},{2,1},{5,6},{6,5},{9,10},{10,9},{13,14},{14,13},{17,18},{18,... | collective-permute-start | bytes 786440 | tf_op jit(solution)/shard_map/ppermute | solution.py:22
  29.5 3.5 %second_early_kernel.1 = (bf16[32,16,128]{2,1,0:T(8,128)(2,1)S(1)}, bf16[32,16,128]{2,1,0:T(8,128)(2,1)S(1)}, bf16[32,16,128]{2,1,0:T(8,128)(2,1)S(1)}, f32[64,8,128]{2,1,0:T(8,128)S(1)}) custom-call(s32[8,256]{1,0:T(8,128)S(1)} %get-tuple-element.40.idx, bf16[64,16,128]{2,1,0:T(8,128)(2,1)S(1)} %enter_first_kernel.1.own.refs_4_, ...), custom_call_target="tpu_custom_call" | custom-call | flops 1409286144 | bytes 2170880 | tf_op jit(solution)/shard_map/second_early_kernel/pallas_call | solution.py:492
  32.9 0.6 collective-permute-done.5.got
  33.5 3.9 %second_late_kernel.1 = (f32[64,8,128]{2,1,0:T(8,128)S(1)}, f32[64,128]{1,0:T(8,128)S(1)}) custom-call(s32[8,256]{1,0:T(8,128)S(1)} %get-tuple-element.40.idx, bf16[64,16,128]{2,1,0:T(8,128)(2,1)S(1)} %enter_first_kernel.1.own.refs_4_, bf16[64,16,128]{2,1,0:T(8,128)(2,1)S(1)} %collective-permute-done.5.got, ...), custom_call_target="tpu_custom_call" | custom-call | flops 1879048192 | bytes 2465792 | tf_op jit(solution)/shard_map/second_late_kernel/pallas_call | solution.py:492
  37.4 3.7 %collective-permute-start.9 = (f32[64,128]{1,0:T(8,128)S(1)}, f32[64,128]{1,0:T(8,128)S(1)}, u32[]{:S(2)}, u32[]{:S(2)}) collective-permute-start(f32[64,128]{1,0:T(8,128)S(1)} %get-tuple-element.48), channel_id=1, source_target_pairs={{0,12},{1,13},{2,14},{3,15},{16,28},{17,29},{18,30},{19,31}} | collective-permute-start | bytes 98312 | tf_op jit(solution)/shard_map/ppermute | solution.py:33
  41.1 1.3 %collective-permute-start.8 = (f32[64,128]{1,0:T(8,128)S(1)}, f32[64,128]{1,0:T(8,128)S(1)}, u32[]{:S(2)}, u32[]{:S(2)}) collective-permute-start(f32[64,128]{1,0:T(8,128)S(1)} %get-tuple-element.48), channel_id=1, source_target_pairs={{0,4},{4,8},{8,12},{1,5},{5,9},{9,13},{2,6},{6,10},{10,14},{3,7},{... | collective-permute-start | bytes 98312 | tf_op jit(solution)/shard_map/ppermute | solution.py:33
  42.4 2.7 %collective-permute-start.7 = (f32[64,128]{1,0:T(8,128)S(1)}, f32[64,128]{1,0:T(8,128)S(1)}, u32[]{:S(2)}, u32[]{:S(2)}) collective-permute-start(f32[64,128]{1,0:T(8,128)S(1)} %get-tuple-element.48), channel_id=1, source_target_pairs={{0,8},{4,12},{1,9},{5,13},{2,10},{6,14},{3,11},{7,15},{16,24},{20,... | collective-permute-start | bytes 98312 | tf_op jit(solution)/shard_map/ppermute | solution.py:33
  45.1 0.7 %scan_sum_kernel.1 = (f32[64,8,128]{2,1,0:T(8,128)S(1)}, f32[64,8,128]{2,1,0:T(8,128)S(1)}) custom-call(f32[64,8,128]{2,1,0:T(8,128)S(1)} %get-tuple-element.49.values, f32[64,8,128]{2,1,0:T(8,128)S(1)} %get-tuple-element.42.values.w1, f32[64,8,128]{2,1,0:T(8,128)S(1)} %get-tuple-element.47.coarse, bf16[1024,256]{1,0:T(8,128)(2,1)S(1)} %get-tuple-element.39.pk.refs_5_.refs_7_), custom_call_target="tpu_custom_call" | custom-call | flops 10000000 | bytes 1835008 | tf_op jit(solution)/shard_map/scan_sum_kernel/pallas_call | solution.py:492
  45.8 0.6 %enter_second_kernel.1 = (bf16[64,16,128]{2,1,0:T(8,128)(2,1)S(1)}, bf16[48,16,128]{2,1,0:T(8,128)(2,1)S(1)}, bf16[48,16,128]{2,1,0:T(8,128)(2,1)S(1)}, f32[64,8,128]{2,1,0:T(8,128)S(1)}) custom-call(f32[64,128]{1,0:T(8,128)S(1)} %collective-permute-done.7.refs_0_, f32[64,128]{1,0:T(8,128)S(1)} %collective-permute-done.8.refs_1_, ...), custom_call_target="tpu_custom_call" | custom-call | flops 10000000 | bytes 2293760 | tf_op jit(solution)/shard_map/enter_second_kernel/pallas_call | solution.py:492
  46.5 4.5 %collective-permute-start.10 = (bf16[48,16,128]{2,1,0:T(8,128)(2,1)S(1)}, bf16[48,16,128]{2,1,0:T(8,128)(2,1)S(1)}, u32[]{:S(2)}, u32[]{:S(2)}) collective-permute-start(bf16[48,16,128]{2,1,0:T(8,128)(2,1)S(1)} %get-tuple-element.52), channel_id=1, source_target_pairs={{1,2},{2,1},{5,6},{6,5},{9,10},{10,9},{13,14},{14,13},{17,18},{18,... | collective-permute-start | bytes 589832 | tf_op jit(solution)/shard_map/ppermute | solution.py:22
  51.1 4.0 %third_early_kernel.1 = (f32[32,64,128]{2,1,0:T(8,128)}, bf16[32,16,128]{2,1,0:T(8,128)(2,1)S(1)}, bf16[32,16,128]{2,1,0:T(8,128)(2,1)S(1)}) custom-call(s32[8,256]{1,0:T(8,128)S(1)} %get-tuple-element.40.idx, bf16[64,16,128]{2,1,0:T(8,128)(2,1)S(1)} %get-tuple-element.51.own, bf16[48,16,128]{2,1,0:T(8,128)(2,1)S(1)} %collective-permute-done.11.got, ...), custom_call_target="tpu_custom_call" | custom-call | flops 1056964608 | bytes 4046848 | tf_op jit(solution)/shard_map/third_early_kernel/pallas_call | solution.py:492
  55.0 3.3 %third_late_kernel.1 = f32[32,64,128]{2,1,0:T(8,128)} custom-call(s32[8,256]{1,0:T(8,128)S(1)} %get-tuple-element.40.idx, bf16[64,16,128]{2,1,0:T(8,128)(2,1)S(1)} %get-tuple-element.51.own, bf16[48,16,128]{2,1,0:T(8,128)(2,1)S(1)} %collective-permute-done.10.got, bf16[32,16,128]{2,1,0:T(8,128)(2,1)S(1)} %get-tuple-element.56.strip1, ...), custom_call_target="tpu_custom_call", output_to_operand_aliasing={{}: (8, {})} | custom-call | flops 1056964608 | bytes 4046848 | tf_op jit(solution)/shard_map/third_late_kernel/pallas_call | solution.py:492
  (22 shorter events, 0.2 us)
Async XLA Ops:
  0.0 7.3 %copy-start.2 = (f32[6,128,128]{2,1,0:T(8,128)S(1)}, f32[6,128,128]{2,1,0:T(8,128)}, u32[]{:S(2)}) copy-start(f32[6,128,128]{2,1,0:T(8,128)} %faces.1) | copy-start | bytes 1179652
  0.0 7.3 %copy-start.3 = (f32[128,128]{1,0:T(8,128)S(1)}, f32[128,128]{1,0:T(8,128)}, u32[]{:S(2)}) copy-start(f32[128,128]{1,0:T(8,128)} %diag.1) | copy-start | bytes 196612
  0.0 7.3 %copy-start.4 = (f32[128,128]{1,0:T(8,128)S(1)}, f32[128,128]{1,0:T(8,128)}, u32[]{:S(2)}) copy-start(f32[128,128]{1,0:T(8,128)} %coarse.1) | copy-start | bytes 196612
  2.5 6.3 %collective-permute-start = (bf16[912,128]{1,0:T(8,128)(2,1)}, bf16[912,128]{1,0:T(8,128)(2,1)S(1)}, u32[]{:S(2)}, u32[]{:S(2)}) collective-permute-start(bf16[912,128]{1,0:T(8,128)(2,1)} %get-tuple-element.33), channel_id=1, source_target_pairs={{0,1},{1,0},{2,3},{3,2},{4,5},{5,4},{6,7},{7,6},{8,9},{9,8},{10,11... | collective-permute-start | bytes 700424 | tf_op jit(solution)/shard_map/ppermute | solution.py:22
  2.7 6.2 %copy-start = (bf16[2064,128]{1,0:T(8,128)(2,1)S(1)}, bf16[2064,128]{1,0:T(8,128)(2,1)}, u32[]{:S(2)}) copy-start(bf16[2064,128]{1,0:T(8,128)(2,1)} %get-tuple-element.32.fe) | copy-start | bytes 1585156
  2.7 6.2 %copy-start.1 = (f32[64,128]{1,0:T(8,128)S(1)}, f32[64,128]{1,0:T(8,128)}, u32[]{:S(2)}) copy-start(f32[64,128]{1,0:T(8,128)} %refs_5_.1) | copy-start | bytes 98308
  2.7 8.8 %collective-permute-start.1 = (bf16[912,128]{1,0:T(8,128)(2,1)}, bf16[912,128]{1,0:T(8,128)(2,1)S(1)}, u32[]{:S(2)}, u32[]{:S(2)}) collective-permute-start(bf16[912,128]{1,0:T(8,128)(2,1)} %get-tuple-element.34), channel_id=1, source_target_pairs={{1,2},{2,1},{5,6},{6,5},{9,10},{10,9},{13,14},{14,13},{17,18},{18,... | collective-permute-start | bytes 700424 | tf_op jit(solution)/shard_map/ppermute | solution.py:22
  14.6 9.8 %collective-permute-start.4 = (f32[64,128]{1,0:T(8,128)S(1)}, f32[64,128]{1,0:T(8,128)S(1)}, u32[]{:S(2)}, u32[]{:S(2)}) collective-permute-start(f32[64,128]{1,0:T(8,128)S(1)} %get-tuple-element.41), channel_id=1, source_target_pairs={{0,12},{1,13},{2,14},{3,15},{16,28},{17,29},{18,30},{19,31}} | collective-permute-start | bytes 98312 | tf_op jit(solution)/shard_map/ppermute | solution.py:33
  20.2 4.2 %collective-permute-start.3 = (f32[64,128]{1,0:T(8,128)S(1)}, f32[64,128]{1,0:T(8,128)S(1)}, u32[]{:S(2)}, u32[]{:S(2)}) collective-permute-start(f32[64,128]{1,0:T(8,128)S(1)} %get-tuple-element.41), channel_id=1, source_target_pairs={{0,4},{4,8},{8,12},{1,5},{5,9},{9,13},{2,6},{6,10},{10,14},{3,7},{... | collective-permute-start | bytes 98312 | tf_op jit(solution)/shard_map/ppermute | solution.py:33
  21.5 3.2 %collective-permute-start.2 = (f32[64,128]{1,0:T(8,128)S(1)}, f32[64,128]{1,0:T(8,128)S(1)}, u32[]{:S(2)}, u32[]{:S(2)}) collective-permute-start(f32[64,128]{1,0:T(8,128)S(1)} %get-tuple-element.41), channel_id=1, source_target_pairs={{0,8},{4,12},{1,9},{5,13},{2,10},{6,14},{3,11},{7,15},{16,24},{20,... | collective-permute-start | bytes 98312 | tf_op jit(solution)/shard_map/ppermute | solution.py:33
  25.2 4.2 %collective-permute-start.6 = (bf16[64,16,128]{2,1,0:T(8,128)(2,1)S(1)}, bf16[64,16,128]{2,1,0:T(8,128)(2,1)S(1)}, u32[]{:S(2)}, u32[]{:S(2)}) collective-permute-start(bf16[64,16,128]{2,1,0:T(8,128)(2,1)S(1)} %enter_first_kernel.1.own.refs_4_), channel_id=1, source_target_pairs={{0,1},{1,0},{2,3},{3,2},{4,5},{5,4},{6,7},{7,6},{8,9},{9,8},{10,11... | collective-permute-start | bytes 786440 | tf_op jit(solution)/shard_map/ppermute | solution.py:22
  25.3 8.2 %collective-permute-start.5 = (bf16[64,16,128]{2,1,0:T(8,128)(2,1)S(1)}, bf16[64,16,128]{2,1,0:T(8,128)(2,1)S(1)}, u32[]{:S(2)}, u32[]{:S(2)}) collective-permute-start(bf16[64,16,128]{2,1,0:T(8,128)(2,1)S(1)} %enter_first_kernel.1.own.refs_4_), channel_id=1, source_target_pairs={{1,2},{2,1},{5,6},{6,5},{9,10},{10,9},{13,14},{14,13},{17,18},{18,... | collective-permute-start | bytes 786440 | tf_op jit(solution)/shard_map/ppermute | solution.py:22
  37.4 8.4 %collective-permute-start.9 = (f32[64,128]{1,0:T(8,128)S(1)}, f32[64,128]{1,0:T(8,128)S(1)}, u32[]{:S(2)}, u32[]{:S(2)}) collective-permute-start(f32[64,128]{1,0:T(8,128)S(1)} %get-tuple-element.48), channel_id=1, source_target_pairs={{0,12},{1,13},{2,14},{3,15},{16,28},{17,29},{18,30},{19,31}} | collective-permute-start | bytes 98312 | tf_op jit(solution)/shard_map/ppermute | solution.py:33
  41.1 4.7 %collective-permute-start.8 = (f32[64,128]{1,0:T(8,128)S(1)}, f32[64,128]{1,0:T(8,128)S(1)}, u32[]{:S(2)}, u32[]{:S(2)}) collective-permute-start(f32[64,128]{1,0:T(8,128)S(1)} %get-tuple-element.48), channel_id=1, source_target_pairs={{0,4},{4,8},{8,12},{1,5},{5,9},{9,13},{2,6},{6,10},{10,14},{3,7},{... | collective-permute-start | bytes 98312 | tf_op jit(solution)/shard_map/ppermute | solution.py:33
  42.4 3.5 %collective-permute-start.7 = (f32[64,128]{1,0:T(8,128)S(1)}, f32[64,128]{1,0:T(8,128)S(1)}, u32[]{:S(2)}, u32[]{:S(2)}) collective-permute-start(f32[64,128]{1,0:T(8,128)S(1)} %get-tuple-element.48), channel_id=1, source_target_pairs={{0,8},{4,12},{1,9},{5,13},{2,10},{6,14},{3,11},{7,15},{16,24},{20,... | collective-permute-start | bytes 98312 | tf_op jit(solution)/shard_map/ppermute | solution.py:33
  46.5 4.6 %collective-permute-start.11 = (bf16[48,16,128]{2,1,0:T(8,128)(2,1)S(1)}, bf16[48,16,128]{2,1,0:T(8,128)(2,1)S(1)}, u32[]{:S(2)}, u32[]{:S(2)}) collective-permute-start(bf16[48,16,128]{2,1,0:T(8,128)(2,1)S(1)} %get-tuple-element.53), channel_id=1, source_target_pairs={{0,1},{1,0},{2,3},{3,2},{4,5},{5,4},{6,7},{7,6},{8,9},{9,8},{10,11... | collective-permute-start | bytes 589832 | tf_op jit(solution)/shard_map/ppermute | solution.py:22
  46.5 8.5 %collective-permute-start.10 = (bf16[48,16,128]{2,1,0:T(8,128)(2,1)S(1)}, bf16[48,16,128]{2,1,0:T(8,128)(2,1)S(1)}, u32[]{:S(2)}, u32[]{:S(2)}) collective-permute-start(bf16[48,16,128]{2,1,0:T(8,128)(2,1)S(1)} %get-tuple-element.52), channel_id=1, source_target_pairs={{1,2},{2,1},{5,6},{6,5},{9,10},{10,9},{13,14},{14,13},{17,18},{18,... | collective-permute-start | bytes 589832 | tf_op jit(solution)/shard_map/ppermute | solution.py:22

commit v8 on v7

--- a/solution.py
+++ b/solution.py
@@ -22,17 +22,12 @@
     return lax.ppermute(value, "space", pairs)
 
 
-def shift_order(count):
-    return (2, 1, 3) if count == 4 else tuple(range(1, count))
-
-
 def earlier(value):
     count = lax.axis_size("tm")
-    shifts = shift_order(count)
     if count <= 8:
-        return [lax.ppermute(value, "tm", [(i, i + s) for i in range(count - s)]) for s in shifts]
+        return [lax.ppermute(value, "tm", [(i, i + s) for i in range(count - s)]) for s in range(1, count)]
     every = lax.all_gather(value, "tm")
-    at = lax.axis_index("tm") - jnp.array(shifts)
+    at = lax.axis_index("tm") - jnp.arange(1, count)
     picked = jnp.where((at >= 0)[:, None, None], jnp.take(every, jnp.maximum(at, 0), axis=0), 0.0)
     return [picked[s] for s in range(count - 1)]
 
@@ -84,8 +79,7 @@
 
 
 def enter(arrivals, we, pk, y, n):
-    by_shift = dict(zip(shift_order(len(arrivals) + 1), arrivals))
-    value = jnp.concatenate([by_shift[shift][...] for shift in sorted(by_shift)], axis=1)
+    value = jnp.concatenate([a[...] for a in arrivals], axis=1)
     entry = product_rows(split_rows(value), we[...])
     y[pl.ds(0, n, stride=8), :] = entry
     rows = split_rows(entry)
@@ -220,7 +214,7 @@
     return src[pl.ds(base * 8, size * 8), :].astype(F32).reshape(size, 8, 128)
 
 
-def put_tables(fe, got_even, got_odd, idx_v, columns, square, full, n, even):
+def put_tables(fe, got_even, got_odd, idx_v, full, n, even):
     lane = lax.broadcasted_iota(jnp.int32, (8, 128), 1)
 
     def table(ref):
@@ -232,12 +226,13 @@
     for at, offs in ((0, low), (128, high)):
         value = jnp.where(offs != 0.0, lane + at + offs.astype(jnp.int32), full)
         idx_v[:, pl.ds(at, 128)] = value
+
+
+def push_init(init, got_even, got_odd, w, idx_v, columns, square, i16, base, count, n, even):
+    for at in (0, 128):
         square[...] = jnp.zeros_like(square)
-        square[0:8, :] = value.astype(F32)
+        square[0:8, :] = idx_v[:, pl.ds(at, 128)].astype(F32)
         columns[pl.ds(at, 128), :] = square[...].T
-
-
-def push_init(init, got_even, got_odd, w, columns, i16, base, count, n, even):
     i16[...] = jnp.zeros_like(i16)
     lead = init[...].astype(BF16)
     i16[pl.ds(n, n), 0:128] = lead
@@ -257,8 +252,7 @@
         cols.append(jnp.dot(hot, i16[...], preferred_element_type=F32).astype(BF16))
     leads = jnp.concatenate([c[:, 0:128] for c in cols], axis=1)
     rests = jnp.concatenate([c[:, 128:256] for c in cols], axis=1)
-    pushed = product_rows(jnp.concatenate([leads, rests], axis=0), w[...])
-    return pushed * (lax.axis_index("tm") == 0).astype(F32)
+    return product_rows(jnp.concatenate([leads, rests], axis=0), w[...])
 
 
 STRIPS = (5 * REACH, 4 * REACH, 3 * REACH)
@@ -282,15 +276,19 @@
     def body(even):
         n = init.shape[0]
         full = 3 * n
-        put_tables(fe, got, None, idx_v, columns, square, full, n, even)
+        put_tables(fe, got, None, idx_v, full, n, even)
         copy = pltpu.make_async_copy(idx_v, idx, sem)
         copy.start()
         count = 6 * REACH
         base = mirrored(REACH, count, full, even)
-        pushed = push_init(init, got, None, w, columns, i16, base, count, n, even)
         put_force(force, fe, got, even, 0, n)
         y[pl.ds(0, count * 8), :] = force[pl.ds(base * 8, count * 8), :].astype(F32)
-        y[pl.ds(0, count, stride=8), :] = y[pl.ds(0, count, stride=8), :] + pushed
+
+        def add_init():
+            pushed = push_init(init, got, None, w, idx_v, columns, square, i16, base, count, n, even)
+            y[pl.ds(0, count, stride=8), :] = y[pl.ds(0, count, stride=8), :] + pushed
+
+        pl.when(lax.axis_index("tm") == 0)(add_init)
         s1[pl.ds(base, count)] = split(y[pl.ds(0, count * 8), :].reshape(count, 8, 128))
         for state in (s1, s2, s3):
             state[full] = jnp.zeros((16, 128), BF16)
@@ -312,15 +310,19 @@
     def body(even):
         n = init.shape[0]
         full = 3 * n
-        put_tables(fe, got_even, got_odd, idx_out, columns, square, full, n, even)
+        put_tables(fe, got_even, got_odd, idx_out, full, n, even)
         copy = pltpu.make_async_copy(idx_out, idx, sem)
         copy.start()
         count = 4 * REACH
         base = mirrored(7 * REACH, count, full, even)
-        pushed = push_init(init, got_even, got_odd, w, columns, i16, base, count, n, even)
         put_force(force, fe, got_odd, not even, 0, n)
         y[...] = force[pl.ds(base * 8, count * 8), :].astype(F32)
-        y[pl.ds(0, count, stride=8), :] = y[pl.ds(0, count, stride=8), :] + pushed
+
+        def add_init():
+            pushed = push_init(init, got_even, got_odd, w, idx_out, columns, square, i16, base, count, n, even)
+            y[pl.ds(0, count, stride=8), :] = y[pl.ds(0, count, stride=8), :] + pushed
+
+        pl.when(lax.axis_index("tm") == 0)(add_init)
         s1[pl.ds(base, count)] = split(y[...].reshape(count, 8, 128))
         get_strips((strip1, strip2, strip3), (s1, s2, s3), full, even)
         copy.wait()

time: 58.8 us -> 58 us (0.986)
  starting transfers between devices: 30.2 us -> 29.6 us
    ppermute x6, starting transfers between devices: 16.7 us -> 15.8 us  [earlier(): lax.ppermute(value, 'tm', [(i, i + s) for i in range(count - s)])]
  transfers between devices with their start and end apart: 12 -> 12, of which waited for: 3 -> 4; matrix products, arithmetic and copies ran while one was open for 0% -> 0% of each run, Pallas kernels for 22% -> 21%
where the time goes in v8:
time: 58 us; the launch traced here: 57.7 us
  starting transfers between devices  29.6 us (51%)
  Pallas kernels  26.4 us (46%)
  waiting for transfers between devices  1.33 us (2%)
    pallas_call x12, Pallas kernels, call(): pl.pallas_call(kernel, out_shape=outs, name=kernel.__name__, in_specs=spe...  26.4 us
    ppermute x6, starting transfers between devices, earlier(): lax.ppermute(value, 'tm', [(i, i + s) for i in range(count - s)])  15.8 us
    ppermute x6, starting transfers between devices, swapped(): return lax.ppermute(value, 'space', pairs)  13.8 us
  transfers between devices with their start and end apart: 12, of which 4 were waited for; matrix products, arithmetic and copies ran while one was open for 0% of the time, Pallas kernels for 21%

profile of v8, /device:TPU:1, one launch (start us, length us, event | category | flops | bytes accessed | tf_op | source)
XLA Modules:
  0.0 57.7 jit_solution(14123911432889796067)
XLA Ops:
  0.0 2.5 %pack_kernel.1 = (bf16[2064,128]{1,0:T(8,128)(2,1)}, bf16[912,128]{1,0:T(8,128)(2,1)}, bf16[912,128]{1,0:T(8,128)(2,1)}) custom-call(bf16[8,4,64,128]{3,2,1,0:T(8,128)(2,1)} %bitcast.3, f32[64,128]{1,0:T(8,128)} %refs_5_.1, s32[6,64]{1,0:T(8,128)} %bitcast.4, s32[6,64]{1,0:T(8,128)} %bitcast.5), custom_call_target="tpu_custom_call" | custom-call | flops 3000000000 | bytes 1555456 | tf_op jit(solution)/shard_map/pack_kernel/pallas_call | solution.py:494
  2.7 4.6 %collective-permute-start.1 = (bf16[912,128]{1,0:T(8,128)(2,1)}, bf16[912,128]{1,0:T(8,128)(2,1)S(1)}, u32[]{:S(2)}, u32[]{:S(2)}) collective-permute-start(bf16[912,128]{1,0:T(8,128)(2,1)} %get-tuple-element.34), channel_id=1, source_target_pairs={{1,2},{2,1},{5,6},{6,5},{9,10},{10,9},{13,14},{14,13},{17,18},{18,... | collective-permute-start | bytes 700424 | tf_op jit(solution)/shard_map/ppermute | solution.py:22
  7.3 1.5 %weight_kernel.1 = (bf16[896,256]{1,0:T(8,128)(2,1)S(1)}, bf16[1024,256]{1,0:T(8,128)(2,1)S(1)}, bf16[384,256]{1,0:T(8,128)(2,1)S(1)}) custom-call(f32[128,128]{1,0:T(8,128)S(1)} %copy-done.3, f32[6,128,128]{2,1,0:T(8,128)S(1)} %copy-done.2, f32[128,128]{1,0:T(8,128)S(1)} %copy-done.4), custom_call_target="tpu_custom_call" | custom-call | flops 1000000000 | bytes 1703936 | tf_op jit(solution)/shard_map/weight_kernel/pallas_call | solution.py:494
  8.9 1.9 %first_early_kernel.1 = (bf16[32,16,128]{2,1,0:T(8,128)(2,1)S(1)}, bf16[32,16,128]{2,1,0:T(8,128)(2,1)S(1)}, bf16[32,16,128]{2,1,0:T(8,128)(2,1)S(1)}) custom-call(bf16[2064,128]{1,0:T(8,128)(2,1)S(1)} %copy-done, f32[64,128]{1,0:T(8,128)S(1)} %copy-done.1, bf16[912,128]{1,0:T(8,128)(2,1)S(1)} %collective-permute-done.got.got_even.pay, ...), custom_call_target="tpu_custom_call" | custom-call | flops 704643072 | bytes 1646592 | tf_op jit(solution)/shard_map/first_early_kernel/pallas_call | solution.py:494
  10.9 0.4 collective-permute-done.1.got_odd.pay
  11.2 3.2 %first_late_kernel.1 = (f32[64,8,128]{2,1,0:T(8,128)S(1)}, f32[64,128]{1,0:T(8,128)S(1)}, s32[8,256]{1,0:T(8,128)S(1)}) custom-call(bf16[2064,128]{1,0:T(8,128)(2,1)S(1)} %copy-done, f32[64,128]{1,0:T(8,128)S(1)} %copy-done.1, bf16[912,128]{1,0:T(8,128)(2,1)S(1)} %collective-permute-done.got.got_even.pay, ...), custom_call_target="tpu_custom_call" | custom-call | flops 1409286144 | bytes 2707456 | tf_op jit(solution)/shard_map/first_late_kernel/pallas_call | solution.py:494
  14.4 5.8 %collective-permute-start.4 = (f32[64,128]{1,0:T(8,128)S(1)}, f32[64,128]{1,0:T(8,128)S(1)}, u32[]{:S(2)}, u32[]{:S(2)}) collective-permute-start(f32[64,128]{1,0:T(8,128)S(1)} %get-tuple-element.41), channel_id=1, source_target_pairs={{0,12},{1,13},{2,14},{3,15},{16,28},{17,29},{18,30},{19,31}} | collective-permute-start | bytes 98312 | tf_op jit(solution)/shard_map/ppermute | solution.py:28
  20.3 1.3 %collective-permute-start.3 = (f32[64,128]{1,0:T(8,128)S(1)}, f32[64,128]{1,0:T(8,128)S(1)}, u32[]{:S(2)}, u32[]{:S(2)}) collective-permute-start(f32[64,128]{1,0:T(8,128)S(1)} %get-tuple-element.41), channel_id=1, source_target_pairs={{0,8},{4,12},{1,9},{5,13},{2,10},{6,14},{3,11},{7,15},{16,24},{20,... | collective-permute-start | bytes 98312 | tf_op jit(solution)/shard_map/ppermute | solution.py:28
  21.6 2.2 %collective-permute-start.2 = (f32[64,128]{1,0:T(8,128)S(1)}, f32[64,128]{1,0:T(8,128)S(1)}, u32[]{:S(2)}, u32[]{:S(2)}) collective-permute-start(f32[64,128]{1,0:T(8,128)S(1)} %get-tuple-element.41), channel_id=1, source_target_pairs={{0,4},{4,8},{8,12},{1,5},{5,9},{9,13},{2,6},{6,10},{10,14},{3,7},{... | collective-permute-start | bytes 98312 | tf_op jit(solution)/shard_map/ppermute | solution.py:28
  23.7 0.7 %scan_kernel.1.refs_3_ = f32[64,8,128]{2,1,0:T(8,128)S(1)} custom-call(f32[64,8,128]{2,1,0:T(8,128)S(1)} %get-tuple-element.42.values.w1, bf16[1024,256]{1,0:T(8,128)(2,1)S(1)} %get-tuple-element.39.pk.refs_5_.refs_7_), custom_call_target="tpu_custom_call" | custom-call | flops 10000000 | bytes 1048576 | tf_op jit(solution)/shard_map/scan_kernel/pallas_call | solution.py:494
  24.5 0.3 collective-permute-done.2.refs_0_
  24.8 0.6 enter_first_kernel.1.own.refs_4_
  25.4 4.2 %collective-permute-start.5 = (bf16[64,16,128]{2,1,0:T(8,128)(2,1)S(1)}, bf16[64,16,128]{2,1,0:T(8,128)(2,1)S(1)}, u32[]{:S(2)}, u32[]{:S(2)}) collective-permute-start(bf16[64,16,128]{2,1,0:T(8,128)(2,1)S(1)} %enter_first_kernel.1.own.refs_4_), channel_id=1, source_target_pairs={{1,2},{2,1},{5,6},{6,5},{9,10},{10,9},{13,14},{14,13},{17,18},{18,... | collective-permute-start | bytes 786440 | tf_op jit(solution)/shard_map/ppermute | solution.py:22
  29.6 3.5 %second_early_kernel.1 = (bf16[32,16,128]{2,1,0:T(8,128)(2,1)S(1)}, bf16[32,16,128]{2,1,0:T(8,128)(2,1)S(1)}, bf16[32,16,128]{2,1,0:T(8,128)(2,1)S(1)}, f32[64,8,128]{2,1,0:T(8,128)S(1)}) custom-call(s32[8,256]{1,0:T(8,128)S(1)} %get-tuple-element.40.idx, bf16[64,16,128]{2,1,0:T(8,128)(2,1)S(1)} %enter_first_kernel.1.own.refs_4_, ...), custom_call_target="tpu_custom_call" | custom-call | flops 1409286144 | bytes 2170880 | tf_op jit(solution)/shard_map/second_early_kernel/pallas_call | solution.py:494
  33.0 0.6 %collective-permute-done.5.got = bf16[64,16,128]{2,1,0:T(8,128)(2,1)S(1)} collective-permute-done((bf16[64,16,128]{2,1,0:T(8,128)(2,1)S(1)}, bf16[64,16,128]{2,1,0:T(8,128)(2,1)S(1)}, u32[]{:S(2)}, u32[]{:S(2)}) %collective-permute-start.5) | collective-permute-done | bytes 262176 | tf_op jit(solution)/shard_map/ppermute | solution.py:22
  33.6 3.9 %second_late_kernel.1 = (f32[64,8,128]{2,1,0:T(8,128)S(1)}, f32[64,128]{1,0:T(8,128)S(1)}) custom-call(s32[8,256]{1,0:T(8,128)S(1)} %get-tuple-element.40.idx, bf16[64,16,128]{2,1,0:T(8,128)(2,1)S(1)} %enter_first_kernel.1.own.refs_4_, bf16[64,16,128]{2,1,0:T(8,128)(2,1)S(1)} %collective-permute-done.5.got, ...), custom_call_target="tpu_custom_call" | custom-call | flops 1879048192 | bytes 2465792 | tf_op jit(solution)/shard_map/second_late_kernel/pallas_call | solution.py:494
  37.5 2.7 %collective-permute-start.9 = (f32[64,128]{1,0:T(8,128)S(1)}, f32[64,128]{1,0:T(8,128)S(1)}, u32[]{:S(2)}, u32[]{:S(2)}) collective-permute-start(f32[64,128]{1,0:T(8,128)S(1)} %get-tuple-element.48), channel_id=1, source_target_pairs={{0,12},{1,13},{2,14},{3,15},{16,28},{17,29},{18,30},{19,31}} | collective-permute-start | bytes 98312 | tf_op jit(solution)/shard_map/ppermute | solution.py:28
  40.2 1.3 %collective-permute-start.8 = (f32[64,128]{1,0:T(8,128)S(1)}, f32[64,128]{1,0:T(8,128)S(1)}, u32[]{:S(2)}, u32[]{:S(2)}) collective-permute-start(f32[64,128]{1,0:T(8,128)S(1)} %get-tuple-element.48), channel_id=1, source_target_pairs={{0,8},{4,12},{1,9},{5,13},{2,10},{6,14},{3,11},{7,15},{16,24},{20,... | collective-permute-start | bytes 98312 | tf_op jit(solution)/shard_map/ppermute | solution.py:28
  41.6 2.4 %collective-permute-start.7 = (f32[64,128]{1,0:T(8,128)S(1)}, f32[64,128]{1,0:T(8,128)S(1)}, u32[]{:S(2)}, u32[]{:S(2)}) collective-permute-start(f32[64,128]{1,0:T(8,128)S(1)} %get-tuple-element.48), channel_id=1, source_target_pairs={{0,4},{4,8},{8,12},{1,5},{5,9},{9,13},{2,6},{6,10},{10,14},{3,7},{... | collective-permute-start | bytes 98312 | tf_op jit(solution)/shard_map/ppermute | solution.py:28
  44.0 0.7 %scan_sum_kernel.1 = (f32[64,8,128]{2,1,0:T(8,128)S(1)}, f32[64,8,128]{2,1,0:T(8,128)S(1)}) custom-call(f32[64,8,128]{2,1,0:T(8,128)S(1)} %get-tuple-element.49.values, f32[64,8,128]{2,1,0:T(8,128)S(1)} %get-tuple-element.42.values.w1, f32[64,8,128]{2,1,0:T(8,128)S(1)} %get-tuple-element.47.coarse, bf16[1024,256]{1,0:T(8,128)(2,1)S(1)} %get-tuple-element.39.pk.refs_5_.refs_7_), custom_call_target="tpu_custom_call" | custom-call | flops 10000000 | bytes 1835008 | tf_op jit(solution)/shard_map/scan_sum_kernel/pallas_call | solution.py:494
  44.7 0.6 %enter_second_kernel.1 = (bf16[64,16,128]{2,1,0:T(8,128)(2,1)S(1)}, bf16[48,16,128]{2,1,0:T(8,128)(2,1)S(1)}, bf16[48,16,128]{2,1,0:T(8,128)(2,1)S(1)}, f32[64,8,128]{2,1,0:T(8,128)S(1)}) custom-call(f32[64,128]{1,0:T(8,128)S(1)} %collective-permute-done.7.refs_0_, f32[64,128]{1,0:T(8,128)S(1)} %collective-permute-done.8.refs_1_, ...), custom_call_target="tpu_custom_call" | custom-call | flops 10000000 | bytes 2293760 | tf_op jit(solution)/shard_map/enter_second_kernel/pallas_call | solution.py:494
  45.4 4.8 %collective-permute-start.10 = (bf16[48,16,128]{2,1,0:T(8,128)(2,1)S(1)}, bf16[48,16,128]{2,1,0:T(8,128)(2,1)S(1)}, u32[]{:S(2)}, u32[]{:S(2)}) collective-permute-start(bf16[48,16,128]{2,1,0:T(8,128)(2,1)S(1)} %get-tuple-element.52), channel_id=1, source_target_pairs={{1,2},{2,1},{5,6},{6,5},{9,10},{10,9},{13,14},{14,13},{17,18},{18,... | collective-permute-start | bytes 589832 | tf_op jit(solution)/shard_map/ppermute | solution.py:22
  50.2 4.0 %third_early_kernel.1 = (f32[32,64,128]{2,1,0:T(8,128)}, bf16[32,16,128]{2,1,0:T(8,128)(2,1)S(1)}, bf16[32,16,128]{2,1,0:T(8,128)(2,1)S(1)}) custom-call(s32[8,256]{1,0:T(8,128)S(1)} %get-tuple-element.40.idx, bf16[64,16,128]{2,1,0:T(8,128)(2,1)S(1)} %get-tuple-element.51.own, bf16[48,16,128]{2,1,0:T(8,128)(2,1)S(1)} %collective-permute-done.11.got, ...), custom_call_target="tpu_custom_call" | custom-call | flops 1056964608 | bytes 4046848 | tf_op jit(solution)/shard_map/third_early_kernel/pallas_call | solution.py:494
  54.2 3.3 %third_late_kernel.1 = f32[32,64,128]{2,1,0:T(8,128)} custom-call(s32[8,256]{1,0:T(8,128)S(1)} %get-tuple-element.40.idx, bf16[64,16,128]{2,1,0:T(8,128)(2,1)S(1)} %get-tuple-element.51.own, bf16[48,16,128]{2,1,0:T(8,128)(2,1)S(1)} %collective-permute-done.10.got, bf16[32,16,128]{2,1,0:T(8,128)(2,1)S(1)} %get-tuple-element.56.strip1, ...), custom_call_target="tpu_custom_call", output_to_operand_aliasing={{}: (8, {})} | custom-call | flops 1056964608 | bytes 4046848 | tf_op jit(solution)/shard_map/third_late_kernel/pallas_call | solution.py:494
  (22 shorter events, 0.4 us)
Async XLA Ops:
  0.0 7.3 %copy-start.2 = (f32[6,128,128]{2,1,0:T(8,128)S(1)}, f32[6,128,128]{2,1,0:T(8,128)}, u32[]{:S(2)}) copy-start(f32[6,128,128]{2,1,0:T(8,128)} %faces.1) | copy-start | bytes 1179652
  0.0 7.3 %copy-start.3 = (f32[128,128]{1,0:T(8,128)S(1)}, f32[128,128]{1,0:T(8,128)}, u32[]{:S(2)}) copy-start(f32[128,128]{1,0:T(8,128)} %diag.1) | copy-start | bytes 196612
  0.0 7.3 %copy-start.4 = (f32[128,128]{1,0:T(8,128)S(1)}, f32[128,128]{1,0:T(8,128)}, u32[]{:S(2)}) copy-start(f32[128,128]{1,0:T(8,128)} %coarse.1) | copy-start | bytes 196612
  2.5 6.3 %collective-permute-start = (bf16[912,128]{1,0:T(8,128)(2,1)}, bf16[912,128]{1,0:T(8,128)(2,1)S(1)}, u32[]{:S(2)}, u32[]{:S(2)}) collective-permute-start(bf16[912,128]{1,0:T(8,128)(2,1)} %get-tuple-element.33), channel_id=1, source_target_pairs={{0,1},{1,0},{2,3},{3,2},{4,5},{5,4},{6,7},{7,6},{8,9},{9,8},{10,11... | collective-permute-start | bytes 700424 | tf_op jit(solution)/shard_map/ppermute | solution.py:22
  2.7 6.2 %copy-start = (bf16[2064,128]{1,0:T(8,128)(2,1)S(1)}, bf16[2064,128]{1,0:T(8,128)(2,1)}, u32[]{:S(2)}) copy-start(bf16[2064,128]{1,0:T(8,128)(2,1)} %get-tuple-element.32.fe) | copy-start | bytes 1585156
  2.7 6.2 %copy-start.1 = (f32[64,128]{1,0:T(8,128)S(1)}, f32[64,128]{1,0:T(8,128)}, u32[]{:S(2)}) copy-start(f32[64,128]{1,0:T(8,128)} %refs_5_.1) | copy-start | bytes 98308
  2.7 8.6 %collective-permute-start.1 = (bf16[912,128]{1,0:T(8,128)(2,1)}, bf16[912,128]{1,0:T(8,128)(2,1)S(1)}, u32[]{:S(2)}, u32[]{:S(2)}) collective-permute-start(bf16[912,128]{1,0:T(8,128)(2,1)} %get-tuple-element.34), channel_id=1, source_target_pairs={{1,2},{2,1},{5,6},{6,5},{9,10},{10,9},{13,14},{14,13},{17,18},{18,... | collective-permute-start | bytes 700424 | tf_op jit(solution)/shard_map/ppermute | solution.py:22
  14.4 10.0 %collective-permute-start.4 = (f32[64,128]{1,0:T(8,128)S(1)}, f32[64,128]{1,0:T(8,128)S(1)}, u32[]{:S(2)}, u32[]{:S(2)}) collective-permute-start(f32[64,128]{1,0:T(8,128)S(1)} %get-tuple-element.41), channel_id=1, source_target_pairs={{0,12},{1,13},{2,14},{3,15},{16,28},{17,29},{18,30},{19,31}} | collective-permute-start | bytes 98312 | tf_op jit(solution)/shard_map/ppermute | solution.py:28
  20.3 4.2 %collective-permute-start.3 = (f32[64,128]{1,0:T(8,128)S(1)}, f32[64,128]{1,0:T(8,128)S(1)}, u32[]{:S(2)}, u32[]{:S(2)}) collective-permute-start(f32[64,128]{1,0:T(8,128)S(1)} %get-tuple-element.41), channel_id=1, source_target_pairs={{0,8},{4,12},{1,9},{5,13},{2,10},{6,14},{3,11},{7,15},{16,24},{20,... | collective-permute-start | bytes 98312 | tf_op jit(solution)/shard_map/ppermute | solution.py:28
  21.6 3.2 %collective-permute-start.2 = (f32[64,128]{1,0:T(8,128)S(1)}, f32[64,128]{1,0:T(8,128)S(1)}, u32[]{:S(2)}, u32[]{:S(2)}) collective-permute-start(f32[64,128]{1,0:T(8,128)S(1)} %get-tuple-element.41), channel_id=1, source_target_pairs={{0,4},{4,8},{8,12},{1,5},{5,9},{9,13},{2,6},{6,10},{10,14},{3,7},{... | collective-permute-start | bytes 98312 | tf_op jit(solution)/shard_map/ppermute | solution.py:28
  25.3 4.3 %collective-permute-start.6 = (bf16[64,16,128]{2,1,0:T(8,128)(2,1)S(1)}, bf16[64,16,128]{2,1,0:T(8,128)(2,1)S(1)}, u32[]{:S(2)}, u32[]{:S(2)}) collective-permute-start(bf16[64,16,128]{2,1,0:T(8,128)(2,1)S(1)} %enter_first_kernel.1.own.refs_4_), channel_id=1, source_target_pairs={{0,1},{1,0},{2,3},{3,2},{4,5},{5,4},{6,7},{7,6},{8,9},{9,8},{10,11... | collective-permute-start | bytes 786440 | tf_op jit(solution)/shard_map/ppermute | solution.py:22
  25.4 8.2 %collective-permute-start.5 = (bf16[64,16,128]{2,1,0:T(8,128)(2,1)S(1)}, bf16[64,16,128]{2,1,0:T(8,128)(2,1)S(1)}, u32[]{:S(2)}, u32[]{:S(2)}) collective-permute-start(bf16[64,16,128]{2,1,0:T(8,128)(2,1)S(1)} %enter_first_kernel.1.own.refs_4_), channel_id=1, source_target_pairs={{1,2},{2,1},{5,6},{6,5},{9,10},{10,9},{13,14},{14,13},{17,18},{18,... | collective-permute-start | bytes 786440 | tf_op jit(solution)/shard_map/ppermute | solution.py:22
  37.5 7.2 %collective-permute-start.9 = (f32[64,128]{1,0:T(8,128)S(1)}, f32[64,128]{1,0:T(8,128)S(1)}, u32[]{:S(2)}, u32[]{:S(2)}) collective-permute-start(f32[64,128]{1,0:T(8,128)S(1)} %get-tuple-element.48), channel_id=1, source_target_pairs={{0,12},{1,13},{2,14},{3,15},{16,28},{17,29},{18,30},{19,31}} | collective-permute-start | bytes 98312 | tf_op jit(solution)/shard_map/ppermute | solution.py:28
  40.2 4.4 %collective-permute-start.8 = (f32[64,128]{1,0:T(8,128)S(1)}, f32[64,128]{1,0:T(8,128)S(1)}, u32[]{:S(2)}, u32[]{:S(2)}) collective-permute-start(f32[64,128]{1,0:T(8,128)S(1)} %get-tuple-element.48), channel_id=1, source_target_pairs={{0,8},{4,12},{1,9},{5,13},{2,10},{6,14},{3,11},{7,15},{16,24},{20,... | collective-permute-start | bytes 98312 | tf_op jit(solution)/shard_map/ppermute | solution.py:28
  41.6 3.2 %collective-permute-start.7 = (f32[64,128]{1,0:T(8,128)S(1)}, f32[64,128]{1,0:T(8,128)S(1)}, u32[]{:S(2)}, u32[]{:S(2)}) collective-permute-start(f32[64,128]{1,0:T(8,128)S(1)} %get-tuple-element.48), channel_id=1, source_target_pairs={{0,4},{4,8},{8,12},{1,5},{5,9},{9,13},{2,6},{6,10},{10,14},{3,7},{... | collective-permute-start | bytes 98312 | tf_op jit(solution)/shard_map/ppermute | solution.py:28
  45.4 4.9 %collective-permute-start.11 = (bf16[48,16,128]{2,1,0:T(8,128)(2,1)S(1)}, bf16[48,16,128]{2,1,0:T(8,128)(2,1)S(1)}, u32[]{:S(2)}, u32[]{:S(2)}) collective-permute-start(bf16[48,16,128]{2,1,0:T(8,128)(2,1)S(1)} %get-tuple-element.53), channel_id=1, source_target_pairs={{0,1},{1,0},{2,3},{3,2},{4,5},{5,4},{6,7},{7,6},{8,9},{9,8},{10,11... | collective-permute-start | bytes 589832 | tf_op jit(solution)/shard_map/ppermute | solution.py:22
  45.4 8.8 %collective-permute-start.10 = (bf16[48,16,128]{2,1,0:T(8,128)(2,1)S(1)}, bf16[48,16,128]{2,1,0:T(8,128)(2,1)S(1)}, u32[]{:S(2)}, u32[]{:S(2)}) collective-permute-start(bf16[48,16,128]{2,1,0:T(8,128)(2,1)S(1)} %get-tuple-element.52), channel_id=1, source_target_pairs={{1,2},{2,1},{5,6},{6,5},{9,10},{10,9},{13,14},{14,13},{17,18},{18,... | collective-permute-start | bytes 589832 | tf_op jit(solution)/shard_map/ppermute | solution.py:22

commit v9 on v8

--- a/solution.py
+++ b/solution.py
@@ -92,6 +92,7 @@
     cols = [src[pl.ds(base, size)].reshape(size * 16, 128)]
     for f in range(6):
         cols.append(jnp.concatenate([src[idx[f, base + e]] for e in range(size)], axis=0))
+    cols.append(cols[0])
     return product(jnp.concatenate(cols, axis=1), w[...])
 
 
@@ -172,6 +173,7 @@
     put_halves(w.at[pl.ds(0, 128)], diag[...].T)
     for f in range(6):
         put_halves(w.at[pl.ds(128 * (f + 1), 128)], faces[f].T)
+    w[pl.ds(128 * 7, 128), :] = jnp.zeros((128, 256), BF16)
 
     def thirds(a):
         one = a.astype(BF16)
@@ -252,7 +254,7 @@
         cols.append(jnp.dot(hot, i16[...], preferred_element_type=F32).astype(BF16))
     leads = jnp.concatenate([c[:, 0:128] for c in cols], axis=1)
     rests = jnp.concatenate([c[:, 128:256] for c in cols], axis=1)
-    return product_rows(jnp.concatenate([leads, rests], axis=0), w[...])
+    return product_rows(jnp.concatenate([leads, rests], axis=0), w[pl.ds(0, 7 * 128), :])
 
 
 STRIPS = (5 * REACH, 4 * REACH, 3 * REACH)
@@ -349,10 +351,34 @@
     total[...] = values[...] + (w1[...] + coarse[...])
 
 
+NEAR = 2 * REACH
+
+
+def put_pay(pay, state, value, side, n):
+    def body(even):
+        near = 0 if even else n - NEAR
+        far = NEAR if even else n - side
+        pay[pl.ds(0, NEAR)] = state[pl.ds(near, NEAR)]
+        count = side - NEAR
+        pay[pl.ds(NEAR, count // 2)] = value[far : far + count].reshape(count // 2, 16, 128).astype(BF16)
+
+    by_parity(body)
+
+
+def put_far(dst, got, right, n):
+    count = 2 * (got.shape[0] - NEAR)
+    dst[pl.ds(2 * n if right else n - NEAR, NEAR)] = got[pl.ds(0, NEAR)]
+    leads = got[pl.ds(NEAR, count // 2)].astype(F32).reshape(count, 8, 128)
+    far = jnp.concatenate([leads, jnp.zeros_like(leads)], axis=1).astype(BF16)
+    dst[pl.ds(2 * n + NEAR if right else n - NEAR - count, count)] = far
+
+
 def enter_first_kernel(*refs):
-    *arrivals, starts, we, pk, state, y = refs
+    *arrivals, starts, we, pk, state, pay_odd, y = refs
     n = starts.shape[0]
-    state[...] = split(enter(arrivals, we, pk, y, n) + starts[...])
+    value = enter(arrivals, we, pk, y, n) + starts[...]
+    state[...] = split(value)
+    put_pay(pay_odd, state, value, n, n)
 
 
 def enter_second_kernel(*refs):
@@ -364,18 +390,22 @@
     y[...] = (value + (old[:, 0:8] + old[:, 8:16])).reshape(n * 8, 128)
     first = (lax.axis_index("tm") == 0).astype(F32)
     y[pl.ds(0, n, stride=8), :] = y[pl.ds(0, n, stride=8), :] + init[...] * first
-    state[...] = split(y[...].reshape(n, 8, 128))
+    value = y[...].reshape(n, 8, 128)
+    state[...] = split(value)
     side = (COARSEN - 1) * REACH
-    even = even_place()
-    pay_even[...] = state[pl.ds(jnp.where(even, n - side, 0), side)]
-    pay_odd[...] = state[pl.ds(jnp.where(even, 0, n - side), side)]
+    pay_even[...] = state[pl.ds(jnp.where(even_place(), n - side, 0), side)]
+    put_pay(pay_odd, state, value, side, n)
+
+
+def put_own(dst, own, n):
+    dst[pl.ds(n, n)] = own[...]
+    dst[3 * n] = jnp.zeros((16, 128), BF16)
 
 
 def put_block(dst, own, got, right, n):
     side = got.shape[0]
-    dst[pl.ds(n, n)] = own[...]
+    put_own(dst, own, n)
     dst[pl.ds(2 * n if right else n - side, side)] = got[...]
-    dst[3 * n] = jnp.zeros((16, 128), BF16)
 
 
 def second_early_kernel(idx, own, got, w, pk, strip1, strip2, strip3, coarse, s0, s1, s2, s3):
@@ -399,7 +429,8 @@
     def body(even):
         n = own.shape[0]
         full = 3 * n
-        put_block(s0, own, got, not even, n)
+        put_own(s0, own, n)
+        put_far(s0, got, not even, n)
         get_strips((strip1, strip2, strip3), (s1, s2, s3), full, even)
         count = 4 * REACH
         for k, src, dst in ((1, s0, s1), (2, s1, s2), (3, s2, s3)):
@@ -464,7 +495,8 @@
     def body(even):
         n = own.shape[0]
         full = 3 * n
-        put_block(s0, own, got, not even, n)
+        put_own(s0, own, n)
+        put_far(s0, got, not even, n)
         get_strips((strip1, strip2), (s1, s2), full, even)
         copies = []
         size = 3 * REACH
@@ -546,7 +578,7 @@
         weight_kernel,
         (diag_block, face_blocks, coarse_block),
         (
-            shape((7 * width, 2 * width), BF16),
+            shape((8 * width, 2 * width), BF16),
             shape((8 * width, 2 * width), BF16),
             shape(((tm - 1) * width, 2 * width), BF16),
         ),
@@ -575,8 +607,11 @@
     )
     arrivals = earlier(end)
     (starts,) = call(scan_kernel, (w1, pk), (tiles,), [])
-    (coarse,) = call(enter_first_kernel, (*arrivals, starts, we, pk), (state,), [rows])
-    got_odd, got_even = swapped(coarse, 1), swapped(coarse, 0)
+    def across(side):
+        return shape((NEAR + (side - NEAR) // 2, 16, width), BF16)
+
+    coarse, end_odd = call(enter_first_kernel, (*arrivals, starts, we, pk), (state, across(n)), [rows])
+    got_odd, got_even = swapped(end_odd, 1), swapped(coarse, 0)
     *strips, moved = call(
         second_early_kernel,
         (idx, coarse, got_even, w, pk),
@@ -595,11 +630,11 @@
     )
     arrivals = earlier(end)
     starts, total = call(scan_sum_kernel, (res, w1, moved, pk), (tiles, tiles), [])
-    side = shape(((COARSEN - 1) * REACH, 16, width), BF16)
+    side = (COARSEN - 1) * REACH
     coarse, end_even, end_odd, corr = call(
         enter_second_kernel,
         (*arrivals, starts, coarse, initial_state, we, pk),
-        (state, side, side, tiles),
+        (state, shape((side, 16, width), BF16), across(side), tiles),
         [rows],
     )
     got_odd, got_even = swapped(end_odd, 1), swapped(end_even, 0)

time: 58 us -> 57.4 us (0.990)
  waiting for transfers between devices: 1.33 us -> 0.74 us
    ppermute x6, waiting for transfers between devices: 0.98 us -> 0.39 us  [swapped(): return lax.ppermute(value, 'space', pairs)]
  transfers between devices with their start and end apart: 12 -> 12, of which waited for: 4 -> 3; matrix products, arithmetic and copies ran while one was open for 0% -> 0% of each run, Pallas kernels for 21% -> 22%
where the time goes in v9:
time: 57.4 us; the launch traced here: 57.1 us
  starting transfers between devices  29.4 us (51%)
  Pallas kernels  26.4 us (46%)
  waiting for transfers between devices  0.74 us (1%)
    pallas_call x12, Pallas kernels, call(): pl.pallas_call(kernel, out_shape=outs, name=kernel.__name__, in_specs=spe...  26.4 us
    ppermute x6, starting transfers between devices, earlier(): lax.ppermute(value, 'tm', [(i, i + s) for i in range(count - s)])  15.8 us
    ppermute x6, starting transfers between devices, swapped(): return lax.ppermute(value, 'space', pairs)  13.7 us
  transfers between devices with their start and end apart: 12, of which 3 were waited for; matrix products, arithmetic and copies ran while one was open for 0% of the time, Pallas kernels for 22%

profile of v9, /device:TPU:1, one launch (start us, length us, event | category | flops | bytes accessed | tf_op | source)
XLA Modules:
  0.0 57.1 jit_solution(10449442210374775919)
XLA Ops:
  0.0 2.5 %pack_kernel.1 = (bf16[2064,128]{1,0:T(8,128)(2,1)}, bf16[912,128]{1,0:T(8,128)(2,1)}, bf16[912,128]{1,0:T(8,128)(2,1)}) custom-call(bf16[8,4,64,128]{3,2,1,0:T(8,128)(2,1)} %bitcast.3, f32[64,128]{1,0:T(8,128)} %refs_5_.1, s32[6,64]{1,0:T(8,128)} %bitcast.4, s32[6,64]{1,0:T(8,128)} %bitcast.5), custom_call_target="tpu_custom_call" | custom-call | flops 3000000000 | bytes 1555456 | tf_op jit(solution)/shard_map/pack_kernel/pallas_call | solution.py:526
  2.5 0.1 collective-permute-start
  2.7 4.6 %collective-permute-start.1 = (bf16[912,128]{1,0:T(8,128)(2,1)}, bf16[912,128]{1,0:T(8,128)(2,1)S(1)}, u32[]{:S(2)}, u32[]{:S(2)}) collective-permute-start(bf16[912,128]{1,0:T(8,128)(2,1)} %get-tuple-element.36), channel_id=1, source_target_pairs={{1,2},{2,1},{5,6},{6,5},{9,10},{10,9},{13,14},{14,13},{17,18},{18,... | collective-permute-start | bytes 700424 | tf_op jit(solution)/shard_map/ppermute | solution.py:22
  7.3 1.5 %weight_kernel.1 = (bf16[1024,256]{1,0:T(8,128)(2,1)S(1)}, bf16[1024,256]{1,0:T(8,128)(2,1)S(1)}, bf16[384,256]{1,0:T(8,128)(2,1)S(1)}) custom-call(f32[128,128]{1,0:T(8,128)S(1)} %copy-done.3, f32[6,128,128]{2,1,0:T(8,128)S(1)} %copy-done.2, f32[128,128]{1,0:T(8,128)S(1)} %copy-done.4), custom_call_target="tpu_custom_call" | custom-call | flops 1000000000 | bytes 1769472 | tf_op jit(solution)/shard_map/weight_kernel/pallas_call | solution.py:526
  8.9 1.9 %first_early_kernel.1 = (bf16[32,16,128]{2,1,0:T(8,128)(2,1)S(1)}, bf16[32,16,128]{2,1,0:T(8,128)(2,1)S(1)}, bf16[32,16,128]{2,1,0:T(8,128)(2,1)S(1)}) custom-call(bf16[2064,128]{1,0:T(8,128)(2,1)S(1)} %copy-done, f32[64,128]{1,0:T(8,128)S(1)} %copy-done.1, bf16[912,128]{1,0:T(8,128)(2,1)S(1)} %collective-permute-done.got.got_even.pay, ...), custom_call_target="tpu_custom_call" | custom-call | flops 704643072 | bytes 1712128 | tf_op jit(solution)/shard_map/first_early_kernel/pallas_call | solution.py:526
  10.9 0.4 collective-permute-done.1.got_odd.pay
  11.2 3.2 %first_late_kernel.1 = (f32[64,8,128]{2,1,0:T(8,128)S(1)}, f32[64,128]{1,0:T(8,128)S(1)}, s32[8,256]{1,0:T(8,128)S(1)}) custom-call(bf16[2064,128]{1,0:T(8,128)(2,1)S(1)} %copy-done, f32[64,128]{1,0:T(8,128)S(1)} %copy-done.1, bf16[912,128]{1,0:T(8,128)(2,1)S(1)} %collective-permute-done.got.got_even.pay, ...), custom_call_target="tpu_custom_call" | custom-call | flops 1409286144 | bytes 2772992 | tf_op jit(solution)/shard_map/first_late_kernel/pallas_call | solution.py:526
  14.4 5.8 %collective-permute-start.4 = (f32[64,128]{1,0:T(8,128)S(1)}, f32[64,128]{1,0:T(8,128)S(1)}, u32[]{:S(2)}, u32[]{:S(2)}) collective-permute-start(f32[64,128]{1,0:T(8,128)S(1)} %get-tuple-element.43), channel_id=1, source_target_pairs={{0,12},{1,13},{2,14},{3,15},{16,28},{17,29},{18,30},{19,31}} | collective-permute-start | bytes 98312 | tf_op jit(solution)/shard_map/ppermute | solution.py:28
  20.3 1.3 %collective-permute-start.3 = (f32[64,128]{1,0:T(8,128)S(1)}, f32[64,128]{1,0:T(8,128)S(1)}, u32[]{:S(2)}, u32[]{:S(2)}) collective-permute-start(f32[64,128]{1,0:T(8,128)S(1)} %get-tuple-element.43), channel_id=1, source_target_pairs={{0,8},{4,12},{1,9},{5,13},{2,10},{6,14},{3,11},{7,15},{16,24},{20,... | collective-permute-start | bytes 98312 | tf_op jit(solution)/shard_map/ppermute | solution.py:28
  21.6 2.2 %collective-permute-start.2 = (f32[64,128]{1,0:T(8,128)S(1)}, f32[64,128]{1,0:T(8,128)S(1)}, u32[]{:S(2)}, u32[]{:S(2)}) collective-permute-start(f32[64,128]{1,0:T(8,128)S(1)} %get-tuple-element.43), channel_id=1, source_target_pairs={{0,4},{4,8},{8,12},{1,5},{5,9},{9,13},{2,6},{6,10},{10,14},{3,7},{... | collective-permute-start | bytes 98312 | tf_op jit(solution)/shard_map/ppermute | solution.py:28
  23.8 0.7 %scan_kernel.1.refs_3_ = f32[64,8,128]{2,1,0:T(8,128)S(1)} custom-call(f32[64,8,128]{2,1,0:T(8,128)S(1)} %get-tuple-element.44.values.w1, bf16[1024,256]{1,0:T(8,128)(2,1)S(1)} %get-tuple-element.41.pk.refs_5_.refs_7_), custom_call_target="tpu_custom_call" | custom-call | flops 10000000 | bytes 1048576 | tf_op jit(solution)/shard_map/scan_kernel/pallas_call | solution.py:526
  24.5 0.3 collective-permute-done.2.refs_0_
  24.8 0.6 enter_first_kernel.1
  25.4 4.2 %collective-permute-start.5 = (bf16[48,16,128]{2,1,0:T(8,128)(2,1)S(1)}, bf16[48,16,128]{2,1,0:T(8,128)(2,1)S(1)}, u32[]{:S(2)}, u32[]{:S(2)}) collective-permute-start(bf16[48,16,128]{2,1,0:T(8,128)(2,1)S(1)} %get-tuple-element.47), channel_id=1, source_target_pairs={{1,2},{2,1},{5,6},{6,5},{9,10},{10,9},{13,14},{14,13},{17,18},{18,... | collective-permute-start | bytes 589832 | tf_op jit(solution)/shard_map/ppermute | solution.py:22
  29.6 3.5 %second_early_kernel.1 = (bf16[32,16,128]{2,1,0:T(8,128)(2,1)S(1)}, bf16[32,16,128]{2,1,0:T(8,128)(2,1)S(1)}, bf16[32,16,128]{2,1,0:T(8,128)(2,1)S(1)}, f32[64,8,128]{2,1,0:T(8,128)S(1)}) custom-call(s32[8,256]{1,0:T(8,128)S(1)} %get-tuple-element.42.idx, bf16[64,16,128]{2,1,0:T(8,128)(2,1)S(1)} %get-tuple-element.46.own.refs_4_, ...), custom_call_target="tpu_custom_call" | custom-call | flops 1409286144 | bytes 2236416 | tf_op jit(solution)/shard_map/second_early_kernel/pallas_call | solution.py:526
  33.1 3.9 %second_late_kernel.1 = (f32[64,8,128]{2,1,0:T(8,128)S(1)}, f32[64,128]{1,0:T(8,128)S(1)}) custom-call(s32[8,256]{1,0:T(8,128)S(1)} %get-tuple-element.42.idx, bf16[64,16,128]{2,1,0:T(8,128)(2,1)S(1)} %get-tuple-element.46.own.refs_4_, bf16[48,16,128]{2,1,0:T(8,128)(2,1)S(1)} %collective-permute-done.5.got, ...), custom_call_target="tpu_custom_call" | custom-call | flops 1879048192 | bytes 2465792 | tf_op jit(solution)/shard_map/second_late_kernel/pallas_call | solution.py:526
  36.9 2.8 %collective-permute-start.9 = (f32[64,128]{1,0:T(8,128)S(1)}, f32[64,128]{1,0:T(8,128)S(1)}, u32[]{:S(2)}, u32[]{:S(2)}) collective-permute-start(f32[64,128]{1,0:T(8,128)S(1)} %get-tuple-element.52), channel_id=1, source_target_pairs={{0,12},{1,13},{2,14},{3,15},{16,28},{17,29},{18,30},{19,31}} | collective-permute-start | bytes 98312 | tf_op jit(solution)/shard_map/ppermute | solution.py:28
  39.7 1.3 %collective-permute-start.8 = (f32[64,128]{1,0:T(8,128)S(1)}, f32[64,128]{1,0:T(8,128)S(1)}, u32[]{:S(2)}, u32[]{:S(2)}) collective-permute-start(f32[64,128]{1,0:T(8,128)S(1)} %get-tuple-element.52), channel_id=1, source_target_pairs={{0,8},{4,12},{1,9},{5,13},{2,10},{6,14},{3,11},{7,15},{16,24},{20,... | collective-permute-start | bytes 98312 | tf_op jit(solution)/shard_map/ppermute | solution.py:28
  41.0 2.4 %collective-permute-start.7 = (f32[64,128]{1,0:T(8,128)S(1)}, f32[64,128]{1,0:T(8,128)S(1)}, u32[]{:S(2)}, u32[]{:S(2)}) collective-permute-start(f32[64,128]{1,0:T(8,128)S(1)} %get-tuple-element.52), channel_id=1, source_target_pairs={{0,4},{4,8},{8,12},{1,5},{5,9},{9,13},{2,6},{6,10},{10,14},{3,7},{... | collective-permute-start | bytes 98312 | tf_op jit(solution)/shard_map/ppermute | solution.py:28
  43.4 0.7 %scan_sum_kernel.1 = (f32[64,8,128]{2,1,0:T(8,128)S(1)}, f32[64,8,128]{2,1,0:T(8,128)S(1)}) custom-call(f32[64,8,128]{2,1,0:T(8,128)S(1)} %get-tuple-element.53.values, f32[64,8,128]{2,1,0:T(8,128)S(1)} %get-tuple-element.44.values.w1, f32[64,8,128]{2,1,0:T(8,128)S(1)} %get-tuple-element.51.coarse, bf16[1024,256]{1,0:T(8,128)(2,1)S(1)} %get-tuple-element.41.pk.refs_5_.refs_7_), custom_call_target="tpu_custom_call" | custom-call | flops 10000000 | bytes 1835008 | tf_op jit(solution)/shard_map/scan_sum_kernel/pallas_call | solution.py:526
  44.2 0.6 %enter_second_kernel.1 = (bf16[64,16,128]{2,1,0:T(8,128)(2,1)S(1)}, bf16[48,16,128]{2,1,0:T(8,128)(2,1)S(1)}, bf16[40,16,128]{2,1,0:T(8,128)(2,1)S(1)}, f32[64,8,128]{2,1,0:T(8,128)S(1)}) custom-call(f32[64,128]{1,0:T(8,128)S(1)} %collective-permute-done.7.refs_0_, f32[64,128]{1,0:T(8,128)S(1)} %collective-permute-done.8.refs_1_, ...), custom_call_target="tpu_custom_call" | custom-call | flops 10000000 | bytes 2260992 | tf_op jit(solution)/shard_map/enter_second_kernel/pallas_call | solution.py:526
  44.9 4.6 %collective-permute-start.10 = (bf16[40,16,128]{2,1,0:T(8,128)(2,1)S(1)}, bf16[40,16,128]{2,1,0:T(8,128)(2,1)S(1)}, u32[]{:S(2)}, u32[]{:S(2)}) collective-permute-start(bf16[40,16,128]{2,1,0:T(8,128)(2,1)S(1)} %get-tuple-element.56), channel_id=1, source_target_pairs={{1,2},{2,1},{5,6},{6,5},{9,10},{10,9},{13,14},{14,13},{17,18},{18,... | collective-permute-start | bytes 491528 | tf_op jit(solution)/shard_map/ppermute | solution.py:22
  49.6 4.0 %third_early_kernel.1 = (f32[32,64,128]{2,1,0:T(8,128)}, bf16[32,16,128]{2,1,0:T(8,128)(2,1)S(1)}, bf16[32,16,128]{2,1,0:T(8,128)(2,1)S(1)}) custom-call(s32[8,256]{1,0:T(8,128)S(1)} %get-tuple-element.42.idx, bf16[64,16,128]{2,1,0:T(8,128)(2,1)S(1)} %get-tuple-element.55.own, bf16[48,16,128]{2,1,0:T(8,128)(2,1)S(1)} %collective-permute-done.11.got, ...), custom_call_target="tpu_custom_call" | custom-call | flops 1056964608 | bytes 4112384 | tf_op jit(solution)/shard_map/third_early_kernel/pallas_call | solution.py:526
  53.6 3.3 %third_late_kernel.1 = f32[32,64,128]{2,1,0:T(8,128)} custom-call(s32[8,256]{1,0:T(8,128)S(1)} %get-tuple-element.42.idx, bf16[64,16,128]{2,1,0:T(8,128)(2,1)S(1)} %get-tuple-element.55.own, bf16[40,16,128]{2,1,0:T(8,128)(2,1)S(1)} %collective-permute-done.10.got, bf16[32,16,128]{2,1,0:T(8,128)(2,1)S(1)} %get-tuple-element.60.strip1, ...), custom_call_target="tpu_custom_call", output_to_operand_aliasing={{}: (8, {})} | custom-call | flops 1056964608 | bytes 4079616 | tf_op jit(solution)/shard_map/third_late_kernel/pallas_call | solution.py:526
  (22 shorter events, 0.2 us)
Async XLA Ops:
  0.0 7.3 %copy-start.2 = (f32[6,128,128]{2,1,0:T(8,128)S(1)}, f32[6,128,128]{2,1,0:T(8,128)}, u32[]{:S(2)}) copy-start(f32[6,128,128]{2,1,0:T(8,128)} %faces.1) | copy-start | bytes 1179652
  0.0 7.3 %copy-start.3 = (f32[128,128]{1,0:T(8,128)S(1)}, f32[128,128]{1,0:T(8,128)}, u32[]{:S(2)}) copy-start(f32[128,128]{1,0:T(8,128)} %diag.1) | copy-start | bytes 196612
  0.0 7.3 %copy-start.4 = (f32[128,128]{1,0:T(8,128)S(1)}, f32[128,128]{1,0:T(8,128)}, u32[]{:S(2)}) copy-start(f32[128,128]{1,0:T(8,128)} %coarse.1) | copy-start | bytes 196612
  2.5 6.3 %collective-permute-start = (bf16[912,128]{1,0:T(8,128)(2,1)}, bf16[912,128]{1,0:T(8,128)(2,1)S(1)}, u32[]{:S(2)}, u32[]{:S(2)}) collective-permute-start(bf16[912,128]{1,0:T(8,128)(2,1)} %get-tuple-element.35), channel_id=1, source_target_pairs={{0,1},{1,0},{2,3},{3,2},{4,5},{5,4},{6,7},{7,6},{8,9},{9,8},{10,11... | collective-permute-start | bytes 700424 | tf_op jit(solution)/shard_map/ppermute | solution.py:22
  2.7 6.2 %copy-start = (bf16[2064,128]{1,0:T(8,128)(2,1)S(1)}, bf16[2064,128]{1,0:T(8,128)(2,1)}, u32[]{:S(2)}) copy-start(bf16[2064,128]{1,0:T(8,128)(2,1)} %get-tuple-element.34.fe) | copy-start | bytes 1585156
  2.7 6.2 %copy-start.1 = (f32[64,128]{1,0:T(8,128)S(1)}, f32[64,128]{1,0:T(8,128)}, u32[]{:S(2)}) copy-start(f32[64,128]{1,0:T(8,128)} %refs_5_.1) | copy-start | bytes 98308
  2.7 8.6 %collective-permute-start.1 = (bf16[912,128]{1,0:T(8,128)(2,1)}, bf16[912,128]{1,0:T(8,128)(2,1)S(1)}, u32[]{:S(2)}, u32[]{:S(2)}) collective-permute-start(bf16[912,128]{1,0:T(8,128)(2,1)} %get-tuple-element.36), channel_id=1, source_target_pairs={{1,2},{2,1},{5,6},{6,5},{9,10},{10,9},{13,14},{14,13},{17,18},{18,... | collective-permute-start | bytes 700424 | tf_op jit(solution)/shard_map/ppermute | solution.py:22
  14.4 10.0 %collective-permute-start.4 = (f32[64,128]{1,0:T(8,128)S(1)}, f32[64,128]{1,0:T(8,128)S(1)}, u32[]{:S(2)}, u32[]{:S(2)}) collective-permute-start(f32[64,128]{1,0:T(8,128)S(1)} %get-tuple-element.43), channel_id=1, source_target_pairs={{0,12},{1,13},{2,14},{3,15},{16,28},{17,29},{18,30},{19,31}} | collective-permute-start | bytes 98312 | tf_op jit(solution)/shard_map/ppermute | solution.py:28
  20.3 4.2 %collective-permute-start.3 = (f32[64,128]{1,0:T(8,128)S(1)}, f32[64,128]{1,0:T(8,128)S(1)}, u32[]{:S(2)}, u32[]{:S(2)}) collective-permute-start(f32[64,128]{1,0:T(8,128)S(1)} %get-tuple-element.43), channel_id=1, source_target_pairs={{0,8},{4,12},{1,9},{5,13},{2,10},{6,14},{3,11},{7,15},{16,24},{20,... | collective-permute-start | bytes 98312 | tf_op jit(solution)/shard_map/ppermute | solution.py:28
  21.6 3.2 %collective-permute-start.2 = (f32[64,128]{1,0:T(8,128)S(1)}, f32[64,128]{1,0:T(8,128)S(1)}, u32[]{:S(2)}, u32[]{:S(2)}) collective-permute-start(f32[64,128]{1,0:T(8,128)S(1)} %get-tuple-element.43), channel_id=1, source_target_pairs={{0,4},{4,8},{8,12},{1,5},{5,9},{9,13},{2,6},{6,10},{10,14},{3,7},{... | collective-permute-start | bytes 98312 | tf_op jit(solution)/shard_map/ppermute | solution.py:28
  25.3 4.2 %collective-permute-start.6 = (bf16[64,16,128]{2,1,0:T(8,128)(2,1)S(1)}, bf16[64,16,128]{2,1,0:T(8,128)(2,1)S(1)}, u32[]{:S(2)}, u32[]{:S(2)}) collective-permute-start(bf16[64,16,128]{2,1,0:T(8,128)(2,1)S(1)} %get-tuple-element.46.own.refs_4_), channel_id=1, source_target_pairs={{0,1},{1,0},{2,3},{3,2},{4,5},{5,4},{6,7},{7,6},{8,9},{9,8},{10,11... | collective-permute-start | bytes 786440 | tf_op jit(solution)/shard_map/ppermute | solution.py:22
  25.4 7.6 %collective-permute-start.5 = (bf16[48,16,128]{2,1,0:T(8,128)(2,1)S(1)}, bf16[48,16,128]{2,1,0:T(8,128)(2,1)S(1)}, u32[]{:S(2)}, u32[]{:S(2)}) collective-permute-start(bf16[48,16,128]{2,1,0:T(8,128)(2,1)S(1)} %get-tuple-element.47), channel_id=1, source_target_pairs={{1,2},{2,1},{5,6},{6,5},{9,10},{10,9},{13,14},{14,13},{17,18},{18,... | collective-permute-start | bytes 589832 | tf_op jit(solution)/shard_map/ppermute | solution.py:22
  36.9 7.2 %collective-permute-start.9 = (f32[64,128]{1,0:T(8,128)S(1)}, f32[64,128]{1,0:T(8,128)S(1)}, u32[]{:S(2)}, u32[]{:S(2)}) collective-permute-start(f32[64,128]{1,0:T(8,128)S(1)} %get-tuple-element.52), channel_id=1, source_target_pairs={{0,12},{1,13},{2,14},{3,15},{16,28},{17,29},{18,30},{19,31}} | collective-permute-start | bytes 98312 | tf_op jit(solution)/shard_map/ppermute | solution.py:28
  39.7 4.4 %collective-permute-start.8 = (f32[64,128]{1,0:T(8,128)S(1)}, f32[64,128]{1,0:T(8,128)S(1)}, u32[]{:S(2)}, u32[]{:S(2)}) collective-permute-start(f32[64,128]{1,0:T(8,128)S(1)} %get-tuple-element.52), channel_id=1, source_target_pairs={{0,8},{4,12},{1,9},{5,13},{2,10},{6,14},{3,11},{7,15},{16,24},{20,... | collective-permute-start | bytes 98312 | tf_op jit(solution)/shard_map/ppermute | solution.py:28
  41.0 3.2 %collective-permute-start.7 = (f32[64,128]{1,0:T(8,128)S(1)}, f32[64,128]{1,0:T(8,128)S(1)}, u32[]{:S(2)}, u32[]{:S(2)}) collective-permute-start(f32[64,128]{1,0:T(8,128)S(1)} %get-tuple-element.52), channel_id=1, source_target_pairs={{0,4},{4,8},{8,12},{1,5},{5,9},{9,13},{2,6},{6,10},{10,14},{3,7},{... | collective-permute-start | bytes 98312 | tf_op jit(solution)/shard_map/ppermute | solution.py:28
  44.8 4.7 %collective-permute-start.11 = (bf16[48,16,128]{2,1,0:T(8,128)(2,1)S(1)}, bf16[48,16,128]{2,1,0:T(8,128)(2,1)S(1)}, u32[]{:S(2)}, u32[]{:S(2)}) collective-permute-start(bf16[48,16,128]{2,1,0:T(8,128)(2,1)S(1)} %get-tuple-element.57), channel_id=1, source_target_pairs={{0,1},{1,0},{2,3},{3,2},{4,5},{5,4},{6,7},{7,6},{8,9},{9,8},{10,11... | collective-permute-start | bytes 589832 | tf_op jit(solution)/shard_map/ppermute | solution.py:22
  44.9 8.6 %collective-permute-start.10 = (bf16[40,16,128]{2,1,0:T(8,128)(2,1)S(1)}, bf16[40,16,128]{2,1,0:T(8,128)(2,1)S(1)}, u32[]{:S(2)}, u32[]{:S(2)}) collective-permute-start(bf16[40,16,128]{2,1,0:T(8,128)(2,1)S(1)} %get-tuple-element.56), channel_id=1, source_target_pairs={{1,2},{2,1},{5,6},{6,5},{9,10},{10,9},{13,14},{14,13},{17,18},{18,... | collective-permute-start | bytes 491528 | tf_op jit(solution)/shard_map/ppermute | solution.py:22

commit v10 on v9

--- a/solution.py
+++ b/solution.py
@@ -92,7 +92,6 @@
     cols = [src[pl.ds(base, size)].reshape(size * 16, 128)]
     for f in range(6):
         cols.append(jnp.concatenate([src[idx[f, base + e]] for e in range(size)], axis=0))
-    cols.append(cols[0])
     return product(jnp.concatenate(cols, axis=1), w[...])
 
 
@@ -119,7 +118,7 @@
     copies = [pltpu.make_async_copy(forcing.at[:, k], landed.at[k], sems.at[k]) for k in range(COARSEN)]
     small = ((conn, conn_v), (pattern, pattern_v), (init, init_v))
     copies += [pltpu.make_async_copy(src, dst, sems.at[COARSEN + i]) for i, (src, dst) in enumerate(small)]
-    for copy in copies:
+    for copy in copies[COARSEN:] + copies[:COARSEN]:
         copy.start()
     for copy in copies[COARSEN:]:
         copy.wait()
@@ -158,13 +157,14 @@
                 begin = pl.multiple_of(k * n * 8 + jnp.where(right, n * 8 - width, 0), 128)
                 pay[pl.ds(at, width), :] = fe[pl.ds(begin, width), :]
         at += width
+        rows_k = pl.ds(k * n * 8, n * 8 + (16 if k == COARSEN - 1 else 0))
+        results.append(pltpu.make_async_copy(fe.at[rows_k], fe_out.at[rows_k], out_sems.at[2 + k]))
+        results[-1].start()
         if k == COARSEN - 2:
             results.append(pltpu.make_async_copy(pay_odd, odd_out, out_sems.at[0]))
             results.append(pltpu.make_async_copy(pay_even, even_out, out_sems.at[1]))
-            results[0].start()
-            results[1].start()
-    results.append(pltpu.make_async_copy(fe, fe_out, out_sems.at[2]))
-    results[2].start()
+            results[-2].start()
+            results[-1].start()
     for result in results:
         result.wait()
 
@@ -173,7 +173,6 @@
     put_halves(w.at[pl.ds(0, 128)], diag[...].T)
     for f in range(6):
         put_halves(w.at[pl.ds(128 * (f + 1), 128)], faces[f].T)
-    w[pl.ds(128 * 7, 128), :] = jnp.zeros((128, 256), BF16)
 
     def thirds(a):
         one = a.astype(BF16)
@@ -254,7 +253,7 @@
         cols.append(jnp.dot(hot, i16[...], preferred_element_type=F32).astype(BF16))
     leads = jnp.concatenate([c[:, 0:128] for c in cols], axis=1)
     rests = jnp.concatenate([c[:, 128:256] for c in cols], axis=1)
-    return product_rows(jnp.concatenate([leads, rests], axis=0), w[pl.ds(0, 7 * 128), :])
+    return product_rows(jnp.concatenate([leads, rests], axis=0), w[...])
 
 
 STRIPS = (5 * REACH, 4 * REACH, 3 * REACH)
@@ -445,33 +444,31 @@
     by_parity(body)
 
 
-def write_out(out, k, value, begin, flip, sems):
-    size = value.shape[0]
-    pitch = size + 8
-    for e in range(size):
-        flip[pl.ds(e, 8, stride=pitch), :] = value[e]
-    rows = pl.ds(begin, size)
-    copies = [
-        pltpu.make_async_copy(flip.at[pl.ds(i * pitch, size)], out.at[i * COARSEN + k, rows], sems.at[k, i])
-        for i in range(8)
-    ]
-    for copy in copies:
-        copy.start()
-    return copies
+def flip_tiles(flip, value, begin):
+    lines = flip.reshape(8 * flip.shape[1], 128)
+    for e in range(value.shape[0]):
+        lines[pl.ds(begin + e, 8, stride=flip.shape[1]), :] = value[e]
+
+
+def write_out(out, k, flip, begin, size, sems):
+    copy = pltpu.make_async_copy(flip.at[:, pl.ds(0, size)], out.at[:, k, pl.ds(begin, size)], sems.at[k])
+    copy.start()
+    return copy
 
 
 def third_early_kernel(
-    idx, own, got, corr, total, fe, pay, w, pk, out, strip1, strip2, s0, s1, s2, force, flip0, flip1, flip2, flip3, sems
+    idx, own, got, corr, total, fe, pay, w, pk, out, strip1, strip2, kept, s0, s1, s2, force, flip0, flip1, flip3, sems
 ):
     def body(even):
         n = own.shape[0]
         full = 3 * n
         points = product(split(corr[...]).reshape(-1, 128), power(pk, 1)) + total[...]
-        copies = write_out(out, COARSEN - 1, points, 0, flip3, sems)
+        flip_tiles(flip3, points, 0)
+        copies = [write_out(out, COARSEN - 1, flip3, 0, n, sems)]
         put_block(s0, own, got, even, n)
         for state in (s1, s2):
             state[full] = jnp.zeros((16, 128), BF16)
-        for k, src, dst, flip in ((0, s0, s1, flip0), (1, s1, s2, flip1), (2, s2, None, flip2)):
+        for k, src, dst, flip in ((0, s0, s1, flip0), (1, s1, s2, flip1), (2, s2, None, None)):
             put_force(force, fe, pay, even, k, n)
             size = (5 - 2 * k) * REACH
             base = mirrored((2 + k) * REACH, size, full, even)
@@ -479,9 +476,12 @@
             if dst is not None:
                 dst[pl.ds(base, size)] = split(value)
             mine = (3 - k) * REACH
-            skip = size - mine
-            kept = value[:mine] if even else value[skip:]
-            copies += write_out(out, k, kept, n - mine if even else 0, flip, sems)
+            value = value[:mine] if even else value[size - mine :]
+            if flip is None:
+                kept[...] = value
+            else:
+                flip_tiles(flip, value, 0)
+                copies.append(write_out(out, k, flip, n - mine if even else 0, mine, sems))
         put_strips((strip1, strip2), (s1, s2), full, even)
         for copy in copies:
             copy.wait()
@@ -490,7 +490,7 @@
 
 
 def third_late_kernel(
-    idx, own, got, strip1, strip2, fe, pay, w, partial, out, s0, s1, s2, force, flip0, flip1, flip2, sems
+    idx, own, got, strip1, strip2, kept, fe, pay, w, partial, out, s0, s1, s2, force, flip0, flip1, flip2, sems
 ):
     def body(even):
         n = own.shape[0]
@@ -500,6 +500,7 @@
         get_strips((strip1, strip2), (s1, s2), full, even)
         copies = []
         size = 3 * REACH
+        flip_tiles(flip2, kept[...], n - REACH if even else 0)
         for k, src, dst, flip in ((0, s0, s1, flip0), (1, s1, s2, flip1), (2, s2, None, flip2)):
             put_force(force, fe, pay, not even, k, n)
             base = mirrored((7 - k) * REACH, size, full, even)
@@ -507,8 +508,13 @@
             if dst is not None:
                 dst[pl.ds(base, size)] = split(value)
             mine = (k + 1) * REACH
-            kept = value[size - mine :] if even else value[:mine]
-            copies += write_out(out, k, kept, 0 if even else n - mine, flip, sems)
+            value = value[size - mine :] if even else value[:mine]
+            if dst is None:
+                flip_tiles(flip, value, 0 if even else n - mine)
+                copies.append(write_out(out, k, flip, 0, n, sems))
+            else:
+                flip_tiles(flip, value, 0)
+                copies.append(write_out(out, k, flip, 0 if even else n - mine, mine, sems))
         for copy in copies:
             copy.wait()
 
@@ -566,7 +572,7 @@
             vmem((pay_rows, width), BF16),
             vmem((pay_rows, width), BF16),
             dma((COARSEN + 3,)),
-            dma((3,)),
+            dma((2 + COARSEN,)),
         ],
         spaces="hhhh",
         flops=3 * 10**9,
@@ -578,7 +584,7 @@
         weight_kernel,
         (diag_block, face_blocks, coarse_block),
         (
-            shape((8 * width, 2 * width), BF16),
+            shape((7 * width, 2 * width), BF16),
             shape((8 * width, 2 * width), BF16),
             shape(((tm - 1) * width, 2 * width), BF16),
         ),
@@ -638,13 +644,16 @@
         [rows],
     )
     got_odd, got_even = swapped(end_odd, 1), swapped(end_even, 0)
-    result = shape((steps, n, width), F32)
-    flips = [vmem((8 * (m * REACH + 8), width), F32) for m in (3, 2, 1)]
+    result = shape((steps // COARSEN, COARSEN, n, width), F32)
+
+    def flip(blocks):
+        return vmem((8, blocks * REACH + 8, width), F32)
+
     out, *strips = call(
         third_early_kernel,
         (idx, coarse, got_even, corr, total, fe, pay_even, w, pk),
-        (result, strip, strip),
-        [spaces] * 3 + [force] + flips + [vmem((8 * (n + 8), width), F32), dma((COARSEN, 8))],
+        (result, strip, strip, shape((REACH, 8, width), F32)),
+        [spaces] * 3 + [force, flip(3), flip(2), vmem((8, n + 8, width), F32), dma((COARSEN,))],
         spaces="s",
         out_spaces="h",
         flops=step_flops * 9 * REACH,
@@ -653,13 +662,13 @@
         third_late_kernel,
         (idx, coarse, got_odd, *strips, fe, pay_odd, w, out),
         (result,),
-        [spaces] * 3 + [force] + flips[::-1] + [dma((COARSEN - 1, 8))],
-        spaces="svvvvvvvh",
+        [spaces] * 3 + [force, flip(1), flip(2), vmem((8, n + 8, width), F32), dma((COARSEN - 1,))],
+        spaces="svvvvvvvvh",
         out_spaces="h",
-        aliases={8: 0},
+        aliases={9: 0},
         flops=step_flops * 9 * REACH,
     )
-    return out
+    return out.reshape(steps, n, width)
 
 
 def solution(mesh):

time: 57.4 us -> 56.7 us (0.988)
  Pallas kernels: 26.4 us -> 25.7 us
    pallas_call x12, Pallas kernels: 26.4 us -> 25.7 us  [call(): pl.pallas_call(kernel, out_shape=outs, name=kernel.__name__, in_specs=spe...]
  transfers between devices with their start and end apart: 12 -> 12, of which waited for: 3 -> 3; matrix products, arithmetic and copies ran while one was open for 0% -> 0% of each run, Pallas kernels for 22% -> 21%
where the time goes in v10:
time: 56.7 us; the launch traced here: 56.4 us
  starting transfers between devices  29.5 us (52%)
  Pallas kernels  25.7 us (45%)
  waiting for transfers between devices  0.75 us (1%)
    pallas_call x12, Pallas kernels, call(): pl.pallas_call(kernel, out_shape=outs, name=kernel.__name__, in_specs=spe...  25.7 us
    ppermute x6, starting transfers between devices, earlier(): lax.ppermute(value, 'tm', [(i, i + s) for i in range(count - s)])  15.8 us
    ppermute x6, starting transfers between devices, swapped(): return lax.ppermute(value, 'space', pairs)  13.7 us
  transfers between devices with their start and end apart: 12, of which 3 were waited for; matrix products, arithmetic and copies ran while one was open for 0% of the time, Pallas kernels for 21%

profile of v10, /device:TPU:1, one launch (start us, length us, event | category | flops | bytes accessed | tf_op | source)
XLA Modules:
  0.0 56.4 jit_solution(2252390956569733228)
XLA Ops:
  0.0 2.3 %pack_kernel.1 = (bf16[2064,128]{1,0:T(8,128)(2,1)}, bf16[912,128]{1,0:T(8,128)(2,1)}, bf16[912,128]{1,0:T(8,128)(2,1)}) custom-call(bf16[8,4,64,128]{3,2,1,0:T(8,128)(2,1)} %bitcast.4, f32[64,128]{1,0:T(8,128)} %refs_5_.1, s32[6,64]{1,0:T(8,128)} %bitcast.5, s32[6,64]{1,0:T(8,128)} %bitcast.6), custom_call_target="tpu_custom_call" | custom-call | flops 3000000000 | bytes 1555456 | tf_op jit(solution)/shard_map/pack_kernel/pallas_call | solution.py:532
  2.3 0.1 collective-permute-start
  2.4 4.6 %collective-permute-start.1 = (bf16[912,128]{1,0:T(8,128)(2,1)}, bf16[912,128]{1,0:T(8,128)(2,1)S(1)}, u32[]{:S(2)}, u32[]{:S(2)}) collective-permute-start(bf16[912,128]{1,0:T(8,128)(2,1)} %get-tuple-element.37), channel_id=1, source_target_pairs={{1,2},{2,1},{5,6},{6,5},{9,10},{10,9},{13,14},{14,13},{17,18},{18,... | collective-permute-start | bytes 700424 | tf_op jit(solution)/shard_map/ppermute | solution.py:22
  7.1 1.5 %weight_kernel.1 = (bf16[896,256]{1,0:T(8,128)(2,1)S(1)}, bf16[1024,256]{1,0:T(8,128)(2,1)S(1)}, bf16[384,256]{1,0:T(8,128)(2,1)S(1)}) custom-call(f32[128,128]{1,0:T(8,128)S(1)} %copy-done.3, f32[6,128,128]{2,1,0:T(8,128)S(1)} %copy-done.2, f32[128,128]{1,0:T(8,128)S(1)} %copy-done.4), custom_call_target="tpu_custom_call" | custom-call | flops 1000000000 | bytes 1703936 | tf_op jit(solution)/shard_map/weight_kernel/pallas_call | solution.py:532
  8.7 1.9 %first_early_kernel.1 = (bf16[32,16,128]{2,1,0:T(8,128)(2,1)S(1)}, bf16[32,16,128]{2,1,0:T(8,128)(2,1)S(1)}, bf16[32,16,128]{2,1,0:T(8,128)(2,1)S(1)}) custom-call(bf16[2064,128]{1,0:T(8,128)(2,1)S(1)} %copy-done, f32[64,128]{1,0:T(8,128)S(1)} %copy-done.1, bf16[912,128]{1,0:T(8,128)(2,1)S(1)} %collective-permute-done.got.got_even.pay, ...), custom_call_target="tpu_custom_call" | custom-call | flops 704643072 | bytes 1646592 | tf_op jit(solution)/shard_map/first_early_kernel/pallas_call | solution.py:532
  10.6 0.4 collective-permute-done.1.got_odd.pay
  11.0 3.2 %first_late_kernel.1 = (f32[64,8,128]{2,1,0:T(8,128)S(1)}, f32[64,128]{1,0:T(8,128)S(1)}, s32[8,256]{1,0:T(8,128)S(1)}) custom-call(bf16[2064,128]{1,0:T(8,128)(2,1)S(1)} %copy-done, f32[64,128]{1,0:T(8,128)S(1)} %copy-done.1, bf16[912,128]{1,0:T(8,128)(2,1)S(1)} %collective-permute-done.got.got_even.pay, ...), custom_call_target="tpu_custom_call" | custom-call | flops 1409286144 | bytes 2707456 | tf_op jit(solution)/shard_map/first_late_kernel/pallas_call | solution.py:532
  14.2 5.8 %collective-permute-start.4 = (f32[64,128]{1,0:T(8,128)S(1)}, f32[64,128]{1,0:T(8,128)S(1)}, u32[]{:S(2)}, u32[]{:S(2)}) collective-permute-start(f32[64,128]{1,0:T(8,128)S(1)} %get-tuple-element.44), channel_id=1, source_target_pairs={{0,12},{1,13},{2,14},{3,15},{16,28},{17,29},{18,30},{19,31}} | collective-permute-start | bytes 98312 | tf_op jit(solution)/shard_map/ppermute | solution.py:28
  20.0 1.3 %collective-permute-start.3 = (f32[64,128]{1,0:T(8,128)S(1)}, f32[64,128]{1,0:T(8,128)S(1)}, u32[]{:S(2)}, u32[]{:S(2)}) collective-permute-start(f32[64,128]{1,0:T(8,128)S(1)} %get-tuple-element.44), channel_id=1, source_target_pairs={{0,8},{4,12},{1,9},{5,13},{2,10},{6,14},{3,11},{7,15},{16,24},{20,... | collective-permute-start | bytes 98312 | tf_op jit(solution)/shard_map/ppermute | solution.py:28
  21.3 2.2 %collective-permute-start.2 = (f32[64,128]{1,0:T(8,128)S(1)}, f32[64,128]{1,0:T(8,128)S(1)}, u32[]{:S(2)}, u32[]{:S(2)}) collective-permute-start(f32[64,128]{1,0:T(8,128)S(1)} %get-tuple-element.44), channel_id=1, source_target_pairs={{0,4},{4,8},{8,12},{1,5},{5,9},{9,13},{2,6},{6,10},{10,14},{3,7},{... | collective-permute-start | bytes 98312 | tf_op jit(solution)/shard_map/ppermute | solution.py:28
  23.5 0.7 %scan_kernel.1.refs_3_ = f32[64,8,128]{2,1,0:T(8,128)S(1)} custom-call(f32[64,8,128]{2,1,0:T(8,128)S(1)} %get-tuple-element.45.values.w1, bf16[1024,256]{1,0:T(8,128)(2,1)S(1)} %get-tuple-element.42.pk.refs_5_.refs_7_), custom_call_target="tpu_custom_call" | custom-call | flops 10000000 | bytes 1048576 | tf_op jit(solution)/shard_map/scan_kernel/pallas_call | solution.py:532
  24.2 0.3 collective-permute-done.2.refs_0_
  24.5 0.6 enter_first_kernel.1
  25.2 4.2 %collective-permute-start.5 = (bf16[48,16,128]{2,1,0:T(8,128)(2,1)S(1)}, bf16[48,16,128]{2,1,0:T(8,128)(2,1)S(1)}, u32[]{:S(2)}, u32[]{:S(2)}) collective-permute-start(bf16[48,16,128]{2,1,0:T(8,128)(2,1)S(1)} %get-tuple-element.48), channel_id=1, source_target_pairs={{1,2},{2,1},{5,6},{6,5},{9,10},{10,9},{13,14},{14,13},{17,18},{18,... | collective-permute-start | bytes 589832 | tf_op jit(solution)/shard_map/ppermute | solution.py:22
  29.4 3.5 %second_early_kernel.1 = (bf16[32,16,128]{2,1,0:T(8,128)(2,1)S(1)}, bf16[32,16,128]{2,1,0:T(8,128)(2,1)S(1)}, bf16[32,16,128]{2,1,0:T(8,128)(2,1)S(1)}, f32[64,8,128]{2,1,0:T(8,128)S(1)}) custom-call(s32[8,256]{1,0:T(8,128)S(1)} %get-tuple-element.43.idx, bf16[64,16,128]{2,1,0:T(8,128)(2,1)S(1)} %get-tuple-element.47.own.refs_4_, ...), custom_call_target="tpu_custom_call" | custom-call | flops 1409286144 | bytes 2170880 | tf_op jit(solution)/shard_map/second_early_kernel/pallas_call | solution.py:532
  32.8 3.9 %second_late_kernel.1 = (f32[64,8,128]{2,1,0:T(8,128)S(1)}, f32[64,128]{1,0:T(8,128)S(1)}) custom-call(s32[8,256]{1,0:T(8,128)S(1)} %get-tuple-element.43.idx, bf16[64,16,128]{2,1,0:T(8,128)(2,1)S(1)} %get-tuple-element.47.own.refs_4_, bf16[48,16,128]{2,1,0:T(8,128)(2,1)S(1)} %collective-permute-done.5.got, ...), custom_call_target="tpu_custom_call" | custom-call | flops 1879048192 | bytes 2400256 | tf_op jit(solution)/shard_map/second_late_kernel/pallas_call | solution.py:532
  36.7 2.8 %collective-permute-start.9 = (f32[64,128]{1,0:T(8,128)S(1)}, f32[64,128]{1,0:T(8,128)S(1)}, u32[]{:S(2)}, u32[]{:S(2)}) collective-permute-start(f32[64,128]{1,0:T(8,128)S(1)} %get-tuple-element.53), channel_id=1, source_target_pairs={{0,12},{1,13},{2,14},{3,15},{16,28},{17,29},{18,30},{19,31}} | collective-permute-start | bytes 98312 | tf_op jit(solution)/shard_map/ppermute | solution.py:28
  39.5 1.3 %collective-permute-start.8 = (f32[64,128]{1,0:T(8,128)S(1)}, f32[64,128]{1,0:T(8,128)S(1)}, u32[]{:S(2)}, u32[]{:S(2)}) collective-permute-start(f32[64,128]{1,0:T(8,128)S(1)} %get-tuple-element.53), channel_id=1, source_target_pairs={{0,8},{4,12},{1,9},{5,13},{2,10},{6,14},{3,11},{7,15},{16,24},{20,... | collective-permute-start | bytes 98312 | tf_op jit(solution)/shard_map/ppermute | solution.py:28
  40.8 2.4 %collective-permute-start.7 = (f32[64,128]{1,0:T(8,128)S(1)}, f32[64,128]{1,0:T(8,128)S(1)}, u32[]{:S(2)}, u32[]{:S(2)}) collective-permute-start(f32[64,128]{1,0:T(8,128)S(1)} %get-tuple-element.53), channel_id=1, source_target_pairs={{0,4},{4,8},{8,12},{1,5},{5,9},{9,13},{2,6},{6,10},{10,14},{3,7},{... | collective-permute-start | bytes 98312 | tf_op jit(solution)/shard_map/ppermute | solution.py:28
  43.2 0.7 %scan_sum_kernel.1 = (f32[64,8,128]{2,1,0:T(8,128)S(1)}, f32[64,8,128]{2,1,0:T(8,128)S(1)}) custom-call(f32[64,8,128]{2,1,0:T(8,128)S(1)} %get-tuple-element.54.values, f32[64,8,128]{2,1,0:T(8,128)S(1)} %get-tuple-element.45.values.w1, f32[64,8,128]{2,1,0:T(8,128)S(1)} %get-tuple-element.52.coarse, bf16[1024,256]{1,0:T(8,128)(2,1)S(1)} %get-tuple-element.42.pk.refs_5_.refs_7_), custom_call_target="tpu_custom_call" | custom-call | flops 10000000 | bytes 1835008 | tf_op jit(solution)/shard_map/scan_sum_kernel/pallas_call | solution.py:532
  44.0 0.6 %enter_second_kernel.1 = (bf16[64,16,128]{2,1,0:T(8,128)(2,1)S(1)}, bf16[48,16,128]{2,1,0:T(8,128)(2,1)S(1)}, bf16[40,16,128]{2,1,0:T(8,128)(2,1)S(1)}, f32[64,8,128]{2,1,0:T(8,128)S(1)}) custom-call(f32[64,128]{1,0:T(8,128)S(1)} %collective-permute-done.7.refs_0_, f32[64,128]{1,0:T(8,128)S(1)} %collective-permute-done.8.refs_1_, ...), custom_call_target="tpu_custom_call" | custom-call | flops 10000000 | bytes 2260992 | tf_op jit(solution)/shard_map/enter_second_kernel/pallas_call | solution.py:532
  44.7 4.6 %collective-permute-start.10 = (bf16[40,16,128]{2,1,0:T(8,128)(2,1)S(1)}, bf16[40,16,128]{2,1,0:T(8,128)(2,1)S(1)}, u32[]{:S(2)}, u32[]{:S(2)}) collective-permute-start(bf16[40,16,128]{2,1,0:T(8,128)(2,1)S(1)} %get-tuple-element.57), channel_id=1, source_target_pairs={{1,2},{2,1},{5,6},{6,5},{9,10},{10,9},{13,14},{14,13},{17,18},{18,... | collective-permute-start | bytes 491528 | tf_op jit(solution)/shard_map/ppermute | solution.py:22
  49.3 3.7 %third_early_kernel.1 = (f32[8,4,64,128]{3,2,1,0:T(8,128)}, bf16[32,16,128]{2,1,0:T(8,128)(2,1)S(1)}, bf16[32,16,128]{2,1,0:T(8,128)(2,1)S(1)}, f32[16,8,128]{2,1,0:T(8,128)S(1)}) custom-call(s32[8,256]{1,0:T(8,128)S(1)} %get-tuple-element.43.idx, bf16[64,16,128]{2,1,0:T(8,128)(2,1)S(1)} %get-tuple-element.56.own, ...), custom_call_target="tpu_custom_call" | custom-call | flops 1056964608 | bytes 4112384 | tf_op jit(solution)/shard_map/third_early_kernel/pallas_call | solution.py:532
  53.1 3.2 %third_late_kernel.1 = f32[8,4,64,128]{3,2,1,0:T(8,128)} custom-call(s32[8,256]{1,0:T(8,128)S(1)} %get-tuple-element.43.idx, bf16[64,16,128]{2,1,0:T(8,128)(2,1)S(1)} %get-tuple-element.56.own, bf16[40,16,128]{2,1,0:T(8,128)(2,1)S(1)} %collective-permute-done.10.got, ...), custom_call_target="tpu_custom_call", output_to_operand_aliasing={{}: (9, {})} | custom-call | flops 1056964608 | bytes 4079616 | tf_op jit(solution)/shard_map/third_late_kernel/pallas_call | solution.py:532
  (22 shorter events, 0.2 us)
Async XLA Ops:
  0.0 7.1 %copy-start.2 = (f32[6,128,128]{2,1,0:T(8,128)S(1)}, f32[6,128,128]{2,1,0:T(8,128)}, u32[]{:S(2)}) copy-start(f32[6,128,128]{2,1,0:T(8,128)} %faces.1) | copy-start | bytes 1179652
  0.0 7.1 %copy-start.3 = (f32[128,128]{1,0:T(8,128)S(1)}, f32[128,128]{1,0:T(8,128)}, u32[]{:S(2)}) copy-start(f32[128,128]{1,0:T(8,128)} %diag.1) | copy-start | bytes 196612
  0.0 7.1 %copy-start.4 = (f32[128,128]{1,0:T(8,128)S(1)}, f32[128,128]{1,0:T(8,128)}, u32[]{:S(2)}) copy-start(f32[128,128]{1,0:T(8,128)} %coarse.1) | copy-start | bytes 196612
  2.3 6.3 %collective-permute-start = (bf16[912,128]{1,0:T(8,128)(2,1)}, bf16[912,128]{1,0:T(8,128)(2,1)S(1)}, u32[]{:S(2)}, u32[]{:S(2)}) collective-permute-start(bf16[912,128]{1,0:T(8,128)(2,1)} %get-tuple-element.36), channel_id=1, source_target_pairs={{0,1},{1,0},{2,3},{3,2},{4,5},{5,4},{6,7},{7,6},{8,9},{9,8},{10,11... | collective-permute-start | bytes 700424 | tf_op jit(solution)/shard_map/ppermute | solution.py:22
  2.4 6.2 %copy-start = (bf16[2064,128]{1,0:T(8,128)(2,1)S(1)}, bf16[2064,128]{1,0:T(8,128)(2,1)}, u32[]{:S(2)}) copy-start(bf16[2064,128]{1,0:T(8,128)(2,1)} %get-tuple-element.35.fe) | copy-start | bytes 1585156
  2.4 6.2 %copy-start.1 = (f32[64,128]{1,0:T(8,128)S(1)}, f32[64,128]{1,0:T(8,128)}, u32[]{:S(2)}) copy-start(f32[64,128]{1,0:T(8,128)} %refs_5_.1) | copy-start | bytes 98308
  2.4 8.6 %collective-permute-start.1 = (bf16[912,128]{1,0:T(8,128)(2,1)}, bf16[912,128]{1,0:T(8,128)(2,1)S(1)}, u32[]{:S(2)}, u32[]{:S(2)}) collective-permute-start(bf16[912,128]{1,0:T(8,128)(2,1)} %get-tuple-element.37), channel_id=1, source_target_pairs={{1,2},{2,1},{5,6},{6,5},{9,10},{10,9},{13,14},{14,13},{17,18},{18,... | collective-permute-start | bytes 700424 | tf_op jit(solution)/shard_map/ppermute | solution.py:22
  14.2 10.0 %collective-permute-start.4 = (f32[64,128]{1,0:T(8,128)S(1)}, f32[64,128]{1,0:T(8,128)S(1)}, u32[]{:S(2)}, u32[]{:S(2)}) collective-permute-start(f32[64,128]{1,0:T(8,128)S(1)} %get-tuple-element.44), channel_id=1, source_target_pairs={{0,12},{1,13},{2,14},{3,15},{16,28},{17,29},{18,30},{19,31}} | collective-permute-start | bytes 98312 | tf_op jit(solution)/shard_map/ppermute | solution.py:28
  20.0 4.2 %collective-permute-start.3 = (f32[64,128]{1,0:T(8,128)S(1)}, f32[64,128]{1,0:T(8,128)S(1)}, u32[]{:S(2)}, u32[]{:S(2)}) collective-permute-start(f32[64,128]{1,0:T(8,128)S(1)} %get-tuple-element.44), channel_id=1, source_target_pairs={{0,8},{4,12},{1,9},{5,13},{2,10},{6,14},{3,11},{7,15},{16,24},{20,... | collective-permute-start | bytes 98312 | tf_op jit(solution)/shard_map/ppermute | solution.py:28
  21.3 3.2 %collective-permute-start.2 = (f32[64,128]{1,0:T(8,128)S(1)}, f32[64,128]{1,0:T(8,128)S(1)}, u32[]{:S(2)}, u32[]{:S(2)}) collective-permute-start(f32[64,128]{1,0:T(8,128)S(1)} %get-tuple-element.44), channel_id=1, source_target_pairs={{0,4},{4,8},{8,12},{1,5},{5,9},{9,13},{2,6},{6,10},{10,14},{3,7},{... | collective-permute-start | bytes 98312 | tf_op jit(solution)/shard_map/ppermute | solution.py:28
  25.1 4.3 %collective-permute-start.6 = (bf16[64,16,128]{2,1,0:T(8,128)(2,1)S(1)}, bf16[64,16,128]{2,1,0:T(8,128)(2,1)S(1)}, u32[]{:S(2)}, u32[]{:S(2)}) collective-permute-start(bf16[64,16,128]{2,1,0:T(8,128)(2,1)S(1)} %get-tuple-element.47.own.refs_4_), channel_id=1, source_target_pairs={{0,1},{1,0},{2,3},{3,2},{4,5},{5,4},{6,7},{7,6},{8,9},{9,8},{10,11... | collective-permute-start | bytes 786440 | tf_op jit(solution)/shard_map/ppermute | solution.py:22
  25.2 7.7 %collective-permute-start.5 = (bf16[48,16,128]{2,1,0:T(8,128)(2,1)S(1)}, bf16[48,16,128]{2,1,0:T(8,128)(2,1)S(1)}, u32[]{:S(2)}, u32[]{:S(2)}) collective-permute-start(bf16[48,16,128]{2,1,0:T(8,128)(2,1)S(1)} %get-tuple-element.48), channel_id=1, source_target_pairs={{1,2},{2,1},{5,6},{6,5},{9,10},{10,9},{13,14},{14,13},{17,18},{18,... | collective-permute-start | bytes 589832 | tf_op jit(solution)/shard_map/ppermute | solution.py:22
  36.7 7.2 %collective-permute-start.9 = (f32[64,128]{1,0:T(8,128)S(1)}, f32[64,128]{1,0:T(8,128)S(1)}, u32[]{:S(2)}, u32[]{:S(2)}) collective-permute-start(f32[64,128]{1,0:T(8,128)S(1)} %get-tuple-element.53), channel_id=1, source_target_pairs={{0,12},{1,13},{2,14},{3,15},{16,28},{17,29},{18,30},{19,31}} | collective-permute-start | bytes 98312 | tf_op jit(solution)/shard_map/ppermute | solution.py:28
  39.5 4.4 %collective-permute-start.8 = (f32[64,128]{1,0:T(8,128)S(1)}, f32[64,128]{1,0:T(8,128)S(1)}, u32[]{:S(2)}, u32[]{:S(2)}) collective-permute-start(f32[64,128]{1,0:T(8,128)S(1)} %get-tuple-element.53), channel_id=1, source_target_pairs={{0,8},{4,12},{1,9},{5,13},{2,10},{6,14},{3,11},{7,15},{16,24},{20,... | collective-permute-start | bytes 98312 | tf_op jit(solution)/shard_map/ppermute | solution.py:28
  40.8 3.2 %collective-permute-start.7 = (f32[64,128]{1,0:T(8,128)S(1)}, f32[64,128]{1,0:T(8,128)S(1)}, u32[]{:S(2)}, u32[]{:S(2)}) collective-permute-start(f32[64,128]{1,0:T(8,128)S(1)} %get-tuple-element.53), channel_id=1, source_target_pairs={{0,4},{4,8},{8,12},{1,5},{5,9},{9,13},{2,6},{6,10},{10,14},{3,7},{... | collective-permute-start | bytes 98312 | tf_op jit(solution)/shard_map/ppermute | solution.py:28
  44.6 4.7 %collective-permute-start.11 = (bf16[48,16,128]{2,1,0:T(8,128)(2,1)S(1)}, bf16[48,16,128]{2,1,0:T(8,128)(2,1)S(1)}, u32[]{:S(2)}, u32[]{:S(2)}) collective-permute-start(bf16[48,16,128]{2,1,0:T(8,128)(2,1)S(1)} %get-tuple-element.58), channel_id=1, source_target_pairs={{0,1},{1,0},{2,3},{3,2},{4,5},{5,4},{6,7},{7,6},{8,9},{9,8},{10,11... | collective-permute-start | bytes 589832 | tf_op jit(solution)/shard_map/ppermute | solution.py:22
  44.7 8.4 %collective-permute-start.10 = (bf16[40,16,128]{2,1,0:T(8,128)(2,1)S(1)}, bf16[40,16,128]{2,1,0:T(8,128)(2,1)S(1)}, u32[]{:S(2)}, u32[]{:S(2)}) collective-permute-start(bf16[40,16,128]{2,1,0:T(8,128)(2,1)S(1)} %get-tuple-element.57), channel_id=1, source_target_pairs={{1,2},{2,1},{5,6},{6,5},{9,10},{10,9},{13,14},{14,13},{17,18},{18,... | collective-permute-start | bytes 491528 | tf_op jit(solution)/shard_map/ppermute | solution.py:22

commit v11 on v10

--- a/solution.py
+++ b/solution.py
@@ -364,7 +364,10 @@
     by_parity(body)
 
 
-def put_far(dst, got, right, n):
+def put_far(dst, own, got, right, n):
+    half = n // 2
+    dst[pl.ds(n + half if right else n, half)] = own[pl.ds(half if right else 0, half)]
+    dst[3 * n] = jnp.zeros((16, 128), BF16)
     count = 2 * (got.shape[0] - NEAR)
     dst[pl.ds(2 * n if right else n - NEAR, NEAR)] = got[pl.ds(0, NEAR)]
     leads = got[pl.ds(NEAR, count // 2)].astype(F32).reshape(count, 8, 128)
@@ -396,25 +399,24 @@
     put_pay(pay_odd, state, value, side, n)
 
 
-def put_own(dst, own, n):
+def put_block(dst, own, got, right, n):
+    side = got.shape[0]
     dst[pl.ds(n, n)] = own[...]
     dst[3 * n] = jnp.zeros((16, 128), BF16)
-
-
-def put_block(dst, own, got, right, n):
-    side = got.shape[0]
-    put_own(dst, own, n)
     dst[pl.ds(2 * n if right else n - side, side)] = got[...]
 
 
-def second_early_kernel(idx, own, got, w, pk, strip1, strip2, strip3, coarse, s0, s1, s2, s3):
+def second_early_kernel(table, own, got, w, pk, strip1, strip2, strip3, coarse, idx, sem, s0, s1, s2, s3):
     def body(even):
+        copy = pltpu.make_async_copy(table, idx, sem)
+        copy.start()
         n = own.shape[0]
         full = 3 * n
         coarse[...] = product(own[...].reshape(n * 16, 128), power(pk, 1))
         put_block(s0, own, got, even, n)
         for state in (s1, s2, s3):
             state[full] = jnp.zeros((16, 128), BF16)
+        copy.wait()
         for k, src, dst in ((1, s0, s1), (2, s1, s2), (3, s2, s3)):
             size = (8 - 2 * k) * REACH
             base = mirrored(k * REACH, size, full, even)
@@ -424,14 +426,16 @@
     by_parity(body)
 
 
-def second_late_kernel(idx, own, got, strip1, strip2, strip3, coarse, w, pk, res, end, s0, s1, s2, s3, y):
+def second_late_kernel(table, own, got, strip1, strip2, strip3, coarse, w, pk, res, end, idx, sem, s0, s1, s2, s3, y):
     def body(even):
+        copy = pltpu.make_async_copy(table, idx, sem)
+        copy.start()
         n = own.shape[0]
         full = 3 * n
-        put_own(s0, own, n)
-        put_far(s0, got, not even, n)
+        put_far(s0, own, got, not even, n)
         get_strips((strip1, strip2, strip3), (s1, s2, s3), full, even)
         count = 4 * REACH
+        copy.wait()
         for k, src, dst in ((1, s0, s1), (2, s1, s2), (3, s2, s3)):
             base = mirrored((8 - k) * REACH, count, full, even)
             dst[pl.ds(base, count)] = split(apply_phi(src, idx, w, base, count))
@@ -457,9 +461,11 @@
 
 
 def third_early_kernel(
-    idx, own, got, corr, total, fe, pay, w, pk, out, strip1, strip2, kept, s0, s1, s2, force, flip0, flip1, flip3, sems
+    table, own, got, corr, total, fe, pay, w, pk, out, strip1, strip2, kept, idx, sem, s0, s1, s2, force, flip0, flip1, flip3, sems
 ):
     def body(even):
+        table_copy = pltpu.make_async_copy(table, idx, sem)
+        table_copy.start()
         n = own.shape[0]
         full = 3 * n
         points = product(split(corr[...]).reshape(-1, 128), power(pk, 1)) + total[...]
@@ -468,6 +474,7 @@
         put_block(s0, own, got, even, n)
         for state in (s1, s2):
             state[full] = jnp.zeros((16, 128), BF16)
+        table_copy.wait()
         for k, src, dst, flip in ((0, s0, s1, flip0), (1, s1, s2, flip1), (2, s2, None, None)):
             put_force(force, fe, pay, even, k, n)
             size = (5 - 2 * k) * REACH
@@ -490,17 +497,19 @@
 
 
 def third_late_kernel(
-    idx, own, got, strip1, strip2, kept, fe, pay, w, partial, out, s0, s1, s2, force, flip0, flip1, flip2, sems
+    table, own, got, strip1, strip2, kept, fe, pay, w, partial, out, idx, sem, s0, s1, s2, force, flip0, flip1, flip2, sems
 ):
     def body(even):
+        table_copy = pltpu.make_async_copy(table, idx, sem)
+        table_copy.start()
         n = own.shape[0]
         full = 3 * n
-        put_own(s0, own, n)
-        put_far(s0, got, not even, n)
+        put_far(s0, own, got, not even, n)
         get_strips((strip1, strip2), (s1, s2), full, even)
         copies = []
         size = 3 * REACH
         flip_tiles(flip2, kept[...], n - REACH if even else 0)
+        table_copy.wait()
         for k, src, dst, flip in ((0, s0, s1, flip0), (1, s1, s2, flip1), (2, s2, None, flip2)):
             put_force(force, fe, pay, not even, k, n)
             base = mirrored((7 - k) * REACH, size, full, even)
@@ -622,16 +631,14 @@
         second_early_kernel,
         (idx, coarse, got_even, w, pk),
         (strip, strip, strip, tiles),
-        [spaces] * 4,
-        spaces="s",
+        [smem, dma] + [spaces] * 4,
         flops=step_flops * 12 * REACH,
     )
     res, end = call(
         second_late_kernel,
         (idx, coarse, got_odd, *strips, moved, w, pk),
         (tiles, ends),
-        [spaces] * 4 + [rows],
-        spaces="s",
+        [smem, dma] + [spaces] * 4 + [rows],
         flops=step_flops * 16 * REACH,
     )
     arrivals = earlier(end)
@@ -653,8 +660,7 @@
         third_early_kernel,
         (idx, coarse, got_even, corr, total, fe, pay_even, w, pk),
         (result, strip, strip, shape((REACH, 8, width), F32)),
-        [spaces] * 3 + [force, flip(3), flip(2), vmem((8, n + 8, width), F32), dma((COARSEN,))],
-        spaces="s",
+        [smem, dma] + [spaces] * 3 + [force, flip(3), flip(2), vmem((8, n + 8, width), F32), dma((COARSEN,))],
         out_spaces="h",
         flops=step_flops * 9 * REACH,
     )
@@ -662,8 +668,8 @@
         third_late_kernel,
         (idx, coarse, got_odd, *strips, fe, pay_odd, w, out),
         (result,),
-        [spaces] * 3 + [force, flip(1), flip(2), vmem((8, n + 8, width), F32), dma((COARSEN - 1,))],
-        spaces="svvvvvvvvh",
+        [smem, dma] + [spaces] * 3 + [force, flip(1), flip(2), vmem((8, n + 8, width), F32), dma((COARSEN - 1,))],
+        spaces="vvvvvvvvvh",
         out_spaces="h",
         aliases={9: 0},
         flops=step_flops * 9 * REACH,

time: 56.7 us -> 56.3 us (level)
  Pallas kernels: 25.7 us -> 25 us
    pallas_call x12, Pallas kernels: 25.7 us -> 25 us  [call(): pl.pallas_call(kernel, out_shape=outs, name=kernel.__name__, in_specs=spe...]
  transfers between devices with their start and end apart: 12 -> 12, of which waited for: 3 -> 4; matrix products, arithmetic and copies ran while one was open for 0% -> 0% of each run, Pallas kernels for 21% -> 20%
where the time goes in v11:
time: 56.3 us; the launch traced here: 56 us
  starting transfers between devices  29.6 us (53%)
  Pallas kernels  25 us (44%)
  waiting for transfers between devices  0.89 us (2%)
    pallas_call x12, Pallas kernels, call(): pl.pallas_call(kernel, out_shape=outs, name=kernel.__name__, in_specs=spe...  25 us
    ppermute x6, starting transfers between devices, earlier(): lax.ppermute(value, 'tm', [(i, i + s) for i in range(count - s)])  15.8 us
    ppermute x6, starting transfers between devices, swapped(): return lax.ppermute(value, 'space', pairs)  13.8 us
  transfers between devices with their start and end apart: 12, of which 4 were waited for; matrix products, arithmetic and copies ran while one was open for 0% of the time, Pallas kernels for 20%

profile of v11, /device:TPU:1, one launch (start us, length us, event | category | flops | bytes accessed | tf_op | source)
XLA Modules:
  0.0 56.0 jit_solution(14883145165406839772)
XLA Ops:
  0.0 2.3 %pack_kernel.1 = (bf16[2064,128]{1,0:T(8,128)(2,1)}, bf16[912,128]{1,0:T(8,128)(2,1)}, bf16[912,128]{1,0:T(8,128)(2,1)}) custom-call(bf16[8,4,64,128]{3,2,1,0:T(8,128)(2,1)} %bitcast.4, f32[64,128]{1,0:T(8,128)} %refs_5_.1, s32[6,64]{1,0:T(8,128)} %bitcast.5, s32[6,64]{1,0:T(8,128)} %bitcast.6), custom_call_target="tpu_custom_call" | custom-call | flops 3000000000 | bytes 1555456 | tf_op jit(solution)/shard_map/pack_kernel/pallas_call | solution.py:541
  2.4 4.6 %collective-permute-start.1 = (bf16[912,128]{1,0:T(8,128)(2,1)}, bf16[912,128]{1,0:T(8,128)(2,1)S(1)}, u32[]{:S(2)}, u32[]{:S(2)}) collective-permute-start(bf16[912,128]{1,0:T(8,128)(2,1)} %get-tuple-element.37), channel_id=1, source_target_pairs={{1,2},{2,1},{5,6},{6,5},{9,10},{10,9},{13,14},{14,13},{17,18},{18,... | collective-permute-start | bytes 700424 | tf_op jit(solution)/shard_map/ppermute | solution.py:22
  7.1 1.5 %weight_kernel.1 = (bf16[896,256]{1,0:T(8,128)(2,1)S(1)}, bf16[1024,256]{1,0:T(8,128)(2,1)S(1)}, bf16[384,256]{1,0:T(8,128)(2,1)S(1)}) custom-call(f32[128,128]{1,0:T(8,128)S(1)} %copy-done.3, f32[6,128,128]{2,1,0:T(8,128)S(1)} %copy-done.2, f32[128,128]{1,0:T(8,128)S(1)} %copy-done.4), custom_call_target="tpu_custom_call" | custom-call | flops 1000000000 | bytes 1703936 | tf_op jit(solution)/shard_map/weight_kernel/pallas_call | solution.py:541
  8.7 1.9 %first_early_kernel.1 = (bf16[32,16,128]{2,1,0:T(8,128)(2,1)S(1)}, bf16[32,16,128]{2,1,0:T(8,128)(2,1)S(1)}, bf16[32,16,128]{2,1,0:T(8,128)(2,1)S(1)}) custom-call(bf16[2064,128]{1,0:T(8,128)(2,1)S(1)} %copy-done, f32[64,128]{1,0:T(8,128)S(1)} %copy-done.1, bf16[912,128]{1,0:T(8,128)(2,1)S(1)} %collective-permute-done.got.got_even.pay, ...), custom_call_target="tpu_custom_call" | custom-call | flops 704643072 | bytes 1646592 | tf_op jit(solution)/shard_map/first_early_kernel/pallas_call | solution.py:541
  10.6 0.4 collective-permute-done.1.got_odd.pay
  11.0 3.2 %first_late_kernel.1 = (f32[64,8,128]{2,1,0:T(8,128)S(1)}, f32[64,128]{1,0:T(8,128)S(1)}, s32[8,256]{1,0:T(8,128)S(1)}) custom-call(bf16[2064,128]{1,0:T(8,128)(2,1)S(1)} %copy-done, f32[64,128]{1,0:T(8,128)S(1)} %copy-done.1, bf16[912,128]{1,0:T(8,128)(2,1)S(1)} %collective-permute-done.got.got_even.pay, ...), custom_call_target="tpu_custom_call" | custom-call | flops 1409286144 | bytes 2707456 | tf_op jit(solution)/shard_map/first_late_kernel/pallas_call | solution.py:541
  14.2 5.8 %collective-permute-start.4 = (f32[64,128]{1,0:T(8,128)S(1)}, f32[64,128]{1,0:T(8,128)S(1)}, u32[]{:S(2)}, u32[]{:S(2)}) collective-permute-start(f32[64,128]{1,0:T(8,128)S(1)} %get-tuple-element.44), channel_id=1, source_target_pairs={{0,12},{1,13},{2,14},{3,15},{16,28},{17,29},{18,30},{19,31}} | collective-permute-start | bytes 98312 | tf_op jit(solution)/shard_map/ppermute | solution.py:28
  20.0 1.3 %collective-permute-start.3 = (f32[64,128]{1,0:T(8,128)S(1)}, f32[64,128]{1,0:T(8,128)S(1)}, u32[]{:S(2)}, u32[]{:S(2)}) collective-permute-start(f32[64,128]{1,0:T(8,128)S(1)} %get-tuple-element.44), channel_id=1, source_target_pairs={{0,8},{4,12},{1,9},{5,13},{2,10},{6,14},{3,11},{7,15},{16,24},{20,... | collective-permute-start | bytes 98312 | tf_op jit(solution)/shard_map/ppermute | solution.py:28
  21.3 2.2 %collective-permute-start.2 = (f32[64,128]{1,0:T(8,128)S(1)}, f32[64,128]{1,0:T(8,128)S(1)}, u32[]{:S(2)}, u32[]{:S(2)}) collective-permute-start(f32[64,128]{1,0:T(8,128)S(1)} %get-tuple-element.44), channel_id=1, source_target_pairs={{0,4},{4,8},{8,12},{1,5},{5,9},{9,13},{2,6},{6,10},{10,14},{3,7},{... | collective-permute-start | bytes 98312 | tf_op jit(solution)/shard_map/ppermute | solution.py:28
  23.5 0.7 %scan_kernel.1.refs_3_ = f32[64,8,128]{2,1,0:T(8,128)S(1)} custom-call(f32[64,8,128]{2,1,0:T(8,128)S(1)} %get-tuple-element.45.values.w1, bf16[1024,256]{1,0:T(8,128)(2,1)S(1)} %get-tuple-element.42.pk.refs_5_.refs_7_), custom_call_target="tpu_custom_call" | custom-call | flops 10000000 | bytes 1048576 | tf_op jit(solution)/shard_map/scan_kernel/pallas_call | solution.py:541
  24.2 0.3 collective-permute-done.2.refs_0_
  24.5 0.6 %enter_first_kernel.1 = (bf16[64,16,128]{2,1,0:T(8,128)(2,1)S(1)}, bf16[48,16,128]{2,1,0:T(8,128)(2,1)S(1)}) custom-call(f32[64,128]{1,0:T(8,128)S(1)} %collective-permute-done.2.refs_0_, f32[64,128]{1,0:T(8,128)S(1)} %collective-permute-done.3.refs_1_, f32[64,128]{1,0:T(8,128)S(1)} %collective-permute-done.4.refs_2_, f32[64,8,128]{2,1,0:T(8,128)S(1)} %scan_kernel.1.refs_3_, ...), custom_call_target="tpu_custom_call" | custom-call | flops 10000000 | bytes 1540096 | tf_op jit(solution)/shard_map/enter_first_kernel/pallas_call | solution.py:541
  25.2 4.2 %collective-permute-start.5 = (bf16[48,16,128]{2,1,0:T(8,128)(2,1)S(1)}, bf16[48,16,128]{2,1,0:T(8,128)(2,1)S(1)}, u32[]{:S(2)}, u32[]{:S(2)}) collective-permute-start(bf16[48,16,128]{2,1,0:T(8,128)(2,1)S(1)} %get-tuple-element.48), channel_id=1, source_target_pairs={{1,2},{2,1},{5,6},{6,5},{9,10},{10,9},{13,14},{14,13},{17,18},{18,... | collective-permute-start | bytes 589832 | tf_op jit(solution)/shard_map/ppermute | solution.py:22
  29.4 3.2 %second_early_kernel.1 = (bf16[32,16,128]{2,1,0:T(8,128)(2,1)S(1)}, bf16[32,16,128]{2,1,0:T(8,128)(2,1)S(1)}, bf16[32,16,128]{2,1,0:T(8,128)(2,1)S(1)}, f32[64,8,128]{2,1,0:T(8,128)S(1)}) custom-call(s32[8,256]{1,0:T(8,128)S(1)} %get-tuple-element.43.table, bf16[64,16,128]{2,1,0:T(8,128)(2,1)S(1)} %get-tuple-element.47.own.refs_4_, ...), custom_call_target="tpu_custom_call" | custom-call | flops 1409286144 | bytes 2170880 | tf_op jit(solution)/shard_map/second_early_kernel/pallas_call | solution.py:541
  32.5 0.1 collective-permute-done.5.got
  32.7 3.8 %second_late_kernel.1 = (f32[64,8,128]{2,1,0:T(8,128)S(1)}, f32[64,128]{1,0:T(8,128)S(1)}) custom-call(s32[8,256]{1,0:T(8,128)S(1)} %get-tuple-element.43.table, bf16[64,16,128]{2,1,0:T(8,128)(2,1)S(1)} %get-tuple-element.47.own.refs_4_, bf16[48,16,128]{2,1,0:T(8,128)(2,1)S(1)} %collective-permute-done.5.got, ...), custom_call_target="tpu_custom_call" | custom-call | flops 1879048192 | bytes 2400256 | tf_op jit(solution)/shard_map/second_late_kernel/pallas_call | solution.py:541
  36.5 2.8 %collective-permute-start.9 = (f32[64,128]{1,0:T(8,128)S(1)}, f32[64,128]{1,0:T(8,128)S(1)}, u32[]{:S(2)}, u32[]{:S(2)}) collective-permute-start(f32[64,128]{1,0:T(8,128)S(1)} %get-tuple-element.53), channel_id=1, source_target_pairs={{0,12},{1,13},{2,14},{3,15},{16,28},{17,29},{18,30},{19,31}} | collective-permute-start | bytes 98312 | tf_op jit(solution)/shard_map/ppermute | solution.py:28
  39.3 1.3 %collective-permute-start.8 = (f32[64,128]{1,0:T(8,128)S(1)}, f32[64,128]{1,0:T(8,128)S(1)}, u32[]{:S(2)}, u32[]{:S(2)}) collective-permute-start(f32[64,128]{1,0:T(8,128)S(1)} %get-tuple-element.53), channel_id=1, source_target_pairs={{0,8},{4,12},{1,9},{5,13},{2,10},{6,14},{3,11},{7,15},{16,24},{20,... | collective-permute-start | bytes 98312 | tf_op jit(solution)/shard_map/ppermute | solution.py:28
  40.5 2.4 %collective-permute-start.7 = (f32[64,128]{1,0:T(8,128)S(1)}, f32[64,128]{1,0:T(8,128)S(1)}, u32[]{:S(2)}, u32[]{:S(2)}) collective-permute-start(f32[64,128]{1,0:T(8,128)S(1)} %get-tuple-element.53), channel_id=1, source_target_pairs={{0,4},{4,8},{8,12},{1,5},{5,9},{9,13},{2,6},{6,10},{10,14},{3,7},{... | collective-permute-start | bytes 98312 | tf_op jit(solution)/shard_map/ppermute | solution.py:28
  43.0 0.7 %scan_sum_kernel.1 = (f32[64,8,128]{2,1,0:T(8,128)S(1)}, f32[64,8,128]{2,1,0:T(8,128)S(1)}) custom-call(f32[64,8,128]{2,1,0:T(8,128)S(1)} %get-tuple-element.54.values, f32[64,8,128]{2,1,0:T(8,128)S(1)} %get-tuple-element.45.values.w1, f32[64,8,128]{2,1,0:T(8,128)S(1)} %get-tuple-element.52.coarse, bf16[1024,256]{1,0:T(8,128)(2,1)S(1)} %get-tuple-element.42.pk.refs_5_.refs_7_), custom_call_target="tpu_custom_call" | custom-call | flops 10000000 | bytes 1835008 | tf_op jit(solution)/shard_map/scan_sum_kernel/pallas_call | solution.py:541
  43.8 0.6 %enter_second_kernel.1 = (bf16[64,16,128]{2,1,0:T(8,128)(2,1)S(1)}, bf16[48,16,128]{2,1,0:T(8,128)(2,1)S(1)}, bf16[40,16,128]{2,1,0:T(8,128)(2,1)S(1)}, f32[64,8,128]{2,1,0:T(8,128)S(1)}) custom-call(f32[64,128]{1,0:T(8,128)S(1)} %collective-permute-done.7.refs_0_, f32[64,128]{1,0:T(8,128)S(1)} %collective-permute-done.8.refs_1_, ...), custom_call_target="tpu_custom_call" | custom-call | flops 10000000 | bytes 2260992 | tf_op jit(solution)/shard_map/enter_second_kernel/pallas_call | solution.py:541
  44.5 4.8 %collective-permute-start.10 = (bf16[40,16,128]{2,1,0:T(8,128)(2,1)S(1)}, bf16[40,16,128]{2,1,0:T(8,128)(2,1)S(1)}, u32[]{:S(2)}, u32[]{:S(2)}) collective-permute-start(bf16[40,16,128]{2,1,0:T(8,128)(2,1)S(1)} %get-tuple-element.57), channel_id=1, source_target_pairs={{1,2},{2,1},{5,6},{6,5},{9,10},{10,9},{13,14},{14,13},{17,18},{18,... | collective-permute-start | bytes 491528 | tf_op jit(solution)/shard_map/ppermute | solution.py:22
  49.3 3.4 %third_early_kernel.1 = (f32[8,4,64,128]{3,2,1,0:T(8,128)}, bf16[32,16,128]{2,1,0:T(8,128)(2,1)S(1)}, bf16[32,16,128]{2,1,0:T(8,128)(2,1)S(1)}, f32[16,8,128]{2,1,0:T(8,128)S(1)}) custom-call(s32[8,256]{1,0:T(8,128)S(1)} %get-tuple-element.43.table, bf16[64,16,128]{2,1,0:T(8,128)(2,1)S(1)} %get-tuple-element.56.own, ...), custom_call_target="tpu_custom_call" | custom-call | flops 1056964608 | bytes 4112384 | tf_op jit(solution)/shard_map/third_early_kernel/pallas_call | solution.py:541
  52.7 3.2 %third_late_kernel.1 = f32[8,4,64,128]{3,2,1,0:T(8,128)} custom-call(s32[8,256]{1,0:T(8,128)S(1)} %get-tuple-element.43.table, bf16[64,16,128]{2,1,0:T(8,128)(2,1)S(1)} %get-tuple-element.56.own, bf16[40,16,128]{2,1,0:T(8,128)(2,1)S(1)} %collective-permute-done.10.got, ...), custom_call_target="tpu_custom_call", output_to_operand_aliasing={{}: (9, {})} | custom-call | flops 1056964608 | bytes 4079616 | tf_op jit(solution)/shard_map/third_late_kernel/pallas_call | solution.py:541
  (22 shorter events, 0.3 us)
Async XLA Ops:
  0.0 7.1 %copy-start.2 = (f32[6,128,128]{2,1,0:T(8,128)S(1)}, f32[6,128,128]{2,1,0:T(8,128)}, u32[]{:S(2)}) copy-start(f32[6,128,128]{2,1,0:T(8,128)} %faces.1) | copy-start | bytes 1179652
  0.0 7.1 %copy-start.3 = (f32[128,128]{1,0:T(8,128)S(1)}, f32[128,128]{1,0:T(8,128)}, u32[]{:S(2)}) copy-start(f32[128,128]{1,0:T(8,128)} %diag.1) | copy-start | bytes 196612
  0.0 7.1 %copy-start.4 = (f32[128,128]{1,0:T(8,128)S(1)}, f32[128,128]{1,0:T(8,128)}, u32[]{:S(2)}) copy-start(f32[128,128]{1,0:T(8,128)} %coarse.1) | copy-start | bytes 196612
  2.3 6.3 %collective-permute-start = (bf16[912,128]{1,0:T(8,128)(2,1)}, bf16[912,128]{1,0:T(8,128)(2,1)S(1)}, u32[]{:S(2)}, u32[]{:S(2)}) collective-permute-start(bf16[912,128]{1,0:T(8,128)(2,1)} %get-tuple-element.36), channel_id=1, source_target_pairs={{0,1},{1,0},{2,3},{3,2},{4,5},{5,4},{6,7},{7,6},{8,9},{9,8},{10,11... | collective-permute-start | bytes 700424 | tf_op jit(solution)/shard_map/ppermute | solution.py:22
  2.4 6.2 %copy-start = (bf16[2064,128]{1,0:T(8,128)(2,1)S(1)}, bf16[2064,128]{1,0:T(8,128)(2,1)}, u32[]{:S(2)}) copy-start(bf16[2064,128]{1,0:T(8,128)(2,1)} %get-tuple-element.35.fe) | copy-start | bytes 1585156
  2.4 6.2 %copy-start.1 = (f32[64,128]{1,0:T(8,128)S(1)}, f32[64,128]{1,0:T(8,128)}, u32[]{:S(2)}) copy-start(f32[64,128]{1,0:T(8,128)} %refs_5_.1) | copy-start | bytes 98308
  2.4 8.6 %collective-permute-start.1 = (bf16[912,128]{1,0:T(8,128)(2,1)}, bf16[912,128]{1,0:T(8,128)(2,1)S(1)}, u32[]{:S(2)}, u32[]{:S(2)}) collective-permute-start(bf16[912,128]{1,0:T(8,128)(2,1)} %get-tuple-element.37), channel_id=1, source_target_pairs={{1,2},{2,1},{5,6},{6,5},{9,10},{10,9},{13,14},{14,13},{17,18},{18,... | collective-permute-start | bytes 700424 | tf_op jit(solution)/shard_map/ppermute | solution.py:22
  14.2 10.0 %collective-permute-start.4 = (f32[64,128]{1,0:T(8,128)S(1)}, f32[64,128]{1,0:T(8,128)S(1)}, u32[]{:S(2)}, u32[]{:S(2)}) collective-permute-start(f32[64,128]{1,0:T(8,128)S(1)} %get-tuple-element.44), channel_id=1, source_target_pairs={{0,12},{1,13},{2,14},{3,15},{16,28},{17,29},{18,30},{19,31}} | collective-permute-start | bytes 98312 | tf_op jit(solution)/shard_map/ppermute | solution.py:28
  20.0 4.2 %collective-permute-start.3 = (f32[64,128]{1,0:T(8,128)S(1)}, f32[64,128]{1,0:T(8,128)S(1)}, u32[]{:S(2)}, u32[]{:S(2)}) collective-permute-start(f32[64,128]{1,0:T(8,128)S(1)} %get-tuple-element.44), channel_id=1, source_target_pairs={{0,8},{4,12},{1,9},{5,13},{2,10},{6,14},{3,11},{7,15},{16,24},{20,... | collective-permute-start | bytes 98312 | tf_op jit(solution)/shard_map/ppermute | solution.py:28
  21.3 3.2 %collective-permute-start.2 = (f32[64,128]{1,0:T(8,128)S(1)}, f32[64,128]{1,0:T(8,128)S(1)}, u32[]{:S(2)}, u32[]{:S(2)}) collective-permute-start(f32[64,128]{1,0:T(8,128)S(1)} %get-tuple-element.44), channel_id=1, source_target_pairs={{0,4},{4,8},{8,12},{1,5},{5,9},{9,13},{2,6},{6,10},{10,14},{3,7},{... | collective-permute-start | bytes 98312 | tf_op jit(solution)/shard_map/ppermute | solution.py:28
  25.1 4.3 %collective-permute-start.6 = (bf16[64,16,128]{2,1,0:T(8,128)(2,1)S(1)}, bf16[64,16,128]{2,1,0:T(8,128)(2,1)S(1)}, u32[]{:S(2)}, u32[]{:S(2)}) collective-permute-start(bf16[64,16,128]{2,1,0:T(8,128)(2,1)S(1)} %get-tuple-element.47.own.refs_4_), channel_id=1, source_target_pairs={{0,1},{1,0},{2,3},{3,2},{4,5},{5,4},{6,7},{7,6},{8,9},{9,8},{10,11... | collective-permute-start | bytes 786440 | tf_op jit(solution)/shard_map/ppermute | solution.py:22
  25.2 7.5 %collective-permute-start.5 = (bf16[48,16,128]{2,1,0:T(8,128)(2,1)S(1)}, bf16[48,16,128]{2,1,0:T(8,128)(2,1)S(1)}, u32[]{:S(2)}, u32[]{:S(2)}) collective-permute-start(bf16[48,16,128]{2,1,0:T(8,128)(2,1)S(1)} %get-tuple-element.48), channel_id=1, source_target_pairs={{1,2},{2,1},{5,6},{6,5},{9,10},{10,9},{13,14},{14,13},{17,18},{18,... | collective-permute-start | bytes 589832 | tf_op jit(solution)/shard_map/ppermute | solution.py:22
  36.5 7.2 %collective-permute-start.9 = (f32[64,128]{1,0:T(8,128)S(1)}, f32[64,128]{1,0:T(8,128)S(1)}, u32[]{:S(2)}, u32[]{:S(2)}) collective-permute-start(f32[64,128]{1,0:T(8,128)S(1)} %get-tuple-element.53), channel_id=1, source_target_pairs={{0,12},{1,13},{2,14},{3,15},{16,28},{17,29},{18,30},{19,31}} | collective-permute-start | bytes 98312 | tf_op jit(solution)/shard_map/ppermute | solution.py:28
  39.3 4.4 %collective-permute-start.8 = (f32[64,128]{1,0:T(8,128)S(1)}, f32[64,128]{1,0:T(8,128)S(1)}, u32[]{:S(2)}, u32[]{:S(2)}) collective-permute-start(f32[64,128]{1,0:T(8,128)S(1)} %get-tuple-element.53), channel_id=1, source_target_pairs={{0,8},{4,12},{1,9},{5,13},{2,10},{6,14},{3,11},{7,15},{16,24},{20,... | collective-permute-start | bytes 98312 | tf_op jit(solution)/shard_map/ppermute | solution.py:28
  40.5 3.2 %collective-permute-start.7 = (f32[64,128]{1,0:T(8,128)S(1)}, f32[64,128]{1,0:T(8,128)S(1)}, u32[]{:S(2)}, u32[]{:S(2)}) collective-permute-start(f32[64,128]{1,0:T(8,128)S(1)} %get-tuple-element.53), channel_id=1, source_target_pairs={{0,4},{4,8},{8,12},{1,5},{5,9},{9,13},{2,6},{6,10},{10,14},{3,7},{... | collective-permute-start | bytes 98312 | tf_op jit(solution)/shard_map/ppermute | solution.py:28
  44.4 4.9 %collective-permute-start.11 = (bf16[48,16,128]{2,1,0:T(8,128)(2,1)S(1)}, bf16[48,16,128]{2,1,0:T(8,128)(2,1)S(1)}, u32[]{:S(2)}, u32[]{:S(2)}) collective-permute-start(bf16[48,16,128]{2,1,0:T(8,128)(2,1)S(1)} %get-tuple-element.58), channel_id=1, source_target_pairs={{0,1},{1,0},{2,3},{3,2},{4,5},{5,4},{6,7},{7,6},{8,9},{9,8},{10,11... | collective-permute-start | bytes 589832 | tf_op jit(solution)/shard_map/ppermute | solution.py:22
  44.5 8.2 %collective-permute-start.10 = (bf16[40,16,128]{2,1,0:T(8,128)(2,1)S(1)}, bf16[40,16,128]{2,1,0:T(8,128)(2,1)S(1)}, u32[]{:S(2)}, u32[]{:S(2)}) collective-permute-start(bf16[40,16,128]{2,1,0:T(8,128)(2,1)S(1)} %get-tuple-element.57), channel_id=1, source_target_pairs={{1,2},{2,1},{5,6},{6,5},{9,10},{10,9},{13,14},{14,13},{17,18},{18,... | collective-permute-start | bytes 491528 | tf_op jit(solution)/shard_map/ppermute | solution.py:22

commit v12 on v11

--- a/solution.py
+++ b/solution.py
@@ -88,10 +88,10 @@
     return y[...].reshape(n, 8, 128)
 
 
-def apply_phi(src, idx, w, base, size):
+def apply_phi(src, idx, origin, w, base, size):
     cols = [src[pl.ds(base, size)].reshape(size * 16, 128)]
     for f in range(6):
-        cols.append(jnp.concatenate([src[idx[f, base + e]] for e in range(size)], axis=0))
+        cols.append(jnp.concatenate([src[idx[f, base - origin + e]] for e in range(size)], axis=0))
     return product(jnp.concatenate(cols, axis=1), w[...])
 
 
@@ -215,25 +215,26 @@
     return src[pl.ds(base * 8, size * 8), :].astype(F32).reshape(size, 8, 128)
 
 
-def put_tables(fe, got_even, got_odd, idx_v, full, n, even):
-    lane = lax.broadcasted_iota(jnp.int32, (8, 128), 1)
-
-    def table(ref):
-        return 0.0 if ref is None else ref[pl.ds(ref.shape[0] - 16, 16), :].astype(F32)[0:8]
-
-    from_even, from_odd = table(got_even), table(got_odd)
-    low = jnp.where(lane < n, from_odd if even else from_even, table(fe))
-    high = jnp.where(lane < n, from_even if even else from_odd, 0.0)
-    for at, offs in ((0, low), (128, high)):
-        value = jnp.where(offs != 0.0, lane + at + offs.astype(jnp.int32), full)
-        idx_v[:, pl.ds(at, 128)] = value
-
-
-def push_init(init, got_even, got_odd, w, idx_v, columns, square, i16, base, count, n, even):
-    for at in (0, 128):
-        square[...] = jnp.zeros_like(square)
-        square[0:8, :] = idx_v[:, pl.ds(at, 128)].astype(F32)
-        columns[pl.ds(at, 128), :] = square[...].T
+def origin_of(even, late, n):
+    return n if even != late else 0
+
+
+def put_table(table, fe, got, even, late):
+    n = table.shape[1] // 2
+    lane = lax.broadcasted_iota(jnp.int32, table.shape, 1)
+
+    def part(ref):
+        return ref[pl.ds(ref.shape[0] - 16, 16), :].astype(F32)[0:8]
+
+    origin = origin_of(even, late, n)
+    offs = jnp.where(lane < n, part(fe), part(got)) if origin else jnp.where(lane < n, part(got), part(fe))
+    table[...] = jnp.where(offs != 0.0, lane + origin + offs.astype(jnp.int32), 3 * n)
+
+
+def push_init(init, got_even, got_odd, w, table, origin, columns, square, i16, base, count, n, even):
+    square[...] = jnp.zeros_like(square)
+    square[0:8, :] = table[...].astype(F32)
+    columns[...] = square[...].T
     i16[...] = jnp.zeros_like(i16)
     lead = init[...].astype(BF16)
     i16[pl.ds(n, n), 0:128] = lead
@@ -245,7 +246,7 @@
             i16[pl.ds(to, n), 0:128] = ref[pl.ds(at - 2 * n, n), :]
             i16[pl.ds(to, n), 128:256] = ref[pl.ds(at - n, n), :]
     rows = pl.ds(base, count)
-    place = columns[rows, :]
+    place = columns[pl.ds(base - origin, count), :]
     spot = lax.broadcasted_iota(jnp.int32, (count, 256), 1).astype(F32)
     cols = [i16[rows, :]]
     for f in range(6):
@@ -272,13 +273,14 @@
 
 
 def first_early_kernel(
-    fe, init, got, w, strip1, strip2, strip3, s1, s2, s3, force, y, i16, columns, square, idx_v, idx, sem
+    fe, init, got, w, strip1, strip2, strip3, table, s1, s2, s3, force, y, i16, columns, square, idx, sem
 ):
     def body(even):
         n = init.shape[0]
         full = 3 * n
-        put_tables(fe, got, None, idx_v, full, n, even)
-        copy = pltpu.make_async_copy(idx_v, idx, sem)
+        origin = origin_of(even, False, n)
+        put_table(table, fe, got, even, False)
+        copy = pltpu.make_async_copy(table, idx, sem)
         copy.start()
         count = 6 * REACH
         base = mirrored(REACH, count, full, even)
@@ -286,7 +288,7 @@
         y[pl.ds(0, count * 8), :] = force[pl.ds(base * 8, count * 8), :].astype(F32)
 
         def add_init():
-            pushed = push_init(init, got, None, w, idx_v, columns, square, i16, base, count, n, even)
+            pushed = push_init(init, got, None, w, table, origin, columns, square, i16, base, count, n, even)
             y[pl.ds(0, count, stride=8), :] = y[pl.ds(0, count, stride=8), :] + pushed
 
         pl.when(lax.axis_index("tm") == 0)(add_init)
@@ -298,21 +300,22 @@
             put_force(force, fe, got, even, k, n)
             size = (6 - 2 * k) * REACH
             base = mirrored((k + 1) * REACH, size, full, even)
-            dst[pl.ds(base, size)] = split(apply_phi(src, idx, w, base, size) + force_at(force, base, size))
+            dst[pl.ds(base, size)] = split(apply_phi(src, idx, origin, w, base, size) + force_at(force, base, size))
         put_strips((strip1, strip2, strip3), (s1, s2, s3), full, even)
 
     by_parity(body)
 
 
 def first_late_kernel(
-    fe, init, got_even, got_odd, strip1, strip2, strip3, w, pk, w1, end, idx_out,
+    fe, init, got_even, got_odd, strip1, strip2, strip3, w, pk, w1, end, table,
     s1, s2, s3, force, y, i16, columns, square, idx, sem
 ):
     def body(even):
         n = init.shape[0]
         full = 3 * n
-        put_tables(fe, got_even, got_odd, idx_out, full, n, even)
-        copy = pltpu.make_async_copy(idx_out, idx, sem)
+        origin = origin_of(even, True, n)
+        put_table(table, fe, got_odd, even, True)
+        copy = pltpu.make_async_copy(table, idx, sem)
         copy.start()
         count = 4 * REACH
         base = mirrored(7 * REACH, count, full, even)
@@ -320,7 +323,7 @@
         y[...] = force[pl.ds(base * 8, count * 8), :].astype(F32)
 
         def add_init():
-            pushed = push_init(init, got_even, got_odd, w, idx_out, columns, square, i16, base, count, n, even)
+            pushed = push_init(init, got_even, got_odd, w, table, origin, columns, square, i16, base, count, n, even)
             y[pl.ds(0, count, stride=8), :] = y[pl.ds(0, count, stride=8), :] + pushed
 
         pl.when(lax.axis_index("tm") == 0)(add_init)
@@ -330,7 +333,7 @@
         for k, src, dst in ((1, s1, s2), (2, s2, s3), (3, s3, None)):
             put_force(force, fe, got_odd, not even, k, n)
             base = mirrored((7 - k) * REACH, count, full, even)
-            value = apply_phi(src, idx, w, base, count) + force_at(force, base, count)
+            value = apply_phi(src, idx, origin, w, base, count) + force_at(force, base, count)
             if dst is None:
                 w1[...] = value
                 y[...] = value.reshape(n * 8, 128)
@@ -411,6 +414,7 @@
         copy = pltpu.make_async_copy(table, idx, sem)
         copy.start()
         n = own.shape[0]
+        origin = origin_of(even, False, n)
         full = 3 * n
         coarse[...] = product(own[...].reshape(n * 16, 128), power(pk, 1))
         put_block(s0, own, got, even, n)
@@ -420,7 +424,7 @@
         for k, src, dst in ((1, s0, s1), (2, s1, s2), (3, s2, s3)):
             size = (8 - 2 * k) * REACH
             base = mirrored(k * REACH, size, full, even)
-            dst[pl.ds(base, size)] = split(apply_phi(src, idx, w, base, size))
+            dst[pl.ds(base, size)] = split(apply_phi(src, idx, origin, w, base, size))
         put_strips((strip1, strip2, strip3), (s1, s2, s3), full, even)
 
     by_parity(body)
@@ -431,6 +435,7 @@
         copy = pltpu.make_async_copy(table, idx, sem)
         copy.start()
         n = own.shape[0]
+        origin = origin_of(even, True, n)
         full = 3 * n
         put_far(s0, own, got, not even, n)
         get_strips((strip1, strip2, strip3), (s1, s2, s3), full, even)
@@ -438,8 +443,8 @@
         copy.wait()
         for k, src, dst in ((1, s0, s1), (2, s1, s2), (3, s2, s3)):
             base = mirrored((8 - k) * REACH, count, full, even)
-            dst[pl.ds(base, count)] = split(apply_phi(src, idx, w, base, count))
-        value = apply_phi(s3, idx, w, n, n)
+            dst[pl.ds(base, count)] = split(apply_phi(src, idx, origin, w, base, count))
+        value = apply_phi(s3, idx, origin, w, n, n)
         value = value - coarse[...]
         res[...] = value
         y[...] = value.reshape(n * 8, 128)
@@ -467,6 +472,7 @@
         table_copy = pltpu.make_async_copy(table, idx, sem)
         table_copy.start()
         n = own.shape[0]
+        origin = origin_of(even, False, n)
         full = 3 * n
         points = product(split(corr[...]).reshape(-1, 128), power(pk, 1)) + total[...]
         flip_tiles(flip3, points, 0)
@@ -479,7 +485,7 @@
             put_force(force, fe, pay, even, k, n)
             size = (5 - 2 * k) * REACH
             base = mirrored((2 + k) * REACH, size, full, even)
-            value = apply_phi(src, idx, w, base, size) + force_at(force, base, size)
+            value = apply_phi(src, idx, origin, w, base, size) + force_at(force, base, size)
             if dst is not None:
                 dst[pl.ds(base, size)] = split(value)
             mine = (3 - k) * REACH
@@ -503,6 +509,7 @@
         table_copy = pltpu.make_async_copy(table, idx, sem)
         table_copy.start()
         n = own.shape[0]
+        origin = origin_of(even, True, n)
         full = 3 * n
         put_far(s0, own, got, not even, n)
         get_strips((strip1, strip2), (s1, s2), full, even)
@@ -513,7 +520,7 @@
         for k, src, dst, flip in ((0, s0, s1, flip0), (1, s1, s2, flip1), (2, s2, None, flip2)):
             put_force(force, fe, pay, not even, k, n)
             base = mirrored((7 - k) * REACH, size, full, even)
-            value = apply_phi(src, idx, w, base, size) + force_at(force, base, size)
+            value = apply_phi(src, idx, origin, w, base, size) + force_at(force, base, size)
             if dst is not None:
                 dst[pl.ds(base, size)] = split(value)
             mine = (k + 1) * REACH
@@ -604,19 +611,20 @@
     force = vmem((full * 8, width), BF16)
     rows = vmem((n * 8, width), F32)
     strip = shape((STRIP, 16, width), BF16)
-    tables = [vmem((256, 256), BF16), vmem((256, 128), F32), vmem((128, 128), F32)]
-    smem = pltpu.SMEM((8, 256), jnp.int32)
-    strips = call(
+    tables = [vmem((256, 256), BF16), vmem((128, 128), F32), vmem((128, 128), F32)]
+    smem = pltpu.SMEM((8, 2 * n), jnp.int32)
+    table = shape((8, 2 * n), jnp.int32)
+    *strips, table_early = call(
         first_early_kernel,
         (fe, initial_state, pay_even, w),
-        (strip, strip, strip),
-        [spaces] * 3 + [force, vmem((6 * REACH * 8, width), F32)] + tables + [vmem((8, 256), jnp.int32), smem, dma],
+        (strip, strip, strip, table),
+        [spaces] * 3 + [force, vmem((6 * REACH * 8, width), F32)] + tables + [smem, dma],
         flops=step_flops * 6 * REACH,
     )
-    w1, end, idx = call(
+    w1, end, table_late = call(
         first_late_kernel,
         (fe, initial_state, pay_even, pay_odd, *strips, w, pk),
-        (tiles, ends, shape((8, 256), jnp.int32)),
+        (tiles, ends, table),
         [spaces] * 3 + [force, rows] + tables + [smem, dma],
         flops=step_flops * 12 * REACH,
     )
@@ -629,14 +637,14 @@
     got_odd, got_even = swapped(end_odd, 1), swapped(coarse, 0)
     *strips, moved = call(
         second_early_kernel,
-        (idx, coarse, got_even, w, pk),
+        (table_early, coarse, got_even, w, pk),
         (strip, strip, strip, tiles),
         [smem, dma] + [spaces] * 4,
         flops=step_flops * 12 * REACH,
     )
     res, end = call(
         second_late_kernel,
-        (idx, coarse, got_odd, *strips, moved, w, pk),
+        (table_late, coarse, got_odd, *strips, moved, w, pk),
         (tiles, ends),
         [smem, dma] + [spaces] * 4 + [rows],
         flops=step_flops * 16 * REACH,
@@ -658,7 +666,7 @@
 
     out, *strips = call(
         third_early_kernel,
-        (idx, coarse, got_even, corr, total, fe, pay_even, w, pk),
+        (table_early, coarse, got_even, corr, total, fe, pay_even, w, pk),
         (result, strip, strip, shape((REACH, 8, width), F32)),
         [smem, dma] + [spaces] * 3 + [force, flip(3), flip(2), vmem((8, n + 8, width), F32), dma((COARSEN,))],
         out_spaces="h",
@@ -666,7 +674,7 @@
     )
     (out,) = call(
         third_late_kernel,
-        (idx, coarse, got_odd, *strips, fe, pay_odd, w, out),
+        (table_late, coarse, got_odd, *strips, fe, pay_odd, w, out),
         (result,),
         [smem, dma] + [spaces] * 3 + [force, flip(1), flip(2), vmem((8, n + 8, width), F32), dma((COARSEN - 1,))],
         spaces="vvvvvvvvvh",

time: 56.3 us -> 56 us (level)
  transfers between devices with their start and end apart: 12 -> 12, of which waited for: 4 -> 3; matrix products, arithmetic and copies ran while one was open for 0% -> 0% of each run, Pallas kernels for 20% -> 20%
where the time goes in v12:
time: 56 us; the launch traced here: 55.7 us
  starting transfers between devices  29.6 us (53%)
  Pallas kernels  24.7 us (44%)
  waiting for transfers between devices  0.97 us (2%)
    pallas_call x12, Pallas kernels, call(): pl.pallas_call(kernel, out_shape=outs, name=kernel.__name__, in_specs=spe...  24.7 us
    ppermute x6, starting transfers between devices, earlier(): lax.ppermute(value, 'tm', [(i, i + s) for i in range(count - s)])  15.7 us
    ppermute x6, starting transfers between devices, swapped(): return lax.ppermute(value, 'space', pairs)  13.8 us
  transfers between devices with their start and end apart: 12, of which 3 were waited for; matrix products, arithmetic and copies ran while one was open for 0% of the time, Pallas kernels for 20%

profile of v12, /device:TPU:1, one launch (start us, length us, event | category | flops | bytes accessed | tf_op | source)
XLA Modules:
  0.0 55.7 jit_solution(9766192574415687665)
XLA Ops:
  0.0 2.3 %pack_kernel.1 = (bf16[2064,128]{1,0:T(8,128)(2,1)}, bf16[912,128]{1,0:T(8,128)(2,1)}, bf16[912,128]{1,0:T(8,128)(2,1)}) custom-call(bf16[8,4,64,128]{3,2,1,0:T(8,128)(2,1)} %bitcast.4, f32[64,128]{1,0:T(8,128)} %refs_5_.1, s32[6,64]{1,0:T(8,128)} %bitcast.5, s32[6,64]{1,0:T(8,128)} %bitcast.6), custom_call_target="tpu_custom_call" | custom-call | flops 3000000000 | bytes 1555456 | tf_op jit(solution)/shard_map/pack_kernel/pallas_call | solution.py:548
  2.4 4.6 %collective-permute-start.1 = (bf16[912,128]{1,0:T(8,128)(2,1)}, bf16[912,128]{1,0:T(8,128)(2,1)S(1)}, u32[]{:S(2)}, u32[]{:S(2)}) collective-permute-start(bf16[912,128]{1,0:T(8,128)(2,1)} %get-tuple-element.38), channel_id=1, source_target_pairs={{1,2},{2,1},{5,6},{6,5},{9,10},{10,9},{13,14},{14,13},{17,18},{18,... | collective-permute-start | bytes 700424 | tf_op jit(solution)/shard_map/ppermute | solution.py:22
  7.1 1.5 %weight_kernel.1 = (bf16[896,256]{1,0:T(8,128)(2,1)S(1)}, bf16[1024,256]{1,0:T(8,128)(2,1)S(1)}, bf16[384,256]{1,0:T(8,128)(2,1)S(1)}) custom-call(f32[128,128]{1,0:T(8,128)S(1)} %copy-done.3, f32[6,128,128]{2,1,0:T(8,128)S(1)} %copy-done.2, f32[128,128]{1,0:T(8,128)S(1)} %copy-done.4), custom_call_target="tpu_custom_call" | custom-call | flops 1000000000 | bytes 1703936 | tf_op jit(solution)/shard_map/weight_kernel/pallas_call | solution.py:548
  8.7 1.9 %first_early_kernel.1 = (bf16[32,16,128]{2,1,0:T(8,128)(2,1)S(1)}, bf16[32,16,128]{2,1,0:T(8,128)(2,1)S(1)}, bf16[32,16,128]{2,1,0:T(8,128)(2,1)S(1)}, s32[8,128]{1,0:T(8,128)S(1)}) custom-call(bf16[2064,128]{1,0:T(8,128)(2,1)S(1)} %copy-done, f32[64,128]{1,0:T(8,128)S(1)} %copy-done.1, bf16[912,128]{1,0:T(8,128)(2,1)S(1)} %collective-permute-done.got.got_even.pay, ...), custom_call_target="tpu_custom_call" | custom-call | flops 704643072 | bytes 1650688 | tf_op jit(solution)/shard_map/first_early_kernel/pallas_call | solution.py:548
  10.6 0.4 collective-permute-done.1.got_odd.pay
  11.0 3.2 %first_late_kernel.1 = (f32[64,8,128]{2,1,0:T(8,128)S(1)}, f32[64,128]{1,0:T(8,128)S(1)}, s32[8,128]{1,0:T(8,128)S(1)}) custom-call(bf16[2064,128]{1,0:T(8,128)(2,1)S(1)} %copy-done, f32[64,128]{1,0:T(8,128)S(1)} %copy-done.1, bf16[912,128]{1,0:T(8,128)(2,1)S(1)} %collective-permute-done.got.got_even.pay, ...), custom_call_target="tpu_custom_call" | custom-call | flops 1409286144 | bytes 2703360 | tf_op jit(solution)/shard_map/first_late_kernel/pallas_call | solution.py:548
  14.2 5.8 %collective-permute-start.4 = (f32[64,128]{1,0:T(8,128)S(1)}, f32[64,128]{1,0:T(8,128)S(1)}, u32[]{:S(2)}, u32[]{:S(2)}) collective-permute-start(f32[64,128]{1,0:T(8,128)S(1)} %get-tuple-element.45), channel_id=1, source_target_pairs={{0,12},{1,13},{2,14},{3,15},{16,28},{17,29},{18,30},{19,31}} | collective-permute-start | bytes 98312 | tf_op jit(solution)/shard_map/ppermute | solution.py:28
  20.0 1.3 %collective-permute-start.3 = (f32[64,128]{1,0:T(8,128)S(1)}, f32[64,128]{1,0:T(8,128)S(1)}, u32[]{:S(2)}, u32[]{:S(2)}) collective-permute-start(f32[64,128]{1,0:T(8,128)S(1)} %get-tuple-element.45), channel_id=1, source_target_pairs={{0,8},{4,12},{1,9},{5,13},{2,10},{6,14},{3,11},{7,15},{16,24},{20,... | collective-permute-start | bytes 98312 | tf_op jit(solution)/shard_map/ppermute | solution.py:28
  21.3 2.2 %collective-permute-start.2 = (f32[64,128]{1,0:T(8,128)S(1)}, f32[64,128]{1,0:T(8,128)S(1)}, u32[]{:S(2)}, u32[]{:S(2)}) collective-permute-start(f32[64,128]{1,0:T(8,128)S(1)} %get-tuple-element.45), channel_id=1, source_target_pairs={{0,4},{4,8},{8,12},{1,5},{5,9},{9,13},{2,6},{6,10},{10,14},{3,7},{... | collective-permute-start | bytes 98312 | tf_op jit(solution)/shard_map/ppermute | solution.py:28
  23.5 0.7 %scan_kernel.1.refs_3_ = f32[64,8,128]{2,1,0:T(8,128)S(1)} custom-call(f32[64,8,128]{2,1,0:T(8,128)S(1)} %get-tuple-element.46.values.w1, bf16[1024,256]{1,0:T(8,128)(2,1)S(1)} %get-tuple-element.43.pk.refs_5_.refs_7_), custom_call_target="tpu_custom_call" | custom-call | flops 10000000 | bytes 1048576 | tf_op jit(solution)/shard_map/scan_kernel/pallas_call | solution.py:548
  24.2 0.3 collective-permute-done.2.refs_0_
  24.5 0.6 enter_first_kernel.1
  25.1 4.2 %collective-permute-start.5 = (bf16[48,16,128]{2,1,0:T(8,128)(2,1)S(1)}, bf16[48,16,128]{2,1,0:T(8,128)(2,1)S(1)}, u32[]{:S(2)}, u32[]{:S(2)}) collective-permute-start(bf16[48,16,128]{2,1,0:T(8,128)(2,1)S(1)} %get-tuple-element.49), channel_id=1, source_target_pairs={{1,2},{2,1},{5,6},{6,5},{9,10},{10,9},{13,14},{14,13},{17,18},{18,... | collective-permute-start | bytes 589832 | tf_op jit(solution)/shard_map/ppermute | solution.py:22
  29.3 3.1 %second_early_kernel.1 = (bf16[32,16,128]{2,1,0:T(8,128)(2,1)S(1)}, bf16[32,16,128]{2,1,0:T(8,128)(2,1)S(1)}, bf16[32,16,128]{2,1,0:T(8,128)(2,1)S(1)}, f32[64,8,128]{2,1,0:T(8,128)S(1)}) custom-call(s32[8,128]{1,0:T(8,128)S(1)} %get-tuple-element.50.table, bf16[64,16,128]{2,1,0:T(8,128)(2,1)S(1)} %get-tuple-element.48.own.refs_4_, ...), custom_call_target="tpu_custom_call" | custom-call | flops 1409286144 | bytes 2166784 | tf_op jit(solution)/shard_map/second_early_kernel/pallas_call | solution.py:548
  32.4 0.2 collective-permute-done.5.got
  32.6 3.7 %second_late_kernel.1 = (f32[64,8,128]{2,1,0:T(8,128)S(1)}, f32[64,128]{1,0:T(8,128)S(1)}) custom-call(s32[8,128]{1,0:T(8,128)S(1)} %get-tuple-element.44.table, bf16[64,16,128]{2,1,0:T(8,128)(2,1)S(1)} %get-tuple-element.48.own.refs_4_, bf16[48,16,128]{2,1,0:T(8,128)(2,1)S(1)} %collective-permute-done.5.got, ...), custom_call_target="tpu_custom_call" | custom-call | flops 1879048192 | bytes 2396160 | tf_op jit(solution)/shard_map/second_late_kernel/pallas_call | solution.py:548
  36.4 2.8 %collective-permute-start.9 = (f32[64,128]{1,0:T(8,128)S(1)}, f32[64,128]{1,0:T(8,128)S(1)}, u32[]{:S(2)}, u32[]{:S(2)}) collective-permute-start(f32[64,128]{1,0:T(8,128)S(1)} %get-tuple-element.55), channel_id=1, source_target_pairs={{0,12},{1,13},{2,14},{3,15},{16,28},{17,29},{18,30},{19,31}} | collective-permute-start | bytes 98312 | tf_op jit(solution)/shard_map/ppermute | solution.py:28
  39.1 1.3 %collective-permute-start.8 = (f32[64,128]{1,0:T(8,128)S(1)}, f32[64,128]{1,0:T(8,128)S(1)}, u32[]{:S(2)}, u32[]{:S(2)}) collective-permute-start(f32[64,128]{1,0:T(8,128)S(1)} %get-tuple-element.55), channel_id=1, source_target_pairs={{0,8},{4,12},{1,9},{5,13},{2,10},{6,14},{3,11},{7,15},{16,24},{20,... | collective-permute-start | bytes 98312 | tf_op jit(solution)/shard_map/ppermute | solution.py:28
  40.4 2.4 %collective-permute-start.7 = (f32[64,128]{1,0:T(8,128)S(1)}, f32[64,128]{1,0:T(8,128)S(1)}, u32[]{:S(2)}, u32[]{:S(2)}) collective-permute-start(f32[64,128]{1,0:T(8,128)S(1)} %get-tuple-element.55), channel_id=1, source_target_pairs={{0,4},{4,8},{8,12},{1,5},{5,9},{9,13},{2,6},{6,10},{10,14},{3,7},{... | collective-permute-start | bytes 98312 | tf_op jit(solution)/shard_map/ppermute | solution.py:28
  42.8 0.7 %scan_sum_kernel.1 = (f32[64,8,128]{2,1,0:T(8,128)S(1)}, f32[64,8,128]{2,1,0:T(8,128)S(1)}) custom-call(f32[64,8,128]{2,1,0:T(8,128)S(1)} %get-tuple-element.56.values, f32[64,8,128]{2,1,0:T(8,128)S(1)} %get-tuple-element.46.values.w1, f32[64,8,128]{2,1,0:T(8,128)S(1)} %get-tuple-element.54.coarse, bf16[1024,256]{1,0:T(8,128)(2,1)S(1)} %get-tuple-element.43.pk.refs_5_.refs_7_), custom_call_target="tpu_custom_call" | custom-call | flops 10000000 | bytes 1835008 | tf_op jit(solution)/shard_map/scan_sum_kernel/pallas_call | solution.py:548
  43.6 0.6 %enter_second_kernel.1 = (bf16[64,16,128]{2,1,0:T(8,128)(2,1)S(1)}, bf16[48,16,128]{2,1,0:T(8,128)(2,1)S(1)}, bf16[40,16,128]{2,1,0:T(8,128)(2,1)S(1)}, f32[64,8,128]{2,1,0:T(8,128)S(1)}) custom-call(f32[64,128]{1,0:T(8,128)S(1)} %collective-permute-done.7.refs_0_, f32[64,128]{1,0:T(8,128)S(1)} %collective-permute-done.8.refs_1_, ...), custom_call_target="tpu_custom_call" | custom-call | flops 10000000 | bytes 2260992 | tf_op jit(solution)/shard_map/enter_second_kernel/pallas_call | solution.py:548
  44.3 4.8 %collective-permute-start.10 = (bf16[40,16,128]{2,1,0:T(8,128)(2,1)S(1)}, bf16[40,16,128]{2,1,0:T(8,128)(2,1)S(1)}, u32[]{:S(2)}, u32[]{:S(2)}) collective-permute-start(bf16[40,16,128]{2,1,0:T(8,128)(2,1)S(1)} %get-tuple-element.59), channel_id=1, source_target_pairs={{1,2},{2,1},{5,6},{6,5},{9,10},{10,9},{13,14},{14,13},{17,18},{18,... | collective-permute-start | bytes 491528 | tf_op jit(solution)/shard_map/ppermute | solution.py:22
  49.1 3.3 %third_early_kernel.1 = (f32[8,4,64,128]{3,2,1,0:T(8,128)}, bf16[32,16,128]{2,1,0:T(8,128)(2,1)S(1)}, bf16[32,16,128]{2,1,0:T(8,128)(2,1)S(1)}, f32[16,8,128]{2,1,0:T(8,128)S(1)}) custom-call(s32[8,128]{1,0:T(8,128)S(1)} %get-tuple-element.50.table, bf16[64,16,128]{2,1,0:T(8,128)(2,1)S(1)} %get-tuple-element.58.own, ...), custom_call_target="tpu_custom_call" | custom-call | flops 1056964608 | bytes 4108288 | tf_op jit(solution)/shard_map/third_early_kernel/pallas_call | solution.py:548
  52.5 3.1 %third_late_kernel.1 = f32[8,4,64,128]{3,2,1,0:T(8,128)} custom-call(s32[8,128]{1,0:T(8,128)S(1)} %get-tuple-element.44.table, bf16[64,16,128]{2,1,0:T(8,128)(2,1)S(1)} %get-tuple-element.58.own, bf16[40,16,128]{2,1,0:T(8,128)(2,1)S(1)} %collective-permute-done.10.got, ...), custom_call_target="tpu_custom_call", output_to_operand_aliasing={{}: (9, {})} | custom-call | flops 1056964608 | bytes 4075520 | tf_op jit(solution)/shard_map/third_late_kernel/pallas_call | solution.py:548
  (22 shorter events, 0.3 us)
Async XLA Ops:
  0.0 7.1 %copy-start.2 = (f32[6,128,128]{2,1,0:T(8,128)S(1)}, f32[6,128,128]{2,1,0:T(8,128)}, u32[]{:S(2)}) copy-start(f32[6,128,128]{2,1,0:T(8,128)} %faces.1) | copy-start | bytes 1179652
  0.0 7.1 %copy-start.3 = (f32[128,128]{1,0:T(8,128)S(1)}, f32[128,128]{1,0:T(8,128)}, u32[]{:S(2)}) copy-start(f32[128,128]{1,0:T(8,128)} %diag.1) | copy-start | bytes 196612
  0.0 7.1 %copy-start.4 = (f32[128,128]{1,0:T(8,128)S(1)}, f32[128,128]{1,0:T(8,128)}, u32[]{:S(2)}) copy-start(f32[128,128]{1,0:T(8,128)} %coarse.1) | copy-start | bytes 196612
  2.3 6.3 %collective-permute-start = (bf16[912,128]{1,0:T(8,128)(2,1)}, bf16[912,128]{1,0:T(8,128)(2,1)S(1)}, u32[]{:S(2)}, u32[]{:S(2)}) collective-permute-start(bf16[912,128]{1,0:T(8,128)(2,1)} %get-tuple-element.37), channel_id=1, source_target_pairs={{0,1},{1,0},{2,3},{3,2},{4,5},{5,4},{6,7},{7,6},{8,9},{9,8},{10,11... | collective-permute-start | bytes 700424 | tf_op jit(solution)/shard_map/ppermute | solution.py:22
  2.4 6.2 %copy-start = (bf16[2064,128]{1,0:T(8,128)(2,1)S(1)}, bf16[2064,128]{1,0:T(8,128)(2,1)}, u32[]{:S(2)}) copy-start(bf16[2064,128]{1,0:T(8,128)(2,1)} %get-tuple-element.36.fe) | copy-start | bytes 1585156
  2.4 6.2 %copy-start.1 = (f32[64,128]{1,0:T(8,128)S(1)}, f32[64,128]{1,0:T(8,128)}, u32[]{:S(2)}) copy-start(f32[64,128]{1,0:T(8,128)} %refs_5_.1) | copy-start | bytes 98308
  2.4 8.6 %collective-permute-start.1 = (bf16[912,128]{1,0:T(8,128)(2,1)}, bf16[912,128]{1,0:T(8,128)(2,1)S(1)}, u32[]{:S(2)}, u32[]{:S(2)}) collective-permute-start(bf16[912,128]{1,0:T(8,128)(2,1)} %get-tuple-element.38), channel_id=1, source_target_pairs={{1,2},{2,1},{5,6},{6,5},{9,10},{10,9},{13,14},{14,13},{17,18},{18,... | collective-permute-start | bytes 700424 | tf_op jit(solution)/shard_map/ppermute | solution.py:22
  14.2 10.0 %collective-permute-start.4 = (f32[64,128]{1,0:T(8,128)S(1)}, f32[64,128]{1,0:T(8,128)S(1)}, u32[]{:S(2)}, u32[]{:S(2)}) collective-permute-start(f32[64,128]{1,0:T(8,128)S(1)} %get-tuple-element.45), channel_id=1, source_target_pairs={{0,12},{1,13},{2,14},{3,15},{16,28},{17,29},{18,30},{19,31}} | collective-permute-start | bytes 98312 | tf_op jit(solution)/shard_map/ppermute | solution.py:28
  20.0 4.2 %collective-permute-start.3 = (f32[64,128]{1,0:T(8,128)S(1)}, f32[64,128]{1,0:T(8,128)S(1)}, u32[]{:S(2)}, u32[]{:S(2)}) collective-permute-start(f32[64,128]{1,0:T(8,128)S(1)} %get-tuple-element.45), channel_id=1, source_target_pairs={{0,8},{4,12},{1,9},{5,13},{2,10},{6,14},{3,11},{7,15},{16,24},{20,... | collective-permute-start | bytes 98312 | tf_op jit(solution)/shard_map/ppermute | solution.py:28
  21.3 3.2 %collective-permute-start.2 = (f32[64,128]{1,0:T(8,128)S(1)}, f32[64,128]{1,0:T(8,128)S(1)}, u32[]{:S(2)}, u32[]{:S(2)}) collective-permute-start(f32[64,128]{1,0:T(8,128)S(1)} %get-tuple-element.45), channel_id=1, source_target_pairs={{0,4},{4,8},{8,12},{1,5},{5,9},{9,13},{2,6},{6,10},{10,14},{3,7},{... | collective-permute-start | bytes 98312 | tf_op jit(solution)/shard_map/ppermute | solution.py:28
  25.0 4.3 %collective-permute-start.6 = (bf16[64,16,128]{2,1,0:T(8,128)(2,1)S(1)}, bf16[64,16,128]{2,1,0:T(8,128)(2,1)S(1)}, u32[]{:S(2)}, u32[]{:S(2)}) collective-permute-start(bf16[64,16,128]{2,1,0:T(8,128)(2,1)S(1)} %get-tuple-element.48.own.refs_4_), channel_id=1, source_target_pairs={{0,1},{1,0},{2,3},{3,2},{4,5},{5,4},{6,7},{7,6},{8,9},{9,8},{10,11... | collective-permute-start | bytes 786440 | tf_op jit(solution)/shard_map/ppermute | solution.py:22
  25.1 7.5 %collective-permute-start.5 = (bf16[48,16,128]{2,1,0:T(8,128)(2,1)S(1)}, bf16[48,16,128]{2,1,0:T(8,128)(2,1)S(1)}, u32[]{:S(2)}, u32[]{:S(2)}) collective-permute-start(bf16[48,16,128]{2,1,0:T(8,128)(2,1)S(1)} %get-tuple-element.49), channel_id=1, source_target_pairs={{1,2},{2,1},{5,6},{6,5},{9,10},{10,9},{13,14},{14,13},{17,18},{18,... | collective-permute-start | bytes 589832 | tf_op jit(solution)/shard_map/ppermute | solution.py:22
  36.4 7.2 %collective-permute-start.9 = (f32[64,128]{1,0:T(8,128)S(1)}, f32[64,128]{1,0:T(8,128)S(1)}, u32[]{:S(2)}, u32[]{:S(2)}) collective-permute-start(f32[64,128]{1,0:T(8,128)S(1)} %get-tuple-element.55), channel_id=1, source_target_pairs={{0,12},{1,13},{2,14},{3,15},{16,28},{17,29},{18,30},{19,31}} | collective-permute-start | bytes 98312 | tf_op jit(solution)/shard_map/ppermute | solution.py:28
  39.1 4.4 %collective-permute-start.8 = (f32[64,128]{1,0:T(8,128)S(1)}, f32[64,128]{1,0:T(8,128)S(1)}, u32[]{:S(2)}, u32[]{:S(2)}) collective-permute-start(f32[64,128]{1,0:T(8,128)S(1)} %get-tuple-element.55), channel_id=1, source_target_pairs={{0,8},{4,12},{1,9},{5,13},{2,10},{6,14},{3,11},{7,15},{16,24},{20,... | collective-permute-start | bytes 98312 | tf_op jit(solution)/shard_map/ppermute | solution.py:28
  40.4 3.2 %collective-permute-start.7 = (f32[64,128]{1,0:T(8,128)S(1)}, f32[64,128]{1,0:T(8,128)S(1)}, u32[]{:S(2)}, u32[]{:S(2)}) collective-permute-start(f32[64,128]{1,0:T(8,128)S(1)} %get-tuple-element.55), channel_id=1, source_target_pairs={{0,4},{4,8},{8,12},{1,5},{5,9},{9,13},{2,6},{6,10},{10,14},{3,7},{... | collective-permute-start | bytes 98312 | tf_op jit(solution)/shard_map/ppermute | solution.py:28
  44.3 4.9 %collective-permute-start.11 = (bf16[48,16,128]{2,1,0:T(8,128)(2,1)S(1)}, bf16[48,16,128]{2,1,0:T(8,128)(2,1)S(1)}, u32[]{:S(2)}, u32[]{:S(2)}) collective-permute-start(bf16[48,16,128]{2,1,0:T(8,128)(2,1)S(1)} %get-tuple-element.60), channel_id=1, source_target_pairs={{0,1},{1,0},{2,3},{3,2},{4,5},{5,4},{6,7},{7,6},{8,9},{9,8},{10,11... | collective-permute-start | bytes 589832 | tf_op jit(solution)/shard_map/ppermute | solution.py:22
  44.3 8.1 %collective-permute-start.10 = (bf16[40,16,128]{2,1,0:T(8,128)(2,1)S(1)}, bf16[40,16,128]{2,1,0:T(8,128)(2,1)S(1)}, u32[]{:S(2)}, u32[]{:S(2)}) collective-permute-start(bf16[40,16,128]{2,1,0:T(8,128)(2,1)S(1)} %get-tuple-element.59), channel_id=1, source_target_pairs={{1,2},{2,1},{5,6},{6,5},{9,10},{10,9},{13,14},{14,13},{17,18},{18,... | collective-permute-start | bytes 491528 | tf_op jit(solution)/shard_map/ppermute | solution.py:22

commit v13 on v12

--- a/solution.py
+++ b/solution.py
@@ -386,11 +386,19 @@
     put_pay(pay_odd, state, value, n, n)
 
 
+def coarse_points(corr, total, pk):
+    return product(split(corr).reshape(-1, 128), power(pk, 1)) + total[...]
+
+
 def enter_second_kernel(*refs):
-    *arrivals, starts, before, init, we, pk, state, pay_even, pay_odd, corr, y = refs
+    *arrivals, starts, total, before, init, we, pk, state, pay_even, pay_odd, corr, y = refs
     n = starts.shape[0]
     value = enter(arrivals, we, pk, y, n) + starts[...]
-    corr[...] = value
+
+    def keep(even):
+        corr[...] = value if even else coarse_points(value, total, pk)
+
+    by_parity(keep)
     old = before[...].astype(F32)
     y[...] = (value + (old[:, 0:8] + old[:, 8:16])).reshape(n * 8, 128)
     first = (lax.axis_index("tm") == 0).astype(F32)
@@ -474,14 +482,19 @@
         n = own.shape[0]
         origin = origin_of(even, False, n)
         full = 3 * n
-        points = product(split(corr[...]).reshape(-1, 128), power(pk, 1)) + total[...]
+        points = coarse_points(corr[...], total, pk) if even else corr[...]
         flip_tiles(flip3, points, 0)
         copies = [write_out(out, COARSEN - 1, flip3, 0, n, sems)]
         put_block(s0, own, got, even, n)
         for state in (s1, s2):
             state[full] = jnp.zeros((16, 128), BF16)
         table_copy.wait()
-        for k, src, dst, flip in ((0, s0, s1, flip0), (1, s1, s2, flip1), (2, s2, None, None)):
+        steps = [(0, s0, s1, flip0), (1, s1, s2, flip1)]
+        if even:
+            steps.append((2, s2, None, None))
+        else:
+            kept[...] = jnp.zeros_like(kept)
+        for k, src, dst, flip in steps:
             put_force(force, fe, pay, even, k, n)
             size = (5 - 2 * k) * REACH
             base = mirrored((2 + k) * REACH, size, full, even)
@@ -495,7 +508,8 @@
             else:
                 flip_tiles(flip, value, 0)
                 copies.append(write_out(out, k, flip, n - mine if even else 0, mine, sems))
-        put_strips((strip1, strip2), (s1, s2), full, even)
+        for strip, state, low, size in ((strip1, s1, 5 * REACH, 2 * REACH), (strip2, s2, 3 * REACH, 3 * REACH)):
+            strip[...] = state[pl.ds(mirrored(low, size, full, even), size)]
         for copy in copies:
             copy.wait()
 
@@ -512,18 +526,21 @@
         origin = origin_of(even, True, n)
         full = 3 * n
         put_far(s0, own, got, not even, n)
-        get_strips((strip1, strip2), (s1, s2), full, even)
+        for strip, state, low, size in ((strip1, s1, 5 * REACH, 2 * REACH), (strip2, s2, 3 * REACH, 3 * REACH)):
+            state[pl.ds(mirrored(low, size, full, even), size)] = strip[...]
+            state[full] = jnp.zeros((16, 128), BF16)
         copies = []
-        size = 3 * REACH
-        flip_tiles(flip2, kept[...], n - REACH if even else 0)
+        if even:
+            flip_tiles(flip2, kept[...], n - REACH)
         table_copy.wait()
         for k, src, dst, flip in ((0, s0, s1, flip0), (1, s1, s2, flip1), (2, s2, None, flip2)):
             put_force(force, fe, pay, not even, k, n)
-            base = mirrored((7 - k) * REACH, size, full, even)
+            size = 3 * REACH if even or dst is not None else n
+            base = mirrored(7 * REACH - k * REACH if size < n else n, size, full, even)
             value = apply_phi(src, idx, origin, w, base, size) + force_at(force, base, size)
             if dst is not None:
                 dst[pl.ds(base, size)] = split(value)
-            mine = (k + 1) * REACH
+            mine = min((k + 1) * REACH, size) if size < n else n
             value = value[size - mine :] if even else value[:mine]
             if dst is None:
                 flip_tiles(flip, value, 0 if even else n - mine)
@@ -654,7 +671,7 @@
     side = (COARSEN - 1) * REACH
     coarse, end_even, end_odd, corr = call(
         enter_second_kernel,
-        (*arrivals, starts, coarse, initial_state, we, pk),
+        (*arrivals, starts, total, coarse, initial_state, we, pk),
         (state, shape((side, 16, width), BF16), across(side), tiles),
         [rows],
     )
@@ -667,7 +684,7 @@
     out, *strips = call(
         third_early_kernel,
         (table_early, coarse, got_even, corr, total, fe, pay_even, w, pk),
-        (result, strip, strip, shape((REACH, 8, width), F32)),
+        (result, strip, shape((3 * REACH, 16, width), BF16), shape((REACH, 8, width), F32)),
         [smem, dma] + [spaces] * 3 + [force, flip(3), flip(2), vmem((8, n + 8, width), F32), dma((COARSEN,))],
         out_spaces="h",
         flops=step_flops * 9 * REACH,

time: 56 us -> 55.9 us (level)
  transfers between devices with their start and end apart: 12 -> 12, of which waited for: 3 -> 4; matrix products, arithmetic and copies ran while one was open for 0% -> 0% of each run, Pallas kernels for 20% -> 19%
where the time goes in v13:
time: 55.9 us; the launch traced here: 55.6 us
  starting transfers between devices  29.3 us (52%)
  Pallas kernels  24.8 us (44%)
  waiting for transfers between devices  1.07 us (2%)
    pallas_call x12, Pallas kernels, call(): pl.pallas_call(kernel, out_shape=outs, name=kernel.__name__, in_specs=spe...  24.8 us
    ppermute x6, starting transfers between devices, earlier(): lax.ppermute(value, 'tm', [(i, i + s) for i in range(count - s)])  15.7 us
    ppermute x6, starting transfers between devices, swapped(): return lax.ppermute(value, 'space', pairs)  13.5 us
  transfers between devices with their start and end apart: 12, of which 4 were waited for; matrix products, arithmetic and copies ran while one was open for 0% of the time, Pallas kernels for 19%

profile of v13, /device:TPU:1, one launch (start us, length us, event | category | flops | bytes accessed | tf_op | source)
XLA Modules:
  0.0 55.6 jit_solution(13901987453244615671)
XLA Ops:
  0.0 2.3 %pack_kernel.1 = (bf16[2064,128]{1,0:T(8,128)(2,1)}, bf16[912,128]{1,0:T(8,128)(2,1)}, bf16[912,128]{1,0:T(8,128)(2,1)}) custom-call(bf16[8,4,64,128]{3,2,1,0:T(8,128)(2,1)} %bitcast.4, f32[64,128]{1,0:T(8,128)} %refs_6_.1, s32[6,64]{1,0:T(8,128)} %bitcast.5, s32[6,64]{1,0:T(8,128)} %bitcast.6), custom_call_target="tpu_custom_call" | custom-call | flops 3000000000 | bytes 1555456 | tf_op jit(solution)/shard_map/pack_kernel/pallas_call | solution.py:565
  2.4 4.6 %collective-permute-start.1 = (bf16[912,128]{1,0:T(8,128)(2,1)}, bf16[912,128]{1,0:T(8,128)(2,1)S(1)}, u32[]{:S(2)}, u32[]{:S(2)}) collective-permute-start(bf16[912,128]{1,0:T(8,128)(2,1)} %get-tuple-element.38), channel_id=1, source_target_pairs={{1,2},{2,1},{5,6},{6,5},{9,10},{10,9},{13,14},{14,13},{17,18},{18,... | collective-permute-start | bytes 700424 | tf_op jit(solution)/shard_map/ppermute | solution.py:22
  7.1 1.5 %weight_kernel.1 = (bf16[896,256]{1,0:T(8,128)(2,1)S(1)}, bf16[1024,256]{1,0:T(8,128)(2,1)S(1)}, bf16[384,256]{1,0:T(8,128)(2,1)S(1)}) custom-call(f32[128,128]{1,0:T(8,128)S(1)} %copy-done.3, f32[6,128,128]{2,1,0:T(8,128)S(1)} %copy-done.2, f32[128,128]{1,0:T(8,128)S(1)} %copy-done.4), custom_call_target="tpu_custom_call" | custom-call | flops 1000000000 | bytes 1703936 | tf_op jit(solution)/shard_map/weight_kernel/pallas_call | solution.py:565
  8.7 1.9 %first_early_kernel.1 = (bf16[32,16,128]{2,1,0:T(8,128)(2,1)S(1)}, bf16[32,16,128]{2,1,0:T(8,128)(2,1)S(1)}, bf16[32,16,128]{2,1,0:T(8,128)(2,1)S(1)}, s32[8,128]{1,0:T(8,128)S(1)}) custom-call(bf16[2064,128]{1,0:T(8,128)(2,1)S(1)} %copy-done, f32[64,128]{1,0:T(8,128)S(1)} %copy-done.1, bf16[912,128]{1,0:T(8,128)(2,1)S(1)} %collective-permute-done.got.got_even.pay, ...), custom_call_target="tpu_custom_call" | custom-call | flops 704643072 | bytes 1650688 | tf_op jit(solution)/shard_map/first_early_kernel/pallas_call | solution.py:565
  10.6 0.4 collective-permute-done.1.got_odd.pay
  11.0 3.2 %first_late_kernel.1 = (f32[64,8,128]{2,1,0:T(8,128)S(1)}, f32[64,128]{1,0:T(8,128)S(1)}, s32[8,128]{1,0:T(8,128)S(1)}) custom-call(bf16[2064,128]{1,0:T(8,128)(2,1)S(1)} %copy-done, f32[64,128]{1,0:T(8,128)S(1)} %copy-done.1, bf16[912,128]{1,0:T(8,128)(2,1)S(1)} %collective-permute-done.got.got_even.pay, ...), custom_call_target="tpu_custom_call" | custom-call | flops 1409286144 | bytes 2703360 | tf_op jit(solution)/shard_map/first_late_kernel/pallas_call | solution.py:565
  14.2 5.8 %collective-permute-start.4 = (f32[64,128]{1,0:T(8,128)S(1)}, f32[64,128]{1,0:T(8,128)S(1)}, u32[]{:S(2)}, u32[]{:S(2)}) collective-permute-start(f32[64,128]{1,0:T(8,128)S(1)} %get-tuple-element.45), channel_id=1, source_target_pairs={{0,12},{1,13},{2,14},{3,15},{16,28},{17,29},{18,30},{19,31}} | collective-permute-start | bytes 98312 | tf_op jit(solution)/shard_map/ppermute | solution.py:28
  20.0 1.3 %collective-permute-start.3 = (f32[64,128]{1,0:T(8,128)S(1)}, f32[64,128]{1,0:T(8,128)S(1)}, u32[]{:S(2)}, u32[]{:S(2)}) collective-permute-start(f32[64,128]{1,0:T(8,128)S(1)} %get-tuple-element.45), channel_id=1, source_target_pairs={{0,8},{4,12},{1,9},{5,13},{2,10},{6,14},{3,11},{7,15},{16,24},{20,... | collective-permute-start | bytes 98312 | tf_op jit(solution)/shard_map/ppermute | solution.py:28
  21.3 2.2 %collective-permute-start.2 = (f32[64,128]{1,0:T(8,128)S(1)}, f32[64,128]{1,0:T(8,128)S(1)}, u32[]{:S(2)}, u32[]{:S(2)}) collective-permute-start(f32[64,128]{1,0:T(8,128)S(1)} %get-tuple-element.45), channel_id=1, source_target_pairs={{0,4},{4,8},{8,12},{1,5},{5,9},{9,13},{2,6},{6,10},{10,14},{3,7},{... | collective-permute-start | bytes 98312 | tf_op jit(solution)/shard_map/ppermute | solution.py:28
  23.5 0.7 %scan_kernel.1.refs_3_ = f32[64,8,128]{2,1,0:T(8,128)S(1)} custom-call(f32[64,8,128]{2,1,0:T(8,128)S(1)} %get-tuple-element.46.values.w1, bf16[1024,256]{1,0:T(8,128)(2,1)S(1)} %get-tuple-element.43.pk.refs_5_.refs_8_), custom_call_target="tpu_custom_call" | custom-call | flops 10000000 | bytes 1048576 | tf_op jit(solution)/shard_map/scan_kernel/pallas_call | solution.py:565
  24.2 0.3 collective-permute-done.2.refs_0_
  24.5 0.6 %enter_first_kernel.1 = (bf16[64,16,128]{2,1,0:T(8,128)(2,1)S(1)}, bf16[48,16,128]{2,1,0:T(8,128)(2,1)S(1)}) custom-call(f32[64,128]{1,0:T(8,128)S(1)} %collective-permute-done.2.refs_0_, f32[64,128]{1,0:T(8,128)S(1)} %collective-permute-done.3.refs_1_, f32[64,128]{1,0:T(8,128)S(1)} %collective-permute-done.4.refs_2_, f32[64,8,128]{2,1,0:T(8,128)S(1)} %scan_kernel.1.refs_3_, ...), custom_call_target="tpu_custom_call" | custom-call | flops 10000000 | bytes 1540096 | tf_op jit(solution)/shard_map/enter_first_kernel/pallas_call | solution.py:565
  25.1 4.2 %collective-permute-start.5 = (bf16[48,16,128]{2,1,0:T(8,128)(2,1)S(1)}, bf16[48,16,128]{2,1,0:T(8,128)(2,1)S(1)}, u32[]{:S(2)}, u32[]{:S(2)}) collective-permute-start(bf16[48,16,128]{2,1,0:T(8,128)(2,1)S(1)} %get-tuple-element.49), channel_id=1, source_target_pairs={{1,2},{2,1},{5,6},{6,5},{9,10},{10,9},{13,14},{14,13},{17,18},{18,... | collective-permute-start | bytes 589832 | tf_op jit(solution)/shard_map/ppermute | solution.py:22
  29.3 3.1 %second_early_kernel.1 = (bf16[32,16,128]{2,1,0:T(8,128)(2,1)S(1)}, bf16[32,16,128]{2,1,0:T(8,128)(2,1)S(1)}, bf16[32,16,128]{2,1,0:T(8,128)(2,1)S(1)}, f32[64,8,128]{2,1,0:T(8,128)S(1)}) custom-call(s32[8,128]{1,0:T(8,128)S(1)} %get-tuple-element.50.table, bf16[64,16,128]{2,1,0:T(8,128)(2,1)S(1)} %get-tuple-element.48.own.refs_5_, ...), custom_call_target="tpu_custom_call" | custom-call | flops 1409286144 | bytes 2166784 | tf_op jit(solution)/shard_map/second_early_kernel/pallas_call | solution.py:565
  32.4 0.2 collective-permute-done.5.got
  32.6 3.7 %second_late_kernel.1 = (f32[64,8,128]{2,1,0:T(8,128)S(1)}, f32[64,128]{1,0:T(8,128)S(1)}) custom-call(s32[8,128]{1,0:T(8,128)S(1)} %get-tuple-element.44.table, bf16[64,16,128]{2,1,0:T(8,128)(2,1)S(1)} %get-tuple-element.48.own.refs_5_, bf16[48,16,128]{2,1,0:T(8,128)(2,1)S(1)} %collective-permute-done.5.got, ...), custom_call_target="tpu_custom_call" | custom-call | flops 1879048192 | bytes 2396160 | tf_op jit(solution)/shard_map/second_late_kernel/pallas_call | solution.py:565
  36.4 2.8 %collective-permute-start.9 = (f32[64,128]{1,0:T(8,128)S(1)}, f32[64,128]{1,0:T(8,128)S(1)}, u32[]{:S(2)}, u32[]{:S(2)}) collective-permute-start(f32[64,128]{1,0:T(8,128)S(1)} %get-tuple-element.55), channel_id=1, source_target_pairs={{0,12},{1,13},{2,14},{3,15},{16,28},{17,29},{18,30},{19,31}} | collective-permute-start | bytes 98312 | tf_op jit(solution)/shard_map/ppermute | solution.py:28
  39.1 1.3 %collective-permute-start.8 = (f32[64,128]{1,0:T(8,128)S(1)}, f32[64,128]{1,0:T(8,128)S(1)}, u32[]{:S(2)}, u32[]{:S(2)}) collective-permute-start(f32[64,128]{1,0:T(8,128)S(1)} %get-tuple-element.55), channel_id=1, source_target_pairs={{0,8},{4,12},{1,9},{5,13},{2,10},{6,14},{3,11},{7,15},{16,24},{20,... | collective-permute-start | bytes 98312 | tf_op jit(solution)/shard_map/ppermute | solution.py:28
  40.4 2.4 %collective-permute-start.7 = (f32[64,128]{1,0:T(8,128)S(1)}, f32[64,128]{1,0:T(8,128)S(1)}, u32[]{:S(2)}, u32[]{:S(2)}) collective-permute-start(f32[64,128]{1,0:T(8,128)S(1)} %get-tuple-element.55), channel_id=1, source_target_pairs={{0,4},{4,8},{8,12},{1,5},{5,9},{9,13},{2,6},{6,10},{10,14},{3,7},{... | collective-permute-start | bytes 98312 | tf_op jit(solution)/shard_map/ppermute | solution.py:28
  42.9 0.7 %scan_sum_kernel.1 = (f32[64,8,128]{2,1,0:T(8,128)S(1)}, f32[64,8,128]{2,1,0:T(8,128)S(1)}) custom-call(f32[64,8,128]{2,1,0:T(8,128)S(1)} %get-tuple-element.56.values, f32[64,8,128]{2,1,0:T(8,128)S(1)} %get-tuple-element.46.values.w1, f32[64,8,128]{2,1,0:T(8,128)S(1)} %get-tuple-element.54.coarse, bf16[1024,256]{1,0:T(8,128)(2,1)S(1)} %get-tuple-element.43.pk.refs_5_.refs_8_), custom_call_target="tpu_custom_call" | custom-call | flops 10000000 | bytes 1835008 | tf_op jit(solution)/shard_map/scan_sum_kernel/pallas_call | solution.py:565
  43.6 1.0 %enter_second_kernel.1 = (bf16[64,16,128]{2,1,0:T(8,128)(2,1)S(1)}, bf16[48,16,128]{2,1,0:T(8,128)(2,1)S(1)}, bf16[40,16,128]{2,1,0:T(8,128)(2,1)S(1)}, f32[64,8,128]{2,1,0:T(8,128)S(1)}) custom-call(f32[64,128]{1,0:T(8,128)S(1)} %collective-permute-done.7.refs_0_, f32[64,128]{1,0:T(8,128)S(1)} %collective-permute-done.8.refs_1_, ...), custom_call_target="tpu_custom_call" | custom-call | flops 10000000 | bytes 2523136 | tf_op jit(solution)/shard_map/enter_second_kernel/pallas_call | solution.py:565
  44.7 4.5 %collective-permute-start.10 = (bf16[40,16,128]{2,1,0:T(8,128)(2,1)S(1)}, bf16[40,16,128]{2,1,0:T(8,128)(2,1)S(1)}, u32[]{:S(2)}, u32[]{:S(2)}) collective-permute-start(bf16[40,16,128]{2,1,0:T(8,128)(2,1)S(1)} %get-tuple-element.60), channel_id=1, source_target_pairs={{1,2},{2,1},{5,6},{6,5},{9,10},{10,9},{13,14},{14,13},{17,18},{18,... | collective-permute-start | bytes 491528 | tf_op jit(solution)/shard_map/ppermute | solution.py:22
  49.2 2.9 %third_early_kernel.1 = (f32[8,4,64,128]{3,2,1,0:T(8,128)}, bf16[32,16,128]{2,1,0:T(8,128)(2,1)S(1)}, bf16[48,16,128]{2,1,0:T(8,128)(2,1)S(1)}, f32[16,8,128]{2,1,0:T(8,128)S(1)}) custom-call(s32[8,128]{1,0:T(8,128)S(1)} %get-tuple-element.50.table, bf16[64,16,128]{2,1,0:T(8,128)(2,1)S(1)} %get-tuple-element.59.own, ...), custom_call_target="tpu_custom_call" | custom-call | flops 1056964608 | bytes 4173824 | tf_op jit(solution)/shard_map/third_early_kernel/pallas_call | solution.py:565
  52.2 3.2 %third_late_kernel.1 = f32[8,4,64,128]{3,2,1,0:T(8,128)} custom-call(s32[8,128]{1,0:T(8,128)S(1)} %get-tuple-element.44.table, bf16[64,16,128]{2,1,0:T(8,128)(2,1)S(1)} %get-tuple-element.59.own, bf16[40,16,128]{2,1,0:T(8,128)(2,1)S(1)} %collective-permute-done.10.got, ...), custom_call_target="tpu_custom_call", output_to_operand_aliasing={{}: (9, {})} | custom-call | flops 1056964608 | bytes 4141056 | tf_op jit(solution)/shard_map/third_late_kernel/pallas_call | solution.py:565
  (22 shorter events, 0.5 us)
Async XLA Ops:
  0.0 7.1 %copy-start.2 = (f32[6,128,128]{2,1,0:T(8,128)S(1)}, f32[6,128,128]{2,1,0:T(8,128)}, u32[]{:S(2)}) copy-start(f32[6,128,128]{2,1,0:T(8,128)} %faces.1) | copy-start | bytes 1179652
  0.0 7.1 %copy-start.3 = (f32[128,128]{1,0:T(8,128)S(1)}, f32[128,128]{1,0:T(8,128)}, u32[]{:S(2)}) copy-start(f32[128,128]{1,0:T(8,128)} %diag.1) | copy-start | bytes 196612
  0.0 7.1 %copy-start.4 = (f32[128,128]{1,0:T(8,128)S(1)}, f32[128,128]{1,0:T(8,128)}, u32[]{:S(2)}) copy-start(f32[128,128]{1,0:T(8,128)} %coarse.1) | copy-start | bytes 196612
  2.3 6.3 %collective-permute-start = (bf16[912,128]{1,0:T(8,128)(2,1)}, bf16[912,128]{1,0:T(8,128)(2,1)S(1)}, u32[]{:S(2)}, u32[]{:S(2)}) collective-permute-start(bf16[912,128]{1,0:T(8,128)(2,1)} %get-tuple-element.37), channel_id=1, source_target_pairs={{0,1},{1,0},{2,3},{3,2},{4,5},{5,4},{6,7},{7,6},{8,9},{9,8},{10,11... | collective-permute-start | bytes 700424 | tf_op jit(solution)/shard_map/ppermute | solution.py:22
  2.4 6.2 %copy-start = (bf16[2064,128]{1,0:T(8,128)(2,1)S(1)}, bf16[2064,128]{1,0:T(8,128)(2,1)}, u32[]{:S(2)}) copy-start(bf16[2064,128]{1,0:T(8,128)(2,1)} %get-tuple-element.36.fe) | copy-start | bytes 1585156
  2.4 6.2 %copy-start.1 = (f32[64,128]{1,0:T(8,128)S(1)}, f32[64,128]{1,0:T(8,128)}, u32[]{:S(2)}) copy-start(f32[64,128]{1,0:T(8,128)} %refs_6_.1) | copy-start | bytes 98308
  2.4 8.6 %collective-permute-start.1 = (bf16[912,128]{1,0:T(8,128)(2,1)}, bf16[912,128]{1,0:T(8,128)(2,1)S(1)}, u32[]{:S(2)}, u32[]{:S(2)}) collective-permute-start(bf16[912,128]{1,0:T(8,128)(2,1)} %get-tuple-element.38), channel_id=1, source_target_pairs={{1,2},{2,1},{5,6},{6,5},{9,10},{10,9},{13,14},{14,13},{17,18},{18,... | collective-permute-start | bytes 700424 | tf_op jit(solution)/shard_map/ppermute | solution.py:22
  14.2 10.0 %collective-permute-start.4 = (f32[64,128]{1,0:T(8,128)S(1)}, f32[64,128]{1,0:T(8,128)S(1)}, u32[]{:S(2)}, u32[]{:S(2)}) collective-permute-start(f32[64,128]{1,0:T(8,128)S(1)} %get-tuple-element.45), channel_id=1, source_target_pairs={{0,12},{1,13},{2,14},{3,15},{16,28},{17,29},{18,30},{19,31}} | collective-permute-start | bytes 98312 | tf_op jit(solution)/shard_map/ppermute | solution.py:28
  20.0 4.2 %collective-permute-start.3 = (f32[64,128]{1,0:T(8,128)S(1)}, f32[64,128]{1,0:T(8,128)S(1)}, u32[]{:S(2)}, u32[]{:S(2)}) collective-permute-start(f32[64,128]{1,0:T(8,128)S(1)} %get-tuple-element.45), channel_id=1, source_target_pairs={{0,8},{4,12},{1,9},{5,13},{2,10},{6,14},{3,11},{7,15},{16,24},{20,... | collective-permute-start | bytes 98312 | tf_op jit(solution)/shard_map/ppermute | solution.py:28
  21.3 3.2 %collective-permute-start.2 = (f32[64,128]{1,0:T(8,128)S(1)}, f32[64,128]{1,0:T(8,128)S(1)}, u32[]{:S(2)}, u32[]{:S(2)}) collective-permute-start(f32[64,128]{1,0:T(8,128)S(1)} %get-tuple-element.45), channel_id=1, source_target_pairs={{0,4},{4,8},{8,12},{1,5},{5,9},{9,13},{2,6},{6,10},{10,14},{3,7},{... | collective-permute-start | bytes 98312 | tf_op jit(solution)/shard_map/ppermute | solution.py:28
  25.0 4.2 %collective-permute-start.6 = (bf16[64,16,128]{2,1,0:T(8,128)(2,1)S(1)}, bf16[64,16,128]{2,1,0:T(8,128)(2,1)S(1)}, u32[]{:S(2)}, u32[]{:S(2)}) collective-permute-start(bf16[64,16,128]{2,1,0:T(8,128)(2,1)S(1)} %get-tuple-element.48.own.refs_5_), channel_id=1, source_target_pairs={{0,1},{1,0},{2,3},{3,2},{4,5},{5,4},{6,7},{7,6},{8,9},{9,8},{10,11... | collective-permute-start | bytes 786440 | tf_op jit(solution)/shard_map/ppermute | solution.py:22
  25.1 7.5 %collective-permute-start.5 = (bf16[48,16,128]{2,1,0:T(8,128)(2,1)S(1)}, bf16[48,16,128]{2,1,0:T(8,128)(2,1)S(1)}, u32[]{:S(2)}, u32[]{:S(2)}) collective-permute-start(bf16[48,16,128]{2,1,0:T(8,128)(2,1)S(1)} %get-tuple-element.49), channel_id=1, source_target_pairs={{1,2},{2,1},{5,6},{6,5},{9,10},{10,9},{13,14},{14,13},{17,18},{18,... | collective-permute-start | bytes 589832 | tf_op jit(solution)/shard_map/ppermute | solution.py:22
  36.4 7.2 %collective-permute-start.9 = (f32[64,128]{1,0:T(8,128)S(1)}, f32[64,128]{1,0:T(8,128)S(1)}, u32[]{:S(2)}, u32[]{:S(2)}) collective-permute-start(f32[64,128]{1,0:T(8,128)S(1)} %get-tuple-element.55), channel_id=1, source_target_pairs={{0,12},{1,13},{2,14},{3,15},{16,28},{17,29},{18,30},{19,31}} | collective-permute-start | bytes 98312 | tf_op jit(solution)/shard_map/ppermute | solution.py:28
  39.1 4.4 %collective-permute-start.8 = (f32[64,128]{1,0:T(8,128)S(1)}, f32[64,128]{1,0:T(8,128)S(1)}, u32[]{:S(2)}, u32[]{:S(2)}) collective-permute-start(f32[64,128]{1,0:T(8,128)S(1)} %get-tuple-element.55), channel_id=1, source_target_pairs={{0,8},{4,12},{1,9},{5,13},{2,10},{6,14},{3,11},{7,15},{16,24},{20,... | collective-permute-start | bytes 98312 | tf_op jit(solution)/shard_map/ppermute | solution.py:28
  40.4 3.2 %collective-permute-start.7 = (f32[64,128]{1,0:T(8,128)S(1)}, f32[64,128]{1,0:T(8,128)S(1)}, u32[]{:S(2)}, u32[]{:S(2)}) collective-permute-start(f32[64,128]{1,0:T(8,128)S(1)} %get-tuple-element.55), channel_id=1, source_target_pairs={{0,4},{4,8},{8,12},{1,5},{5,9},{9,13},{2,6},{6,10},{10,14},{3,7},{... | collective-permute-start | bytes 98312 | tf_op jit(solution)/shard_map/ppermute | solution.py:28
  44.6 4.6 %collective-permute-start.11 = (bf16[48,16,128]{2,1,0:T(8,128)(2,1)S(1)}, bf16[48,16,128]{2,1,0:T(8,128)(2,1)S(1)}, u32[]{:S(2)}, u32[]{:S(2)}) collective-permute-start(bf16[48,16,128]{2,1,0:T(8,128)(2,1)S(1)} %get-tuple-element.61), channel_id=1, source_target_pairs={{0,1},{1,0},{2,3},{3,2},{4,5},{5,4},{6,7},{7,6},{8,9},{9,8},{10,11... | collective-permute-start | bytes 589832 | tf_op jit(solution)/shard_map/ppermute | solution.py:22
  44.7 7.5 %collective-permute-start.10 = (bf16[40,16,128]{2,1,0:T(8,128)(2,1)S(1)}, bf16[40,16,128]{2,1,0:T(8,128)(2,1)S(1)}, u32[]{:S(2)}, u32[]{:S(2)}) collective-permute-start(bf16[40,16,128]{2,1,0:T(8,128)(2,1)S(1)} %get-tuple-element.60), channel_id=1, source_target_pairs={{1,2},{2,1},{5,6},{6,5},{9,10},{10,9},{13,14},{14,13},{17,18},{18,... | collective-permute-start | bytes 491528 | tf_op jit(solution)/shard_map/ppermute | solution.py:22

commit v14 on v13

--- a/solution.py
+++ b/solution.py
@@ -23,13 +23,7 @@
 
 
 def earlier(value):
-    count = lax.axis_size("tm")
-    if count <= 8:
-        return [lax.ppermute(value, "tm", [(i, i + s) for i in range(count - s)]) for s in range(1, count)]
-    every = lax.all_gather(value, "tm")
-    at = lax.axis_index("tm") - jnp.arange(1, count)
-    picked = jnp.where((at >= 0)[:, None, None], jnp.take(every, jnp.maximum(at, 0), axis=0), 0.0)
-    return [picked[s] for s in range(count - 1)]
+    return [lax.all_gather(value, "tm")]
 
 
 def split(u):
@@ -79,7 +73,8 @@
 
 
 def enter(arrivals, we, pk, y, n):
-    value = jnp.concatenate([a[...] for a in arrivals], axis=1)
+    (ends,) = arrivals
+    value = jnp.concatenate([ends[i] for i in range(ends.shape[0])], axis=1)
     entry = product_rows(split_rows(value), we[...])
     y[pl.ds(0, n, stride=8), :] = entry
     rows = split_rows(entry)
@@ -195,11 +190,14 @@
     for k in range(8):
         put_halves(pk.at[pl.ds(128 * (7 - k), 128)], powers[k])
 
+    t = lax.axis_index("tm")
+    we[...] = jnp.zeros_like(we)
+
     def body(k, current):
-        put_halves(we.at[pl.ds(pl.multiple_of(k * 128, 128), 128)], current)
+        put_halves(we.at[pl.ds(pl.multiple_of((t - 1 - k) * 128, 128), 128)], current)
         return mul(current, powers[8])
 
-    lax.fori_loop(0, we.shape[0] // 128, body, one)
+    lax.fori_loop(0, t, body, one)
 
 
 def put_force(dst, own, got, right, k, n):
@@ -619,7 +617,7 @@
         (
             shape((7 * width, 2 * width), BF16),
             shape((8 * width, 2 * width), BF16),
-            shape(((tm - 1) * width, 2 * width), BF16),
+            shape((tm * width, 2 * width), BF16),
         ),
         [],
         flops=10**9,

time: 55.9 us -> 65.5 us (1.17)
  blocking collectives: 0 us -> 21.7 us
  starting transfers between devices: 29.3 us -> 17.4 us
    all_gather x0 -> x2, blocking collectives: none -> 21.7 us  [earlier(): return [lax.all_gather(value, 'tm')]]
    ppermute x6 -> x0, starting transfers between devices: 15.7 us -> none  [earlier(): lax.ppermute(value, 'tm', [(i, i + s) for i in range(count - s)])]
    ppermute x6, starting transfers between devices: 13.5 us -> 17.4 us  [swapped(): return lax.ppermute(value, 'space', pairs)]
  transfers between devices with their start and end apart: 12 -> 6, of which waited for: 4 -> 3; matrix products, arithmetic and copies ran while one was open for 0% -> 0% of each run, Pallas kernels for 19% -> 14%
where the time goes in v14:
time: 65.5 us; the launch traced here: 65.3 us
  Pallas kernels  24.4 us (37%)
  blocking collectives  21.7 us (33%)
  starting transfers between devices  17.4 us (27%)
  waiting for transfers between devices  1.34 us (2%)
    pallas_call x12, Pallas kernels, call(): pl.pallas_call(kernel, out_shape=outs, name=kernel.__name__, in_specs=spe...  24.4 us
    all_gather x2, blocking collectives, earlier(): return [lax.all_gather(value, 'tm')]  21.7 us
    ppermute x6, starting transfers between devices, swapped(): return lax.ppermute(value, 'space', pairs)  17.4 us
    ppermute x6, waiting for transfers between devices, swapped(): return lax.ppermute(value, 'space', pairs)  1.34 us
  transfers between devices with their start and end apart: 6, of which 3 were waited for; matrix products, arithmetic and copies ran while one was open for 0% of the time, Pallas kernels for 14%

profile of v14, /device:TPU:1, one launch (start us, length us, event | category | flops | bytes accessed | tf_op | source)
XLA Modules:
  0.0 65.3 jit_solution(7319949210305759706)
XLA Ops:
  0.0 2.3 %pack_kernel.1 = (bf16[2064,128]{1,0:T(8,128)(2,1)}, bf16[912,128]{1,0:T(8,128)(2,1)}, bf16[912,128]{1,0:T(8,128)(2,1)}) custom-call(bf16[8,4,64,128]{3,2,1,0:T(8,128)(2,1)} %bitcast.8, f32[64,128]{1,0:T(8,128)} %refs_4_.1, s32[6,64]{1,0:T(8,128)} %bitcast.9, s32[6,64]{1,0:T(8,128)} %bitcast.10), custom_call_target="tpu_custom_call" | custom-call | flops 3000000000 | bytes 1555456 | tf_op jit(solution)/shard_map/pack_kernel/pallas_call | solution.py:563
  2.3 0.1 collective-permute-start
  2.4 4.6 %collective-permute-start.1 = (bf16[912,128]{1,0:T(8,128)(2,1)}, bf16[912,128]{1,0:T(8,128)(2,1)S(1)}, u32[]{:S(2)}, u32[]{:S(2)}) collective-permute-start(bf16[912,128]{1,0:T(8,128)(2,1)} %get-tuple-element.38), channel_id=1, source_target_pairs={{1,2},{2,1},{5,6},{6,5},{9,10},{10,9},{13,14},{14,13},{17,18},{18,... | collective-permute-start | bytes 700424 | tf_op jit(solution)/shard_map/ppermute | solution.py:22
  7.1 0.9 %weight_kernel.1 = (bf16[896,256]{1,0:T(8,128)(2,1)S(1)}, bf16[1024,256]{1,0:T(8,128)(2,1)S(1)}, bf16[512,256]{1,0:T(8,128)(2,1)S(1)}) custom-call(f32[128,128]{1,0:T(8,128)S(1)} %copy-done.3, f32[6,128,128]{2,1,0:T(8,128)S(1)} %copy-done.2, f32[128,128]{1,0:T(8,128)S(1)} %copy-done.4), custom_call_target="tpu_custom_call" | custom-call | flops 1000000000 | bytes 1769472 | tf_op jit(solution)/shard_map/weight_kernel/pallas_call | solution.py:563
  8.0 0.0 collective-permute-done.got.got_even.pay
  8.1 1.9 %first_early_kernel.1 = (bf16[32,16,128]{2,1,0:T(8,128)(2,1)S(1)}, bf16[32,16,128]{2,1,0:T(8,128)(2,1)S(1)}, bf16[32,16,128]{2,1,0:T(8,128)(2,1)S(1)}, s32[8,128]{1,0:T(8,128)S(1)}) custom-call(bf16[2064,128]{1,0:T(8,128)(2,1)S(1)} %copy-done, f32[64,128]{1,0:T(8,128)S(1)} %copy-done.1, bf16[912,128]{1,0:T(8,128)(2,1)S(1)} %collective-permute-done.got.got_even.pay, ...), custom_call_target="tpu_custom_call" | custom-call | flops 704643072 | bytes 1650688 | tf_op jit(solution)/shard_map/first_early_kernel/pallas_call | solution.py:563
  10.0 1.0 %collective-permute-done.1.got_odd.pay = bf16[912,128]{1,0:T(8,128)(2,1)S(1)} collective-permute-done((bf16[912,128]{1,0:T(8,128)(2,1)}, bf16[912,128]{1,0:T(8,128)(2,1)S(1)}, u32[]{:S(2)}, u32[]{:S(2)}) %collective-permute-start.1) | collective-permute-done | bytes 233504 | tf_op jit(solution)/shard_map/ppermute | solution.py:22
  11.0 3.1 %first_late_kernel.1 = (f32[64,8,128]{2,1,0:T(8,128)S(1)}, f32[64,128]{1,0:T(8,128)S(1)}, s32[8,128]{1,0:T(8,128)S(1)}) custom-call(bf16[2064,128]{1,0:T(8,128)(2,1)S(1)} %copy-done, f32[64,128]{1,0:T(8,128)S(1)} %copy-done.1, bf16[912,128]{1,0:T(8,128)(2,1)S(1)} %collective-permute-done.got.got_even.pay, ...), custom_call_target="tpu_custom_call" | custom-call | flops 1409286144 | bytes 2703360 | tf_op jit(solution)/shard_map/first_late_kernel/pallas_call | solution.py:563
  14.2 11.2 %all-gather = f32[256,128]{1,0:T(8,128)S(1)} all-gather(f32[64,128]{1,0:T(8,128)S(1)} %get-tuple-element.45), channel_id=2, replica_groups=mesh['groups'=2,'tm'=4,'space'=4] {'tm'}, dimensions={0}, use_global_device_ids=true | all-gather | bytes 163840 | tf_op jit(solution)/shard_map/all_gather | solution.py:26
  25.4 0.7 %scan_kernel.1.refs_1_ = f32[64,8,128]{2,1,0:T(8,128)S(1)} custom-call(f32[64,8,128]{2,1,0:T(8,128)S(1)} %get-tuple-element.46.values.w1, bf16[1024,256]{1,0:T(8,128)(2,1)S(1)} %get-tuple-element.43.pk.refs_3_.refs_6_), custom_call_target="tpu_custom_call" | custom-call | flops 10000000 | bytes 1048576 | tf_op jit(solution)/shard_map/scan_kernel/pallas_call | solution.py:563
  26.1 0.6 enter_first_kernel.1
  26.7 0.1 collective-permute-start.3
  26.8 6.0 %collective-permute-start.2 = (bf16[48,16,128]{2,1,0:T(8,128)(2,1)S(1)}, bf16[48,16,128]{2,1,0:T(8,128)(2,1)S(1)}, u32[]{:S(2)}, u32[]{:S(2)}) collective-permute-start(bf16[48,16,128]{2,1,0:T(8,128)(2,1)S(1)} %get-tuple-element.49), channel_id=1, source_target_pairs={{1,2},{2,1},{5,6},{6,5},{9,10},{10,9},{13,14},{14,13},{17,18},{18,... | collective-permute-start | bytes 589832 | tf_op jit(solution)/shard_map/ppermute | solution.py:22
  32.8 3.1 %second_early_kernel.1 = (bf16[32,16,128]{2,1,0:T(8,128)(2,1)S(1)}, bf16[32,16,128]{2,1,0:T(8,128)(2,1)S(1)}, bf16[32,16,128]{2,1,0:T(8,128)(2,1)S(1)}, f32[64,8,128]{2,1,0:T(8,128)S(1)}) custom-call(s32[8,128]{1,0:T(8,128)S(1)} %get-tuple-element.50.table, bf16[64,16,128]{2,1,0:T(8,128)(2,1)S(1)} %get-tuple-element.48.own.refs_3_, ...), custom_call_target="tpu_custom_call" | custom-call | flops 1409286144 | bytes 2166784 | tf_op jit(solution)/shard_map/second_early_kernel/pallas_call | solution.py:563
  35.9 0.2 collective-permute-done.2.got
  36.1 3.7 %second_late_kernel.1 = (f32[64,8,128]{2,1,0:T(8,128)S(1)}, f32[64,128]{1,0:T(8,128)S(1)}) custom-call(s32[8,128]{1,0:T(8,128)S(1)} %get-tuple-element.44.table, bf16[64,16,128]{2,1,0:T(8,128)(2,1)S(1)} %get-tuple-element.48.own.refs_3_, bf16[48,16,128]{2,1,0:T(8,128)(2,1)S(1)} %collective-permute-done.2.got, ...), custom_call_target="tpu_custom_call" | custom-call | flops 1879048192 | bytes 2396160 | tf_op jit(solution)/shard_map/second_late_kernel/pallas_call | solution.py:563
  39.8 0.7 %scan_sum_kernel.1 = (f32[64,8,128]{2,1,0:T(8,128)S(1)}, f32[64,8,128]{2,1,0:T(8,128)S(1)}) custom-call(f32[64,8,128]{2,1,0:T(8,128)S(1)} %get-tuple-element.56.values, f32[64,8,128]{2,1,0:T(8,128)S(1)} %get-tuple-element.46.values.w1, f32[64,8,128]{2,1,0:T(8,128)S(1)} %get-tuple-element.54.coarse, bf16[1024,256]{1,0:T(8,128)(2,1)S(1)} %get-tuple-element.43.pk.refs_3_.refs_6_), custom_call_target="tpu_custom_call" | custom-call | flops 10000000 | bytes 1835008 | tf_op jit(solution)/shard_map/scan_sum_kernel/pallas_call | solution.py:563
  40.5 10.5 %all-gather.1 = f32[256,128]{1,0:T(8,128)S(1)} all-gather(f32[64,128]{1,0:T(8,128)S(1)} %get-tuple-element.55), channel_id=3, replica_groups=mesh['groups'=2,'tm'=4,'space'=4] {'tm'}, dimensions={0}, use_global_device_ids=true | all-gather | bytes 163840 | tf_op jit(solution)/shard_map/all_gather | solution.py:26
  51.0 1.2 %enter_second_kernel.1 = (bf16[64,16,128]{2,1,0:T(8,128)(2,1)S(1)}, bf16[48,16,128]{2,1,0:T(8,128)(2,1)S(1)}, bf16[40,16,128]{2,1,0:T(8,128)(2,1)S(1)}, f32[64,8,128]{2,1,0:T(8,128)S(1)}) custom-call(f32[4,64,128]{2,1,0:T(8,128)S(1)} %bitcast.7, f32[64,8,128]{2,1,0:T(8,128)S(1)} %get-tuple-element.57.refs_1_, ...), custom_call_target="tpu_custom_call" | custom-call | flops 10000000 | bytes 2621440 | tf_op jit(solution)/shard_map/enter_second_kernel/pallas_call | solution.py:563
  52.2 0.1 collective-permute-start.5
  52.3 6.6 %collective-permute-start.4 = (bf16[40,16,128]{2,1,0:T(8,128)(2,1)S(1)}, bf16[40,16,128]{2,1,0:T(8,128)(2,1)S(1)}, u32[]{:S(2)}, u32[]{:S(2)}) collective-permute-start(bf16[40,16,128]{2,1,0:T(8,128)(2,1)S(1)} %get-tuple-element.60), channel_id=1, source_target_pairs={{1,2},{2,1},{5,6},{6,5},{9,10},{10,9},{13,14},{14,13},{17,18},{18,... | collective-permute-start | bytes 491528 | tf_op jit(solution)/shard_map/ppermute | solution.py:22
  58.9 2.9 %third_early_kernel.1 = (f32[8,4,64,128]{3,2,1,0:T(8,128)}, bf16[32,16,128]{2,1,0:T(8,128)(2,1)S(1)}, bf16[48,16,128]{2,1,0:T(8,128)(2,1)S(1)}, f32[16,8,128]{2,1,0:T(8,128)S(1)}) custom-call(s32[8,128]{1,0:T(8,128)S(1)} %get-tuple-element.50.table, bf16[64,16,128]{2,1,0:T(8,128)(2,1)S(1)} %get-tuple-element.59.own, ...), custom_call_target="tpu_custom_call" | custom-call | flops 1056964608 | bytes 4173824 | tf_op jit(solution)/shard_map/third_early_kernel/pallas_call | solution.py:563
  61.8 0.1 collective-permute-done.4.got
  61.9 3.2 %third_late_kernel.1 = f32[8,4,64,128]{3,2,1,0:T(8,128)} custom-call(s32[8,128]{1,0:T(8,128)S(1)} %get-tuple-element.44.table, bf16[64,16,128]{2,1,0:T(8,128)(2,1)S(1)} %get-tuple-element.59.own, bf16[40,16,128]{2,1,0:T(8,128)(2,1)S(1)} %collective-permute-done.4.got, ...), custom_call_target="tpu_custom_call", output_to_operand_aliasing={{}: (9, {})} | custom-call | flops 1056964608 | bytes 4141056 | tf_op jit(solution)/shard_map/third_late_kernel/pallas_call | solution.py:563
  (12 shorter events, 0.0 us)
Async XLA Ops:
  0.0 7.1 %copy-start.2 = (f32[6,128,128]{2,1,0:T(8,128)S(1)}, f32[6,128,128]{2,1,0:T(8,128)}, u32[]{:S(2)}) copy-start(f32[6,128,128]{2,1,0:T(8,128)} %faces.1) | copy-start | bytes 1179652
  0.0 7.1 %copy-start.3 = (f32[128,128]{1,0:T(8,128)S(1)}, f32[128,128]{1,0:T(8,128)}, u32[]{:S(2)}) copy-start(f32[128,128]{1,0:T(8,128)} %diag.1) | copy-start | bytes 196612
  0.0 7.1 %copy-start.4 = (f32[128,128]{1,0:T(8,128)S(1)}, f32[128,128]{1,0:T(8,128)}, u32[]{:S(2)}) copy-start(f32[128,128]{1,0:T(8,128)} %coarse.1) | copy-start | bytes 196612
  2.3 5.7 %collective-permute-start = (bf16[912,128]{1,0:T(8,128)(2,1)}, bf16[912,128]{1,0:T(8,128)(2,1)S(1)}, u32[]{:S(2)}, u32[]{:S(2)}) collective-permute-start(bf16[912,128]{1,0:T(8,128)(2,1)} %get-tuple-element.37), channel_id=1, source_target_pairs={{0,1},{1,0},{2,3},{3,2},{4,5},{5,4},{6,7},{7,6},{8,9},{9,8},{10,11... | collective-permute-start | bytes 700424 | tf_op jit(solution)/shard_map/ppermute | solution.py:22
  2.4 5.6 %copy-start = (bf16[2064,128]{1,0:T(8,128)(2,1)S(1)}, bf16[2064,128]{1,0:T(8,128)(2,1)}, u32[]{:S(2)}) copy-start(bf16[2064,128]{1,0:T(8,128)(2,1)} %get-tuple-element.36.fe) | copy-start | bytes 1585156
  2.4 5.6 %copy-start.1 = (f32[64,128]{1,0:T(8,128)S(1)}, f32[64,128]{1,0:T(8,128)}, u32[]{:S(2)}) copy-start(f32[64,128]{1,0:T(8,128)} %refs_4_.1) | copy-start | bytes 98308
  2.4 8.6 %collective-permute-start.1 = (bf16[912,128]{1,0:T(8,128)(2,1)}, bf16[912,128]{1,0:T(8,128)(2,1)S(1)}, u32[]{:S(2)}, u32[]{:S(2)}) collective-permute-start(bf16[912,128]{1,0:T(8,128)(2,1)} %get-tuple-element.38), channel_id=1, source_target_pairs={{1,2},{2,1},{5,6},{6,5},{9,10},{10,9},{13,14},{14,13},{17,18},{18,... | collective-permute-start | bytes 700424 | tf_op jit(solution)/shard_map/ppermute | solution.py:22
  26.7 6.1 %collective-permute-start.3 = (bf16[64,16,128]{2,1,0:T(8,128)(2,1)S(1)}, bf16[64,16,128]{2,1,0:T(8,128)(2,1)S(1)}, u32[]{:S(2)}, u32[]{:S(2)}) collective-permute-start(bf16[64,16,128]{2,1,0:T(8,128)(2,1)S(1)} %get-tuple-element.48.own.refs_3_), channel_id=1, source_target_pairs={{0,1},{1,0},{2,3},{3,2},{4,5},{5,4},{6,7},{7,6},{8,9},{9,8},{10,11... | collective-permute-start | bytes 786440 | tf_op jit(solution)/shard_map/ppermute | solution.py:22
  26.8 9.3 %collective-permute-start.2 = (bf16[48,16,128]{2,1,0:T(8,128)(2,1)S(1)}, bf16[48,16,128]{2,1,0:T(8,128)(2,1)S(1)}, u32[]{:S(2)}, u32[]{:S(2)}) collective-permute-start(bf16[48,16,128]{2,1,0:T(8,128)(2,1)S(1)} %get-tuple-element.49), channel_id=1, source_target_pairs={{1,2},{2,1},{5,6},{6,5},{9,10},{10,9},{13,14},{14,13},{17,18},{18,... | collective-permute-start | bytes 589832 | tf_op jit(solution)/shard_map/ppermute | solution.py:22
  52.2 6.6 %collective-permute-start.5 = (bf16[48,16,128]{2,1,0:T(8,128)(2,1)S(1)}, bf16[48,16,128]{2,1,0:T(8,128)(2,1)S(1)}, u32[]{:S(2)}, u32[]{:S(2)}) collective-permute-start(bf16[48,16,128]{2,1,0:T(8,128)(2,1)S(1)} %get-tuple-element.61), channel_id=1, source_target_pairs={{0,1},{1,0},{2,3},{3,2},{4,5},{5,4},{6,7},{7,6},{8,9},{9,8},{10,11... | collective-permute-start | bytes 589832 | tf_op jit(solution)/shard_map/ppermute | solution.py:22
  52.3 9.5 %collective-permute-start.4 = (bf16[40,16,128]{2,1,0:T(8,128)(2,1)S(1)}, bf16[40,16,128]{2,1,0:T(8,128)(2,1)S(1)}, u32[]{:S(2)}, u32[]{:S(2)}) collective-permute-start(bf16[40,16,128]{2,1,0:T(8,128)(2,1)S(1)} %get-tuple-element.60), channel_id=1, source_target_pairs={{1,2},{2,1},{5,6},{6,5},{9,10},{10,9},{13,14},{14,13},{17,18},{18,... | collective-permute-start | bytes 491528 | tf_op jit(solution)/shard_map/ppermute | solution.py:22

commit v15 on v13

--- a/solution.py
+++ b/solution.py
@@ -158,13 +158,13 @@
                 pay[pl.ds(at, width), :] = fe[pl.ds(begin, width), :]
         at += width
         rows_k = pl.ds(k * n * 8, n * 8 + (16 if k == COARSEN - 1 else 0))
-        results.append(pltpu.make_async_copy(fe.at[rows_k], fe_out.at[rows_k], out_sems.at[2 + k]))
-        results[-1].start()
         if k == COARSEN - 2:
             results.append(pltpu.make_async_copy(pay_odd, odd_out, out_sems.at[0]))
             results.append(pltpu.make_async_copy(pay_even, even_out, out_sems.at[1]))
             results[-2].start()
             results[-1].start()
+        results.append(pltpu.make_async_copy(fe.at[rows_k], fe_out.at[rows_k], out_sems.at[2 + k]))
+        results[-1].start()
     for result in results:
         result.wait()
 

time: 55.9 us -> 55.9 us (level)
  no operation moved by 1% of the time
where the time goes in v15:
time: 55.9 us; the launch traced here: 55.6 us
  starting transfers between devices  29.3 us (52%)
  Pallas kernels  24.8 us (44%)
  waiting for transfers between devices  1.08 us (2%)
    pallas_call x12, Pallas kernels, call(): pl.pallas_call(kernel, out_shape=outs, name=kernel.__name__, in_specs=spe...  24.8 us
    ppermute x6, starting transfers between devices, earlier(): lax.ppermute(value, 'tm', [(i, i + s) for i in range(count - s)])  15.7 us
    ppermute x6, starting transfers between devices, swapped(): return lax.ppermute(value, 'space', pairs)  13.6 us
  transfers between devices with their start and end apart: 12, of which 4 were waited for; matrix products, arithmetic and copies ran while one was open for 0% of the time, Pallas kernels for 19%

profile of v15, /device:TPU:1, one launch (start us, length us, event | category | flops | bytes accessed | tf_op | source)
XLA Modules:
  0.0 55.6 jit_solution(13653604037541696426)
XLA Ops:
  0.0 2.3 %pack_kernel.1 = (bf16[2064,128]{1,0:T(8,128)(2,1)}, bf16[912,128]{1,0:T(8,128)(2,1)}, bf16[912,128]{1,0:T(8,128)(2,1)}) custom-call(bf16[8,4,64,128]{3,2,1,0:T(8,128)(2,1)} %bitcast.4, f32[64,128]{1,0:T(8,128)} %refs_6_.1, s32[6,64]{1,0:T(8,128)} %bitcast.5, s32[6,64]{1,0:T(8,128)} %bitcast.6), custom_call_target="tpu_custom_call" | custom-call | flops 3000000000 | bytes 1555456 | tf_op jit(solution)/shard_map/pack_kernel/pallas_call | solution.py:565
  2.4 4.6 %collective-permute-start.1 = (bf16[912,128]{1,0:T(8,128)(2,1)}, bf16[912,128]{1,0:T(8,128)(2,1)S(1)}, u32[]{:S(2)}, u32[]{:S(2)}) collective-permute-start(bf16[912,128]{1,0:T(8,128)(2,1)} %get-tuple-element.38), channel_id=1, source_target_pairs={{1,2},{2,1},{5,6},{6,5},{9,10},{10,9},{13,14},{14,13},{17,18},{18,... | collective-permute-start | bytes 700424 | tf_op jit(solution)/shard_map/ppermute | solution.py:22
  7.1 1.5 %weight_kernel.1 = (bf16[896,256]{1,0:T(8,128)(2,1)S(1)}, bf16[1024,256]{1,0:T(8,128)(2,1)S(1)}, bf16[384,256]{1,0:T(8,128)(2,1)S(1)}) custom-call(f32[128,128]{1,0:T(8,128)S(1)} %copy-done.3, f32[6,128,128]{2,1,0:T(8,128)S(1)} %copy-done.2, f32[128,128]{1,0:T(8,128)S(1)} %copy-done.4), custom_call_target="tpu_custom_call" | custom-call | flops 1000000000 | bytes 1703936 | tf_op jit(solution)/shard_map/weight_kernel/pallas_call | solution.py:565
  8.7 1.9 %first_early_kernel.1 = (bf16[32,16,128]{2,1,0:T(8,128)(2,1)S(1)}, bf16[32,16,128]{2,1,0:T(8,128)(2,1)S(1)}, bf16[32,16,128]{2,1,0:T(8,128)(2,1)S(1)}, s32[8,128]{1,0:T(8,128)S(1)}) custom-call(bf16[2064,128]{1,0:T(8,128)(2,1)S(1)} %copy-done, f32[64,128]{1,0:T(8,128)S(1)} %copy-done.1, bf16[912,128]{1,0:T(8,128)(2,1)S(1)} %collective-permute-done.got.got_even.pay, ...), custom_call_target="tpu_custom_call" | custom-call | flops 704643072 | bytes 1650688 | tf_op jit(solution)/shard_map/first_early_kernel/pallas_call | solution.py:565
  10.6 0.4 collective-permute-done.1.got_odd.pay
  11.0 3.1 %first_late_kernel.1 = (f32[64,8,128]{2,1,0:T(8,128)S(1)}, f32[64,128]{1,0:T(8,128)S(1)}, s32[8,128]{1,0:T(8,128)S(1)}) custom-call(bf16[2064,128]{1,0:T(8,128)(2,1)S(1)} %copy-done, f32[64,128]{1,0:T(8,128)S(1)} %copy-done.1, bf16[912,128]{1,0:T(8,128)(2,1)S(1)} %collective-permute-done.got.got_even.pay, ...), custom_call_target="tpu_custom_call" | custom-call | flops 1409286144 | bytes 2703360 | tf_op jit(solution)/shard_map/first_late_kernel/pallas_call | solution.py:565
  14.2 5.8 %collective-permute-start.4 = (f32[64,128]{1,0:T(8,128)S(1)}, f32[64,128]{1,0:T(8,128)S(1)}, u32[]{:S(2)}, u32[]{:S(2)}) collective-permute-start(f32[64,128]{1,0:T(8,128)S(1)} %get-tuple-element.45), channel_id=1, source_target_pairs={{0,12},{1,13},{2,14},{3,15},{16,28},{17,29},{18,30},{19,31}} | collective-permute-start | bytes 98312 | tf_op jit(solution)/shard_map/ppermute | solution.py:28
  20.0 1.3 %collective-permute-start.3 = (f32[64,128]{1,0:T(8,128)S(1)}, f32[64,128]{1,0:T(8,128)S(1)}, u32[]{:S(2)}, u32[]{:S(2)}) collective-permute-start(f32[64,128]{1,0:T(8,128)S(1)} %get-tuple-element.45), channel_id=1, source_target_pairs={{0,8},{4,12},{1,9},{5,13},{2,10},{6,14},{3,11},{7,15},{16,24},{20,... | collective-permute-start | bytes 98312 | tf_op jit(solution)/shard_map/ppermute | solution.py:28
  21.3 2.2 %collective-permute-start.2 = (f32[64,128]{1,0:T(8,128)S(1)}, f32[64,128]{1,0:T(8,128)S(1)}, u32[]{:S(2)}, u32[]{:S(2)}) collective-permute-start(f32[64,128]{1,0:T(8,128)S(1)} %get-tuple-element.45), channel_id=1, source_target_pairs={{0,4},{4,8},{8,12},{1,5},{5,9},{9,13},{2,6},{6,10},{10,14},{3,7},{... | collective-permute-start | bytes 98312 | tf_op jit(solution)/shard_map/ppermute | solution.py:28
  23.5 0.7 %scan_kernel.1.refs_3_ = f32[64,8,128]{2,1,0:T(8,128)S(1)} custom-call(f32[64,8,128]{2,1,0:T(8,128)S(1)} %get-tuple-element.46.values.w1, bf16[1024,256]{1,0:T(8,128)(2,1)S(1)} %get-tuple-element.43.pk.refs_5_.refs_8_), custom_call_target="tpu_custom_call" | custom-call | flops 10000000 | bytes 1048576 | tf_op jit(solution)/shard_map/scan_kernel/pallas_call | solution.py:565
  24.2 0.3 collective-permute-done.2.refs_0_
  24.5 0.6 %enter_first_kernel.1 = (bf16[64,16,128]{2,1,0:T(8,128)(2,1)S(1)}, bf16[48,16,128]{2,1,0:T(8,128)(2,1)S(1)}) custom-call(f32[64,128]{1,0:T(8,128)S(1)} %collective-permute-done.2.refs_0_, f32[64,128]{1,0:T(8,128)S(1)} %collective-permute-done.3.refs_1_, f32[64,128]{1,0:T(8,128)S(1)} %collective-permute-done.4.refs_2_, f32[64,8,128]{2,1,0:T(8,128)S(1)} %scan_kernel.1.refs_3_, ...), custom_call_target="tpu_custom_call" | custom-call | flops 10000000 | bytes 1540096 | tf_op jit(solution)/shard_map/enter_first_kernel/pallas_call | solution.py:565
  25.1 4.2 %collective-permute-start.5 = (bf16[48,16,128]{2,1,0:T(8,128)(2,1)S(1)}, bf16[48,16,128]{2,1,0:T(8,128)(2,1)S(1)}, u32[]{:S(2)}, u32[]{:S(2)}) collective-permute-start(bf16[48,16,128]{2,1,0:T(8,128)(2,1)S(1)} %get-tuple-element.49), channel_id=1, source_target_pairs={{1,2},{2,1},{5,6},{6,5},{9,10},{10,9},{13,14},{14,13},{17,18},{18,... | collective-permute-start | bytes 589832 | tf_op jit(solution)/shard_map/ppermute | solution.py:22
  29.3 3.1 %second_early_kernel.1 = (bf16[32,16,128]{2,1,0:T(8,128)(2,1)S(1)}, bf16[32,16,128]{2,1,0:T(8,128)(2,1)S(1)}, bf16[32,16,128]{2,1,0:T(8,128)(2,1)S(1)}, f32[64,8,128]{2,1,0:T(8,128)S(1)}) custom-call(s32[8,128]{1,0:T(8,128)S(1)} %get-tuple-element.50.table, bf16[64,16,128]{2,1,0:T(8,128)(2,1)S(1)} %get-tuple-element.48.own.refs_5_, ...), custom_call_target="tpu_custom_call" | custom-call | flops 1409286144 | bytes 2166784 | tf_op jit(solution)/shard_map/second_early_kernel/pallas_call | solution.py:565
  32.4 0.2 collective-permute-done.5.got
  32.6 3.7 %second_late_kernel.1 = (f32[64,8,128]{2,1,0:T(8,128)S(1)}, f32[64,128]{1,0:T(8,128)S(1)}) custom-call(s32[8,128]{1,0:T(8,128)S(1)} %get-tuple-element.44.table, bf16[64,16,128]{2,1,0:T(8,128)(2,1)S(1)} %get-tuple-element.48.own.refs_5_, bf16[48,16,128]{2,1,0:T(8,128)(2,1)S(1)} %collective-permute-done.5.got, ...), custom_call_target="tpu_custom_call" | custom-call | flops 1879048192 | bytes 2396160 | tf_op jit(solution)/shard_map/second_late_kernel/pallas_call | solution.py:565
  36.4 2.8 %collective-permute-start.9 = (f32[64,128]{1,0:T(8,128)S(1)}, f32[64,128]{1,0:T(8,128)S(1)}, u32[]{:S(2)}, u32[]{:S(2)}) collective-permute-start(f32[64,128]{1,0:T(8,128)S(1)} %get-tuple-element.55), channel_id=1, source_target_pairs={{0,12},{1,13},{2,14},{3,15},{16,28},{17,29},{18,30},{19,31}} | collective-permute-start | bytes 98312 | tf_op jit(solution)/shard_map/ppermute | solution.py:28
  39.1 1.3 %collective-permute-start.8 = (f32[64,128]{1,0:T(8,128)S(1)}, f32[64,128]{1,0:T(8,128)S(1)}, u32[]{:S(2)}, u32[]{:S(2)}) collective-permute-start(f32[64,128]{1,0:T(8,128)S(1)} %get-tuple-element.55), channel_id=1, source_target_pairs={{0,8},{4,12},{1,9},{5,13},{2,10},{6,14},{3,11},{7,15},{16,24},{20,... | collective-permute-start | bytes 98312 | tf_op jit(solution)/shard_map/ppermute | solution.py:28
  40.4 2.4 %collective-permute-start.7 = (f32[64,128]{1,0:T(8,128)S(1)}, f32[64,128]{1,0:T(8,128)S(1)}, u32[]{:S(2)}, u32[]{:S(2)}) collective-permute-start(f32[64,128]{1,0:T(8,128)S(1)} %get-tuple-element.55), channel_id=1, source_target_pairs={{0,4},{4,8},{8,12},{1,5},{5,9},{9,13},{2,6},{6,10},{10,14},{3,7},{... | collective-permute-start | bytes 98312 | tf_op jit(solution)/shard_map/ppermute | solution.py:28
  42.8 0.7 %scan_sum_kernel.1 = (f32[64,8,128]{2,1,0:T(8,128)S(1)}, f32[64,8,128]{2,1,0:T(8,128)S(1)}) custom-call(f32[64,8,128]{2,1,0:T(8,128)S(1)} %get-tuple-element.56.values, f32[64,8,128]{2,1,0:T(8,128)S(1)} %get-tuple-element.46.values.w1, f32[64,8,128]{2,1,0:T(8,128)S(1)} %get-tuple-element.54.coarse, bf16[1024,256]{1,0:T(8,128)(2,1)S(1)} %get-tuple-element.43.pk.refs_5_.refs_8_), custom_call_target="tpu_custom_call" | custom-call | flops 10000000 | bytes 1835008 | tf_op jit(solution)/shard_map/scan_sum_kernel/pallas_call | solution.py:565
  43.6 1.0 %enter_second_kernel.1 = (bf16[64,16,128]{2,1,0:T(8,128)(2,1)S(1)}, bf16[48,16,128]{2,1,0:T(8,128)(2,1)S(1)}, bf16[40,16,128]{2,1,0:T(8,128)(2,1)S(1)}, f32[64,8,128]{2,1,0:T(8,128)S(1)}) custom-call(f32[64,128]{1,0:T(8,128)S(1)} %collective-permute-done.7.refs_0_, f32[64,128]{1,0:T(8,128)S(1)} %collective-permute-done.8.refs_1_, ...), custom_call_target="tpu_custom_call" | custom-call | flops 10000000 | bytes 2523136 | tf_op jit(solution)/shard_map/enter_second_kernel/pallas_call | solution.py:565
  44.7 4.5 %collective-permute-start.10 = (bf16[40,16,128]{2,1,0:T(8,128)(2,1)S(1)}, bf16[40,16,128]{2,1,0:T(8,128)(2,1)S(1)}, u32[]{:S(2)}, u32[]{:S(2)}) collective-permute-start(bf16[40,16,128]{2,1,0:T(8,128)(2,1)S(1)} %get-tuple-element.60), channel_id=1, source_target_pairs={{1,2},{2,1},{5,6},{6,5},{9,10},{10,9},{13,14},{14,13},{17,18},{18,... | collective-permute-start | bytes 491528 | tf_op jit(solution)/shard_map/ppermute | solution.py:22
  49.2 2.9 %third_early_kernel.1 = (f32[8,4,64,128]{3,2,1,0:T(8,128)}, bf16[32,16,128]{2,1,0:T(8,128)(2,1)S(1)}, bf16[48,16,128]{2,1,0:T(8,128)(2,1)S(1)}, f32[16,8,128]{2,1,0:T(8,128)S(1)}) custom-call(s32[8,128]{1,0:T(8,128)S(1)} %get-tuple-element.50.table, bf16[64,16,128]{2,1,0:T(8,128)(2,1)S(1)} %get-tuple-element.59.own, ...), custom_call_target="tpu_custom_call" | custom-call | flops 1056964608 | bytes 4173824 | tf_op jit(solution)/shard_map/third_early_kernel/pallas_call | solution.py:565
  52.2 3.2 %third_late_kernel.1 = f32[8,4,64,128]{3,2,1,0:T(8,128)} custom-call(s32[8,128]{1,0:T(8,128)S(1)} %get-tuple-element.44.table, bf16[64,16,128]{2,1,0:T(8,128)(2,1)S(1)} %get-tuple-element.59.own, bf16[40,16,128]{2,1,0:T(8,128)(2,1)S(1)} %collective-permute-done.10.got, ...), custom_call_target="tpu_custom_call", output_to_operand_aliasing={{}: (9, {})} | custom-call | flops 1056964608 | bytes 4141056 | tf_op jit(solution)/shard_map/third_late_kernel/pallas_call | solution.py:565
  (22 shorter events, 0.5 us)
Async XLA Ops:
  0.0 7.1 %copy-start.2 = (f32[6,128,128]{2,1,0:T(8,128)S(1)}, f32[6,128,128]{2,1,0:T(8,128)}, u32[]{:S(2)}) copy-start(f32[6,128,128]{2,1,0:T(8,128)} %faces.1) | copy-start | bytes 1179652
  0.0 7.1 %copy-start.3 = (f32[128,128]{1,0:T(8,128)S(1)}, f32[128,128]{1,0:T(8,128)}, u32[]{:S(2)}) copy-start(f32[128,128]{1,0:T(8,128)} %diag.1) | copy-start | bytes 196612
  0.0 7.1 %copy-start.4 = (f32[128,128]{1,0:T(8,128)S(1)}, f32[128,128]{1,0:T(8,128)}, u32[]{:S(2)}) copy-start(f32[128,128]{1,0:T(8,128)} %coarse.1) | copy-start | bytes 196612
  2.3 6.3 %collective-permute-start = (bf16[912,128]{1,0:T(8,128)(2,1)}, bf16[912,128]{1,0:T(8,128)(2,1)S(1)}, u32[]{:S(2)}, u32[]{:S(2)}) collective-permute-start(bf16[912,128]{1,0:T(8,128)(2,1)} %get-tuple-element.37), channel_id=1, source_target_pairs={{0,1},{1,0},{2,3},{3,2},{4,5},{5,4},{6,7},{7,6},{8,9},{9,8},{10,11... | collective-permute-start | bytes 700424 | tf_op jit(solution)/shard_map/ppermute | solution.py:22
  2.4 6.2 %copy-start = (bf16[2064,128]{1,0:T(8,128)(2,1)S(1)}, bf16[2064,128]{1,0:T(8,128)(2,1)}, u32[]{:S(2)}) copy-start(bf16[2064,128]{1,0:T(8,128)(2,1)} %get-tuple-element.36.fe) | copy-start | bytes 1585156
  2.4 6.2 %copy-start.1 = (f32[64,128]{1,0:T(8,128)S(1)}, f32[64,128]{1,0:T(8,128)}, u32[]{:S(2)}) copy-start(f32[64,128]{1,0:T(8,128)} %refs_6_.1) | copy-start | bytes 98308
  2.4 8.6 %collective-permute-start.1 = (bf16[912,128]{1,0:T(8,128)(2,1)}, bf16[912,128]{1,0:T(8,128)(2,1)S(1)}, u32[]{:S(2)}, u32[]{:S(2)}) collective-permute-start(bf16[912,128]{1,0:T(8,128)(2,1)} %get-tuple-element.38), channel_id=1, source_target_pairs={{1,2},{2,1},{5,6},{6,5},{9,10},{10,9},{13,14},{14,13},{17,18},{18,... | collective-permute-start | bytes 700424 | tf_op jit(solution)/shard_map/ppermute | solution.py:22
  14.2 10.0 %collective-permute-start.4 = (f32[64,128]{1,0:T(8,128)S(1)}, f32[64,128]{1,0:T(8,128)S(1)}, u32[]{:S(2)}, u32[]{:S(2)}) collective-permute-start(f32[64,128]{1,0:T(8,128)S(1)} %get-tuple-element.45), channel_id=1, source_target_pairs={{0,12},{1,13},{2,14},{3,15},{16,28},{17,29},{18,30},{19,31}} | collective-permute-start | bytes 98312 | tf_op jit(solution)/shard_map/ppermute | solution.py:28
  20.0 4.2 %collective-permute-start.3 = (f32[64,128]{1,0:T(8,128)S(1)}, f32[64,128]{1,0:T(8,128)S(1)}, u32[]{:S(2)}, u32[]{:S(2)}) collective-permute-start(f32[64,128]{1,0:T(8,128)S(1)} %get-tuple-element.45), channel_id=1, source_target_pairs={{0,8},{4,12},{1,9},{5,13},{2,10},{6,14},{3,11},{7,15},{16,24},{20,... | collective-permute-start | bytes 98312 | tf_op jit(solution)/shard_map/ppermute | solution.py:28
  21.3 3.2 %collective-permute-start.2 = (f32[64,128]{1,0:T(8,128)S(1)}, f32[64,128]{1,0:T(8,128)S(1)}, u32[]{:S(2)}, u32[]{:S(2)}) collective-permute-start(f32[64,128]{1,0:T(8,128)S(1)} %get-tuple-element.45), channel_id=1, source_target_pairs={{0,4},{4,8},{8,12},{1,5},{5,9},{9,13},{2,6},{6,10},{10,14},{3,7},{... | collective-permute-start | bytes 98312 | tf_op jit(solution)/shard_map/ppermute | solution.py:28
  25.0 4.3 %collective-permute-start.6 = (bf16[64,16,128]{2,1,0:T(8,128)(2,1)S(1)}, bf16[64,16,128]{2,1,0:T(8,128)(2,1)S(1)}, u32[]{:S(2)}, u32[]{:S(2)}) collective-permute-start(bf16[64,16,128]{2,1,0:T(8,128)(2,1)S(1)} %get-tuple-element.48.own.refs_5_), channel_id=1, source_target_pairs={{0,1},{1,0},{2,3},{3,2},{4,5},{5,4},{6,7},{7,6},{8,9},{9,8},{10,11... | collective-permute-start | bytes 786440 | tf_op jit(solution)/shard_map/ppermute | solution.py:22
  25.1 7.5 %collective-permute-start.5 = (bf16[48,16,128]{2,1,0:T(8,128)(2,1)S(1)}, bf16[48,16,128]{2,1,0:T(8,128)(2,1)S(1)}, u32[]{:S(2)}, u32[]{:S(2)}) collective-permute-start(bf16[48,16,128]{2,1,0:T(8,128)(2,1)S(1)} %get-tuple-element.49), channel_id=1, source_target_pairs={{1,2},{2,1},{5,6},{6,5},{9,10},{10,9},{13,14},{14,13},{17,18},{18,... | collective-permute-start | bytes 589832 | tf_op jit(solution)/shard_map/ppermute | solution.py:22
  36.4 7.2 %collective-permute-start.9 = (f32[64,128]{1,0:T(8,128)S(1)}, f32[64,128]{1,0:T(8,128)S(1)}, u32[]{:S(2)}, u32[]{:S(2)}) collective-permute-start(f32[64,128]{1,0:T(8,128)S(1)} %get-tuple-element.55), channel_id=1, source_target_pairs={{0,12},{1,13},{2,14},{3,15},{16,28},{17,29},{18,30},{19,31}} | collective-permute-start | bytes 98312 | tf_op jit(solution)/shard_map/ppermute | solution.py:28
  39.1 4.4 %collective-permute-start.8 = (f32[64,128]{1,0:T(8,128)S(1)}, f32[64,128]{1,0:T(8,128)S(1)}, u32[]{:S(2)}, u32[]{:S(2)}) collective-permute-start(f32[64,128]{1,0:T(8,128)S(1)} %get-tuple-element.55), channel_id=1, source_target_pairs={{0,8},{4,12},{1,9},{5,13},{2,10},{6,14},{3,11},{7,15},{16,24},{20,... | collective-permute-start | bytes 98312 | tf_op jit(solution)/shard_map/ppermute | solution.py:28
  40.4 3.2 %collective-permute-start.7 = (f32[64,128]{1,0:T(8,128)S(1)}, f32[64,128]{1,0:T(8,128)S(1)}, u32[]{:S(2)}, u32[]{:S(2)}) collective-permute-start(f32[64,128]{1,0:T(8,128)S(1)} %get-tuple-element.55), channel_id=1, source_target_pairs={{0,4},{4,8},{8,12},{1,5},{5,9},{9,13},{2,6},{6,10},{10,14},{3,7},{... | collective-permute-start | bytes 98312 | tf_op jit(solution)/shard_map/ppermute | solution.py:28
  44.6 4.6 %collective-permute-start.11 = (bf16[48,16,128]{2,1,0:T(8,128)(2,1)S(1)}, bf16[48,16,128]{2,1,0:T(8,128)(2,1)S(1)}, u32[]{:S(2)}, u32[]{:S(2)}) collective-permute-start(bf16[48,16,128]{2,1,0:T(8,128)(2,1)S(1)} %get-tuple-element.61), channel_id=1, source_target_pairs={{0,1},{1,0},{2,3},{3,2},{4,5},{5,4},{6,7},{7,6},{8,9},{9,8},{10,11... | collective-permute-start | bytes 589832 | tf_op jit(solution)/shard_map/ppermute | solution.py:22
  44.7 7.5 %collective-permute-start.10 = (bf16[40,16,128]{2,1,0:T(8,128)(2,1)S(1)}, bf16[40,16,128]{2,1,0:T(8,128)(2,1)S(1)}, u32[]{:S(2)}, u32[]{:S(2)}) collective-permute-start(bf16[40,16,128]{2,1,0:T(8,128)(2,1)S(1)} %get-tuple-element.60), channel_id=1, source_target_pairs={{1,2},{2,1},{5,6},{6,5},{9,10},{10,9},{13,14},{14,13},{17,18},{18,... | collective-permute-start | bytes 491528 | tf_op jit(solution)/shard_map/ppermute | solution.py:22
